TPU v7x, 32 devices: a whole 2x2x4 slice. The times are simulated.
32 devices in a mesh: dp: 8 (over z, x), tensor: 4 (over y, core).
Axes of the slice: x: 2, y: 2, z: 4, core: 2. Of those that a mesh axis runs over, the one named last changes fastest.
Arguments:
- hidden_in: bfloat16 [4096, 2048], P(('dp', 'tensor')), may hold values from -6 to 6
- out_grad: bfloat16 [4096, 2048], P(('dp', 'tensor')), may hold values from -6 to 6
- w_query: bfloat16 [2048, 2048], P('dp', 'tensor'), may hold values from -0.125 to 0.125
- w_key: bfloat16 [2048, 2048], P('dp', 'tensor'), may hold values from -0.125 to 0.125
- w_value: bfloat16 [2048, 2048], P('dp', 'tensor'), may hold values from -0.125 to 0.125
- w_out: bfloat16 [2048, 2048], P('dp', 'tensor'), may hold values from -0.125 to 0.125
- w_gate: bfloat16 [2048, 8192], P('dp', 'tensor'), may hold values from -0.125 to 0.125
- w_up: bfloat16 [2048, 8192], P('dp', 'tensor'), may hold values from -0.125 to 0.125
- w_down: bfloat16 [2048, 8192], P('dp', 'tensor'), may hold values from -0.0625 to 0.0625
- gains: float32 [4, 2048], replicated, may hold values from 0.25 to 1.75
- seg_ids: int32 [4096], P('dp'), may hold values from 0 to 63, as said below
- positions: int32 [4096], P('dp'), may hold values from 0 to 511, as said below
Outputs:
- hidden_out: bfloat16 [4096, 2048], P(('dp', 'tensor'))
- in_grad: float32 [4096, 2048], P(('dp', 'tensor'))
- w_query_grad: float32 [2048, 2048], P('dp', 'tensor')
- w_key_grad: float32 [2048, 2048], P('dp', 'tensor')
- w_value_grad: float32 [2048, 2048], P('dp', 'tensor')
- w_out_grad: float32 [2048, 2048], P('dp', 'tensor')
- w_gate_grad: float32 [2048, 8192], P('dp', 'tensor')
- w_up_grad: float32 [2048, 8192], P('dp', 'tensor')
- w_down_grad: float32 [2048, 8192], P('dp', 'tensor')
- gains_grad: float32 [4, 2048], replicated
Inputs may be any that keep to these rules, and one draw needn't show every extreme that they name: Within each sequence of 512 consecutive tokens, seg_ids start at 0 and never fall; each id marks one document; documents start only at tokens whose index within the sequence is a multiple of 8. positions count 0, 1, 2, ... from the first token of each document.
All inputs are finite; a program needn't handle non-finite values.
Results may differ from a plain program's by a relative error of at most 0.02.
Values may be sent and summed in bfloat16 or wider, within the bound.
No kernel may reach another device: no remote copies, remote signals or barrier semaphores. Data moves between devices by JAX's collectives and lax.ppermute only.
A program may use at most 320 MiB of HBM per device.

v0:
```python
import jax
import jax.numpy as jnp
from jax import lax
from jax.sharding import PartitionSpec as P

HEAD_DIM = 128


EPS = 1e-06
THETA = 500000.0
NEG = -1e30


def rope_tables(pos_row, head_dim):
    half_dim = head_dim // 2
    inverse = THETA ** (-(jnp.arange(half_dim, dtype=jnp.float32) * 2.0 / head_dim))
    angles = pos_row.astype(jnp.float32)[:, None] * inverse[None, :]
    return (jnp.cos(angles)[:, None, :], jnp.sin(angles)[:, None, :])


def rotate(values, cos_tab, sin_tab):
    half_dim = values.shape[-1] // 2
    first_half, second_half = (values[..., :half_dim], values[..., half_dim:])
    return jnp.concatenate(
        [
            first_half * cos_tab - second_half * sin_tab,
            second_half * cos_tab + first_half * sin_tab,
        ],
        -1,
    )


def unrotate(values, cos_tab, sin_tab):
    half_dim = values.shape[-1] // 2
    first_half, second_half = (values[..., :half_dim], values[..., half_dim:])
    return jnp.concatenate(
        [
            first_half * cos_tab + second_half * sin_tab,
            second_half * cos_tab - first_half * sin_tab,
        ],
        -1,
    )


def contract_cols(left_mat, right_mat):
    return lax.dot_general(
        left_mat, right_mat, (((1,), (1,)), ((), ())), preferred_element_type=jnp.float32
    )


def contract_rows(left_mat, right_mat):
    return lax.dot_general(
        left_mat, right_mat, (((0,), (0,)), ((), ())), preferred_element_type=jnp.float32
    )


def on_device(
    hidden_in,
    out_grad,
    w_query,
    w_key,
    w_value,
    w_out,
    w_gate,
    w_up,
    w_down,
    gains,
    seg_ids,
    positions,
):
    query_w, key_w, value_w, out_w, gate_w, up_w, down_w = (
        lax.all_gather(w_query, "dp", axis=0, tiled=True),
        lax.all_gather(w_key, "dp", axis=0, tiled=True),
        lax.all_gather(w_value, "dp", axis=0, tiled=True),
        lax.all_gather(w_out, "dp", axis=0, tiled=True),
        lax.all_gather(w_gate, "dp", axis=0, tiled=True),
        lax.all_gather(w_up, "dp", axis=0, tiled=True),
        lax.all_gather(w_down, "dp", axis=0, tiled=True),
    )
    seq_len = seg_ids.shape[0]
    model_width = hidden_in.shape[1]
    head_cols = w_query.shape[1]
    unit_cols = w_gate.shape[1]
    n_heads = head_cols // HEAD_DIM
    score_scale = HEAD_DIM ** (-0.5)
    offset = lax.axis_index("tensor") * head_cols
    gain_query = lax.dynamic_slice_in_dim(gains[0], offset, head_cols)
    gain_key = lax.dynamic_slice_in_dim(gains[1], offset, head_cols)
    cos_tab, sin_tab = rope_tables(positions, HEAD_DIM)
    x_rows = hidden_in.astype(jnp.float32)
    gathered = lax.all_gather(hidden_in, "tensor", axis=0, tiled=True)
    queries = jnp.dot(gathered, query_w, preferred_element_type=jnp.float32)
    key_proj = jnp.dot(gathered, key_w, preferred_element_type=jnp.float32)
    value_low = (
        jnp.dot(gathered, value_w, preferred_element_type=jnp.float32)
        .astype(jnp.bfloat16)
        .reshape(seq_len, n_heads, HEAD_DIM)
    )
    squares = lax.psum(
        jnp.stack([jnp.sum(queries * queries, -1), jnp.sum(key_proj * key_proj, -1)], 1), "tensor"
    )
    norm_query = lax.rsqrt(squares[:, 0:1] / model_width + EPS)
    norm_key = lax.rsqrt(squares[:, 1:2] / model_width + EPS)
    query_hat = queries * norm_query
    key_hat = key_proj * norm_key
    q_rot = rotate(
        (query_hat * gain_query).reshape(seq_len, n_heads, HEAD_DIM), cos_tab, sin_tab
    ).astype(jnp.bfloat16)
    k_rot = rotate(
        (key_hat * gain_key).reshape(seq_len, n_heads, HEAD_DIM), cos_tab, sin_tab
    ).astype(jnp.bfloat16)
    token_ids = jnp.arange(seq_len, dtype=jnp.int32)
    block_rows = min(512, seq_len)

    def block_scores(row_start):
        scores = (
            jnp.einsum("qhd,khd->hqk", q_rot, k_rot, preferred_element_type=jnp.float32)
            * score_scale
        )
        same_doc = (seg_ids[row_start : row_start + block_rows, None] == seg_ids[None, :]) & (
            token_ids[row_start : row_start + block_rows, None] >= token_ids[None, :]
        )
        return jnp.where(same_doc[None], scores, NEG)

    row_start = 0
    scores = block_scores(row_start)
    row_max = jnp.max(scores, -1, keepdims=True)
    exp_scores = jnp.exp(scores - row_max)
    row_total = jnp.sum(exp_scores, -1, keepdims=True)
    prob_low = (exp_scores / row_total).astype(jnp.bfloat16)
    attn_blocks = jnp.einsum(
        "hqk,khd->qhd", prob_low, value_low, preferred_element_type=jnp.float32
    ).astype(jnp.bfloat16)
    lse_blocks = row_max + jnp.log(row_total)
    attn_low = attn_blocks.reshape(seq_len, head_cols)
    attn_sum = lax.psum_scatter(
        contract_cols(attn_low, out_w), "tensor", scatter_dimension=0, tiled=True
    )
    norm_attn = lax.rsqrt(jnp.mean(attn_sum * attn_sum, -1, keepdims=True) + EPS)
    attn_hat = attn_sum * norm_attn
    resid = x_rows + attn_hat * gains[2]
    mlp_in = lax.all_gather(resid.astype(jnp.bfloat16), "tensor", axis=0, tiled=True)
    gate_proj = jnp.dot(mlp_in, gate_w, preferred_element_type=jnp.float32)
    up_proj = jnp.dot(mlp_in, up_w, preferred_element_type=jnp.float32)
    sig_gate = jax.nn.sigmoid(gate_proj)
    act_gate = gate_proj * sig_gate
    hidden_act = (act_gate * up_proj).astype(jnp.bfloat16)
    mlp_sum = lax.psum_scatter(
        contract_cols(hidden_act, down_w), "tensor", scatter_dimension=0, tiled=True
    )
    norm_mlp = lax.rsqrt(jnp.mean(mlp_sum * mlp_sum, -1, keepdims=True) + EPS)
    mlp_hat = mlp_sum * norm_mlp
    hidden_out = (resid + mlp_hat * gains[3]).astype(jnp.bfloat16)
    grad_out = out_grad.astype(jnp.float32)
    gain_post = jnp.sum(grad_out * mlp_hat, 0)
    scaled_grad = grad_out * gains[3]
    grad_mlp = norm_mlp * (
        scaled_grad - mlp_hat * jnp.mean(mlp_hat * scaled_grad, -1, keepdims=True)
    )
    grad_mlp_all = lax.all_gather(grad_mlp.astype(jnp.bfloat16), "tensor", axis=0, tiled=True)
    back_weights = (
        lax.all_gather(w_query, "dp", axis=0, tiled=True),
        lax.all_gather(w_key, "dp", axis=0, tiled=True),
        lax.all_gather(w_value, "dp", axis=0, tiled=True),
        lax.all_gather(w_out, "dp", axis=0, tiled=True),
        lax.all_gather(w_gate, "dp", axis=0, tiled=True),
        lax.all_gather(w_up, "dp", axis=0, tiled=True),
        lax.all_gather(w_down, "dp", axis=0, tiled=True),
    )
    query_w, key_w, value_w, out_w, gate_w, up_w, down_w = back_weights
    grad_act = jnp.dot(grad_mlp_all, down_w, preferred_element_type=jnp.float32)
    grad_gate = (grad_act * up_proj * (sig_gate * (1.0 + gate_proj * (1.0 - sig_gate)))).astype(
        jnp.bfloat16
    )
    grad_up = (grad_act * act_gate).astype(jnp.bfloat16)
    mlp_right = jnp.concatenate([grad_gate, grad_up], 1)
    grad_resid = grad_out + lax.psum_scatter(
        contract_cols(grad_gate, gate_w) + contract_cols(grad_up, up_w),
        "tensor",
        scatter_dimension=0,
        tiled=True,
    )
    gain_attn = jnp.sum(grad_resid * attn_hat, 0)
    scaled_grad = grad_resid * gains[2]
    grad_attn = norm_attn * (
        scaled_grad - attn_hat * jnp.mean(attn_hat * scaled_grad, -1, keepdims=True)
    )
    grad_attn_all = lax.all_gather(grad_attn.astype(jnp.bfloat16), "tensor", axis=0, tiled=True)
    grad_heads = (
        jnp.dot(grad_attn_all, out_w, preferred_element_type=jnp.float32)
        .astype(jnp.bfloat16)
        .reshape(seq_len, n_heads, HEAD_DIM)
    )
    row_start = 0
    scores = block_scores(row_start)
    prob_full = jnp.exp(scores - lse_blocks)
    prob_low = prob_full.astype(jnp.bfloat16)
    grad_prob = jnp.einsum(
        "qhd,khd->hqk", grad_heads, value_low, preferred_element_type=jnp.float32
    )
    row_dot = jnp.sum(prob_full * grad_prob, -1, keepdims=True)
    grad_scores = (prob_full * (grad_prob - row_dot)).astype(jnp.bfloat16)
    grad_q_blocks = (
        jnp.einsum("hqk,khd->qhd", grad_scores, k_rot, preferred_element_type=jnp.float32)
        * score_scale
    )
    grad_key_rot = (
        jnp.einsum("hqk,qhd->khd", grad_scores, q_rot, preferred_element_type=jnp.float32)
        * score_scale
    )
    grad_value = jnp.einsum(
        "hqk,qhd->khd", prob_low, grad_heads, preferred_element_type=jnp.float32
    )
    grad_value_low = grad_value.astype(jnp.bfloat16).reshape(seq_len, head_cols)
    grad_query_n = unrotate(grad_q_blocks, cos_tab, sin_tab).reshape(seq_len, head_cols)
    grad_key_n = unrotate(grad_key_rot, cos_tab, sin_tab).reshape(seq_len, head_cols)
    grad_query_hat = grad_query_n * gain_query
    grad_key_hat = grad_key_n * gain_key
    inner_sums = lax.psum(
        jnp.stack(
            [jnp.sum(query_hat * grad_query_hat, -1), jnp.sum(key_hat * grad_key_hat, -1)], 1
        ),
        "tensor",
    )
    grad_query_low = (
        norm_query * (grad_query_hat - query_hat * inner_sums[:, 0:1] / model_width)
    ).astype(jnp.bfloat16)
    grad_key_low = (norm_key * (grad_key_hat - key_hat * inner_sums[:, 1:2] / model_width)).astype(
        jnp.bfloat16
    )
    in_part = (
        contract_cols(grad_query_low, query_w)
        + contract_cols(grad_key_low, key_w)
        + contract_cols(grad_value_low, value_w)
    )
    in_grad = grad_resid + lax.psum_scatter(
        in_part.astype(jnp.bfloat16), "tensor", scatter_dimension=0, tiled=True
    ).astype(jnp.float32)
    gain_rows = jnp.zeros((4, model_width), jnp.float32)
    head_gains = jnp.stack([jnp.sum(grad_query_n * query_hat, 0), jnp.sum(grad_key_n * key_hat, 0)])
    gain_rows = lax.dynamic_update_slice(gain_rows, head_gains, (jnp.int32(0), offset))
    gain_rows = gain_rows.at[2].set(gain_attn).at[3].set(gain_post)
    gains_grad = lax.psum(gain_rows, ("dp", "tensor"))
    qkv_right = jnp.concatenate([grad_query_low, grad_key_low, grad_value_low], 1)
    pieces = [
        contract_rows(gathered, qkv_right),
        contract_rows(grad_attn_all, attn_low),
        contract_rows(mlp_in, mlp_right),
        contract_rows(grad_mlp_all, hidden_act),
    ]
    grad_stack = lax.psum_scatter(
        jnp.concatenate(pieces, 1).astype(jnp.bfloat16), "dp", scatter_dimension=0, tiled=True
    ).astype(jnp.float32)
    edges = [
        0,
        head_cols,
        2 * head_cols,
        3 * head_cols,
        4 * head_cols,
        4 * head_cols + unit_cols,
        4 * head_cols + 2 * unit_cols,
        4 * head_cols + 3 * unit_cols,
    ]
    parts_out = [grad_stack[:, edges[i] : edges[i + 1]] for i in range(7)]
    return (
        hidden_out,
        in_grad,
        parts_out[0],
        parts_out[1],
        parts_out[2],
        parts_out[3],
        parts_out[4],
        parts_out[5],
        parts_out[6],
        gains_grad,
    )


def solution(mesh):
    return jax.shard_map(
        on_device,
        mesh=mesh,
        in_specs=(
            P(("dp", "tensor"), None),
            P(("dp", "tensor"), None),
            P("dp", "tensor"),
            P("dp", "tensor"),
            P("dp", "tensor"),
            P("dp", "tensor"),
            P("dp", "tensor"),
            P("dp", "tensor"),
            P("dp", "tensor"),
            P(),
            P("dp"),
            P("dp"),
        ),
        out_specs=(
            P(("dp", "tensor"), None),
            P(("dp", "tensor"), None),
            P("dp", "tensor"),
            P("dp", "tensor"),
            P("dp", "tensor"),
            P("dp", "tensor"),
            P("dp", "tensor"),
            P("dp", "tensor"),
            P("dp", "tensor"),
            P(),
        ),
        check_vma=False,
    )
```

profile of v0, /device:TPU:0, one launch (start us, length us, event | category | flops | bytes accessed | tf_op | source)
XLA Modules:
  0.0 1519.6 jit_solution(9701611199392743199)
XLA Ops:
  12.3 1.7 fusion.30
  13.9 1.7 multiply_cosine_fusion
  15.7 19.2 %all-gather.12.cloned.1.call-done = bf16[512,2048]{1,0:T(8,128)(2,1)} async-done(((bf16[128,2048]{1,0:T(8,128)(2,1)}), bf16[512,2048]{1,0:T(8,128)(2,1)}) %all-gather.12.cloned.1.call-update) | async-done | bytes 2097168 | tf_op jit(solution)/shard_map/all_gather | solution.py:91
  34.9 51.4 %all-gather.16.cloned.1.call-done = bf16[2048,512]{1,0:T(8,128)(2,1)} async-done(((bf16[256,512]{1,0:T(8,128)(2,1)}), bf16[2048,512]{1,0:T(8,128)(2,1)}) %all-gather.16.cloned.1.call-update) | async-done | bytes 2097168 | tf_op jit(solution)/shard_map/all_gather | solution.py:72
  86.3 3.5 multiply_reduce_fusion.8
  89.9 46.4 %all-gather.18.cloned.1.call-done = bf16[2048,512]{1,0:T(8,128)(2,1)} async-done(((bf16[256,512]{1,0:T(8,128)(2,1)}), bf16[2048,512]{1,0:T(8,128)(2,1)}) %all-gather.18.cloned.1.call-update) | async-done | bytes 2097168 | tf_op jit(solution)/shard_map/all_gather | solution.py:73
  136.3 3.5 multiply_reduce_fusion.7
  139.8 5.7 psum.21
  146.9 1.4 copy.71
  149.5 1.4 copy.73
  150.9 2.4 copy.74
  153.3 1.9 subtract_convert_fusion.1
  156.0 1.4 fusion.47
  157.4 2.0 copy-done
  159.9 26.3 %all-gather.14.cloned.1.call-done = bf16[2048,512]{1,0:T(8,128)(2,1)} async-done(((bf16[256,512]{1,0:T(8,128)(2,1)}), bf16[2048,512]{1,0:T(8,128)(2,1)}) %all-gather.14.cloned.1.call-update) | async-done | bytes 2097168 | tf_op jit(solution)/shard_map/all_gather | solution.py:74
  186.2 3.0 convolution_convert_fusion.5
  190.3 45.7 %all-gather.20.cloned.1.call-done = bf16[2048,512]{1,0:T(8,128)(2,1)} async-done(((bf16[256,512]{1,0:T(8,128)(2,1)}), bf16[2048,512]{1,0:T(8,128)(2,1)}) %all-gather.20.cloned.1.call-update) | async-done | bytes 2097168 | tf_op jit(solution)/shard_map/all_gather | solution.py:75
  236.0 4.9 fusion.48
  241.7 42.4 %reduce-scatter.6.cloned.1.call-done = f32[128,2048]{1,0:T(8,128)} async-done(((f32[512,2048]{1,0:T(8,128)}), f32[128,2048]{1,0:T(8,128)}) %reduce-scatter.6.cloned.1.call-update) | async-done | bytes 1048592 | tf_op jit(solution)/shard_map/reduce_scatter | solution.py:136
  284.1 1.4 multiply_reduce_fusion.6
  285.5 2.3 fusion.31
  289.3 122.1 %all-gather.24.cloned.1.call-done = bf16[2048,2048]{1,0:T(8,128)(2,1)} async-done(((bf16[256,2048]{1,0:T(8,128)(2,1)}), bf16[2048,2048]{1,0:T(8,128)(2,1)}) %all-gather.24.cloned.1.call-update) | async-done | bytes 8388624 | tf_op jit(solution)/shard_map/all_gather | solution.py:76
  411.4 23.0 %all-gather.22.cloned.1.call-done = bf16[512,2048]{1,0:T(8,128)(2,1)} async-done(((bf16[128,2048]{1,0:T(8,128)(2,1)}), bf16[512,2048]{1,0:T(8,128)(2,1)}) %all-gather.22.cloned.1.call-update) | async-done | bytes 2097168 | tf_op jit(solution)/shard_map/all_gather | solution.py:142
  434.4 10.6 fusion.49
  445.1 116.7 %all-gather.26.cloned.1.call-done = bf16[2048,2048]{1,0:T(8,128)(2,1)} async-done(((bf16[256,2048]{1,0:T(8,128)(2,1)}), bf16[2048,2048]{1,0:T(8,128)(2,1)}) %all-gather.26.cloned.1.call-update) | async-done | bytes 8388624 | tf_op jit(solution)/shard_map/all_gather | solution.py:77
  561.7 10.8 multiply_convert_fusion.3
  572.5 114.6 %all-gather.28.cloned.1.call-done = bf16[2048,2048]{1,0:T(8,128)(2,1)} async-done(((bf16[256,2048]{1,0:T(8,128)(2,1)}), bf16[2048,2048]{1,0:T(8,128)(2,1)}) %all-gather.28.cloned.1.call-update) | async-done | bytes 8388624 | tf_op jit(solution)/shard_map/all_gather | solution.py:78
  687.1 10.6 fusion.50
  697.7 42.8 %reduce-scatter.8.cloned.1.call-done = f32[128,2048]{1,0:T(8,128)} async-done(((f32[512,2048]{1,0:T(8,128)}), f32[128,2048]{1,0:T(8,128)}) %reduce-scatter.8.cloned.1.call-update) | async-done | bytes 1048592 | tf_op jit(solution)/shard_map/reduce_scatter | solution.py:148
  740.5 1.4 multiply_reduce_fusion.5
  741.9 1.6 fusion.27
  743.5 2.3 fusion.26
  746.3 22.3 %all-gather.30.cloned.1.call-done = bf16[512,2048]{1,0:T(8,128)(2,1)} async-done(((bf16[128,2048]{1,0:T(8,128)(2,1)}), bf16[512,2048]{1,0:T(8,128)(2,1)}) %all-gather.30.cloned.1.call-update) | async-done | bytes 2097168 | tf_op jit(solution)/shard_map/all_gather | solution.py:160
  768.6 12.0 multiply_convert_fusion.1
  780.7 8.5 fusion.51
  789.2 9.5 convolution_add_fusion
  798.8 44.6 %reduce-scatter.10.cloned.1.call-done = f32[128,2048]{1,0:T(8,128)} async-done(((f32[512,2048]{1,0:T(8,128)}), f32[128,2048]{1,0:T(8,128)}) %reduce-scatter.10.cloned.1.call-update) | async-done | bytes 1048592 | tf_op jit(solution)/shard_map/reduce_scatter | solution.py:177
  843.4 1.6 multiply_reduce_fusion.1
  845.0 2.7 multiply_convert_fusion.6
  848.0 15.1 convolution_convert_fusion
  863.1 7.4 all-gather.32.cloned.1.call-done
  870.5 3.0 convolution_convert_fusion.4
  878.1 1.6 fusion.18
  880.8 1.9 pad_maximum_fusion.1
  882.7 2.6 copy.51
  885.3 2.5 copy.55
  887.9 1.5 fusion.28
  889.4 1.6 fusion.29
  891.0 6.1 psum.22
  897.1 1.6 multiply_convert_fusion.5
  898.7 1.5 multiply_convert_fusion.4
  900.2 1.3 fusion.52
  903.7 2.7 add_convert_fusion
  906.5 10.4 convolution_convert_fusion.1
  916.9 2.6 convolution_convert_fusion.3
  919.5 2.9 copy.59
  922.3 8.0 fusion
  930.3 8.7 copy.58
  939.0 22.2 %pad_maximum_fusion = bf16[2048,8192]{1,0:T(8,128)(2,1)} fusion(bf16[2048,2048]{1,0:T(8,128)(2,1)} %convolution_convert_fusion.1, bf16[2048,4096]{1,0:T(8,128)(2,1)} %convolution_convert_fusion, bf16[2048,512]{1,0:T(8,128)(2,1)S(1)} %copy.59, bf16[2048,1536]{1,0:T(8,128)(2,1)} %copy.58), kind=kLoop, calls=%fused_computation | loop fusion | flops 134217728 | bytes 67108864 | tf_op jit(solution)/shard_map/concatenate | solution.py:252
  961.6 43.8 %psum.23 = f32[4,2048]{1,0:T(4,128)} all-reduce(f32[4,2048]{1,0:T(4,128)S(1)} %scatter.9), channel_id=1, replica_groups=mesh['dp'=8,'tensor'=4] {'dp','tensor'}, use_global_device_ids=true, to_apply=%region_22.23 | all-reduce | flops 8192 | bytes 65536 | tf_op jit(solution)/shard_map/psum | solution.py:243
  1005.4 2.2 convert_add_fusion.1
  1007.6 499.2 %reduce-scatter.14.cloned.1.call-done = bf16[256,8192]{1,0:T(8,128)(2,1)} async-done(((bf16[2048,8192]{1,0:T(8,128)(2,1)}), bf16[256,8192]{1,0:T(8,128)(2,1)}) %reduce-scatter.14.cloned.1.call-update) | async-done | bytes 4194320 | tf_op jit(solution)/shard_map/reduce_scatter | solution.py:251
  1506.8 2.8 fusion.42
  1509.7 2.9 fusion.41
  (139 shorter events, 21.2 us)
Async XLA Ops:
  7.2 27.7 %all-gather.12.cloned.1.call-start = ((), (), s32[]{:S(2)}) async-start(), calls=%async_computation.5 | async-start | bytes 2621440 | tf_op jit(solution)/shard_map/all_gather | solution.py:91
  7.9 78.4 %all-gather.16.cloned.1.call-start = ((), (), s32[]{:S(2)}) async-start(), calls=%async_computation.7 | async-start | bytes 2359296 | tf_op jit(solution)/shard_map/all_gather | solution.py:72
  8.7 127.6 %all-gather.18.cloned.1.call-start = ((), (), s32[]{:S(2)}) async-start(), calls=%async_computation.8 | async-start | bytes 2359296 | tf_op jit(solution)/shard_map/all_gather | solution.py:73
  9.4 176.8 %all-gather.14.cloned.1.call-start = ((), (), s32[]{:S(2)}) async-start(), calls=%async_computation.6 | async-start | bytes 2359296 | tf_op jit(solution)/shard_map/all_gather | solution.py:74
  10.0 226.0 %all-gather.20.cloned.1.call-start = ((), (), s32[]{:S(2)}) async-start(), calls=%async_computation.9 | async-start | bytes 2359296 | tf_op jit(solution)/shard_map/all_gather | solution.py:75
  10.6 273.5 %reduce-scatter.6.cloned.1.call-start = ((), (), s32[]{:S(2)}) async-start(), calls=%async_computation.10 | async-start | bytes 5242880 | tf_op jit(solution)/shard_map/reduce_scatter | solution.py:136
  89.9 55.7 %copy-start.10 = (f32[512,512]{0,1:T(8,128)}, f32[512,512]{0,1:T(8,128)S(1)}, u32[]{:S(2)}) copy-start(f32[512,512]{0,1:T(8,128)S(1)} %get-tuple-element.82) | copy-start | bytes 3145732
  139.8 8.7 copy-start.8
  153.2 2.7 copy-start.30
  155.2 0.8 copy-start.13
  155.2 2.2 copy-start.15
  155.2 2.2 copy-start.17
  155.2 2.2 copy-start.19
  156.0 30.3 %copy-start.33 = (bf16[512,2048]{1,0:T(8,128)(2,1)S(1)}, bf16[512,2048]{1,0:T(8,128)(2,1)}, u32[]{:S(2)}) copy-start(bf16[512,2048]{1,0:T(8,128)(2,1)} %all-gather.12.cloned.1.call-done) | copy-start | bytes 6291460
  157.3 2.0 copy-start
  186.2 3.1 copy-start.1
  189.3 1.0 copy-start.31
  190.3 50.6 %copy-start.28 = (bf16[4,128,512]{2,1,0:T(8,128)(2,1)}, bf16[4,128,512]{2,1,0:T(8,128)(2,1)S(1)}, u32[]{:S(2)}) copy-start(bf16[4,128,512]{2,1,0:T(8,128)(2,1)S(1)} %fusion.21) | copy-start | bytes 1572868
  240.9 44.6 %copy-start.12 = (bf16[128,2048]{1,0:T(8,128)(2,1)S(1)}, bf16[128,2048]{1,0:T(8,128)(2,1)}, u32[]{:S(2)}) copy-start(bf16[128,2048]{1,0:T(8,128)(2,1)} %param.16) | copy-start | bytes 1572868
  240.9 170.5 %all-gather.24.cloned.1.call-start = ((), (), s32[]{:S(2)}) async-start(), calls=%async_computation.12 | async-start | bytes 9437184 | tf_op jit(solution)/shard_map/all_gather | solution.py:76
  241.7 192.7 %all-gather.22.cloned.1.call-start = ((), (), s32[]{:S(2)}) async-start(), calls=%async_computation.11 | async-start | bytes 2621440 | tf_op jit(solution)/shard_map/all_gather | solution.py:142
  287.8 274.0 %all-gather.26.cloned.1.call-start = ((), (), s32[]{:S(2)}) async-start(), calls=%async_computation.13 | async-start | bytes 9437184 | tf_op jit(solution)/shard_map/all_gather | solution.py:77
  288.5 398.6 %all-gather.28.cloned.1.call-start = ((), (), s32[]{:S(2)}) async-start(), calls=%async_computation.14 | async-start | bytes 9437184 | tf_op jit(solution)/shard_map/all_gather | solution.py:78
  289.1 451.4 %reduce-scatter.8.cloned.1.call-start = ((), (), s32[]{:S(2)}) async-start(), calls=%async_computation.15 | async-start | bytes 5242880 | tf_op jit(solution)/shard_map/reduce_scatter | solution.py:148
  434.4 127.3 %copy-start.34 = (bf16[512,2048]{1,0:T(8,128)(2,1)S(1)}, bf16[512,2048]{1,0:T(8,128)(2,1)}, u32[]{:S(2)}) copy-start(bf16[512,2048]{1,0:T(8,128)(2,1)} %all-gather.22.cloned.1.call-done) | copy-start | bytes 6291460
  697.6 44.3 %copy-start.6 = (bf16[128,2048]{1,0:T(8,128)(2,1)S(1)}, bf16[128,2048]{1,0:T(8,128)(2,1)}, u32[]{:S(2)}) copy-start(bf16[128,2048]{1,0:T(8,128)(2,1)} %param.17) | copy-start | bytes 1572868
  697.7 71.0 %all-gather.30.cloned.1.call-start = ((), (), s32[]{:S(2)}) async-start(), calls=%async_computation.16 | async-start | bytes 2621440 | tf_op jit(solution)/shard_map/all_gather | solution.py:160
  745.9 97.6 %reduce-scatter.10.cloned.1.call-start = ((), (), s32[]{:S(2)}) async-start(), calls=%async_computation.17 | async-start | bytes 5242880 | tf_op jit(solution)/shard_map/reduce_scatter | solution.py:177
  780.7 8.5 copy-start.36
  780.7 8.5 copy-start.37
  798.7 44.7 %copy-start.4 = (f32[128,2048]{1,0:T(8,128)S(1)}, f32[128,2048]{1,0:T(8,128)}, u32[]{:S(2)}) copy-start(f32[128,2048]{1,0:T(8,128)} %reduce-scatter.6.cloned.1.call-done) | copy-start | bytes 3145732
  798.7 46.3 %copy-start.5 = (f32[128,2048]{1,0:T(8,128)S(1)}, f32[128,2048]{1,0:T(8,128)}, u32[]{:S(2)}) copy-start(f32[128,2048]{1,0:T(8,128)} %reduce-scatter.8.cloned.1.call-done) | copy-start | bytes 3145732
  798.7 71.8 %all-gather.32.cloned.1.call-start = ((), (), s32[]{:S(2)}) async-start(), calls=%async_computation.18 | async-start | bytes 2621440 | tf_op jit(solution)/shard_map/all_gather | solution.py:188
  847.8 157.6 %reduce-scatter.12.cloned.1.call-start = ((), (), s32[]{:S(2)}) async-start(), calls=%async_computation.19 | async-start | bytes 2621440 | tf_op jit(solution)/shard_map/reduce_scatter | solution.py:236
  848.0 22.5 %copy-start.27 = (bf16[2048,512]{1,0:T(8,128)(2,1)S(1)}, bf16[2048,512]{1,0:T(8,128)(2,1)}, u32[]{:S(2)}) copy-start(bf16[2048,512]{1,0:T(8,128)(2,1)} %all-gather.20.cloned.1.call-done) | copy-start | bytes 6291460
  863.1 10.5 copy-start.32
  870.5 3.1 copy-start.2
  874.6 1.2 copy-start.18
  874.6 1.2 copy-start.20
  875.8 1.0 copy-start.14
  875.8 1.2 copy-start.16
  877.0 2.7 copy-start.22
  880.8 7.1 copy-start.9
  882.7 6.7 copy-start.11
  897.1 3.1 copy-start.25
  900.2 1.3 copy-start.21
  900.2 1.8 copy-start.26
  902.0 1.6 copy-start.23
  902.0 1.7 copy-start.24
  906.4 10.5 copy-start.29
  906.4 600.4 %reduce-scatter.14.cloned.1.call-start = ((), (), s32[]{:S(2)}) async-start(), calls=%async_computation.20 | async-start | bytes 37748736 | tf_op jit(solution)/shard_map/reduce_scatter | solution.py:251
  906.5 10.4 copy-start.35
  961.2 44.2 %copy-start.7 = (f32[128,2048]{1,0:T(8,128)S(1)}, f32[128,2048]{1,0:T(8,128)}, u32[]{:S(2)}) copy-start(f32[128,2048]{1,0:T(8,128)} %reduce-scatter.10.cloned.1.call-done) | copy-start | bytes 3145732
  1506.8 2.9 copy-start.3
Sparse Core Ops, SparseCore 0:
  9.6 25.2 all-gather.11
  37.0 49.2 all-gather.15
  88.5 47.7 all-gather.17
  138.3 47.9 all-gather.13
  188.2 47.7 all-gather.19
  241.1 42.9 reduce-scatter.5
  286.4 124.9 all-gather.23
  413.6 20.7 all-gather.21
  436.8 124.9 all-gather.25
  563.9 123.1 all-gather.27
  697.8 42.6 reduce-scatter.7
  746.0 22.5 all-gather.29
  798.9 44.4 reduce-scatter.9
  847.9 22.5 all-gather.31
  906.5 32.4 reduce-scatter.11
  961.4 545.3 reduce-scatter.13
where the time goes:
time: 1530 us; the launch traced here: 1520 us
  waiting for transfers between devices  1230 us (80%)
  matrix products  128 us (8%)
  blocking collectives  55.6 us (4%)
  other arithmetic  55 us (4%)
  local copies, waits for them, and re-layouts  35.2 us (2%)
    reduce_scatter x1, waiting for transfers between devices, on_device(): lax.psum_scatter(jnp.concatenate(pieces, 1).astype(jnp.bfloat16), 'dp', s...  499 us
    all_gather x1, waiting for transfers between devices, on_device(): lax.all_gather(w_gate, 'dp', axis=0, tiled=True)  122 us
    all_gather x1, waiting for transfers between devices, on_device(): lax.all_gather(w_up, 'dp', axis=0, tiled=True)  117 us
    all_gather x1, waiting for transfers between devices, on_device(): lax.all_gather(w_down, 'dp', axis=0, tiled=True)  115 us
    all_gather x1, waiting for transfers between devices, on_device(): lax.all_gather(w_query, 'dp', axis=0, tiled=True)  51.4 us
    all_gather x1, waiting for transfers between devices, on_device(): lax.all_gather(w_key, 'dp', axis=0, tiled=True)  46.4 us
    all_gather x1, waiting for transfers between devices, on_device(): lax.all_gather(w_out, 'dp', axis=0, tiled=True)  45.7 us
    reduce_scatter x1, waiting for transfers between devices, on_device(): lax.psum_scatter(contract_cols(grad_gate, gate_w) + contract_cols(grad_up...  44.6 us
  transfers between devices with their start and end apart: 16, of which 15 were waited for; matrix products, arithmetic and copies ran while one was open for 8% of the time, Pallas kernels for 0%

commit v1 on v0

v1 whole, which is shorter than its diff:
```python
import jax
import jax.numpy as jnp
from jax import lax
from jax.sharding import Mesh, PartitionSpec as P

HEAD_DIM = 128
EPS = 1e-06
THETA = 500000.0
NEG = -1e30
F32 = jnp.float32
BF16 = jnp.bfloat16


def dot_rows_cols(left, right):
    return jnp.dot(left, right, preferred_element_type=F32)


def contract_cols(left, right):
    return lax.dot_general(left, right, (((1,), (1,)), ((), ())), preferred_element_type=F32)


def contract_rows(left, right):
    return lax.dot_general(left, right, (((0,), (0,)), ((), ())), preferred_element_type=F32)


def swap(values, axis):
    return lax.ppermute(values, axis, [(0, 1), (1, 0)])


def pick(flag, yes, no):
    return jnp.where(flag, yes, no)


class Layout:
    def __init__(self, n_dp, n_tensor):
        self.dp_axes = tuple(f"d{i}" for i in range(n_dp.bit_length() - 1))
        self.tensor_axes = tuple(f"t{i}" for i in range(n_tensor.bit_length() - 1))
        self.col_axis = self.dp_axes[1]
        self.row_axes = tuple(a for a in self.dp_axes if a != self.col_axis)
        self.core, self.side = self.tensor_axes[1], self.tensor_axes[0]
        self.n_dp = n_dp
        self.n_bits = len(self.dp_axes)

    def shape_of(self):
        return (2,) * (len(self.dp_axes) + len(self.tensor_axes))

    def dp_mask(self, axis):
        return 1 << (self.n_bits - 1 - self.dp_axes.index(axis))

    def block_order(self):
        order = []
        for j in range(1 << len(self.row_axes)):
            block = 0
            for i, axis in enumerate(self.row_axes):
                if (j >> i) & 1:
                    block |= self.dp_mask(axis)
            order += [block, block | self.dp_mask(self.col_axis)]
        return order

    def flip_blocks(self, blocks):
        for axis in self.row_axes:
            flag, mask = lax.axis_index(axis) == 1, self.dp_mask(axis)
            blocks = [pick(flag, blocks[b ^ mask], blocks[b]) for b in range(len(blocks))]
        return blocks

    def to_relative(self, values):
        width = values.shape[-1] // self.n_dp
        blocks = [values[..., b * width : (b + 1) * width] for b in range(self.n_dp)]
        blocks = self.flip_blocks(blocks)
        return jnp.concatenate([blocks[b] for b in self.block_order()], -1)

    def from_relative(self, values):
        width = values.shape[-1] // self.n_dp
        blocks = [None] * self.n_dp
        for place, b in enumerate(self.block_order()):
            blocks[b] = values[..., place * width : (place + 1) * width]
        return jnp.concatenate(self.flip_blocks(blocks), -1)


def rope_tables(pos_row):
    half_dim = HEAD_DIM // 2
    inverse = THETA ** (-(jnp.arange(half_dim, dtype=F32) * 2.0 / HEAD_DIM))
    angles = pos_row.astype(F32)[..., None] * inverse
    return jnp.cos(angles)[..., None, :], jnp.sin(angles)[..., None, :]


def rotate(values, cos_tab, sin_tab):
    half_dim = values.shape[-1] // 2
    first, second = values[..., :half_dim], values[..., half_dim:]
    return jnp.concatenate(
        [first * cos_tab - second * sin_tab, second * cos_tab + first * sin_tab], -1
    )


def unrotate(values, cos_tab, sin_tab):
    half_dim = values.shape[-1] // 2
    first, second = values[..., :half_dim], values[..., half_dim:]
    return jnp.concatenate(
        [first * cos_tab + second * sin_tab, second * cos_tab - first * sin_tab], -1
    )


def block_program(lay):
    col, side, core = lay.col_axis, lay.side, lay.core

    def my(axis):
        return lax.axis_index(axis)

    def halve_columns(weight):
        half = weight.shape[1] // 2
        low, high = weight[:, :half], weight[:, half:]
        first = my(col) == 0
        got = swap(pick(first, high, low), col)
        mine = pick(first, low, high)
        return jnp.concatenate([pick(first, mine, got), pick(first, got, mine)], 0)

    def gather_rows(block):
        pieces = [block]
        for axis in lay.row_axes:
            pieces = pieces + [swap(piece, axis) for piece in pieces]
        return pieces

    def scatter_rows(pieces):
        for axis in reversed(lay.row_axes):
            half = len(pieces) // 2
            received = [swap(piece.astype(BF16), axis) for piece in pieces[half:]]
            pieces = [a.astype(F32) + b.astype(F32) for a, b in zip(pieces[:half], received)]
        (total,) = pieces
        half = total.shape[0] // 2
        top, bottom = total[:half], total[half:]
        first = my(col) == 0
        got = swap(pick(first, bottom, top).astype(BF16), col).astype(F32)
        mine = pick(first, top, bottom)
        return pick(first, mine, got), pick(first, got, mine)

    def gather_tokens(own):
        half = own.shape[0] // 2
        a0, b0 = own[:half], own[half:]
        a_side, b_col = swap(a0, side), swap(b0, col)
        a_col, a_both = swap(a0, col), swap(a_side, col)
        b_side, b_both = swap(b0, side), swap(b_col, side)
        mine = jnp.concatenate([a0, b0, a_side, b_side, a_col, b_col, a_both, b_both], 0)
        return jnp.concatenate([mine, swap(mine, core)], 0)

    def scatter_tokens(part):
        n = part.shape[0] // 2
        part = part[:n] + swap(part[n:].astype(BF16), core).astype(F32)
        half = n // 8
        a0, b0, a_side, b_side, a_col, b_col, a_both, b_both = (
            part[i * half : (i + 1) * half] for i in range(8)
        )

        def add(own, other, axis):
            return own + swap(other.astype(BF16), axis).astype(F32)

        a1 = add(a_side, a_both, col)
        a0 = add(a0, a_col, col)
        b1 = add(b_col, b_both, side)
        b0 = add(b0, b_side, side)
        return jnp.concatenate([add(a0, a1, side), add(b0, b1, col)], 0)

    def token_rows(values):
        quarters = values.reshape(4, -1)
        rows = [quarters[0:1], quarters[1:2], quarters[2:3], quarters[3:4]]
        for axis, mask in ((side, 2), (core, 1)):
            flag = my(axis) == 1
            rows = [pick(flag, rows[i ^ mask], rows[i]) for i in range(4)]
        own = jnp.concatenate(rows, 0)
        other = swap(own, col)
        order = [own[0:1], own[2:3], other[0:1], other[2:3], own[1:2], own[3:4], other[1:2], other[3:4]]
        return jnp.concatenate(order, 0)

    def add_all(values, axes):
        for axis in axes:
            values = values + swap(values, axis)
        return values

    def add_stats(rows):
        rows = rows.reshape(-1, 2, 2, 2, rows.shape[1] // 8)
        for dim, axis in ((1, core), (2, col), (3, side)):
            rows = rows + jnp.flip(swap(rows, axis), dim)
        return rows.reshape(rows.shape[0], -1)

    def on_device(
        hidden_in, out_grad, w_query, w_key, w_value, w_out, w_gate, w_up, w_down, gains, seg_ids, positions
    ):
        model_width = hidden_in.shape[1]
        head_cols = w_query.shape[1] // 2
        n_heads = head_cols // HEAD_DIM
        n_tokens = hidden_in.shape[0] * 8
        seq_len = n_tokens // 2
        score_scale = HEAD_DIM ** (-0.5)
        place = my(side) * 4 + my(core) * 2 + my(col)
        offset = place * head_cols
        gain_query = lax.dynamic_slice_in_dim(gains[0], offset, head_cols)
        gain_key = lax.dynamic_slice_in_dim(gains[1], offset, head_cols)
        gain_post = lay.to_relative(gains[2:4])
        gain_attn, gain_mlp = gain_post[0:1], gain_post[1:2]

        x_low = lay.to_relative(hidden_in)
        grad_out = lay.to_relative(out_grad).astype(F32)
        x_all = gather_tokens(x_low)

        qkv_pieces = gather_rows(
            jnp.concatenate([halve_columns(w) for w in (w_query, w_key, w_value)], 1)
        )
        out_pieces = gather_rows(halve_columns(w_out))
        gate_pieces = gather_rows(halve_columns(w_gate))
        up_pieces = gather_rows(halve_columns(w_up))
        down_pieces = gather_rows(halve_columns(w_down))
        n_pieces = len(qkv_pieces)
        piece = model_width // n_pieces
        qkv_w = jnp.concatenate(qkv_pieces, 0)
        out_w = jnp.concatenate(out_pieces, 0)
        gate_w = jnp.concatenate(gate_pieces, 0)
        up_w = jnp.concatenate(up_pieces, 0)
        down_w = jnp.concatenate(down_pieces, 0)

        pos_rows = token_rows(positions)
        seg_rows = token_rows(seg_ids)
        ids_rows = token_rows(jnp.arange(seq_len, dtype=jnp.int32))
        per = seq_len // 4

        def by_seq(rows):
            return rows.reshape(2, 2, 2 * per).transpose(1, 0, 2).reshape(2, seq_len)

        def heads_of(values):
            return (
                values.reshape(2, 2, 2 * per, n_heads, HEAD_DIM)
                .transpose(1, 0, 2, 3, 4)
                .reshape(2, seq_len, n_heads, HEAD_DIM)
            )

        def tokens_of(values):
            return (
                values.reshape(2, 2, 2 * per, n_heads, HEAD_DIM)
                .transpose(1, 0, 2, 3, 4)
                .reshape(n_tokens, head_cols)
            )

        seg_seq, ids_seq = by_seq(seg_rows), by_seq(ids_rows)
        cos_tab, sin_tab = rope_tables(by_seq(pos_rows))
        mask = (seg_seq[:, :, None] == seg_seq[:, None, :]) & (ids_seq[:, :, None] >= ids_seq[:, None, :])

        qkv = dot_rows_cols(x_all, qkv_w)
        queries, key_proj = qkv[:, :head_cols], qkv[:, head_cols : 2 * head_cols]
        value_low = heads_of(qkv[:, 2 * head_cols :].astype(BF16))
        squares = add_stats(
            jnp.stack([jnp.sum(queries * queries, -1), jnp.sum(key_proj * key_proj, -1)], 0)
        )
        norm_query = lax.rsqrt(squares[0] / model_width + EPS)[:, None]
        norm_key = lax.rsqrt(squares[1] / model_width + EPS)[:, None]
        query_hat = queries * norm_query
        key_hat = key_proj * norm_key
        q_rot = rotate(heads_of(query_hat * gain_query), cos_tab, sin_tab).astype(BF16)
        k_rot = rotate(heads_of(key_hat * gain_key), cos_tab, sin_tab).astype(BF16)
        scores = jnp.einsum("bqhd,bkhd->bhqk", q_rot, k_rot, preferred_element_type=F32) * score_scale
        scores = jnp.where(mask[:, None], scores, NEG)
        row_max = jnp.max(scores, -1, keepdims=True)
        exp_scores = jnp.exp(scores - row_max)
        row_total = jnp.sum(exp_scores, -1, keepdims=True)
        prob_full = exp_scores / row_total
        prob_low = prob_full.astype(BF16)
        attn_low = tokens_of(
            jnp.einsum("bhqk,bkhd->bqhd", prob_low, value_low, preferred_element_type=F32).astype(BF16)
        )
        attn_sum = scatter_tokens(contract_cols(attn_low, out_w))
        norm_attn = lax.rsqrt(jnp.mean(attn_sum * attn_sum, -1, keepdims=True) + EPS)
        attn_hat = attn_sum * norm_attn
        resid = x_low.astype(F32) + attn_hat * gain_attn

        mlp_in = gather_tokens(resid.astype(BF16))
        gate_proj = dot_rows_cols(mlp_in, gate_w)
        up_proj = dot_rows_cols(mlp_in, up_w)
        sig_gate = jax.nn.sigmoid(gate_proj)
        act_gate = gate_proj * sig_gate
        hidden_act = (act_gate * up_proj).astype(BF16)
        mlp_sum = jnp.concatenate(
            [scatter_tokens(contract_cols(hidden_act, piece_w)) for piece_w in down_pieces], 1
        )
        norm_mlp = lax.rsqrt(jnp.mean(mlp_sum * mlp_sum, -1, keepdims=True) + EPS)
        mlp_hat = mlp_sum * norm_mlp
        hidden_out = lay.from_relative((resid + mlp_hat * gain_mlp).astype(BF16))

        gain_row_mlp = jnp.sum(grad_out * mlp_hat, 0, keepdims=True)
        scaled = grad_out * gain_mlp
        grad_mlp = norm_mlp * (scaled - mlp_hat * jnp.mean(mlp_hat * scaled, -1, keepdims=True))
        grad_mlp_all = gather_tokens(grad_mlp.astype(BF16))

        def weight_grad(left, right):
            return [
                contract_rows(left[:, i * piece : (i + 1) * piece], right).astype(BF16) for i in range(n_pieces)
            ]

        down_out = scatter_rows(weight_grad(grad_mlp_all, hidden_act))
        grad_act = dot_rows_cols(grad_mlp_all, down_w)
        grad_gate = (grad_act * up_proj * (sig_gate * (1.0 + gate_proj * (1.0 - sig_gate)))).astype(BF16)
        grad_up = (grad_act * act_gate).astype(BF16)
        grad_resid = grad_out + scatter_tokens(contract_cols(grad_gate, gate_w) + contract_cols(grad_up, up_w))
        gate_out = scatter_rows(weight_grad(mlp_in, grad_gate))
        up_out = scatter_rows(weight_grad(mlp_in, grad_up))

        gain_row_attn = jnp.sum(grad_resid * attn_hat, 0, keepdims=True)
        scaled = grad_resid * gain_attn
        grad_attn = norm_attn * (scaled - attn_hat * jnp.mean(attn_hat * scaled, -1, keepdims=True))
        grad_attn_all = gather_tokens(grad_attn.astype(BF16))
        grad_heads = heads_of(dot_rows_cols(grad_attn_all, out_w).astype(BF16))
        out_grad_pieces = weight_grad(grad_attn_all, attn_low)
        grad_prob = jnp.einsum("bqhd,bkhd->bhqk", grad_heads, value_low, preferred_element_type=F32)
        row_dot = jnp.sum(prob_full * grad_prob, -1, keepdims=True)
        grad_scores = (prob_full * (grad_prob - row_dot)).astype(BF16)
        grad_q_rot = jnp.einsum("bhqk,bkhd->bqhd", grad_scores, k_rot, preferred_element_type=F32) * score_scale
        grad_k_rot = jnp.einsum("bhqk,bqhd->bkhd", grad_scores, q_rot, preferred_element_type=F32) * score_scale
        grad_value = jnp.einsum("bhqk,bqhd->bkhd", prob_low, grad_heads, preferred_element_type=F32)
        grad_value_low = tokens_of(grad_value.astype(BF16))
        grad_query_n = tokens_of(unrotate(grad_q_rot, cos_tab, sin_tab))
        grad_key_n = tokens_of(unrotate(grad_k_rot, cos_tab, sin_tab))
        grad_query_hat = grad_query_n * gain_query
        grad_key_hat = grad_key_n * gain_key
        inner = add_stats(
            jnp.stack([jnp.sum(query_hat * grad_query_hat, -1), jnp.sum(key_hat * grad_key_hat, -1)], 0)
        )
        grad_query_low = (norm_query * (grad_query_hat - query_hat * inner[0][:, None] / model_width)).astype(BF16)
        grad_key_low = (norm_key * (grad_key_hat - key_hat * inner[1][:, None] / model_width)).astype(BF16)
        qkv_right = jnp.concatenate([grad_query_low, grad_key_low, grad_value_low], 1)
        in_grad = grad_resid + scatter_tokens(contract_cols(qkv_right, qkv_w))
        qkv_grad_pieces = weight_grad(x_all, qkv_right)
        attn_a, attn_b = scatter_rows(
            [jnp.concatenate([a, b], 1) for a, b in zip(qkv_grad_pieces, out_grad_pieces)]
        )
        attn_outs = [
            jnp.concatenate(
                [attn_a[:, i * head_cols : (i + 1) * head_cols], attn_b[:, i * head_cols : (i + 1) * head_cols]], 1
            )
            for i in range(4)
        ]

        head_gains = jnp.stack([jnp.sum(grad_query_n * query_hat, 0), jnp.sum(grad_key_n * key_hat, 0)])
        head_rows = lax.dynamic_update_slice(jnp.zeros((2, model_width), F32), head_gains, (jnp.int32(0), offset))
        post_rows = lay.from_relative(jnp.concatenate([gain_row_attn, gain_row_mlp], 0))
        gains_grad = add_all(
            jnp.concatenate([head_rows, post_rows], 0), lay.tensor_axes[::-1] + lay.dp_axes[::-1]
        )
        return (
            hidden_out,
            lay.from_relative(in_grad),
            attn_outs[0],
            attn_outs[1],
            attn_outs[2],
            attn_outs[3],
            jnp.concatenate(gate_out, 1),
            jnp.concatenate(up_out, 1),
            jnp.concatenate(down_out, 1),
            gains_grad,
        )

    return on_device


def solution(mesh):
    lay = Layout(mesh.shape["dp"], mesh.shape["tensor"])
    fine = Mesh(mesh.devices.reshape(lay.shape_of()), lay.dp_axes + lay.tensor_axes)
    tokens = P(lay.dp_axes + lay.tensor_axes, None)
    weights = P(lay.dp_axes, lay.tensor_axes)
    rows = P(lay.dp_axes)
    return jax.shard_map(
        block_program(lay),
        mesh=fine,
        in_specs=(tokens, tokens) + (weights,) * 7 + (P(), rows, rows),
        out_specs=(tokens, tokens) + (weights,) * 7 + (P(),),
        check_vma=False,
    )
```

time: 1530 us -> 915 us (0.60)
  waiting for transfers between devices: 1230 us -> 508 us
  starting transfers between devices: 1.42 us -> 120 us
  blocking collectives: 55.6 us -> 0 us
  other arithmetic: 55 us -> 98.5 us
  local copies, waits for them, and re-layouts: 35.2 us -> 69.3 us
  matrix products: 128 us -> 111 us
    reduce_scatter x5 -> x0, waiting for transfers between devices: 629 us -> none  [the longest x1 499 us: on_device(): lax.psum_scatter(jnp.concatenate(pieces, 1).astype(jnp.bfloat16), 'dp', s...]
    all_gather x11 -> x0, waiting for transfers between devices: 595 us -> none  [the longest x1 122 us: on_device(): lax.all_gather(w_gate, 'dp', axis=0, tiled=True)]
    ppermute x0 -> x129, waiting for transfers between devices: none -> 508 us  [swap(): return lax.ppermute(values, axis, [(0, 1), (1, 0)])]
    ppermute x0 -> x129, starting transfers between devices: none -> 120 us  [swap(): return lax.ppermute(values, axis, [(0, 1), (1, 0)])]
    psum x3 -> x0, blocking collectives: 55.6 us -> none  [the longest x1 43.8 us: on_device(): gains_grad = lax.psum(gain_rows, ('dp', 'tensor'))]
    unnamed x0 -> x53, other arithmetic: none -> 30.6 us
    reshape x0 -> x17, local copies, waits for them, and re-layouts: none -> 26 us  [the longest x6 8.76 us: tokens_of(): values.reshape(2, 2, 2 * per, n_heads, HEAD_DIM).transpose(1, 0, 2, 3, 4)]
    dot_general x24 -> x38, matrix products: 128 us -> 105 us  [the longest x20 35.8 us: contract_rows(): lax.dot_general(left, right, (((0,), (0,)), ((), ())), preferred_element_...]
  transfers between devices with their start and end apart: 16 -> 129, of which waited for: 15 -> 65; matrix products, arithmetic and copies ran while one was open for 8% -> 19% of each run, Pallas kernels for 0% -> 0%
where the time goes in v1:
time: 915 us; the launch traced here: 910 us
  waiting for transfers between devices  508 us (56%)
  starting transfers between devices  120 us (13%)
  matrix products  111 us (12%)
  other arithmetic  98.5 us (11%)
  local copies, waits for them, and re-layouts  69.3 us (8%)
    ppermute x129, waiting for transfers between devices, swap(): return lax.ppermute(values, axis, [(0, 1), (1, 0)])  508 us
    ppermute x129, starting transfers between devices, swap(): return lax.ppermute(values, axis, [(0, 1), (1, 0)])  120 us
    dot_general x20, matrix products, contract_rows(): lax.dot_general(left, right, (((0,), (0,)), ((), ())), preferred_element_...  35.8 us
    dot_general x5, matrix products, dot_rows_cols(): return jnp.dot(left, right, preferred_element_type=F32)  32.1 us
    unnamed x53, other arithmetic  30.6 us
    dot_general x8, matrix products, contract_cols(): lax.dot_general(left, right, (((1,), (1,)), ((), ())), preferred_element_...  27.9 us
    unnamed x225, local copies, waits for them, and re-layouts  22.7 us
  transfers between devices with their start and end apart: 129, of which 65 were waited for; matrix products, arithmetic and copies ran while one was open for 19% of the time, Pallas kernels for 0%

profile of v1, /device:TPU:0, one launch (start us, length us, event | category | flops | bytes accessed | tf_op | source)
XLA Modules:
  0.0 910.0 jit_solution(2454383406166965005)
XLA Ops:
  24.7 3.0 collective-permute-start.3
  47.2 3.6 collective-permute-done.9
  69.8 3.0 collective-permute-done.7
  73.3 2.7 collective-permute-start.10
  80.5 4.0 multiply_cosine_fusion
  87.3 22.5 %collective-permute-done.10 = bf16[512,768]{1,0:T(8,128)(2,1)} collective-permute-done((bf16[512,768]{1,0:T(8,128)(2,1)S(1)}, bf16[512,768]{1,0:T(8,128)(2,1)}, u32[]{:S(2)}, u32[]{:S(2)}) %collective-permute-start.10) | collective-permute-done | bytes 786464 | tf_op jit(solution)/shard_map/ppermute | solution.py:27
  115.8 14.4 %collective-permute-done.12 = bf16[512,768]{1,0:T(8,128)(2,1)S(1)} collective-permute-done((bf16[512,768]{1,0:T(8,128)(2,1)}, bf16[512,768]{1,0:T(8,128)(2,1)S(1)}, u32[]{:S(2)}, u32[]{:S(2)}) %collective-permute-start.12) | collective-permute-done | bytes 786464 | tf_op jit(solution)/shard_map/ppermute | solution.py:27
  130.3 6.1 fusion.107
  142.3 2.9 collective-permute-done.16
  160.9 3.1 reshape.246
  167.9 5.7 fusion.136
  173.6 2.6 fusion.10
  177.3 2.7 fusion.46
  191.0 3.1 collective-permute-start.24
  194.6 3.6 collective-permute-done.28
  202.0 3.5 collective-permute-done.24
  208.1 5.4 collective-permute-done.29
  216.5 6.9 collective-permute-done.30
  223.5 2.8 collective-permute-done.31
  226.4 10.4 %collective-permute-done.33 = bf16[64,2048]{1,0:T(8,128)(2,1)S(1)} collective-permute-done((bf16[64,2048]{1,0:T(8,128)(2,1)S(1)}, bf16[64,2048]{1,0:T(8,128)(2,1)S(1)}, u32[]{:S(2)}, u32[]{:S(2)}) %collective-permute-start.33) | collective-permute-done | bytes 262176 | tf_op jit(solution)/shard_map/ppermute | solution.py:27
  236.8 2.5 collective-permute-start.34
  239.3 3.1 collective-permute-done.32
  243.0 26.0 %collective-permute-done.34 = bf16[64,2048]{1,0:T(8,128)(2,1)S(1)} collective-permute-done((bf16[64,2048]{1,0:T(8,128)(2,1)S(1)}, bf16[64,2048]{1,0:T(8,128)(2,1)S(1)}, u32[]{:S(2)}, u32[]{:S(2)}) %collective-permute-start.34) | collective-permute-done | bytes 262176 | tf_op jit(solution)/shard_map/ppermute | solution.py:27
  269.0 3.0 collective-permute-start.53
  272.8 26.2 %collective-permute-done.38 = bf16[512,1024]{1,0:T(8,128)(2,1)S(1)} collective-permute-done((bf16[512,1024]{1,0:T(8,128)(2,1)S(1)}, bf16[512,1024]{1,0:T(8,128)(2,1)S(1)}, u32[]{:S(2)}, u32[]{:S(2)}) %collective-permute-start.38) | collective-permute-done | bytes 1048608 | tf_op jit(solution)/shard_map/ppermute | solution.py:27
  300.2 21.3 %collective-permute-done.42 = bf16[512,1024]{1,0:T(8,128)(2,1)S(1)} collective-permute-done((bf16[512,1024]{1,0:T(8,128)(2,1)S(1)}, bf16[512,1024]{1,0:T(8,128)(2,1)S(1)}, u32[]{:S(2)}, u32[]{:S(2)}) %collective-permute-start.42) | collective-permute-done | bytes 1048608 | tf_op jit(solution)/shard_map/ppermute | solution.py:27
  322.1 18.3 %collective-permute-done.53 = bf16[512,1024]{1,0:T(8,128)(2,1)S(1)} collective-permute-done((bf16[512,1024]{1,0:T(8,128)(2,1)S(1)}, bf16[512,1024]{1,0:T(8,128)(2,1)S(1)}, u32[]{:S(2)}, u32[]{:S(2)}) %collective-permute-start.53) | collective-permute-done | bytes 1048608 | tf_op jit(solution)/shard_map/ppermute | solution.py:27
  346.0 22.4 %collective-permute-done.44 = bf16[512,1024]{1,0:T(8,128)(2,1)S(1)} collective-permute-done((bf16[512,1024]{1,0:T(8,128)(2,1)S(1)}, bf16[512,1024]{1,0:T(8,128)(2,1)S(1)}, u32[]{:S(2)}, u32[]{:S(2)}) %collective-permute-start.44) | collective-permute-done | bytes 1048608 | tf_op jit(solution)/shard_map/ppermute | solution.py:27
  370.6 6.6 fusion.137
  377.2 8.1 multiply_convert_fusion.3
  445.8 3.4 collective-permute-done.81
  450.2 3.3 collective-permute-done.83
  453.7 8.1 multiply_convert_fusion.2
  484.3 7.2 fusion.141
  495.6 8.2 convolution_add_fusion
  504.3 36.1 %collective-permute-done.121 = bf16[512,1024]{1,0:T(8,128)(2,1)} collective-permute-done((bf16[512,1024]{1,0:T(8,128)(2,1)}, bf16[512,1024]{1,0:T(8,128)(2,1)}, u32[]{:S(2)}, u32[]{:S(2)}) %collective-permute-start.121) | collective-permute-done | bytes 1048608 | tf_op jit(solution)/shard_map/ppermute | solution.py:27
  546.7 16.2 %collective-permute-done.117 = bf16[512,1024]{1,0:T(8,128)(2,1)} collective-permute-done((bf16[512,1024]{1,0:T(8,128)(2,1)}, bf16[512,1024]{1,0:T(8,128)(2,1)}, u32[]{:S(2)}, u32[]{:S(2)}) %collective-permute-start.117) | collective-permute-done | bytes 1048608 | tf_op jit(solution)/shard_map/ppermute | solution.py:27
  565.6 19.7 %collective-permute-done.113 = bf16[512,1024]{1,0:T(8,128)(2,1)} collective-permute-done((bf16[512,1024]{1,0:T(8,128)(2,1)}, bf16[512,1024]{1,0:T(8,128)(2,1)}, u32[]{:S(2)}, u32[]{:S(2)}) %collective-permute-start.113) | collective-permute-done | bytes 1048608 | tf_op jit(solution)/shard_map/ppermute | solution.py:27
  595.8 2.5 fusion.109
  598.4 9.3 %collective-permute-done.116 = bf16[512,1024]{1,0:T(8,128)(2,1)S(1)} collective-permute-done((bf16[512,1024]{1,0:T(8,128)(2,1)}, bf16[512,1024]{1,0:T(8,128)(2,1)S(1)}, u32[]{:S(2)}, u32[]{:S(2)}) %collective-permute-start.116) | collective-permute-done | bytes 1048608 | tf_op jit(solution)/shard_map/ppermute | solution.py:27
  609.3 49.0 %collective-permute-done.118 = bf16[512,1024]{1,0:T(8,128)(2,1)S(1)} collective-permute-done((bf16[512,1024]{1,0:T(8,128)(2,1)S(1)}, bf16[512,1024]{1,0:T(8,128)(2,1)S(1)}, u32[]{:S(2)}, u32[]{:S(2)}) %collective-permute-start.118) | collective-permute-done | bytes 1048608 | tf_op jit(solution)/shard_map/ppermute | solution.py:27
  661.0 18.7 %collective-permute-done.114 = bf16[512,1024]{1,0:T(8,128)(2,1)S(1)} collective-permute-done((bf16[512,1024]{1,0:T(8,128)(2,1)S(1)}, bf16[512,1024]{1,0:T(8,128)(2,1)S(1)}, u32[]{:S(2)}, u32[]{:S(2)}) %collective-permute-start.114) | collective-permute-done | bytes 1048608 | tf_op jit(solution)/shard_map/ppermute | solution.py:27
  680.5 6.5 collective-permute-done.86
  687.1 2.5 collective-permute-start.87
  692.1 3.1 collective-permute-done.87
  695.3 3.6 collective-permute-done.90
  705.4 7.3 collective-permute-done.91
  713.9 13.1 %collective-permute-done.94 = bf16[64,2048]{1,0:T(8,128)(2,1)S(1)} collective-permute-done((bf16[64,2048]{1,0:T(8,128)(2,1)S(1)}, bf16[64,2048]{1,0:T(8,128)(2,1)S(1)}, u32[]{:S(2)}, u32[]{:S(2)}) %collective-permute-start.94) | collective-permute-done | bytes 262176 | tf_op jit(solution)/shard_map/ppermute | solution.py:27
  727.4 5.2 collective-permute-done.93
  732.7 3.4 collective-permute-done.95
  741.9 3.3 convolution_convert_fusion.18
  750.5 4.0 fusion.11
  763.7 3.0 pad_maximum_fusion.10
  769.2 3.1 reshape.255
  778.1 3.0 collective-permute-done.99
  784.7 2.6 copy.101
  794.0 4.6 fusion.106
  809.9 18.4 %collective-permute-done.126 = f32[4,2048]{1,0:T(4,128)S(1)} collective-permute-done((f32[4,2048]{1,0:T(4,128)S(1)}, f32[4,2048]{1,0:T(4,128)S(1)}, u32[]{:S(2)}, u32[]{:S(2)}) %collective-permute-start.126) | collective-permute-done | bytes 32800 | tf_op jit(solution)/shard_map/ppermute | solution.py:27
  834.4 3.1 collective-permute-done.128
  843.4 12.9 %collective-permute-done.108 = bf16[512,1024]{1,0:T(8,128)(2,1)S(1)} collective-permute-done((bf16[512,1024]{1,0:T(8,128)(2,1)S(1)}, bf16[512,1024]{1,0:T(8,128)(2,1)S(1)}, u32[]{:S(2)}, u32[]{:S(2)}) %collective-permute-start.108) | collective-permute-done | bytes 1048608 | tf_op jit(solution)/shard_map/ppermute | solution.py:27
  857.7 26.6 %collective-permute-done.110 = bf16[512,1024]{1,0:T(8,128)(2,1)S(1)} collective-permute-done((bf16[512,1024]{1,0:T(8,128)(2,1)S(1)}, bf16[512,1024]{1,0:T(8,128)(2,1)S(1)}, u32[]{:S(2)}, u32[]{:S(2)}) %collective-permute-start.110) | collective-permute-done | bytes 1048608 | tf_op jit(solution)/shard_map/ppermute | solution.py:27
  888.9 4.3 collective-permute-done.104
  893.2 2.7 collective-permute-done.107
  897.9 7.9 collective-permute-done.111
  (691 shorter events, 331.0 us)
Async XLA Ops:
  24.7 32.8 %collective-permute-start.3 = (bf16[64,2048]{1,0:T(8,128)(2,1)}, bf16[64,2048]{1,0:T(8,128)(2,1)}, u32[]{:S(2)}, u32[]{:S(2)}) collective-permute-start(bf16[64,2048]{1,0:T(8,128)(2,1)} %get-tuple-element.172), channel_id=1, source_target_pairs={{0,8},{8,0},{1,9},{9,1},{2,10},{10,2},{3,11},{11,3},{4,12},{12,4},... | collective-permute-start | bytes 786440 | tf_op jit(solution)/shard_map/ppermute | solution.py:27
  27.8 28.0 %collective-permute-start.1 = (bf16[64,2048]{1,0:T(8,128)(2,1)}, bf16[64,2048]{1,0:T(8,128)(2,1)}, u32[]{:S(2)}, u32[]{:S(2)}) collective-permute-start(bf16[64,2048]{1,0:T(8,128)(2,1)} %get-tuple-element.172), channel_id=1, source_target_pairs={{0,2},{2,0},{1,3},{3,1},{4,6},{6,4},{5,7},{7,5},{8,10},{10,8},{9,1... | collective-permute-start | bytes 786440 | tf_op jit(solution)/shard_map/ppermute | solution.py:27
  29.3 30.3 %collective-permute-start.2 = (bf16[64,2048]{1,0:T(8,128)(2,1)}, bf16[64,2048]{1,0:T(8,128)(2,1)}, u32[]{:S(2)}, u32[]{:S(2)}) collective-permute-start(bf16[64,2048]{1,0:T(8,128)(2,1)} %get-tuple-element.173), channel_id=1, source_target_pairs={{0,8},{8,0},{1,9},{9,1},{2,10},{10,2},{3,11},{11,3},{4,12},{12,4},... | collective-permute-start | bytes 786440 | tf_op jit(solution)/shard_map/ppermute | solution.py:27
  29.7 22.1 %collective-permute-start = (bf16[64,2048]{1,0:T(8,128)(2,1)}, bf16[64,2048]{1,0:T(8,128)(2,1)}, u32[]{:S(2)}, u32[]{:S(2)}) collective-permute-start(bf16[64,2048]{1,0:T(8,128)(2,1)} %get-tuple-element.173), channel_id=1, source_target_pairs={{0,2},{2,0},{1,3},{3,1},{4,6},{6,4},{5,7},{7,5},{8,10},{10,8},{9,1... | collective-permute-start | bytes 786440 | tf_op jit(solution)/shard_map/ppermute | solution.py:27
  30.4 15.4 %collective-permute-start.13 = (s32[4,128]{1,0:T(4,128)}, s32[4,128]{1,0:T(4,128)}, u32[]{:S(2)}, u32[]{:S(2)}) collective-permute-start(s32[4,128]{1,0:T(4,128)} %pad_add_fusion), channel_id=1, source_target_pairs={{0,8},{8,0},{1,9},{9,1},{2,10},{10,2},{3,11},{11,3},{4,12},{12,4},... | collective-permute-start | bytes 6152 | tf_op jit(solution)/shard_map/ppermute | solution.py:27
  50.8 22.5 %collective-permute-start.18 = (s32[4,128]{1,0:T(4,128)S(1)}, s32[4,128]{1,0:T(4,128)S(1)}, u32[]{:S(2)}, u32[]{:S(2)}) collective-permute-start(s32[4,128]{1,0:T(4,128)S(1)} %pad_add_fusion.2), channel_id=1, source_target_pairs={{0,8},{8,0},{1,9},{9,1},{2,10},{10,2},{3,11},{11,3},{4,12},{12,4},... | collective-permute-start | bytes 6152 | tf_op jit(solution)/shard_map/ppermute | solution.py:27
  51.8 25.7 %collective-permute-start.14 = (s32[4,128]{1,0:T(4,128)}, s32[4,128]{1,0:T(4,128)}, u32[]{:S(2)}, u32[]{:S(2)}) collective-permute-start(s32[4,128]{1,0:T(4,128)} %pad_add_fusion.1), channel_id=1, source_target_pairs={{0,8},{8,0},{1,9},{9,1},{2,10},{10,2},{3,11},{11,3},{4,12},{12,4},... | collective-permute-start | bytes 6152 | tf_op jit(solution)/shard_map/ppermute | solution.py:27
  55.7 30.0 %collective-permute-start.19 = (bf16[256,256]{1,0:T(8,128)(2,1)}, bf16[256,256]{1,0:T(8,128)(2,1)}, u32[]{:S(2)}, u32[]{:S(2)}) collective-permute-start(bf16[256,256]{1,0:T(8,128)(2,1)} %broadcast_select_fusion.14), channel_id=1, source_target_pairs={{0,8},{8,0},{1,9},{9,1},{2,10},{10,2},{3,11},{11,3},{4,12},{12,4},... | collective-permute-start | bytes 393224 | tf_op jit(solution)/shard_map/ppermute | solution.py:27
  69.7 43.7 %collective-permute-start.6 = (bf16[512,2048]{1,0:T(8,128)(2,1)}, bf16[512,2048]{1,0:T(8,128)(2,1)S(1)}, u32[]{:S(2)}, u32[]{:S(2)}) collective-permute-start(bf16[512,2048]{1,0:T(8,128)(2,1)} %get-tuple-element.216), channel_id=1, source_target_pairs={{0,1},{1,0},{2,3},{3,2},{4,5},{5,4},{6,7},{7,6},{8,9},{9,8},{10,11... | collective-permute-start | bytes 6291464 | tf_op jit(solution)/shard_map/ppermute | solution.py:27
  72.8 117.9 %collective-permute-start.45 = (bf16[256,1024]{1,0:T(8,128)(2,1)}, bf16[256,1024]{1,0:T(8,128)(2,1)}, u32[]{:S(2)}, u32[]{:S(2)}) collective-permute-start(bf16[256,1024]{1,0:T(8,128)(2,1)} %broadcast_select_fusion.2), channel_id=1, source_target_pairs={{0,8},{8,0},{1,9},{9,1},{2,10},{10,2},{3,11},{11,3},{4,12},{12,4},... | collective-permute-start | bytes 1572872 | tf_op jit(solution)/shard_map/ppermute | solution.py:27
  73.3 36.5 %collective-permute-start.10 = (bf16[512,768]{1,0:T(8,128)(2,1)S(1)}, bf16[512,768]{1,0:T(8,128)(2,1)}, u32[]{:S(2)}, u32[]{:S(2)}) collective-permute-start(bf16[512,768]{1,0:T(8,128)(2,1)S(1)} %maximum_maximum_fusion.1), channel_id=1, source_target_pairs={{0,16},{16,0},{1,17},{17,1},{2,18},{18,2},{3,19},{19,3},{4,20},{20... | collective-permute-start | bytes 2359304 | tf_op jit(solution)/shard_map/ppermute | solution.py:27
  77.5 107.0 %collective-permute-start.41 = (bf16[256,1024]{1,0:T(8,128)(2,1)}, bf16[256,1024]{1,0:T(8,128)(2,1)}, u32[]{:S(2)}, u32[]{:S(2)}) collective-permute-start(bf16[256,1024]{1,0:T(8,128)(2,1)} %broadcast_select_fusion.6), channel_id=1, source_target_pairs={{0,8},{8,0},{1,9},{9,1},{2,10},{10,2},{3,11},{11,3},{4,12},{12,4},... | collective-permute-start | bytes 1572872 | tf_op jit(solution)/shard_map/ppermute | solution.py:27
  85.7 29.3 %collective-permute-start.11 = (bf16[512,768]{1,0:T(8,128)(2,1)S(1)}, bf16[512,768]{1,0:T(8,128)(2,1)S(1)}, u32[]{:S(2)}, u32[]{:S(2)}) collective-permute-start(bf16[512,768]{1,0:T(8,128)(2,1)S(1)} %maximum_maximum_fusion.1), channel_id=1, source_target_pairs={{0,4},{4,0},{1,5},{5,1},{2,6},{6,2},{3,7},{7,3},{8,12},{12,8},{9,1... | collective-permute-start | bytes 2359304 | tf_op jit(solution)/shard_map/ppermute | solution.py:27
  109.8 20.4 %collective-permute-start.12 = (bf16[512,768]{1,0:T(8,128)(2,1)}, bf16[512,768]{1,0:T(8,128)(2,1)S(1)}, u32[]{:S(2)}, u32[]{:S(2)}) collective-permute-start(bf16[512,768]{1,0:T(8,128)(2,1)} %collective-permute-done.10), channel_id=1, source_target_pairs={{0,4},{4,0},{1,5},{5,1},{2,6},{6,2},{3,7},{7,3},{8,12},{12,8},{9,1... | collective-permute-start | bytes 2359304 | tf_op jit(solution)/shard_map/ppermute | solution.py:27
  113.4 67.5 %collective-permute-start.37 = (bf16[256,1024]{1,0:T(8,128)(2,1)}, bf16[256,1024]{1,0:T(8,128)(2,1)}, u32[]{:S(2)}, u32[]{:S(2)}) collective-permute-start(bf16[256,1024]{1,0:T(8,128)(2,1)} %broadcast_select_fusion.10), channel_id=1, source_target_pairs={{0,8},{8,0},{1,9},{9,1},{2,10},{10,2},{3,11},{11,3},{4,12},{12,4},... | collective-permute-start | bytes 1572872 | tf_op jit(solution)/shard_map/ppermute | solution.py:27
  115.1 26.5 %collective-permute-start.21 = (bf16[512,256]{1,0:T(8,128)(2,1)S(1)}, bf16[512,256]{1,0:T(8,128)(2,1)S(1)}, u32[]{:S(2)}, u32[]{:S(2)}) collective-permute-start(bf16[512,256]{1,0:T(8,128)(2,1)S(1)} %pad_maximum_fusion.19), channel_id=1, source_target_pairs={{0,4},{4,0},{1,5},{5,1},{2,6},{6,2},{3,7},{7,3},{8,12},{12,8},{9,1... | collective-permute-start | bytes 786440 | tf_op jit(solution)/shard_map/ppermute | solution.py:27
  183.0 89.2 %collective-permute-start.39 = (bf16[512,1024]{1,0:T(8,128)(2,1)S(1)}, bf16[512,1024]{1,0:T(8,128)(2,1)S(1)}, u32[]{:S(2)}, u32[]{:S(2)}) collective-permute-start(bf16[512,1024]{1,0:T(8,128)(2,1)S(1)} %pad_maximum_fusion.6), channel_id=1, source_target_pairs={{0,4},{4,0},{1,5},{5,1},{2,6},{6,2},{3,7},{7,3},{8,12},{12,8},{9,1... | collective-permute-start | bytes 3145736 | tf_op jit(solution)/shard_map/ppermute | solution.py:27
  191.0 14.5 %collective-permute-start.24 = (bf16[64,2048]{1,0:T(8,128)(2,1)S(1)}, bf16[64,2048]{1,0:T(8,128)(2,1)S(1)}, u32[]{:S(2)}, u32[]{:S(2)}) collective-permute-start(bf16[64,2048]{1,0:T(8,128)(2,1)S(1)} %get-tuple-element.114), channel_id=1, source_target_pairs={{0,8},{8,0},{1,9},{9,1},{2,10},{10,2},{3,11},{11,3},{4,12},{12,4},... | collective-permute-start | bytes 786440 | tf_op jit(solution)/shard_map/ppermute | solution.py:27
  205.5 93.5 %collective-permute-start.38 = (bf16[512,1024]{1,0:T(8,128)(2,1)S(1)}, bf16[512,1024]{1,0:T(8,128)(2,1)S(1)}, u32[]{:S(2)}, u32[]{:S(2)}) collective-permute-start(bf16[512,1024]{1,0:T(8,128)(2,1)S(1)} %pad_maximum_fusion.6), channel_id=1, source_target_pairs={{0,16},{16,0},{1,17},{17,1},{2,18},{18,2},{3,19},{19,3},{4,20},{20... | collective-permute-start | bytes 3145736 | tf_op jit(solution)/shard_map/ppermute | solution.py:27
  214.8 22.0 %collective-permute-start.33 = (bf16[64,2048]{1,0:T(8,128)(2,1)S(1)}, bf16[64,2048]{1,0:T(8,128)(2,1)S(1)}, u32[]{:S(2)}, u32[]{:S(2)}) collective-permute-start(bf16[64,2048]{1,0:T(8,128)(2,1)S(1)} %get-tuple-element.170), channel_id=1, source_target_pairs={{0,8},{8,0},{1,9},{9,1},{2,10},{10,2},{3,11},{11,3},{4,12},{12,4},... | collective-permute-start | bytes 786440 | tf_op jit(solution)/shard_map/ppermute | solution.py:27
  223.5 19.0 %collective-permute-start.32 = (bf16[64,2048]{1,0:T(8,128)(2,1)S(1)}, bf16[64,2048]{1,0:T(8,128)(2,1)S(1)}, u32[]{:S(2)}, u32[]{:S(2)}) collective-permute-start(bf16[64,2048]{1,0:T(8,128)(2,1)S(1)} %get-tuple-element.171), channel_id=1, source_target_pairs={{0,8},{8,0},{1,9},{9,1},{2,10},{10,2},{3,11},{11,3},{4,12},{12,4},... | collective-permute-start | bytes 786440 | tf_op jit(solution)/shard_map/ppermute | solution.py:27
  226.3 95.2 %collective-permute-start.42 = (bf16[512,1024]{1,0:T(8,128)(2,1)S(1)}, bf16[512,1024]{1,0:T(8,128)(2,1)S(1)}, u32[]{:S(2)}, u32[]{:S(2)}) collective-permute-start(bf16[512,1024]{1,0:T(8,128)(2,1)S(1)} %pad_maximum_fusion.7), channel_id=1, source_target_pairs={{0,16},{16,0},{1,17},{17,1},{2,18},{18,2},{3,19},{19,3},{4,20},{20... | collective-permute-start | bytes 3145736 | tf_op jit(solution)/shard_map/ppermute | solution.py:27
  236.8 32.2 %collective-permute-start.34 = (bf16[64,2048]{1,0:T(8,128)(2,1)S(1)}, bf16[64,2048]{1,0:T(8,128)(2,1)S(1)}, u32[]{:S(2)}, u32[]{:S(2)}) collective-permute-start(bf16[64,2048]{1,0:T(8,128)(2,1)S(1)} %collective-permute-done.30), channel_id=1, source_target_pairs={{0,8},{8,0},{1,9},{9,1},{2,10},{10,2},{3,11},{11,3},{4,12},{12,4},... | collective-permute-start | bytes 786440 | tf_op jit(solution)/shard_map/ppermute | solution.py:27
  242.4 29.7 %collective-permute-start.35 = (bf16[64,2048]{1,0:T(8,128)(2,1)S(1)}, bf16[64,2048]{1,0:T(8,128)(2,1)S(1)}, u32[]{:S(2)}, u32[]{:S(2)}) collective-permute-start(bf16[64,2048]{1,0:T(8,128)(2,1)S(1)} %collective-permute-done.33), channel_id=1, source_target_pairs={{0,2},{2,0},{1,3},{3,1},{4,6},{6,4},{5,7},{7,5},{8,10},{10,8},{9,1... | collective-permute-start | bytes 786440 | tf_op jit(solution)/shard_map/ppermute | solution.py:27
  269.0 71.4 %collective-permute-start.53 = (bf16[512,1024]{1,0:T(8,128)(2,1)S(1)}, bf16[512,1024]{1,0:T(8,128)(2,1)S(1)}, u32[]{:S(2)}, u32[]{:S(2)}) collective-permute-start(bf16[512,1024]{1,0:T(8,128)(2,1)S(1)} %pad_maximum_fusion.8), channel_id=1, source_target_pairs={{0,16},{16,0},{1,17},{17,1},{2,18},{18,2},{3,19},{19,3},{4,20},{20... | collective-permute-start | bytes 3145736 | tf_op jit(solution)/shard_map/ppermute | solution.py:27
  272.1 96.3 %collective-permute-start.36 = (bf16[512,2048]{1,0:T(8,128)(2,1)S(1)}, bf16[512,2048]{1,0:T(8,128)(2,1)S(1)}, u32[]{:S(2)}, u32[]{:S(2)}) collective-permute-start(bf16[512,2048]{1,0:T(8,128)(2,1)S(1)} %get-tuple-element.204), channel_id=1, source_target_pairs={{0,1},{1,0},{2,3},{3,2},{4,5},{5,4},{6,7},{7,6},{8,9},{9,8},{10,11... | collective-permute-start | bytes 6291464 | tf_op jit(solution)/shard_map/ppermute | solution.py:27
  272.2 69.7 %collective-permute-start.43 = (bf16[512,1024]{1,0:T(8,128)(2,1)S(1)}, bf16[512,1024]{1,0:T(8,128)(2,1)S(1)}, u32[]{:S(2)}, u32[]{:S(2)}) collective-permute-start(bf16[512,1024]{1,0:T(8,128)(2,1)S(1)} %pad_maximum_fusion.7), channel_id=1, source_target_pairs={{0,4},{4,0},{1,5},{5,1},{2,6},{6,2},{3,7},{7,3},{8,12},{12,8},{9,1... | collective-permute-start | bytes 3145736 | tf_op jit(solution)/shard_map/ppermute | solution.py:27
  299.1 44.5 %collective-permute-start.61 = (bf16[512,1024]{1,0:T(8,128)(2,1)S(1)}, bf16[512,1024]{1,0:T(8,128)(2,1)S(1)}, u32[]{:S(2)}, u32[]{:S(2)}) collective-permute-start(bf16[512,1024]{1,0:T(8,128)(2,1)S(1)} %pad_maximum_fusion.8), channel_id=1, source_target_pairs={{0,4},{4,0},{1,5},{5,1},{2,6},{6,2},{3,7},{7,3},{8,12},{12,8},{9,1... | collective-permute-start | bytes 3145736 | tf_op jit(solution)/shard_map/ppermute | solution.py:27
  321.5 24.4 %collective-permute-start.40 = (bf16[512,1024]{1,0:T(8,128)(2,1)S(1)}, bf16[512,1024]{1,0:T(8,128)(2,1)S(1)}, u32[]{:S(2)}, u32[]{:S(2)}) collective-permute-start(bf16[512,1024]{1,0:T(8,128)(2,1)S(1)} %collective-permute-done.38), channel_id=1, source_target_pairs={{0,4},{4,0},{1,5},{5,1},{2,6},{6,2},{3,7},{7,3},{8,12},{12,8},{9,1... | collective-permute-start | bytes 3145736 | tf_op jit(solution)/shard_map/ppermute | solution.py:27
  340.4 28.0 %collective-permute-start.44 = (bf16[512,1024]{1,0:T(8,128)(2,1)S(1)}, bf16[512,1024]{1,0:T(8,128)(2,1)S(1)}, u32[]{:S(2)}, u32[]{:S(2)}) collective-permute-start(bf16[512,1024]{1,0:T(8,128)(2,1)S(1)} %collective-permute-done.42), channel_id=1, source_target_pairs={{0,4},{4,0},{1,5},{5,1},{2,6},{6,2},{3,7},{7,3},{8,12},{12,8},{9,1... | collective-permute-start | bytes 3145736 | tf_op jit(solution)/shard_map/ppermute | solution.py:27
  341.9 45.8 %collective-permute-start.69 = (bf16[512,1024]{1,0:T(8,128)(2,1)S(1)}, bf16[512,1024]{1,0:T(8,128)(2,1)S(1)}, u32[]{:S(2)}, u32[]{:S(2)}) collective-permute-start(bf16[512,1024]{1,0:T(8,128)(2,1)S(1)} %collective-permute-done.53), channel_id=1, source_target_pairs={{0,4},{4,0},{1,5},{5,1},{2,6},{6,2},{3,7},{7,3},{8,12},{12,8},{9,1... | collective-permute-start | bytes 3145736 | tf_op jit(solution)/shard_map/ppermute | solution.py:27
  394.6 22.1 %collective-permute-start.71 = (bf16[64,512]{1,0:T(8,128)(2,1)S(1)}, bf16[64,512]{1,0:T(8,128)(2,1)S(1)}, u32[]{:S(2)}, u32[]{:S(2)}) collective-permute-start(bf16[64,512]{1,0:T(8,128)(2,1)S(1)} %get-tuple-element.166), channel_id=1, source_target_pairs={{0,8},{8,0},{1,9},{9,1},{2,10},{10,2},{3,11},{11,3},{4,12},{12,4},... | collective-permute-start | bytes 196616 | tf_op jit(solution)/shard_map/ppermute | solution.py:27
  395.3 22.3 %collective-permute-start.74 = (bf16[64,512]{1,0:T(8,128)(2,1)S(1)}, bf16[64,512]{1,0:T(8,128)(2,1)S(1)}, u32[]{:S(2)}, u32[]{:S(2)}) collective-permute-start(bf16[64,512]{1,0:T(8,128)(2,1)S(1)} %get-tuple-element.168), channel_id=1, source_target_pairs={{0,2},{2,0},{1,3},{3,1},{4,6},{6,4},{5,7},{7,5},{8,10},{10,8},{9,1... | collective-permute-start | bytes 196616 | tf_op jit(solution)/shard_map/ppermute | solution.py:27
  399.3 22.3 %collective-permute-start.63 = (bf16[64,512]{1,0:T(8,128)(2,1)S(1)}, bf16[64,512]{1,0:T(8,128)(2,1)S(1)}, u32[]{:S(2)}, u32[]{:S(2)}) collective-permute-start(bf16[64,512]{1,0:T(8,128)(2,1)S(1)} %get-tuple-element.162), channel_id=1, source_target_pairs={{0,8},{8,0},{1,9},{9,1},{2,10},{10,2},{3,11},{11,3},{4,12},{12,4},... | collective-permute-start | bytes 196616 | tf_op jit(solution)/shard_map/ppermute | solution.py:27
  491.6 96.5 %collective-permute-start.120 = (bf16[512,1024]{1,0:T(8,128)(2,1)}, bf16[512,1024]{1,0:T(8,128)(2,1)}, u32[]{:S(2)}, u32[]{:S(2)}) collective-permute-start(bf16[512,1024]{1,0:T(8,128)(2,1)} %convolution_convert_fusion.2), channel_id=1, source_target_pairs={{0,4},{4,0},{1,5},{5,1},{2,6},{6,2},{3,7},{7,3},{8,12},{12,8},{9,1... | collective-permute-start | bytes 3145736 | tf_op jit(solution)/shard_map/ppermute | solution.py:27
  492.7 47.7 %collective-permute-start.121 = (bf16[512,1024]{1,0:T(8,128)(2,1)}, bf16[512,1024]{1,0:T(8,128)(2,1)}, u32[]{:S(2)}, u32[]{:S(2)}) collective-permute-start(bf16[512,1024]{1,0:T(8,128)(2,1)} %convolution_convert_fusion), channel_id=1, source_target_pairs={{0,4},{4,0},{1,5},{5,1},{2,6},{6,2},{3,7},{7,3},{8,12},{12,8},{9,1... | collective-permute-start | bytes 3145736 | tf_op jit(solution)/shard_map/ppermute | solution.py:27
  493.6 69.2 %collective-permute-start.117 = (bf16[512,1024]{1,0:T(8,128)(2,1)}, bf16[512,1024]{1,0:T(8,128)(2,1)}, u32[]{:S(2)}, u32[]{:S(2)}) collective-permute-start(bf16[512,1024]{1,0:T(8,128)(2,1)} %convolution_convert_fusion.4), channel_id=1, source_target_pairs={{0,4},{4,0},{1,5},{5,1},{2,6},{6,2},{3,7},{7,3},{8,12},{12,8},{9,1... | collective-permute-start | bytes 3145736 | tf_op jit(solution)/shard_map/ppermute | solution.py:27
  494.7 90.6 %collective-permute-start.113 = (bf16[512,1024]{1,0:T(8,128)(2,1)}, bf16[512,1024]{1,0:T(8,128)(2,1)}, u32[]{:S(2)}, u32[]{:S(2)}) collective-permute-start(bf16[512,1024]{1,0:T(8,128)(2,1)} %convolution_convert_fusion.8), channel_id=1, source_target_pairs={{0,4},{4,0},{1,5},{5,1},{2,6},{6,2},{3,7},{7,3},{8,12},{12,8},{9,1... | collective-permute-start | bytes 3145736 | tf_op jit(solution)/shard_map/ppermute | solution.py:27
  504.2 88.8 %collective-permute-start.84 = (bf16[512,2048]{1,0:T(8,128)(2,1)S(1)}, bf16[512,2048]{1,0:T(8,128)(2,1)S(1)}, u32[]{:S(2)}, u32[]{:S(2)}) collective-permute-start(bf16[512,2048]{1,0:T(8,128)(2,1)S(1)} %slice.2086), channel_id=1, source_target_pairs={{0,1},{1,0},{2,3},{3,2},{4,5},{5,4},{6,7},{7,6},{8,9},{9,8},{10,11... | collective-permute-start | bytes 6291464 | tf_op jit(solution)/shard_map/ppermute | solution.py:27
  542.0 47.6 %collective-permute-start.122 = (bf16[512,1024]{1,0:T(8,128)(2,1)S(1)}, bf16[512,1024]{1,0:T(8,128)(2,1)S(1)}, u32[]{:S(2)}, u32[]{:S(2)}) collective-permute-start(bf16[512,1024]{1,0:T(8,128)(2,1)S(1)} %add_convert_fusion), channel_id=1, source_target_pairs={{0,16},{16,0},{1,17},{17,1},{2,18},{18,2},{3,19},{19,3},{4,20},{20... | collective-permute-start | bytes 3145736 | tf_op jit(solution)/shard_map/ppermute | solution.py:27
  562.8 44.8 %collective-permute-start.116 = (bf16[512,1024]{1,0:T(8,128)(2,1)}, bf16[512,1024]{1,0:T(8,128)(2,1)S(1)}, u32[]{:S(2)}, u32[]{:S(2)}) collective-permute-start(bf16[512,1024]{1,0:T(8,128)(2,1)} %convolution_convert_fusion.6), channel_id=1, source_target_pairs={{0,4},{4,0},{1,5},{5,1},{2,6},{6,2},{3,7},{7,3},{8,12},{12,8},{9,1... | collective-permute-start | bytes 3145736 | tf_op jit(solution)/shard_map/ppermute | solution.py:27
  585.3 74.1 %collective-permute-start.112 = (bf16[512,1024]{1,0:T(8,128)(2,1)S(1)}, bf16[512,1024]{1,0:T(8,128)(2,1)S(1)}, u32[]{:S(2)}, u32[]{:S(2)}) collective-permute-start(bf16[512,1024]{1,0:T(8,128)(2,1)S(1)} %copy-done.37), channel_id=1, source_target_pairs={{0,4},{4,0},{1,5},{5,1},{2,6},{6,2},{3,7},{7,3},{8,12},{12,8},{9,1... | collective-permute-start | bytes 3145736 | tf_op jit(solution)/shard_map/ppermute | solution.py:27
  588.1 70.3 %collective-permute-start.118 = (bf16[512,1024]{1,0:T(8,128)(2,1)S(1)}, bf16[512,1024]{1,0:T(8,128)(2,1)S(1)}, u32[]{:S(2)}, u32[]{:S(2)}) collective-permute-start(bf16[512,1024]{1,0:T(8,128)(2,1)S(1)} %add_convert_fusion.1), channel_id=1, source_target_pairs={{0,16},{16,0},{1,17},{17,1},{2,18},{18,2},{3,19},{19,3},{4,20},{20... | collective-permute-start | bytes 3145736 | tf_op jit(solution)/shard_map/ppermute | solution.py:27
  589.6 90.1 %collective-permute-start.114 = (bf16[512,1024]{1,0:T(8,128)(2,1)S(1)}, bf16[512,1024]{1,0:T(8,128)(2,1)S(1)}, u32[]{:S(2)}, u32[]{:S(2)}) collective-permute-start(bf16[512,1024]{1,0:T(8,128)(2,1)S(1)} %add_convert_fusion.2), channel_id=1, source_target_pairs={{0,16},{16,0},{1,17},{17,1},{2,18},{18,2},{3,19},{19,3},{4,20},{20... | collective-permute-start | bytes 3145736 | tf_op jit(solution)/shard_map/ppermute | solution.py:27
  594.3 108.6 %collective-permute-start.123 = (bf16[256,1024]{1,0:T(8,128)(2,1)S(1)}, bf16[256,1024]{1,0:T(8,128)(2,1)S(1)}, u32[]{:S(2)}, u32[]{:S(2)}) collective-permute-start(bf16[256,1024]{1,0:T(8,128)(2,1)S(1)} %select_convert_fusion), channel_id=1, source_target_pairs={{0,8},{8,0},{1,9},{9,1},{2,10},{10,2},{3,11},{11,3},{4,12},{12,4},... | collective-permute-start | bytes 1572872 | tf_op jit(solution)/shard_map/ppermute | solution.py:27
  607.7 82.4 %collective-permute-start.85 = (bf16[64,2048]{1,0:T(8,128)(2,1)S(1)}, bf16[64,2048]{1,0:T(8,128)(2,1)S(1)}, u32[]{:S(2)}, u32[]{:S(2)}) collective-permute-start(bf16[64,2048]{1,0:T(8,128)(2,1)S(1)} %get-tuple-element.110), channel_id=1, source_target_pairs={{0,8},{8,0},{1,9},{9,1},{2,10},{10,2},{3,11},{11,3},{4,12},{12,4},... | collective-permute-start | bytes 786440 | tf_op jit(solution)/shard_map/ppermute | solution.py:27
  658.3 22.1 %collective-permute-start.89 = (bf16[64,2048]{1,0:T(8,128)(2,1)S(1)}, bf16[64,2048]{1,0:T(8,128)(2,1)S(1)}, u32[]{:S(2)}, u32[]{:S(2)}) collective-permute-start(bf16[64,2048]{1,0:T(8,128)(2,1)S(1)} %get-tuple-element.111), channel_id=1, source_target_pairs={{0,2},{2,0},{1,3},{3,1},{4,6},{6,4},{5,7},{7,5},{8,10},{10,8},{9,1... | collective-permute-start | bytes 786440 | tf_op jit(solution)/shard_map/ppermute | solution.py:27
  659.4 32.4 %collective-permute-start.88 = (bf16[64,2048]{1,0:T(8,128)(2,1)S(1)}, bf16[64,2048]{1,0:T(8,128)(2,1)S(1)}, u32[]{:S(2)}, u32[]{:S(2)}) collective-permute-start(bf16[64,2048]{1,0:T(8,128)(2,1)S(1)} %get-tuple-element.112), channel_id=1, source_target_pairs={{0,2},{2,0},{1,3},{3,1},{4,6},{6,4},{5,7},{7,5},{8,10},{10,8},{9,1... | collective-permute-start | bytes 786440 | tf_op jit(solution)/shard_map/ppermute | solution.py:27
  690.0 47.7 %collective-permute-start.119 = (bf16[256,1024]{1,0:T(8,128)(2,1)S(1)}, bf16[256,1024]{1,0:T(8,128)(2,1)S(1)}, u32[]{:S(2)}, u32[]{:S(2)}) collective-permute-start(bf16[256,1024]{1,0:T(8,128)(2,1)S(1)} %select_convert_fusion.1), channel_id=1, source_target_pairs={{0,8},{8,0},{1,9},{9,1},{2,10},{10,2},{3,11},{11,3},{4,12},{12,4},... | collective-permute-start | bytes 1572872 | tf_op jit(solution)/shard_map/ppermute | solution.py:27
  691.8 47.9 %collective-permute-start.115 = (bf16[256,1024]{1,0:T(8,128)(2,1)S(1)}, bf16[256,1024]{1,0:T(8,128)(2,1)S(1)}, u32[]{:S(2)}, u32[]{:S(2)}) collective-permute-start(bf16[256,1024]{1,0:T(8,128)(2,1)S(1)} %select_convert_fusion.2), channel_id=1, source_target_pairs={{0,8},{8,0},{1,9},{9,1},{2,10},{10,2},{3,11},{11,3},{4,12},{12,4},... | collective-permute-start | bytes 1572872 | tf_op jit(solution)/shard_map/ppermute | solution.py:27
  702.4 24.6 %collective-permute-start.94 = (bf16[64,2048]{1,0:T(8,128)(2,1)S(1)}, bf16[64,2048]{1,0:T(8,128)(2,1)S(1)}, u32[]{:S(2)}, u32[]{:S(2)}) collective-permute-start(bf16[64,2048]{1,0:T(8,128)(2,1)S(1)} %get-tuple-element.150), channel_id=1, source_target_pairs={{0,8},{8,0},{1,9},{9,1},{2,10},{10,2},{3,11},{11,3},{4,12},{12,4},... | collective-permute-start | bytes 786440 | tf_op jit(solution)/shard_map/ppermute | solution.py:27
  702.7 24.5 %collective-permute-start.92 = (bf16[64,2048]{1,0:T(8,128)(2,1)S(1)}, bf16[64,2048]{1,0:T(8,128)(2,1)S(1)}, u32[]{:S(2)}, u32[]{:S(2)}) collective-permute-start(bf16[64,2048]{1,0:T(8,128)(2,1)S(1)} %get-tuple-element.150), channel_id=1, source_target_pairs={{0,2},{2,0},{1,3},{3,1},{4,6},{6,4},{5,7},{7,5},{8,10},{10,8},{9,1... | collective-permute-start | bytes 786440 | tf_op jit(solution)/shard_map/ppermute | solution.py:27
  712.7 19.9 %collective-permute-start.93 = (bf16[64,2048]{1,0:T(8,128)(2,1)S(1)}, bf16[64,2048]{1,0:T(8,128)(2,1)S(1)}, u32[]{:S(2)}, u32[]{:S(2)}) collective-permute-start(bf16[64,2048]{1,0:T(8,128)(2,1)S(1)} %get-tuple-element.151), channel_id=1, source_target_pairs={{0,8},{8,0},{1,9},{9,1},{2,10},{10,2},{3,11},{11,3},{4,12},{12,4},... | collective-permute-start | bytes 786440 | tf_op jit(solution)/shard_map/ppermute | solution.py:27
  789.6 13.3 %collective-permute-start.124 = (f32[4,2048]{1,0:T(4,128)}, f32[4,2048]{1,0:T(4,128)}, u32[]{:S(2)}, u32[]{:S(2)}) collective-permute-start(f32[4,2048]{1,0:T(4,128)} %pad_maximum_fusion.20), channel_id=1, source_target_pairs={{0,1},{1,0},{2,3},{3,2},{4,5},{5,4},{6,7},{7,6},{8,9},{9,8},{10,11... | collective-permute-start | bytes 98312 | tf_op jit(solution)/shard_map/ppermute | solution.py:27
  798.9 39.8 %collective-permute-start.101 = (bf16[512,2048]{1,0:T(8,128)(2,1)S(1)}, bf16[512,2048]{1,0:T(8,128)(2,1)S(1)}, u32[]{:S(2)}, u32[]{:S(2)}) collective-permute-start(bf16[512,2048]{1,0:T(8,128)(2,1)S(1)} %slice.2085), channel_id=1, source_target_pairs={{0,1},{1,0},{2,3},{3,2},{4,5},{5,4},{6,7},{7,6},{8,9},{9,8},{10,11... | collective-permute-start | bytes 6291464 | tf_op jit(solution)/shard_map/ppermute | solution.py:27
  802.0 36.2 %collective-permute-start.109 = (bf16[512,1024]{1,0:T(8,128)(2,1)S(1)}, bf16[512,1024]{1,0:T(8,128)(2,1)S(1)}, u32[]{:S(2)}, u32[]{:S(2)}) collective-permute-start(bf16[512,1024]{1,0:T(8,128)(2,1)S(1)} %pad_maximum_fusion.12), channel_id=1, source_target_pairs={{0,4},{4,0},{1,5},{5,1},{2,6},{6,2},{3,7},{7,3},{8,12},{12,8},{9,1... | collective-permute-start | bytes 3145736 | tf_op jit(solution)/shard_map/ppermute | solution.py:27
  807.7 20.6 %collective-permute-start.126 = (f32[4,2048]{1,0:T(4,128)S(1)}, f32[4,2048]{1,0:T(4,128)S(1)}, u32[]{:S(2)}, u32[]{:S(2)}) collective-permute-start(f32[4,2048]{1,0:T(4,128)S(1)} %add.379), channel_id=1, source_target_pairs={{0,4},{4,0},{1,5},{5,1},{2,6},{6,2},{3,7},{7,3},{8,12},{12,8},{9,1... | collective-permute-start | bytes 98312 | tf_op jit(solution)/shard_map/ppermute | solution.py:27
  832.9 23.4 %collective-permute-start.108 = (bf16[512,1024]{1,0:T(8,128)(2,1)S(1)}, bf16[512,1024]{1,0:T(8,128)(2,1)S(1)}, u32[]{:S(2)}, u32[]{:S(2)}) collective-permute-start(bf16[512,1024]{1,0:T(8,128)(2,1)S(1)} %pad_maximum_fusion.11), channel_id=1, source_target_pairs={{0,4},{4,0},{1,5},{5,1},{2,6},{6,2},{3,7},{7,3},{8,12},{12,8},{9,1... | collective-permute-start | bytes 3145736 | tf_op jit(solution)/shard_map/ppermute | solution.py:27
  838.5 45.8 %collective-permute-start.110 = (bf16[512,1024]{1,0:T(8,128)(2,1)S(1)}, bf16[512,1024]{1,0:T(8,128)(2,1)S(1)}, u32[]{:S(2)}, u32[]{:S(2)}) collective-permute-start(bf16[512,1024]{1,0:T(8,128)(2,1)S(1)} %add_convert_fusion.3), channel_id=1, source_target_pairs={{0,16},{16,0},{1,17},{17,1},{2,18},{18,2},{3,19},{19,3},{4,20},{20... | collective-permute-start | bytes 3145736 | tf_op jit(solution)/shard_map/ppermute | solution.py:27
  839.7 49.2 %collective-permute-start.102 = (bf16[64,2048]{1,0:T(8,128)(2,1)S(1)}, bf16[64,2048]{1,0:T(8,128)(2,1)S(1)}, u32[]{:S(2)}, u32[]{:S(2)}) collective-permute-start(bf16[64,2048]{1,0:T(8,128)(2,1)S(1)} %get-tuple-element.102), channel_id=1, source_target_pairs={{0,8},{8,0},{1,9},{9,1},{2,10},{10,2},{3,11},{11,3},{4,12},{12,4},... | collective-permute-start | bytes 786440 | tf_op jit(solution)/shard_map/ppermute | solution.py:27
  841.4 43.4 %collective-permute-start.106 = (bf16[64,2048]{1,0:T(8,128)(2,1)S(1)}, bf16[64,2048]{1,0:T(8,128)(2,1)S(1)}, u32[]{:S(2)}, u32[]{:S(2)}) collective-permute-start(bf16[64,2048]{1,0:T(8,128)(2,1)S(1)} %get-tuple-element.103), channel_id=1, source_target_pairs={{0,2},{2,0},{1,3},{3,1},{4,6},{6,4},{5,7},{7,5},{8,10},{10,8},{9,1... | collective-permute-start | bytes 786440 | tf_op jit(solution)/shard_map/ppermute | solution.py:27
  843.1 45.8 %collective-permute-start.105 = (bf16[64,2048]{1,0:T(8,128)(2,1)S(1)}, bf16[64,2048]{1,0:T(8,128)(2,1)S(1)}, u32[]{:S(2)}, u32[]{:S(2)}) collective-permute-start(bf16[64,2048]{1,0:T(8,128)(2,1)S(1)} %get-tuple-element.104), channel_id=1, source_target_pairs={{0,2},{2,0},{1,3},{3,1},{4,6},{6,4},{5,7},{7,5},{8,10},{10,8},{9,1... | collective-permute-start | bytes 786440 | tf_op jit(solution)/shard_map/ppermute | solution.py:27
  856.3 28.5 %collective-permute-start.103 = (bf16[64,2048]{1,0:T(8,128)(2,1)S(1)}, bf16[64,2048]{1,0:T(8,128)(2,1)S(1)}, u32[]{:S(2)}, u32[]{:S(2)}) collective-permute-start(bf16[64,2048]{1,0:T(8,128)(2,1)S(1)} %get-tuple-element.105), channel_id=1, source_target_pairs={{0,8},{8,0},{1,9},{9,1},{2,10},{10,2},{3,11},{11,3},{4,12},{12,4},... | collective-permute-start | bytes 786440 | tf_op jit(solution)/shard_map/ppermute | solution.py:27
  886.8 19.0 %collective-permute-start.111 = (bf16[256,1024]{1,0:T(8,128)(2,1)S(1)}, bf16[256,1024]{1,0:T(8,128)(2,1)S(1)}, u32[]{:S(2)}, u32[]{:S(2)}) collective-permute-start(bf16[256,1024]{1,0:T(8,128)(2,1)S(1)} %select_convert_fusion.3), channel_id=1, source_target_pairs={{0,8},{8,0},{1,9},{9,1},{2,10},{10,2},{3,11},{11,3},{4,12},{12,4},... | collective-permute-start | bytes 1572872 | tf_op jit(solution)/shard_map/ppermute | solution.py:27
  (158 other events, 1886.8 us)

commit v2 on v1

v2 whole, which is shorter than its diff:
```python
import jax
import jax.numpy as jnp
from jax import lax
from jax.experimental import pallas as pl
from jax.experimental.pallas import tpu as pltpu
from jax.sharding import Mesh, PartitionSpec as P

HEAD_DIM = 128
EPS = 1e-06
THETA = 500000.0
NEG = -1e30
F32 = jnp.float32
BF16 = jnp.bfloat16


def dot_rows_cols(left, right):
    return jnp.dot(left, right, preferred_element_type=F32)


def contract_cols(left, right):
    return lax.dot_general(left, right, (((1,), (1,)), ((), ())), preferred_element_type=F32)


def contract_rows(left, right):
    return lax.dot_general(left, right, (((0,), (0,)), ((), ())), preferred_element_type=F32)


def swap(values, axis):
    return lax.ppermute(values, axis, [(0, 1), (1, 0)])


def pick(flag, yes, no):
    return jnp.where(flag, yes, no)


def after(values, *done):
    return lax.optimization_barrier((values,) + done)[0] if done else values


class Net:
    def send(self, values, axis):
        return swap(values, axis)


def region(flag, step):
    out = jax.eval_shape(step)
    return lax.cond(flag, step, lambda: jax.tree.map(lambda leaf: jnp.zeros(leaf.shape, leaf.dtype), out))


def meet(*values):
    leaves, tree = jax.tree.flatten(values)
    return jax.tree.unflatten(tree, lax.optimization_barrier(tuple(leaves)))


class Sequence:
    def __init__(self):
        self.done = ()

    def wait(self, *received):
        self.done = self.done + received

    def run(self, step, *operands):
        if self.done:
            operands = lax.optimization_barrier(operands + self.done)[: len(operands)]
        out = step(*operands)
        self.done = out if isinstance(out, tuple) else (out,)
        return out


class Layout:
    def __init__(self, n_dp, n_tensor):
        self.dp_axes = tuple(f"d{i}" for i in range(n_dp.bit_length() - 1))
        self.tensor_axes = tuple(f"t{i}" for i in range(n_tensor.bit_length() - 1))
        self.col_axis = self.dp_axes[1]
        self.far = self.dp_axes[0]
        self.near = tuple(a for a in self.dp_axes if a not in (self.far, self.col_axis))
        self.core, self.side = self.tensor_axes[1], self.tensor_axes[0]
        self.n_dp = n_dp
        self.n_bits = len(self.dp_axes)

    def shape_of(self):
        return (2,) * (len(self.dp_axes) + len(self.tensor_axes))

    def dp_mask(self, axis):
        return 1 << (self.n_bits - 1 - self.dp_axes.index(axis))

    def block_order(self):
        order = []
        for j in range(1 << len(self.near)):
            block = sum(self.dp_mask(axis) for i, axis in enumerate(self.near) if (j >> i) & 1)
            for ahead in (0, self.dp_mask(self.far)):
                order += [block | ahead, block | ahead | self.dp_mask(self.col_axis)]
        return order

    def flip_blocks(self, blocks):
        for axis in self.near:
            flag, mask = lax.axis_index(axis) == 1, self.dp_mask(axis)
            blocks = [pick(flag, blocks[b ^ mask], blocks[b]) for b in range(len(blocks))]
        return blocks

    def to_relative(self, values):
        width = values.shape[-1] // self.n_dp
        blocks = [values[..., b * width : (b + 1) * width] for b in range(self.n_dp)]
        blocks = self.flip_blocks(blocks)
        return jnp.concatenate([blocks[b] for b in self.block_order()], -1)

    def from_relative(self, values):
        width = values.shape[-1] // self.n_dp
        blocks = [None] * self.n_dp
        for place, b in enumerate(self.block_order()):
            blocks[b] = values[..., place * width : (place + 1) * width]
        return jnp.concatenate(self.flip_blocks(blocks), -1)


def rope_tables(pos_col):
    lane = jnp.arange(HEAD_DIM, dtype=jnp.int32)[None, :]
    pair = (lane % (HEAD_DIM // 2)).astype(F32)
    inverse = THETA ** (-(pair * 2.0 / HEAD_DIM))
    angles = pos_col.astype(F32) * inverse
    return jnp.cos(angles), jnp.sin(angles) * jnp.where(lane < HEAD_DIM // 2, -1.0, 1.0)


def load_rows(ref):
    values = ref[...]
    return values.reshape(-1, values.shape[-1])


def head_scores(q_ref, k_ref, norm_ref, gain_q_ref, gain_k_ref, cos_ref, sin_ref, mask_ref):
    norms, cos_tab, sin_tab = load_rows(norm_ref), load_rows(cos_ref), load_rows(sin_ref)

    def rotated(values, gain):
        values = values * gain
        return (values * cos_tab + pltpu.roll(values, HEAD_DIM // 2, 1) * sin_tab).astype(BF16)

    query_hat = load_rows(q_ref) * norms[:, 0:1]
    key_hat = load_rows(k_ref) * norms[:, 1:2]
    q_rot = rotated(query_hat, gain_q_ref[...])
    k_rot = rotated(key_hat, gain_k_ref[...])
    scores = contract_cols(q_rot, k_rot) * HEAD_DIM ** (-0.5)
    scores = jnp.where(mask_ref[0] > 0, scores, NEG)
    exp_scores = jnp.exp(scores - jnp.max(scores, -1, keepdims=True))
    probs = exp_scores / jnp.sum(exp_scores, -1, keepdims=True)
    return query_hat, key_hat, q_rot, k_rot, probs, cos_tab, sin_tab


def attend_kernel(q_ref, k_ref, v_ref, norm_ref, gain_q_ref, gain_k_ref, cos_ref, sin_ref, mask_ref, out_ref):
    probs = head_scores(q_ref, k_ref, norm_ref, gain_q_ref, gain_k_ref, cos_ref, sin_ref, mask_ref)[4]
    out = dot_rows_cols(probs.astype(BF16), load_rows(v_ref).astype(BF16)).astype(BF16)
    out_ref[...] = out.reshape(out_ref.shape)


def attend_back_kernel(
    q_ref, k_ref, v_ref, norm_ref, gain_q_ref, gain_k_ref, cos_ref, sin_ref, mask_ref, grad_ref,
    grad_q_ref, grad_k_ref, grad_v_ref, inner_ref, gains_ref,
):
    query_hat, key_hat, q_rot, k_rot, probs, cos_tab, sin_tab = head_scores(
        q_ref, k_ref, norm_ref, gain_q_ref, gain_k_ref, cos_ref, sin_ref, mask_ref
    )
    grad_head = load_rows(grad_ref)
    grad_prob = contract_cols(grad_head, load_rows(v_ref).astype(BF16))
    row_dot = jnp.sum(probs * grad_prob, -1, keepdims=True)
    grad_scores = (probs * (grad_prob - row_dot)).astype(BF16)
    scale = HEAD_DIM ** (-0.5)

    def unrotated(values):
        return values * cos_tab - pltpu.roll(values, HEAD_DIM // 2, 1) * sin_tab

    grad_q = unrotated(dot_rows_cols(grad_scores, k_rot) * scale)
    grad_k = unrotated(contract_rows(grad_scores, q_rot) * scale)
    grad_v = contract_rows(probs.astype(BF16), grad_head).astype(BF16)
    product_q, product_k = grad_q * query_hat, grad_k * key_hat
    inner_q = jnp.sum(product_q * gain_q_ref[...], -1, keepdims=True)
    inner_k = jnp.sum(product_k * gain_k_ref[...], -1, keepdims=True)
    grad_q_ref[...] = grad_q.reshape(grad_q_ref.shape)
    grad_k_ref[...] = grad_k.reshape(grad_k_ref.shape)
    grad_v_ref[...] = grad_v.reshape(grad_v_ref.shape)
    inner_ref[...] = jnp.concatenate([inner_q, inner_k], 1).reshape(inner_ref.shape)
    gains_ref[...] = jnp.concatenate(
        [jnp.sum(product_q, 0, keepdims=True), jnp.sum(product_k, 0, keepdims=True)], 0
    ).reshape(gains_ref.shape)


def attention(qkv, norms, gain_query, gain_key, cos_tab, sin_tab, mask, grad_heads=None):
    n_tokens = qkv.shape[0]
    rows, n_heads = n_tokens // 4, qkv.shape[1] // (3 * HEAD_DIM)

    def split(values):
        return values.reshape(2, 2, rows, values.shape[-1])

    def columns(first):
        return pl.BlockSpec((2, 1, rows, HEAD_DIM), lambda s, h: (0, s, 0, first + h))

    def whole(width):
        return pl.BlockSpec((2, 1, rows, width), lambda s, h: (0, s, 0, 0))

    gain = pl.BlockSpec((1, HEAD_DIM), lambda s, h: (0, h))
    in_specs = [columns(0), columns(n_heads), columns(2 * n_heads), whole(2), gain, gain, whole(HEAD_DIM), whole(HEAD_DIM)]
    in_specs.append(pl.BlockSpec((1, 2 * rows, 2 * rows), lambda s, h: (s, 0, 0)))
    heads = split(qkv)
    operands = [heads, heads, heads, split(norms), gain_query[None], gain_key[None], split(cos_tab), split(sin_tab), mask]
    shape = (2, 2, rows, n_heads * HEAD_DIM)
    kernel, out_specs, out_shape = attend_kernel, columns(0), jax.ShapeDtypeStruct(shape, BF16)
    if grad_heads is not None:
        in_specs.append(columns(0))
        operands.append(split(grad_heads))
        kernel = attend_back_kernel
        out_specs = (
            columns(0),
            columns(0),
            columns(0),
            pl.BlockSpec((1, 2, 1, rows, 2), lambda s, h: (h, 0, s, 0, 0)),
            pl.BlockSpec((1, 2, HEAD_DIM), lambda s, h: (s, 0, h)),
        )
        out_shape = (
            jax.ShapeDtypeStruct(shape, F32),
            jax.ShapeDtypeStruct(shape, F32),
            jax.ShapeDtypeStruct(shape, BF16),
            jax.ShapeDtypeStruct((n_heads, 2, 2, rows, 2), F32),
            jax.ShapeDtypeStruct((2, 2, n_heads * HEAD_DIM), F32),
        )
    out = pl.pallas_call(
        kernel,
        grid=(2, n_heads),
        in_specs=in_specs,
        out_specs=out_specs,
        out_shape=out_shape,
        compiler_params=pltpu.CompilerParams(vmem_limit_bytes=48 * 1024 * 1024),
        cost_estimate=pl.CostEstimate(flops=1 << 30, bytes_accessed=1 << 23, transcendentals=1 << 20),
    )(*operands)
    if grad_heads is None:
        return out.reshape(n_tokens, -1)
    return tuple(part.reshape(n_tokens, -1) for part in out[:3]) + (out[3], jnp.sum(out[4], 0))


def block_program(lay):
    col, side, core = lay.col_axis, lay.side, lay.core

    def my(axis):
        return lax.axis_index(axis)

    def halves(weights):
        half = [w.shape[1] // 2 for w in weights]
        low = jnp.concatenate([w[:, :h] for w, h in zip(weights, half)], 1)
        high = jnp.concatenate([w[:, h:] for w, h in zip(weights, half)], 1)
        return low, high

    def leaving(weights):
        low, high = halves(weights)
        return pick(my(col) == 0, high, low)

    def both_rows(weights, got):
        low, high = halves(weights)
        first = my(col) == 0
        return jnp.concatenate([pick(first, low, got), pick(first, got, high)], 0)

    def ahead(block):
        return lax.all_gather(block, lay.far, axis=0, tiled=True)

    def beyond(both):
        half = both.shape[0] // 2
        return lax.dynamic_slice_in_dim(both, (1 - my(lay.far)) * half, half, 0)

    def in_two(own, other):
        first = my(lay.far) == 0
        return jnp.concatenate([pick(first, own, other), pick(first, other, own)], 0)

    def behind(total):
        return lax.psum_scatter(total.astype(BF16), lay.far, scatter_dimension=0, tiled=True)

    def spread(net, block):
        pieces = [block]
        for axis in lay.near:
            pieces = pieces + [net.send(piece, axis) for piece in pieces]
        return pieces

    def begin(net, grads):
        return [net.send(grad, lay.near[-1]) for grad in grads]

    def finish(net, keeps, received):
        pieces = [a.astype(F32) + b.astype(F32) for a, b in zip(keeps, received)]
        for axis in reversed(lay.near[:-1]):
            half = len(pieces) // 2
            others = [net.send(piece.astype(BF16), axis) for piece in pieces[half:]]
            pieces = [a + b.astype(F32) for a, b in zip(pieces[:half], others)]
        return pieces[0].astype(BF16)

    def to_leave(total):
        half = total.shape[0] // 2
        return pick(my(col) == 0, total[half:], total[:half]).astype(BF16)

    def owned(total, got):
        half = total.shape[0] // 2
        first = my(col) == 0
        mine, got = pick(first, total[:half], total[half:]), got.astype(F32)
        return pick(first, mine, got), pick(first, got, mine)

    def gather_begin(net, own):
        half = own.shape[0] // 2
        a0, b0 = own[:half], own[half:]
        return a0, b0, net.send(a0, side), net.send(b0, col)

    def gather_middle(net, state):
        a0, b0, a_side, b_col = state
        half = a0.shape[0]
        a_far = net.send(jnp.concatenate([a0, a_side], 0), col)
        b_far = net.send(jnp.concatenate([b0, b_col], 0), side)
        return [a0, b0, a_side, b_far[:half], a_far[:half], b_col, a_far[half:], b_far[half:]], (a_far, b_far)

    def gather_end(net, state):
        mine = jnp.concatenate(state[0], 0)
        other = net.send(mine, core)
        return jnp.concatenate([mine, other], 0), other

    def scatter_begin(net, part):
        n = part.shape[0] // 2
        return part[:n], net.send(part[n:].astype(BF16), core)

    def scatter_second(net, state):
        part = state[0] + state[1].astype(F32)
        half = part.shape[0] // 8
        a0, b0, a_side, b_side, a_col, b_col, a_both, b_both = (part[i * half : (i + 1) * half] for i in range(8))
        received = (
            net.send(jnp.concatenate([a_col, a_both], 0).astype(BF16), col),
            net.send(jnp.concatenate([b_side, b_both], 0).astype(BF16), side),
        )
        return jnp.concatenate([a0, a_side], 0), jnp.concatenate([b0, b_col], 0), received

    def scatter_third(net, state):
        a_sum, b_sum = (own + got.astype(F32) for own, got in zip(state[:2], state[2]))
        half = a_sum.shape[0] // 2
        received = net.send(a_sum[half:].astype(BF16), side), net.send(b_sum[half:].astype(BF16), col)
        return a_sum[:half], b_sum[:half], received

    def scatter_end(state):
        a0, b0, received = state
        return jnp.concatenate([a0 + received[0].astype(F32), b0 + received[1].astype(F32)], 0)

    def token_rows(values, exchange):
        quarters = values.reshape(4, -1)
        rows = [quarters[0:1], quarters[1:2], quarters[2:3], quarters[3:4]]
        for axis, mask in ((side, 2), (core, 1)):
            flag = my(axis) == 1
            rows = [pick(flag, rows[i ^ mask], rows[i]) for i in range(4)]
        own = jnp.concatenate(rows, 0)
        other = exchange(own)
        order = [own[0:1], own[2:3], other[0:1], other[2:3], own[1:2], own[3:4], other[1:2], other[3:4]]
        return jnp.concatenate(order, 0)

    def token_rows_of(positions, seg_ids, net):
        rows = []

        def exchange(own):
            rows.append(own)
            return own

        token_rows(positions, exchange)
        token_rows(seg_ids, exchange)
        other = net.send(jnp.concatenate(rows, 0), col)
        return [
            token_rows(values, lambda own, i=i: other[4 * i : 4 * i + 4])
            for i, values in enumerate((positions, seg_ids))
        ]

    def add_all(net, values, axes):
        for axis in axes:
            received = net.send(values, axis)
            values = values + received
        return values

    def add_stats(net, rows):
        rows = rows.reshape(-1, 2, 2, 2, rows.shape[1] // 8)
        for dim, axis in ((1, core), (2, col), (3, side)):
            received = net.send(rows, axis)
            rows = rows + jnp.flip(received, dim)
        return rows.reshape(rows.shape[0], -1), received

    def on_device(
        hidden_in, out_grad, w_query, w_key, w_value, w_out, w_gate, w_up, w_down, gains, seg_ids, positions
    ):
        model_width = hidden_in.shape[1]
        head_cols = w_query.shape[1] // 2
        n_heads = head_cols // HEAD_DIM
        n_tokens = hidden_in.shape[0] * 8
        seq_len = n_tokens // 2
        score_scale = HEAD_DIM ** (-0.5)
        place = my(side) * 4 + my(core) * 2 + my(col)
        offset = place * head_cols
        per = seq_len // 4

        def by_seq(rows):
            return rows.reshape(2, 2, 2 * per).transpose(1, 0, 2).reshape(2, seq_len)

        net = Net()
        flag = positions[0] >= 0
        n_near = 1 << len(lay.near)
        piece = model_width // n_near
        kept_pieces, sent_pieces = range(n_near // 2), range(n_near // 2, n_near)

        def stack(*parts):
            return jnp.concatenate(parts, 0)

        def by_rows(left, pieces, cols=slice(None)):
            return sum(
                dot_rows_cols(left[:, j * piece : (j + 1) * piece], block[:, cols]) for j, block in enumerate(pieces)
            )

        def weight_grad(seq, left, right, which):
            return [
                seq.run(
                    lambda a, b: contract_rows(a, b).astype(BF16), left[:, j * piece : (j + 1) * piece], right
                )
                for j in which
            ]

        attn_weights = [w_query, w_key, w_value, w_out]

        def part_first():
            block_attn = both_rows(attn_weights, net.send(leaving(attn_weights), col))
            pos_rows, seg_rows = token_rows_of(positions, seg_ids, net)
            return block_attn, leaving([w_gate]), leaving([w_up]), pos_rows, seg_rows, lay.to_relative(hidden_in)

        block_attn, leave_gate, leave_up, pos_rows, seg_rows, x_low = region(flag, part_first)
        far_attn, own_attn = ahead(block_attn), spread(net, block_attn)[1:]

        def part_tokens():
            state = gather_middle(net, gather_begin(net, x_low))
            got_gate = net.send(after(leave_gate, *state[1]), col)
            x_all, other = gather_end(net, state)
            return x_all, leaving([w_down]), both_rows([w_gate], got_gate)

        out = region(flag, part_tokens)
        far_attn, own_attn, (x_all, leave_down, block_gate) = meet(far_attn, own_attn, out)
        relay_attn = spread(net, beyond(far_attn))[1:]
        far_gate, got_up = ahead(block_gate), net.send(leave_up, col)

        def part_tables():
            cos_tab, sin_tab = rope_tables(pos_rows.reshape(n_tokens, 1))
            ids_rows = token_rows(jnp.arange(seq_len, dtype=jnp.int32), lambda rows: rows)
            seg_seq, ids_seq = by_seq(seg_rows), by_seq(ids_rows)
            mask = (seg_seq[:, :, None] == seg_seq[:, None, :]) & (ids_seq[:, :, None] >= ids_seq[:, None, :])
            mask = mask.astype(F32)
            gain_query = lax.dynamic_slice_in_dim(gains[0], offset, head_cols)
            gain_key = lax.dynamic_slice_in_dim(gains[1], offset, head_cols)
            gain_post = lay.to_relative(gains[2:4])
            more = gain_query, gain_key, gain_post[0:1], gain_post[1:2], lay.to_relative(out_grad).astype(F32)
            return cos_tab, sin_tab, mask, more

        out = region(flag, part_tables)
        relay_attn, got_up, (cos_tab, sin_tab, mask, more) = meet(relay_attn, got_up, out)
        gain_query, gain_key, gain_attn, gain_mlp, grad_out = more
        block_up = both_rows([w_up], got_up)
        far_up, own_up = ahead(block_up), spread(net, block_up)[1:]
        qkv_cols, out_cols = slice(3 * head_cols), slice(3 * head_cols, None)


        def part_qkv():
            near_attn = [far_attn, *(in_two(own, other) for own, other in zip(own_attn, relay_attn))]
            qkv = by_rows(x_all, near_attn, qkv_cols)
            squares, _ = add_stats(
                net,
                jnp.stack(
                    [jnp.sum(part * part, -1) for part in (qkv[:, :head_cols], qkv[:, head_cols : 2 * head_cols])], 0
                ),
            )
            return near_attn, qkv, squares

        out = region(flag, part_qkv)
        leave_down, (near_attn, qkv, squares) = meet(leave_down, out)
        got_down = net.send(leave_down, col)

        def part_attend():
            norms = lax.rsqrt(squares / model_width + EPS).T
            attn_low = attention(qkv, norms, gain_query, gain_key, cos_tab, sin_tab, mask)
            out_w = stack(*(block[:, out_cols] for block in near_attn))
            state = scatter_begin(net, contract_cols(attn_low, out_w))
            return attn_low, norms, out_w, state

        out = region(flag, part_attend)
        own_up, far_gate, got_down, (attn_low, norms, out_w, state) = meet(own_up, far_gate, got_down, out)
        near_gate = spread(net, far_gate)
        block_down = both_rows([w_down], got_down)
        far_down = ahead(block_down)

        def part_resid():
            attn_sum = scatter_end(scatter_third(net, scatter_second(net, state)))
            norm_attn = lax.rsqrt(jnp.mean(attn_sum * attn_sum, -1, keepdims=True) + EPS)
            attn_hat = attn_sum * norm_attn
            resid = x_low.astype(F32) + attn_hat * gain_attn
            return norm_attn, attn_hat, resid, gather_begin(net, resid.astype(BF16))

        out = region(flag, part_resid)
        near_gate, far_up, (norm_attn, attn_hat, resid, state) = meet(near_gate, far_up, out)
        relay_up = spread(net, beyond(far_up))[1:]
        own_down = spread(net, block_down)[1:]

        def part_gate():
            mlp_in, _ = gather_end(net, gather_middle(net, state))
            return mlp_in, by_rows(mlp_in, near_gate)

        out = region(flag, part_gate)
        relay_up, own_down, far_down, (mlp_in, gate_proj) = meet(relay_up, own_down, far_down, out)
        relay_down = spread(net, beyond(far_down))[1:]

        def part_up():
            near_up = [far_up, *(in_two(own, other) for own, other in zip(own_up, relay_up))]
            up_proj = by_rows(mlp_in, near_up)
            hidden_act = (gate_proj * jax.nn.sigmoid(gate_proj) * up_proj).astype(BF16)
            return up_proj, hidden_act, stack(*near_gate), stack(*near_up)

        out = region(flag, part_up)
        relay_down, (up_proj, hidden_act, gate_w, up_w) = meet(relay_down, out)

        act_halves = slice(hidden_act.shape[1] // 2), slice(hidden_act.shape[1] // 2, None)

        def part_down():
            down_w = stack(far_down, *(in_two(own, other) for own, other in zip(own_down, relay_down)))
            state = scatter_begin(net, contract_cols(hidden_act, down_w))
            mlp_sum = scatter_end(scatter_third(net, scatter_second(net, state)))
            norm_mlp = lax.rsqrt(jnp.mean(mlp_sum * mlp_sum, -1, keepdims=True) + EPS)
            mlp_hat = mlp_sum * norm_mlp
            scaled = grad_out * gain_mlp
            grad_mlp = norm_mlp * (scaled - mlp_hat * jnp.mean(mlp_hat * scaled, -1, keepdims=True))
            grad_mlp_all, _ = gather_end(net, gather_middle(net, gather_begin(net, grad_mlp.astype(BF16))))
            seq = Sequence()
            sends = [weight_grad(seq, grad_mlp_all, hidden_act[:, half], sent_pieces) for half in act_halves]
            return down_w, mlp_hat, grad_mlp_all, sends

        down_w, mlp_hat, grad_mlp_all, sends = region(flag, part_down)
        got_first, got_second = [begin(net, grads) for grads in sends]

        def part_back_act():
            seq = Sequence()
            keeps_first = weight_grad(seq, grad_mlp_all, hidden_act[:, act_halves[0]], kept_pieces)

            def back_act(grad_mlp_all, down_w):
                sig_gate = jax.nn.sigmoid(gate_proj)
                grad_act = dot_rows_cols(grad_mlp_all, down_w)
                grad_gate = (grad_act * up_proj * (sig_gate * (1.0 + gate_proj * (1.0 - sig_gate)))).astype(BF16)
                return grad_gate, (grad_act * (gate_proj * sig_gate)).astype(BF16)

            grad_gate, grad_up = seq.run(back_act, grad_mlp_all, down_w)
            return keeps_first, grad_gate, grad_up, seq.run(contract_cols, grad_gate, gate_w)

        out = region(flag, part_back_act)
        got_first, (keeps_first, grad_gate, grad_up, grad_part) = meet(got_first, out)
        down_first = behind(finish(net, keeps_first, got_first))

        def part_back_resid():
            seq = Sequence()
            state = scatter_begin(net, seq.run(lambda a, b, c: a + contract_cols(b, c), grad_part, grad_up, up_w))
            keeps_second = weight_grad(seq, grad_mlp_all, hidden_act[:, act_halves[1]], kept_pieces)
            return weight_grad(seq, mlp_in, grad_gate, sent_pieces), keeps_second, state

        out = region(flag, part_back_resid)
        got_second, (sends, keeps_second, state) = meet(got_second, out)
        got_gate = begin(net, sends)
        down_second = behind(finish(net, keeps_second, got_second))

        def part_back_attn():
            seq = Sequence()
            later = scatter_second(net, state)
            keeps_gate = weight_grad(seq, mlp_in, grad_gate, kept_pieces)
            seq.wait(*later[2])
            later = scatter_third(net, later)
            sends = weight_grad(seq, mlp_in, grad_up, sent_pieces)
            seq.wait(*later[2])
            grad_resid = grad_out + scatter_end(later)
            scaled = grad_resid * gain_attn
            grad_attn = norm_attn * (scaled - attn_hat * jnp.mean(attn_hat * scaled, -1, keepdims=True))
            first = gather_begin(net, grad_attn.astype(BF16))
            gain_row_attn = jnp.sum(grad_resid * attn_hat, 0, keepdims=True)
            keeps_up = weight_grad(seq, mlp_in, grad_up, kept_pieces)
            return keeps_gate, sends, keeps_up, grad_resid, first, gain_row_attn

        out = region(flag, part_back_attn)
        got_gate, down_first, out = meet(got_gate, down_first, out)
        keeps_gate, sends, keeps_up, grad_resid, state, gain_row_attn = out
        got_up = begin(net, sends)
        total_gate = behind(finish(net, keeps_gate, got_gate))

        def part_back_heads():
            seq = Sequence()
            grad_attn_all, _ = gather_end(net, gather_middle(net, state))
            grad_heads = dot_rows_cols(grad_attn_all, out_w).astype(BF16)
            grads = attention(qkv, norms, gain_query, gain_key, cos_tab, sin_tab, mask, grad_heads)
            sends = [
                jnp.concatenate(pair, 1)
                for pair in zip(
                    weight_grad(seq, x_all, grads[2], sent_pieces), weight_grad(seq, grad_attn_all, attn_low, sent_pieces)
                )
            ]
            return grad_attn_all, grads, sends

        out = region(flag, part_back_heads)
        got_up, down_second, (grad_attn_all, grads, sends) = meet(got_up, down_second, out)
        grad_query_n, grad_key_n, grad_value_low, inner_parts, head_gains = grads
        got_first = begin(net, sends)
        total_up = behind(finish(net, keeps_up, got_up))
        total_down = jnp.concatenate([down_first, down_second], 1)
        got_down = net.send(to_leave(total_down), col)

        def part_back_qkv():
            seq = Sequence()
            inner, received = add_stats(net, jnp.sum(inner_parts, 0).reshape(n_tokens, 2).T)
            keeps_first = [
                jnp.concatenate(pair, 1)
                for pair in zip(
                    weight_grad(seq, x_all, grad_value_low, kept_pieces),
                    weight_grad(seq, grad_attn_all, attn_low, kept_pieces),
                )
            ]
            seq.wait(received)
            inner = inner.T / model_width

            def through_norm(grad, i, gain):
                hat = qkv[:, i * head_cols : (i + 1) * head_cols] * norms[:, i : i + 1]
                return (norms[:, i : i + 1] * (grad * gain - hat * inner[:, i : i + 1])).astype(BF16)

            qk_right = seq.run(
                lambda a, b: jnp.concatenate(
                    [through_norm(a, 0, gain_query), through_norm(b, 1, gain_key)], 1
                ),
                grad_query_n,
                grad_key_n,
            )
            return qk_right, keeps_first, weight_grad(seq, x_all, qk_right, sent_pieces)

        out = region(flag, part_back_qkv)
        got_first, got_down, total_gate, (qk_right, keeps_first, sends) = meet(got_first, got_down, total_gate, out)
        got_second = begin(net, sends)
        vo_total = behind(finish(net, keeps_first, got_first))
        got_gate = net.send(to_leave(total_gate), col)

        def part_in_part():
            keeps_second = weight_grad(Sequence(), x_all, qk_right, kept_pieces)
            qkv_right = jnp.concatenate([qk_right, grad_value_low], 1)
            in_part = jnp.concatenate([contract_cols(qkv_right, part[:, qkv_cols]) for part in near_attn], 1)
            head_rows = lax.dynamic_update_slice(
                jnp.zeros((2, model_width), F32), head_gains, (jnp.int32(0), offset)
            )
            gain_row_mlp = jnp.sum(grad_out * mlp_hat, 0, keepdims=True)
            post_rows = lay.from_relative(jnp.concatenate([gain_row_attn, gain_row_mlp], 0))
            gain_rows = add_all(net, jnp.concatenate([head_rows, post_rows], 0), (side, core))
            return keeps_second, scatter_begin(net, in_part), gain_rows

        out = region(flag, part_in_part)
        got_second, got_gate, total_up, (keeps_second, state, gain_rows) = meet(got_second, got_gate, total_up, out)
        qk_total = behind(finish(net, keeps_second, got_second))

        def part_outputs():
            later = scatter_second(net, state)
            gains_grad = add_all(net, gain_rows, lay.near + (lay.col_axis, lay.far))
            got_up = net.send(to_leave(total_up), col)
            down_grad = jnp.concatenate(owned(total_down, got_down), 1)
            in_grad = lay.from_relative(grad_resid + scatter_end(scatter_third(net, later)))
            hidden_out = lay.from_relative((resid + mlp_hat * gain_mlp).astype(BF16))
            gate_grad = jnp.concatenate(owned(total_gate, got_gate), 1)
            up_grad = jnp.concatenate(owned(total_up, got_up), 1)
            return in_grad, hidden_out, gate_grad, down_grad, up_grad, gains_grad

        out = region(flag, part_outputs)
        vo_total, (in_grad, hidden_out, gate_grad, down_grad, up_grad, gains_grad) = meet(vo_total, out)
        vo_pair = owned(vo_total, net.send(to_leave(vo_total), col))
        qk_pair = owned(qk_total, net.send(to_leave(qk_total), col))
        query_grad, key_grad, value_grad, out_grad_own = (
            jnp.concatenate([part[:, i * head_cols : (i + 1) * head_cols] for part in pair], 1)
            for pair in (qk_pair, vo_pair)
            for i in range(2)
        )
        return (
            hidden_out,
            in_grad,
            query_grad,
            key_grad,
            value_grad,
            out_grad_own,
            gate_grad,
            up_grad,
            down_grad,
            gains_grad,
        )

    return on_device


def solution(mesh):
    lay = Layout(mesh.shape["dp"], mesh.shape["tensor"])
    fine = Mesh(mesh.devices.reshape(lay.shape_of()), lay.dp_axes + lay.tensor_axes)
    tokens = P(lay.dp_axes + lay.tensor_axes, None)
    weights = P(lay.dp_axes, lay.tensor_axes)
    rows = P(lay.dp_axes)
    return jax.shard_map(
        block_program(lay),
        mesh=fine,
        in_specs=(tokens, tokens) + (weights,) * 7 + (P(), rows, rows),
        out_specs=(tokens, tokens) + (weights,) * 7 + (P(),),
        check_vma=False,
    )
```

time: 915 us -> 768 us (0.84)
  waiting for transfers between devices: 508 us -> 248 us
  local copies, waits for them, and re-layouts: 69.3 us -> 131 us
  starting transfers between devices: 120 us -> 74 us
  other arithmetic: 98.5 us -> 143 us
  Pallas kernels: 0 us -> 21.3 us
  between operations: 3.48 us -> 15.5 us
    ppermute x129 -> x74, waiting for transfers between devices: 508 us -> 248 us  [swap(): return lax.ppermute(values, axis, [(0, 1), (1, 0)])]
    cond x0 -> x127, local copies, waits for them, and re-layouts: none -> 49.7 us
    ppermute x129 -> x74, starting transfers between devices: 120 us -> 73.6 us  [swap(): return lax.ppermute(values, axis, [(0, 1), (1, 0)])]
    unnamed x53 -> x0, other arithmetic: 30.6 us -> none
    slice x24 -> x45, local copies, waits for them, and re-layouts: 4.16 us -> 34.2 us  [the longest x7 14.6 us: weight_grad(): left[:, j * piece:(j + 1) * piece]]
    cond x0 -> x43, other arithmetic: none -> 25.9 us
    reshape x15 -> x2, local copies, waits for them, and re-layouts: 25.9 us -> 0.05 us  [the longest x1 0.03 us: add_stats(): rows = rows.reshape(-1, 2, 2, 2, rows.shape[1] // 8)]
    pallas_call x0 -> x2, Pallas kernels: none -> 21.3 us  [attention(): pl.pallas_call(kernel, grid=(2, n_heads), in_specs=in_specs, out_specs=ou...]
  transfers between devices with their start and end apart: 129 -> 84, of which waited for: 65 -> 40; matrix products, arithmetic and copies ran while one was open for 19% -> 46% of each run, Pallas kernels for 0% -> 3%
where the time goes in v2:
time: 768 us; the launch traced here: 757 us
  waiting for transfers between devices  248 us (32%)
  other arithmetic  143 us (19%)
  local copies, waits for them, and re-layouts  131 us (17%)
  matrix products  119 us (15%)
  starting transfers between devices  74 us (10%)
  Pallas kernels  21.3 us (3%)
  between operations  15.5 us (2%)
    ppermute x74, waiting for transfers between devices, swap(): return lax.ppermute(values, axis, [(0, 1), (1, 0)])  248 us
    ppermute x74, starting transfers between devices, swap(): return lax.ppermute(values, axis, [(0, 1), (1, 0)])  73.6 us
    cond x127, local copies, waits for them, and re-layouts  49.7 us
    dot_general x8, matrix products, dot_rows_cols(): return jnp.dot(left, right, preferred_element_type=F32)  44.3 us
    dot_general x14, matrix products, contract_rows(): lax.dot_general(left, right, (((0,), (0,)), ((), ())), preferred_element_...  42.6 us
    dot_general x6, matrix products, contract_cols(): lax.dot_general(left, right, (((1,), (1,)), ((), ())), preferred_element_...  32.1 us
    cond x43, other arithmetic  25.9 us
    select_n x22, other arithmetic, pick(): return jnp.where(flag, yes, no)  23.7 us
  transfers between devices with their start and end apart: 84, of which 40 were waited for; matrix products, arithmetic and copies ran while one was open for 46% of the time, Pallas kernels for 3%

profile of v2, /device:TPU:0, one launch (start us, length us, event | category | flops | bytes accessed | tf_op | source)
XLA Modules:
  0.0 756.6 jit_solution(5432451748250830024)
XLA Ops:
  9.1 25.2 %conditional.16 = (bf16[512,1024]{1,0:T(8,128)(2,1)}, bf16[256,1024]{1,0:T(8,128)(2,1)}, bf16[256,1024]{1,0:T(8,128)(2,1)}, s32[8,128]{1,0:T(8,128)S(1)}, s32[8,...) conditional(s32[]{:T(128)} %bitcast.56, () %tuple.163, (bf16[256,512]{1,0:T(8,128)(2,1)}, bf16[256,512]{1,0:T(8,128)(2,1)}, ...), branch_computations={%region_0.0_spmd, %region_1.2_spmd} | conditional | flops 12060686 | bytes 28379784 | solution.py:47
  35.9 67.0 %conditional.17 = (bf16[1024,2048]{1,0:T(8,128)(2,1)}, bf16[256,1024]{1,0:T(8,128)(2,1)}, bf16[512,1024]{1,0:T(8,128)(2,1)S(1)}) conditional(s32[]{:T(128)} %bitcast.56, () %tuple.165, (bf16[128,2048]{1,0:T(8,128)(2,1)}, bf16[256,2048]{1,0:T(8,128)(2,1)S(1)}, bf16[256,2048]{1,0:T(8,128)(2,1)}, bf16[256,1024]{1,0:T(8,128)(2,1)}) %tuple.399), branch_computations={%region_2.3_spmd, %region_3.4_spmd} | conditional | flops 4980740 | bytes 42205516 | solution.py:47
  39.8 4.1 collective-permute-done.6
  50.2 6.2 collective-permute-done.7
  57.1 14.7 %collective-permute-done.8 = bf16[128,2048]{1,0:T(8,128)(2,1)S(1)} collective-permute-done((bf16[128,2048]{1,0:T(8,128)(2,1)S(1)}, bf16[128,2048]{1,0:T(8,128)(2,1)S(1)}, u32[]{:S(2)}, u32[]{:S(2)}) %collective-permute-start.8) | collective-permute-done | bytes 524320 | tf_op jit(solution)/shard_map/cond/branch_1_fun/ppermute | solution.py:29
  81.1 20.2 %collective-permute-done.10 = bf16[256,1024]{1,0:T(8,128)(2,1)S(1)} collective-permute-done((bf16[256,1024]{1,0:T(8,128)(2,1)}, bf16[256,1024]{1,0:T(8,128)(2,1)S(1)}, u32[]{:S(2)}, u32[]{:S(2)}) %collective-permute-start.10) | collective-permute-done | bytes 524320 | tf_op jit(solution)/shard_map/cond/branch_1_fun/ppermute | solution.py:29
  106.8 11.2 %conditional.18 = (f32[1024,128]{1,0:T(8,128)}, f32[1024,128]{1,0:T(8,128)}, f32[2,512,512]{2,1,0:T(8,128)S(1)}, f32[256]{0:T(256)S(1)}, f32[256]{0:T(256)S(1)},...) conditional(s32[]{:T(128)} %bitcast.56, () %tuple.168, (s32[8,128]{1,0:T(8,128)S(1)}, ...), branch_computations={%region_4.5_spmd, %region_5.6_spmd} | conditional | flops 2892172 | bytes 6463719 | solution.py:47
  118.0 9.3 %collective-permute-done.57 = bf16[256,1024]{1,0:T(8,128)(2,1)} collective-permute-done((bf16[256,1024]{1,0:T(8,128)(2,1)}, bf16[256,1024]{1,0:T(8,128)(2,1)}, u32[]{:S(2)}, u32[]{:S(2)}) %collective-permute-start.57) | collective-permute-done | bytes 524320 | tf_op jit(solution)/shard_map/ppermute | solution.py:29
  127.3 4.2 collective-permute-done.56
  134.7 29.5 %conditional.19 = (bf16[1024,1024]{1,0:T(8,128)(2,1)}, bf16[1024,1024]{1,0:T(8,128)(2,1)}, f32[1024,768]{0,1:T(8,128)}, f32[2,1024]{1,0:T(2,128)S(1)}) conditional(s32[]{:T(128)} %bitcast.56, () %tuple.171, (bf16[512,1024]{1,0:T(8,128)(2,1)}, bf16[512,1024]{1,0:T(8,128)(2,1)}, bf16[1024,2048]{1,0:T(8,128)(2,1)}, bf16[1024,1024]{1,0:T(8,128)(2,1)}) %tuple.172), branch_computations={%region_6.7_spmd, %region_7.10_spmd} | conditional | flops 3231461376 | bytes 40607968 | solution.py:47
  140.0 5.1 bitcast_add_fusion
  148.1 11.5 %collective-permute-done.1 = f32[2,2,2,2,128]{4,3,2,1,0:T(2,128)S(1)} collective-permute-done((f32[2,2,2,2,128]{4,3,2,1,0:T(2,128)S(1)}, f32[2,2,2,2,128]{4,3,2,1,0:T(2,128)S(1)}, u32[]{:S(2)}, u32[]{:S(2)}) %collective-permute-start.1) | collective-permute-done | bytes 8224 | tf_op jit(solution)/shard_map/cond/branch_1_fun/ppermute | solution.py:29
  164.2 25.4 %conditional.20 = (bf16[1024,256]{1,0:T(8,128)(2,1)}, f32[1024,2]{1,0:T(8,128)}, bf16[2048,256]{1,0:T(8,128)(2,1)}, f32[512,2048]{1,0:T(8,128)}, bf16[512,2048]{1,0:T(8,128)(2,1)}) conditional(s32[]{:T(128)} %bitcast.56, () %tuple.174, (f32[1024,768]{0,1:T(8,128)}, f32[2,1024]{1,0:T(2,128)S(1)}, f32[256]{0:T(256)S(1)}, f32[256]{0:T(256)S(1)}, ...), branch_computations={%region_10.11_spmd, %region_11.12_spmd} | conditional | flops 2149584896 | bytes 58269832 | solution.py:47
  174.6 7.6 %branch_1_fun.2 = bf16[2,2,256,256]{3,2,1,0:T(8,128)(2,1)} custom-call(f32[2,2,256,768]{3,2,1,0:T(8,128)S(1)} %bitcast.114, f32[2,2,256,768]{3,2,1,0:T(8,128)S(1)} %bitcast.115, f32[2,2,256,768]{3,2,1,0:T(8,128)S(1)} %bitcast.116, f32[2,2,256,2]{3,2,1,0:T(8,128)S(1)} %bitcast.117, f32[1,256]{1,0:T(1,128)S(1)} %bitcast.152, f32[1,256]{1,0:T(1,128)S(1)} %bitcast.149, ...), custom_call_target="tpu_custom_call" | custom-call | flops 1073741824 | bytes 8388608 | tf_op jit(solution)/shard_map/cond/branch_1_fun/pallas_call | solution.py:221
  194.3 65.8 %conditional.21 = (f32[128,1]{0,1:T(1,128)}, f32[128,2048]{1,0:T(8,128)}, f32[128,2048]{1,0:T(8,128)}, bf16[64,2048]{1,0:T(8,128)(2,1)}, bf16[64,2048]{1,0:T(8,1...) conditional(s32[]{:T(128)} %bitcast.56, () %tuple.177, (bf16[512,2048]{1,0:T(8,128)(2,1)}, ...), branch_computations={%region_12.13_spmd, %region_13.15_spmd} | conditional | flops 9699456 | bytes 44575528 | solution.py:47
  201.4 26.5 %collective-permute-done.11 = bf16[128,2048]{1,0:T(8,128)(2,1)S(1)} collective-permute-done((bf16[128,2048]{1,0:T(8,128)(2,1)S(1)}, bf16[128,2048]{1,0:T(8,128)(2,1)S(1)}, u32[]{:S(2)}, u32[]{:S(2)}) %collective-permute-start.11) | collective-permute-done | bytes 524320 | tf_op jit(solution)/shard_map/cond/branch_1_fun/ppermute | solution.py:29
  229.9 6.6 collective-permute-done.12
  236.6 6.6 collective-permute-done.14
  249.2 11.0 %collective-permute-done.16 = bf16[64,2048]{1,0:T(8,128)(2,1)} collective-permute-done((bf16[64,2048]{1,0:T(8,128)(2,1)}, bf16[64,2048]{1,0:T(8,128)(2,1)}, u32[]{:S(2)}, u32[]{:S(2)}) %collective-permute-start.16) | collective-permute-done | bytes 262176 | tf_op jit(solution)/shard_map/cond/branch_1_fun/ppermute | solution.py:29
  264.3 39.2 %conditional.22 = (bf16[1024,2048]{1,0:T(8,128)(2,1)}, f32[1024,1024]{1,0:T(8,128)}) conditional(s32[]{:T(128)} %bitcast.56, () %tuple.180, (bf16[64,2048]{1,0:T(8,128)(2,1)}, bf16[64,2048]{1,0:T(8,128)(2,1)}, bf16[64,2048]{1,0:T(8,128)(2,1)}, bf16[64,2048]{1,0:T(8,128)(2,1)}, bf16[1024,1024]{1,0:T(8,128)(2,1)S(1)}, ...), branch_computations={%region_15.16_spmd, %region_16.17_spmd} | conditional | flops 4298113024 | bytes 47448200 | solution.py:47
  278.1 7.5 collective-permute-done.27
  293.0 4.5 fusion.28
  297.5 6.0 fusion.32
  307.7 19.3 %conditional.23 = (f32[1024,1024]{1,0:T(8,128)}, bf16[1024,1024]{1,0:T(8,128)(2,1)S(1)}, bf16[2048,1024]{1,0:T(8,128)(2,1)}, bf16[2048,1024]{1,0:T(8,128)(2,1)}) conditional(s32[]{:T(128)} %bitcast.56, () %tuple.183, (bf16[1024,2048]{1,0:T(8,128)(2,1)}, bf16[1024,1024]{1,0:T(8,128)(2,1)}, bf16[512,1024]{1,0:T(8,128)(2,1)}, ...), branch_computations={%region_17.18_spmd, %region_18.19_spmd} | conditional | flops 4328521728 | bytes 65011840 | solution.py:47
  312.3 3.9 fusion.39
  316.3 6.7 multiply_convert_fusion
  323.0 4.0 pad_maximum_fusion.14
  327.0 4.8 collective-permute-done.63
  331.8 71.2 %conditional.24 = (bf16[2048,1024]{1,0:T(8,128)(2,1)S(1)}, f32[128,2048]{1,0:T(8,128)S(1)}, bf16[1024,2048]{1,0:T(8,128)(2,1)}, bf16[1024,512]{1,0:T(8,128)(2,1)}, bf16[1024,512]{1,0:T(8,128)(2,1)S(1)}) conditional(s32[]{:T(128)} %bitcast.56, () %tuple.162, (bf16[512,1024]{1,0:T(8,128)(2,1)}, bf16[512,1024]{1,0:T(8,128)(2,1)}, ...), branch_computations={%region_19.20_spmd, %region_20.23_spmd} | conditional | flops 6469976064 | bytes 177493056 | solution.py:47
  334.9 4.6 convolution_bitcast_fusion
  339.8 4.1 collective-permute-done.29
  347.0 12.2 %collective-permute-done.30 = bf16[128,2048]{1,0:T(8,128)(2,1)S(1)} collective-permute-done((bf16[128,2048]{1,0:T(8,128)(2,1)S(1)}, bf16[128,2048]{1,0:T(8,128)(2,1)S(1)}, u32[]{:S(2)}, u32[]{:S(2)}) %collective-permute-start.30) | collective-permute-done | bytes 524320 | tf_op jit(solution)/shard_map/cond/branch_1_fun/ppermute | solution.py:29
  361.5 5.5 collective-permute-done.31
  371.5 4.8 collective-permute-done.35
  380.1 8.1 %collective-permute-done.36 = bf16[128,2048]{1,0:T(8,128)(2,1)S(1)} collective-permute-done((bf16[128,2048]{1,0:T(8,128)(2,1)S(1)}, bf16[128,2048]{1,0:T(8,128)(2,1)S(1)}, u32[]{:S(2)}, u32[]{:S(2)}) %collective-permute-start.36) | collective-permute-done | bytes 524320 | tf_op jit(solution)/shard_map/cond/branch_1_fun/ppermute | solution.py:29
  394.9 3.8 convolution_convert_fusion.1
  404.5 23.3 %conditional.25 = (bf16[1024,512]{1,0:T(8,128)(2,1)S(1)}, bf16[1024,1024]{1,0:T(8,128)(2,1)}, bf16[1024,1024]{1,0:T(8,128)(2,1)S(1)}, f32[1024,2048]{1,0:T(8,128)S(1)}) conditional(s32[]{:T(128)} %bitcast.56, () %tuple.188, (bf16[1024,2048]{1,0:T(8,128)(2,1)}, bf16[1024,1024]{1,0:T(8,128)(2,1)}, bf16[2048,1024]{1,0:T(8,128)(2,1)S(1)}, ...), branch_computations={%region_23.24_spmd, %region_24.25_spmd} | conditional | flops 9677832192 | bytes 73400408 | solution.py:47
  410.2 10.5 %multiply_convert_fusion.2 = (bf16[1024,1024]{1,0:T(8,128)(2,1)S(1)}, bf16[1024,1024]{1,0:T(8,128)(2,1)}) fusion(f32[1024,1024]{1,0:T(8,128)} %get-tuple-element.309, f32[1024,1024]{1,0:T(8,128)} %get-tuple-element.308, bf16[1024,2048]{1,0:T(8,128)(2,1)} %get-tuple-element.306, bf16[2048,1024]{1,0:T(8,128)(2,1)S(1)} %copy-done.26), kind=kOutput, calls=%fused_computation.217 | convolution fusion | flops 4308598784 | bytes 20971520 | tf_op jit(solution)/shard_map/cond/branch_1_fun/dot_general | solution.py:17
  420.8 7.0 fusion.126
  436.3 23.4 %conditional.26 = (bf16[1024,1024]{1,0:T(8,128)(2,1)}, bf16[1024,512]{1,0:T(8,128)(2,1)S(1)}, f32[512,2048]{1,0:T(8,128)}, bf16[512,2048]{1,0:T(8,128)(2,1)}) conditional(s32[]{:T(128)} %bitcast.56, () %tuple.187, (bf16[1024,2048]{1,0:T(8,128)(2,1)}, bf16[1024,2048]{1,0:T(8,128)(2,1)}, bf16[1024,1024]{1,0:T(8,128)(2,1)S(1)}, ...), branch_computations={%region_25.26_spmd, %region_26.27_spmd} | conditional | flops 7519862784 | bytes 65011784 | solution.py:47
  436.4 10.2 %convolution_add_fusion = f32[1024,2048]{1,0:T(8,128)S(1)} fusion(f32[1024,2048]{1,0:T(8,128)} %get-tuple-element.317, bf16[1024,1024]{1,0:T(8,128)(2,1)} %get-tuple-element.318, bf16[2048,1024]{1,0:T(8,128)(2,1)} %get-tuple-element.319), kind=kOutput, calls=%fused_computation.225 | convolution fusion | flops 4297064448 | bytes 23068672 | tf_op jit(solution)/shard_map/cond/branch_1_fun/dot_general | solution.py:21
  454.4 5.3 convolution_convert_fusion.2
  464.4 47.5 %conditional.27 = (bf16[1024,1024]{1,0:T(8,128)(2,1)S(1)}, bf16[1024,1024]{1,0:T(8,128)(2,1)}, bf16[1024,1024]{1,0:T(8,128)(2,1)}, f32[128,2048]{1,0:T(8,128)}, ...) conditional(s32[]{:T(128)} %bitcast.56, () %tuple.193, ...), branch_computations={%region_28.29_spmd, %region_29.32_spmd} | conditional | flops 6456080384 | bytes 81882000 | solution.py:47
  464.6 3.8 fusion.97
  471.5 4.8 convolution_convert_fusion.6
  479.2 10.5 %collective-permute-done.40 = bf16[128,2048]{1,0:T(8,128)(2,1)S(1)} collective-permute-done((bf16[128,2048]{1,0:T(8,128)(2,1)S(1)}, bf16[128,2048]{1,0:T(8,128)(2,1)S(1)}, u32[]{:S(2)}, u32[]{:S(2)}) %collective-permute-start.40) | collective-permute-done | bytes 524320 | tf_op jit(solution)/shard_map/cond/branch_1_fun/ppermute | solution.py:29
  506.8 3.8 convolution_convert_fusion.4
  511.9 3.9 add_convert_fusion.2
  516.8 67.5 %conditional.28 = (bf16[1024,2048]{1,0:T(8,128)(2,1)}, f32[1024,256]{1,0:T(8,128)}, f32[1024,256]{1,0:T(8,128)}, bf16[1024,256]{1,0:T(8,128)(2,1)}, f32[2,2,2,25...) conditional(s32[]{:T(128)} %bitcast.56, () %tuple.196, (bf16[64,2048]{1,0:T(8,128)(2,1)}, ...), branch_computations={%region_33.34_spmd, %region_34.36_spmd} | conditional | flops 3226206720 | bytes 72096008 | solution.py:47
  530.1 13.2 %collective-permute-done.47 = bf16[128,2048]{1,0:T(8,128)(2,1)S(1)} collective-permute-done((bf16[128,2048]{1,0:T(8,128)(2,1)S(1)}, bf16[128,2048]{1,0:T(8,128)(2,1)S(1)}, u32[]{:S(2)}, u32[]{:S(2)}) %collective-permute-start.47) | collective-permute-done | bytes 524320 | tf_op jit(solution)/shard_map/cond/branch_1_fun/ppermute | solution.py:29
  561.4 3.9 convolution_convert_fusion.8
  565.3 13.6 %branch_1_fun.3 = (f32[2,2,256,256]{3,2,1,0:T(8,128)}, f32[2,2,256,256]{3,2,1,0:T(8,128)}, bf16[2,2,256,256]{3,2,1,0:T(8,128)(2,1)}, f32[2,2,2,256,2]{4,3,2,1,0:T(8,128)}, f32[2,2,256]{2,1,0:T(2,128)S(1)}) custom-call(f32[2,2,256,768]{3,2,1,0:T(8,128)S(1)} %bitcast.111, f32[2,2,256,768]{3,2,1,0:T(8,128)S(1)} %bitcast.112, f32[2,2,256,768]{3,2,1,0:T(8,128)S(1)} %bitcast.113, ...), custom_call_target="tpu_custom_call" | custom-call | flops 1073741824 | bytes 8388608 | tf_op jit(solution)/shard_map/cond/branch_1_fun/pallas_call | solution.py:221
  584.3 4.6 add_convert_fusion.1
  595.6 38.1 %conditional.29 = (bf16[1024,512]{1,0:T(8,128)(2,1)}, bf16[1024,512]{0,1:T(8,128)(2,1)}, bf16[1024,512]{1,0:T(8,128)(2,1)}) conditional(s32[]{:T(128)} %bitcast.56, () %tuple.199, (f32[1024,2]{1,0:T(8,128)}, bf16[1024,2048]{1,0:T(8,128)(2,1)}, bf16[1024,2048]{1,0:T(8,128)(2,1)}, bf16[1024,256]{1,0:T(8,128)(2,1)}, bf16[1024,256]{1,0:T(8,128)(2,1)}, ...), branch_computations={%region_37.38_spmd, %region_38.40_spmd} | conditional | flops 2155882496 | bytes 43321520 | solution.py:47
  605.2 14.1 %collective-permute-done.50 = f32[2,2,2,2,128]{4,3,2,1,0:T(2,128)S(1)} collective-permute-done((f32[2,2,2,2,128]{4,3,2,1,0:T(2,128)S(1)}, f32[2,2,2,2,128]{4,3,2,1,0:T(2,128)S(1)}, u32[]{:S(2)}, u32[]{:S(2)}) %collective-permute-start.50) | collective-permute-done | bytes 8224 | tf_op jit(solution)/shard_map/cond/branch_1_fun/ppermute | solution.py:29
  642.8 22.1 %conditional.30 = (bf16[1024,512]{1,0:T(8,128)(2,1)S(1)}, f32[512,2048]{0,1:T(8,128)}, bf16[512,2048]{0,1:T(8,128)(2,1)}, f32[4,2048]{1,0:T(4,128)S(1)}) conditional(s32[]{:T(128)} %bitcast.56, () %tuple.203, (bf16[1024,2048]{1,0:T(8,128)(2,1)}, bf16[1024,512]{1,0:T(8,128)(2,1)}, bf16[1024,256]{1,0:T(8,128)(2,1)}, bf16[1024,1024]{1,0:T(8,128)(2,1)}, ...), branch_computations={%region_42.43_spmd, %region_43.45_spmd} | conditional | flops 4301301248 | bytes 123388256 | solution.py:47
  648.4 4.5 fusion.79
  667.6 62.7 %conditional.31 = (f32[128,2048]{1,0:T(8,128)}, bf16[128,2048]{1,0:T(8,128)(2,1)}, f32[256,2048]{1,0:T(8,128)}, f32[256,2048]{1,0:T(8,128)}, f32[256,2048]{1,0:T(8,128)}, /*index=5*/f32[4,2048]{1,0:T(4,128)S(1)}) conditional(s32[]{:T(128)} %bitcast.56, () %tuple.202, (bf16[512,2048]{0,1:T(8,128)(2,1)}, f32[512,2048]{0,1:T(8,128)}, ...), branch_computations={%region_45.46_spmd, %region_46.47_spmd} | conditional | flops 14966790 | bytes 103981616 | solution.py:47
  673.4 5.5 copy.65
  678.9 5.3 fusion.98
  703.0 7.5 collective-permute-done.23
  711.2 4.1 collective-permute-done.24
  731.4 7.4 collective-permute-done.73
  743.0 4.5 collective-permute-done.72
  (601 shorter events, 375.0 us)
Async XLA Ops:
  7.2 95.7 %all-gather.5.cloned.1.call-start = ((), (), s32[]{:S(2)}) async-start(), calls=%async_computation.6 | async-start | bytes 3145728 | tf_op jit(solution)/shard_map/all_gather | solution.py:257
  11.4 18.2 %collective-permute-start.4 = (s32[8,128]{1,0:T(8,128)}, s32[8,128]{1,0:T(8,128)S(1)}, u32[]{:S(2)}, u32[]{:S(2)}) collective-permute-start(s32[8,128]{1,0:T(8,128)} %concatenate.169), channel_id=1, source_target_pairs={{0,8},{8,0},{1,9},{9,1},{2,10},{10,2},{3,11},{11,3},{4,12},{12,4},... | collective-permute-start | bytes 12296 | tf_op jit(solution)/shard_map/cond/branch_1_fun/ppermute | solution.py:29
  17.9 13.8 %collective-permute-start.3 = (bf16[256,1024]{1,0:T(8,128)(2,1)}, bf16[256,1024]{1,0:T(8,128)(2,1)}, u32[]{:S(2)}, u32[]{:S(2)}) collective-permute-start(bf16[256,1024]{1,0:T(8,128)(2,1)} %broadcast_select_fusion.2), channel_id=1, source_target_pairs={{0,8},{8,0},{1,9},{9,1},{2,10},{10,2},{3,11},{11,3},{4,12},{12,4},... | collective-permute-start | bytes 1572872 | tf_op jit(solution)/shard_map/cond/branch_1_fun/ppermute | solution.py:29
  34.3 155.3 %all-gather.7.cloned.1.call-start = ((), (), s32[]{:S(2)}) async-start(), calls=%async_computation.7 | async-start | bytes 3145728 | tf_op jit(solution)/shard_map/all_gather | solution.py:257
  34.3 68.5 %collective-permute-start.55 = (bf16[512,1024]{1,0:T(8,128)(2,1)}, bf16[512,1024]{1,0:T(8,128)(2,1)}, u32[]{:S(2)}, u32[]{:S(2)}) collective-permute-start(bf16[512,1024]{1,0:T(8,128)(2,1)} %get-tuple-element.586), channel_id=1, source_target_pairs={{0,4},{4,0},{1,5},{5,1},{2,6},{6,2},{3,7},{7,3},{8,12},{12,8},{9,1... | collective-permute-start | bytes 3145736 | tf_op jit(solution)/shard_map/ppermute | solution.py:29
  38.3 9.4 %collective-permute-start.5 = (bf16[64,2048]{1,0:T(8,128)(2,1)S(1)}, bf16[64,2048]{1,0:T(8,128)(2,1)S(1)}, u32[]{:S(2)}, u32[]{:S(2)}) collective-permute-start(bf16[64,2048]{1,0:T(8,128)(2,1)S(1)} %get-tuple-element.989), channel_id=1, source_target_pairs={{0,2},{2,0},{1,3},{3,1},{4,6},{6,4},{5,7},{7,5},{8,10},{10,8},{9,1... | collective-permute-start | bytes 786440 | tf_op jit(solution)/shard_map/cond/branch_1_fun/ppermute | solution.py:29
  43.9 12.5 %collective-permute-start.7 = (bf16[128,2048]{1,0:T(8,128)(2,1)S(1)}, bf16[128,2048]{1,0:T(8,128)(2,1)S(1)}, u32[]{:S(2)}, u32[]{:S(2)}) collective-permute-start(bf16[128,2048]{1,0:T(8,128)(2,1)S(1)} %pad_maximum_fusion.4), channel_id=1, source_target_pairs={{0,2},{2,0},{1,3},{3,1},{4,6},{6,4},{5,7},{7,5},{8,10},{10,8},{9,1... | collective-permute-start | bytes 1572872 | tf_op jit(solution)/shard_map/cond/branch_1_fun/ppermute | solution.py:29
  47.7 24.1 %collective-permute-start.8 = (bf16[128,2048]{1,0:T(8,128)(2,1)S(1)}, bf16[128,2048]{1,0:T(8,128)(2,1)S(1)}, u32[]{:S(2)}, u32[]{:S(2)}) collective-permute-start(bf16[128,2048]{1,0:T(8,128)(2,1)S(1)} %pad_maximum_fusion.5), channel_id=1, source_target_pairs={{0,8},{8,0},{1,9},{9,1},{2,10},{10,2},{3,11},{11,3},{4,12},{12,4},... | collective-permute-start | bytes 1572872 | tf_op jit(solution)/shard_map/cond/branch_1_fun/ppermute | solution.py:29
  74.8 26.6 %collective-permute-start.9 = (bf16[512,2048]{1,0:T(8,128)(2,1)}, bf16[512,2048]{1,0:T(8,128)(2,1)S(1)}, u32[]{:S(2)}, u32[]{:S(2)}) collective-permute-start(bf16[512,2048]{1,0:T(8,128)(2,1)} %get-tuple-element.984), channel_id=1, source_target_pairs={{0,1},{1,0},{2,3},{3,2},{4,5},{5,4},{6,7},{7,6},{8,9},{9,8},{10,11... | collective-permute-start | bytes 6291464 | tf_op jit(solution)/shard_map/cond/branch_1_fun/ppermute | solution.py:29
  75.7 25.5 %collective-permute-start.10 = (bf16[256,1024]{1,0:T(8,128)(2,1)}, bf16[256,1024]{1,0:T(8,128)(2,1)S(1)}, u32[]{:S(2)}, u32[]{:S(2)}) collective-permute-start(bf16[256,1024]{1,0:T(8,128)(2,1)} %get-tuple-element.259), channel_id=1, source_target_pairs={{0,8},{8,0},{1,9},{9,1},{2,10},{10,2},{3,11},{11,3},{4,12},{12,4},... | collective-permute-start | bytes 1572872 | tf_op jit(solution)/shard_map/cond/branch_1_fun/ppermute | solution.py:29
  103.9 156.3 %all-gather.9.cloned.1.call-start = ((), (), s32[]{:S(2)}) async-start(), calls=%async_computation.8 | async-start | bytes 3145728 | tf_op jit(solution)/shard_map/all_gather | solution.py:257
  106.2 25.3 %collective-permute-start.56 = (bf16[512,1024]{1,0:T(8,128)(2,1)}, bf16[512,1024]{1,0:T(8,128)(2,1)}, u32[]{:S(2)}, u32[]{:S(2)}) collective-permute-start(bf16[512,1024]{1,0:T(8,128)(2,1)} %constant_dynamic-slice_fusion.4), channel_id=1, source_target_pairs={{0,4},{4,0},{1,5},{5,1},{2,6},{6,2},{3,7},{7,3},{8,12},{12,8},{9,1... | collective-permute-start | bytes 3145736 | tf_op jit(solution)/shard_map/ppermute | solution.py:29
  106.8 20.5 %collective-permute-start.57 = (bf16[256,1024]{1,0:T(8,128)(2,1)}, bf16[256,1024]{1,0:T(8,128)(2,1)}, u32[]{:S(2)}, u32[]{:S(2)}) collective-permute-start(bf16[256,1024]{1,0:T(8,128)(2,1)} %get-tuple-element.593), channel_id=1, source_target_pairs={{0,8},{8,0},{1,9},{9,1},{2,10},{10,2},{3,11},{11,3},{4,12},{12,4},... | collective-permute-start | bytes 1572872 | tf_op jit(solution)/shard_map/ppermute | solution.py:29
  134.0 55.6 %collective-permute-start.58 = (bf16[512,1024]{1,0:T(8,128)(2,1)}, bf16[512,1024]{1,0:T(8,128)(2,1)}, u32[]{:S(2)}, u32[]{:S(2)}) collective-permute-start(bf16[512,1024]{1,0:T(8,128)(2,1)} %pad_maximum_fusion.37), channel_id=1, source_target_pairs={{0,4},{4,0},{1,5},{5,1},{2,6},{6,2},{3,7},{7,3},{8,12},{12,8},{9,1... | collective-permute-start | bytes 3145736 | tf_op jit(solution)/shard_map/ppermute | solution.py:29
  134.6 168.9 %all-gather.11.cloned.1.call-start = ((), (), s32[]{:S(2)}) async-start(), calls=%async_computation.9 | async-start | bytes 3145728 | tf_op jit(solution)/shard_map/all_gather | solution.py:257
  148.1 11.6 %collective-permute-start.1 = (f32[2,2,2,2,128]{4,3,2,1,0:T(2,128)S(1)}, f32[2,2,2,2,128]{4,3,2,1,0:T(2,128)S(1)}, u32[]{:S(2)}, u32[]{:S(2)}) collective-permute-start(f32[2,2,2,2,128]{4,3,2,1,0:T(2,128)S(1)} %reverse_add_fusion.1), channel_id=1, source_target_pairs={{0,8},{8,0},{1,9},{9,1},{2,10},{10,2},{3,11},{11,3},{4,12},{12,4},... | collective-permute-start | bytes 24584 | tf_op jit(solution)/shard_map/cond/branch_1_fun/ppermute | solution.py:29
  164.1 25.5 %collective-permute-start.59 = (bf16[256,1024]{1,0:T(8,128)(2,1)}, bf16[256,1024]{1,0:T(8,128)(2,1)}, u32[]{:S(2)}, u32[]{:S(2)}) collective-permute-start(bf16[256,1024]{1,0:T(8,128)(2,1)} %get-tuple-element.614), channel_id=1, source_target_pairs={{0,8},{8,0},{1,9},{9,1},{2,10},{10,2},{3,11},{11,3},{4,12},{12,4},... | collective-permute-start | bytes 1572872 | tf_op jit(solution)/shard_map/ppermute | solution.py:29
  189.6 70.5 %collective-permute-start.60 = (bf16[1024,1024]{1,0:T(8,128)(2,1)}, bf16[1024,1024]{1,0:T(8,128)(2,1)}, u32[]{:S(2)}, u32[]{:S(2)}) collective-permute-start(bf16[1024,1024]{1,0:T(8,128)(2,1)} %all-gather.7.cloned.1.call-done), channel_id=1, source_target_pairs={{0,4},{4,0},{1,5},{5,1},{2,6},{6,2},{3,7},{7,3},{8,12},{12,8},{9,1... | collective-permute-start | bytes 6291464 | tf_op jit(solution)/shard_map/ppermute | solution.py:29
  193.7 318.2 %reduce-scatter.7.cloned.1.call-start = ((), (), s32[]{:S(2)}) async-start(), calls=%async_computation.10 | async-start | bytes 1572864 | tf_op jit(solution)/shard_map/reduce_scatter | solution.py:268
  193.8 109.7 %collective-permute-start.62 = (bf16[512,1024]{1,0:T(8,128)(2,1)}, bf16[512,1024]{1,0:T(8,128)(2,1)S(1)}, u32[]{:S(2)}, u32[]{:S(2)}) collective-permute-start(bf16[512,1024]{1,0:T(8,128)(2,1)} %pad_maximum_fusion.38), channel_id=1, source_target_pairs={{0,4},{4,0},{1,5},{5,1},{2,6},{6,2},{3,7},{7,3},{8,12},{12,8},{9,1... | collective-permute-start | bytes 3145736 | tf_op jit(solution)/shard_map/ppermute | solution.py:29
  198.2 29.8 %collective-permute-start.11 = (bf16[128,2048]{1,0:T(8,128)(2,1)S(1)}, bf16[128,2048]{1,0:T(8,128)(2,1)S(1)}, u32[]{:S(2)}, u32[]{:S(2)}) collective-permute-start(bf16[128,2048]{1,0:T(8,128)(2,1)S(1)} %pad_maximum_fusion.10), channel_id=1, source_target_pairs={{0,8},{8,0},{1,9},{9,1},{2,10},{10,2},{3,11},{11,3},{4,12},{12,4},... | collective-permute-start | bytes 1572872 | tf_op jit(solution)/shard_map/cond/branch_1_fun/ppermute | solution.py:29
  200.3 29.4 %collective-permute-start.13 = (bf16[128,2048]{1,0:T(8,128)(2,1)S(1)}, bf16[128,2048]{1,0:T(8,128)(2,1)S(1)}, u32[]{:S(2)}, u32[]{:S(2)}) collective-permute-start(bf16[128,2048]{1,0:T(8,128)(2,1)S(1)} %pad_maximum_fusion.11), channel_id=1, source_target_pairs={{0,2},{2,0},{1,3},{3,1},{4,6},{6,4},{5,7},{7,5},{8,10},{10,8},{9,1... | collective-permute-start | bytes 1572872 | tf_op jit(solution)/shard_map/cond/branch_1_fun/ppermute | solution.py:29
  228.1 8.4 %collective-permute-start.12 = (bf16[64,2048]{1,0:T(8,128)(2,1)S(1)}, bf16[64,2048]{1,0:T(8,128)(2,1)S(1)}, u32[]{:S(2)}, u32[]{:S(2)}) collective-permute-start(bf16[64,2048]{1,0:T(8,128)(2,1)S(1)} %slice.1453), channel_id=1, source_target_pairs={{0,2},{2,0},{1,3},{3,1},{4,6},{6,4},{5,7},{7,5},{8,10},{10,8},{9,1... | collective-permute-start | bytes 786440 | tf_op jit(solution)/shard_map/cond/branch_1_fun/ppermute | solution.py:29
  229.8 13.4 %collective-permute-start.14 = (bf16[64,2048]{1,0:T(8,128)(2,1)S(1)}, bf16[64,2048]{1,0:T(8,128)(2,1)S(1)}, u32[]{:S(2)}, u32[]{:S(2)}) collective-permute-start(bf16[64,2048]{1,0:T(8,128)(2,1)S(1)} %slice.1452), channel_id=1, source_target_pairs={{0,8},{8,0},{1,9},{9,1},{2,10},{10,2},{3,11},{11,3},{4,12},{12,4},... | collective-permute-start | bytes 786440 | tf_op jit(solution)/shard_map/cond/branch_1_fun/ppermute | solution.py:29
  247.5 12.7 %collective-permute-start.16 = (bf16[64,2048]{1,0:T(8,128)(2,1)}, bf16[64,2048]{1,0:T(8,128)(2,1)}, u32[]{:S(2)}, u32[]{:S(2)}) collective-permute-start(bf16[64,2048]{1,0:T(8,128)(2,1)} %get-tuple-element.1177), channel_id=1, source_target_pairs={{0,8},{8,0},{1,9},{9,1},{2,10},{10,2},{3,11},{11,3},{4,12},{12,4},... | collective-permute-start | bytes 786440 | tf_op jit(solution)/shard_map/cond/branch_1_fun/ppermute | solution.py:29
  248.6 11.6 %collective-permute-start.15 = (bf16[64,2048]{1,0:T(8,128)(2,1)}, bf16[64,2048]{1,0:T(8,128)(2,1)}, u32[]{:S(2)}, u32[]{:S(2)}) collective-permute-start(bf16[64,2048]{1,0:T(8,128)(2,1)} %get-tuple-element.1176), channel_id=1, source_target_pairs={{0,2},{2,0},{1,3},{3,1},{4,6},{6,4},{5,7},{7,5},{8,10},{10,8},{9,1... | collective-permute-start | bytes 786440 | tf_op jit(solution)/shard_map/cond/branch_1_fun/ppermute | solution.py:29
  262.6 40.9 %collective-permute-start.61 = (bf16[512,1024]{1,0:T(8,128)(2,1)}, bf16[512,1024]{1,0:T(8,128)(2,1)}, u32[]{:S(2)}, u32[]{:S(2)}) collective-permute-start(bf16[512,1024]{1,0:T(8,128)(2,1)} %constant_dynamic-slice_fusion.3), channel_id=1, source_target_pairs={{0,4},{4,0},{1,5},{5,1},{2,6},{6,2},{3,7},{7,3},{8,12},{12,8},{9,1... | collective-permute-start | bytes 3145736 | tf_op jit(solution)/shard_map/ppermute | solution.py:29
  265.6 12.4 %collective-permute-start.26 = (bf16[128,2048]{1,0:T(8,128)(2,1)S(1)}, bf16[128,2048]{1,0:T(8,128)(2,1)S(1)}, u32[]{:S(2)}, u32[]{:S(2)}) collective-permute-start(bf16[128,2048]{1,0:T(8,128)(2,1)S(1)} %pad_maximum_fusion.12), channel_id=1, source_target_pairs={{0,2},{2,0},{1,3},{3,1},{4,6},{6,4},{5,7},{7,5},{8,10},{10,8},{9,1... | collective-permute-start | bytes 1572872 | tf_op jit(solution)/shard_map/cond/branch_1_fun/ppermute | solution.py:29
  267.6 17.9 %collective-permute-start.27 = (bf16[128,2048]{1,0:T(8,128)(2,1)S(1)}, bf16[128,2048]{1,0:T(8,128)(2,1)S(1)}, u32[]{:S(2)}, u32[]{:S(2)}) collective-permute-start(bf16[128,2048]{1,0:T(8,128)(2,1)S(1)} %pad_maximum_fusion.13), channel_id=1, source_target_pairs={{0,8},{8,0},{1,9},{9,1},{2,10},{10,2},{3,11},{11,3},{4,12},{12,4},... | collective-permute-start | bytes 1572872 | tf_op jit(solution)/shard_map/cond/branch_1_fun/ppermute | solution.py:29
  306.2 25.6 %collective-permute-start.63 = (bf16[512,1024]{1,0:T(8,128)(2,1)}, bf16[512,1024]{1,0:T(8,128)(2,1)}, u32[]{:S(2)}, u32[]{:S(2)}) collective-permute-start(bf16[512,1024]{1,0:T(8,128)(2,1)} %constant_dynamic-slice_fusion.2), channel_id=1, source_target_pairs={{0,4},{4,0},{1,5},{5,1},{2,6},{6,2},{3,7},{7,3},{8,12},{12,8},{9,1... | collective-permute-start | bytes 3145736 | tf_op jit(solution)/shard_map/ppermute | solution.py:29
  345.2 14.0 %collective-permute-start.30 = (bf16[128,2048]{1,0:T(8,128)(2,1)S(1)}, bf16[128,2048]{1,0:T(8,128)(2,1)S(1)}, u32[]{:S(2)}, u32[]{:S(2)}) collective-permute-start(bf16[128,2048]{1,0:T(8,128)(2,1)S(1)} %pad_maximum_fusion.18), channel_id=1, source_target_pairs={{0,8},{8,0},{1,9},{9,1},{2,10},{10,2},{3,11},{11,3},{4,12},{12,4},... | collective-permute-start | bytes 1572872 | tf_op jit(solution)/shard_map/cond/branch_1_fun/ppermute | solution.py:29
  345.4 15.6 %collective-permute-start.32 = (bf16[128,2048]{1,0:T(8,128)(2,1)S(1)}, bf16[128,2048]{1,0:T(8,128)(2,1)S(1)}, u32[]{:S(2)}, u32[]{:S(2)}) collective-permute-start(bf16[128,2048]{1,0:T(8,128)(2,1)S(1)} %pad_maximum_fusion.19), channel_id=1, source_target_pairs={{0,2},{2,0},{1,3},{3,1},{4,6},{6,4},{5,7},{7,5},{8,10},{10,8},{9,1... | collective-permute-start | bytes 1572872 | tf_op jit(solution)/shard_map/cond/branch_1_fun/ppermute | solution.py:29
  359.4 7.6 %collective-permute-start.31 = (bf16[64,2048]{1,0:T(8,128)(2,1)S(1)}, bf16[64,2048]{1,0:T(8,128)(2,1)S(1)}, u32[]{:S(2)}, u32[]{:S(2)}) collective-permute-start(bf16[64,2048]{1,0:T(8,128)(2,1)S(1)} %slice.1456), channel_id=1, source_target_pairs={{0,2},{2,0},{1,3},{3,1},{4,6},{6,4},{5,7},{7,5},{8,10},{10,8},{9,1... | collective-permute-start | bytes 786440 | tf_op jit(solution)/shard_map/cond/branch_1_fun/ppermute | solution.py:29
  376.4 11.8 %collective-permute-start.36 = (bf16[128,2048]{1,0:T(8,128)(2,1)S(1)}, bf16[128,2048]{1,0:T(8,128)(2,1)S(1)}, u32[]{:S(2)}, u32[]{:S(2)}) collective-permute-start(bf16[128,2048]{1,0:T(8,128)(2,1)S(1)} %pad_maximum_fusion.20), channel_id=1, source_target_pairs={{0,2},{2,0},{1,3},{3,1},{4,6},{6,4},{5,7},{7,5},{8,10},{10,8},{9,1... | collective-permute-start | bytes 1572872 | tf_op jit(solution)/shard_map/cond/branch_1_fun/ppermute | solution.py:29
  377.9 10.6 %collective-permute-start.37 = (bf16[128,2048]{1,0:T(8,128)(2,1)S(1)}, bf16[128,2048]{1,0:T(8,128)(2,1)S(1)}, u32[]{:S(2)}, u32[]{:S(2)}) collective-permute-start(bf16[128,2048]{1,0:T(8,128)(2,1)S(1)} %pad_maximum_fusion.21), channel_id=1, source_target_pairs={{0,8},{8,0},{1,9},{9,1},{2,10},{10,2},{3,11},{11,3},{4,12},{12,4},... | collective-permute-start | bytes 1572872 | tf_op jit(solution)/shard_map/cond/branch_1_fun/ppermute | solution.py:29
  403.0 25.4 %collective-permute-start.65 = (bf16[1024,512]{1,0:T(8,128)(2,1)}, bf16[1024,512]{1,0:T(8,128)(2,1)S(1)}, u32[]{:S(2)}, u32[]{:S(2)}) collective-permute-start(bf16[1024,512]{1,0:T(8,128)(2,1)} %get-tuple-element.666), channel_id=1, source_target_pairs={{0,4},{4,0},{1,5},{5,1},{2,6},{6,2},{3,7},{7,3},{8,12},{12,8},{9,1... | collective-permute-start | bytes 3145736 | tf_op jit(solution)/shard_map/ppermute | solution.py:29
  434.9 149.5 %reduce-scatter.9.cloned.1.call-start = ((), (), s32[]{:S(2)}) async-start(), calls=%async_computation.11 | async-start | bytes 1572864 | tf_op jit(solution)/shard_map/reduce_scatter | solution.py:268
  434.9 25.4 %collective-permute-start.64 = (bf16[1024,512]{1,0:T(8,128)(2,1)}, bf16[1024,512]{1,0:T(8,128)(2,1)}, u32[]{:S(2)}, u32[]{:S(2)}) collective-permute-start(bf16[1024,512]{1,0:T(8,128)(2,1)} %copy-done.53), channel_id=1, source_target_pairs={{0,4},{4,0},{1,5},{5,1},{2,6},{6,2},{3,7},{7,3},{8,12},{12,8},{9,1... | collective-permute-start | bytes 3145736 | tf_op jit(solution)/shard_map/ppermute | solution.py:29
  446.9 12.8 %collective-permute-start.39 = (bf16[512,2048]{1,0:T(8,128)(2,1)S(1)}, bf16[512,2048]{1,0:T(8,128)(2,1)}, u32[]{:S(2)}, u32[]{:S(2)}) collective-permute-start(bf16[512,2048]{1,0:T(8,128)(2,1)S(1)} %slice.1457), channel_id=1, source_target_pairs={{0,1},{1,0},{2,3},{3,2},{4,5},{5,4},{6,7},{7,6},{8,9},{9,8},{10,11... | collective-permute-start | bytes 6291464 | tf_op jit(solution)/shard_map/cond/branch_1_fun/ppermute | solution.py:29
  460.3 51.6 %collective-permute-start.66 = (bf16[1024,1024]{1,0:T(8,128)(2,1)}, bf16[1024,1024]{1,0:T(8,128)(2,1)}, u32[]{:S(2)}, u32[]{:S(2)}) collective-permute-start(bf16[1024,1024]{1,0:T(8,128)(2,1)} %get-tuple-element.682), channel_id=1, source_target_pairs={{0,4},{4,0},{1,5},{5,1},{2,6},{6,2},{3,7},{7,3},{8,12},{12,8},{9,1... | collective-permute-start | bytes 6291464 | tf_op jit(solution)/shard_map/ppermute | solution.py:29
  464.3 169.4 %reduce-scatter.11.cloned.1.call-start = ((), (), s32[]{:S(2)}) async-start(), calls=%async_computation.12 | async-start | bytes 3145728 | tf_op jit(solution)/shard_map/reduce_scatter | solution.py:268
  468.5 21.2 %collective-permute-start.40 = (bf16[128,2048]{1,0:T(8,128)(2,1)S(1)}, bf16[128,2048]{1,0:T(8,128)(2,1)S(1)}, u32[]{:S(2)}, u32[]{:S(2)}) collective-permute-start(bf16[128,2048]{1,0:T(8,128)(2,1)S(1)} %pad_maximum_fusion.22), channel_id=1, source_target_pairs={{0,8},{8,0},{1,9},{9,1},{2,10},{10,2},{3,11},{11,3},{4,12},{12,4},... | collective-permute-start | bytes 1572872 | tf_op jit(solution)/shard_map/cond/branch_1_fun/ppermute | solution.py:29
  469.8 20.0 %collective-permute-start.41 = (bf16[128,2048]{1,0:T(8,128)(2,1)S(1)}, bf16[128,2048]{1,0:T(8,128)(2,1)S(1)}, u32[]{:S(2)}, u32[]{:S(2)}) collective-permute-start(bf16[128,2048]{1,0:T(8,128)(2,1)S(1)} %pad_maximum_fusion.23), channel_id=1, source_target_pairs={{0,2},{2,0},{1,3},{3,1},{4,6},{6,4},{5,7},{7,5},{8,10},{10,8},{9,1... | collective-permute-start | bytes 1572872 | tf_op jit(solution)/shard_map/cond/branch_1_fun/ppermute | solution.py:29
  489.9 10.0 %collective-permute-start.43 = (bf16[64,2048]{1,0:T(8,128)(2,1)S(1)}, bf16[64,2048]{1,0:T(8,128)(2,1)S(1)}, u32[]{:S(2)}, u32[]{:S(2)}) collective-permute-start(bf16[64,2048]{1,0:T(8,128)(2,1)S(1)} %slice.1458), channel_id=1, source_target_pairs={{0,8},{8,0},{1,9},{9,1},{2,10},{10,2},{3,11},{11,3},{4,12},{12,4},... | collective-permute-start | bytes 786440 | tf_op jit(solution)/shard_map/cond/branch_1_fun/ppermute | solution.py:29
  515.8 149.1 %reduce-scatter.15.cloned.1.call-start = ((), (), s32[]{:S(2)}) async-start(), calls=%async_computation.14 | async-start | bytes 3145728 | tf_op jit(solution)/shard_map/reduce_scatter | solution.py:268
  515.9 68.5 %collective-permute-start.67 = (bf16[1024,1024]{1,0:T(8,128)(2,1)}, bf16[1024,1024]{1,0:T(8,128)(2,1)}, u32[]{:S(2)}, u32[]{:S(2)}) collective-permute-start(bf16[1024,1024]{1,0:T(8,128)(2,1)} %get-tuple-element.698), channel_id=1, source_target_pairs={{0,4},{4,0},{1,5},{5,1},{2,6},{6,2},{3,7},{7,3},{8,12},{12,8},{9,1... | collective-permute-start | bytes 6291464 | tf_op jit(solution)/shard_map/ppermute | solution.py:29
  518.3 11.0 %collective-permute-start.46 = (bf16[128,2048]{1,0:T(8,128)(2,1)S(1)}, bf16[128,2048]{1,0:T(8,128)(2,1)S(1)}, u32[]{:S(2)}, u32[]{:S(2)}) collective-permute-start(bf16[128,2048]{1,0:T(8,128)(2,1)S(1)} %pad_maximum_fusion.25), channel_id=1, source_target_pairs={{0,2},{2,0},{1,3},{3,1},{4,6},{6,4},{5,7},{7,5},{8,10},{10,8},{9,1... | collective-permute-start | bytes 1572872 | tf_op jit(solution)/shard_map/cond/branch_1_fun/ppermute | solution.py:29
  521.2 22.1 %collective-permute-start.47 = (bf16[128,2048]{1,0:T(8,128)(2,1)S(1)}, bf16[128,2048]{1,0:T(8,128)(2,1)S(1)}, u32[]{:S(2)}, u32[]{:S(2)}) collective-permute-start(bf16[128,2048]{1,0:T(8,128)(2,1)S(1)} %pad_maximum_fusion.26), channel_id=1, source_target_pairs={{0,8},{8,0},{1,9},{9,1},{2,10},{10,2},{3,11},{11,3},{4,12},{12,4},... | collective-permute-start | bytes 1572872 | tf_op jit(solution)/shard_map/cond/branch_1_fun/ppermute | solution.py:29
  547.4 9.1 %collective-permute-start.48 = (bf16[512,2048]{1,0:T(8,128)(2,1)}, bf16[512,2048]{1,0:T(8,128)(2,1)}, u32[]{:S(2)}, u32[]{:S(2)}) collective-permute-start(bf16[512,2048]{1,0:T(8,128)(2,1)} %get-tuple-element.1024), channel_id=1, source_target_pairs={{0,1},{1,0},{2,3},{3,2},{4,5},{5,4},{6,7},{7,6},{8,9},{9,8},{10,11... | collective-permute-start | bytes 6291464 | tf_op jit(solution)/shard_map/cond/branch_1_fun/ppermute | solution.py:29
  589.0 141.3 %reduce-scatter.13.cloned.1.call-start = ((), (), s32[]{:S(2)}) async-start(), calls=%async_computation.13 | async-start | bytes 1572864 | tf_op jit(solution)/shard_map/reduce_scatter | solution.py:268
  591.4 42.3 %collective-permute-start.68 = (bf16[1024,512]{1,0:T(8,128)(2,1)}, bf16[1024,512]{1,0:T(8,128)(2,1)}, u32[]{:S(2)}, u32[]{:S(2)}) collective-permute-start(bf16[1024,512]{1,0:T(8,128)(2,1)} %copy.59), channel_id=1, source_target_pairs={{0,4},{4,0},{1,5},{5,1},{2,6},{6,2},{3,7},{7,3},{8,12},{12,8},{9,1... | collective-permute-start | bytes 3145736 | tf_op jit(solution)/shard_map/ppermute | solution.py:29
  593.1 40.6 %collective-permute-start.69 = (bf16[256,1024]{1,0:T(8,128)(2,1)}, bf16[256,1024]{1,0:T(8,128)(2,1)}, u32[]{:S(2)}, u32[]{:S(2)}) collective-permute-start(bf16[256,1024]{1,0:T(8,128)(2,1)} %slice_select_fusion.7), channel_id=1, source_target_pairs={{0,8},{8,0},{1,9},{9,1},{2,10},{10,2},{3,11},{11,3},{4,12},{12,4},... | collective-permute-start | bytes 1572872 | tf_op jit(solution)/shard_map/ppermute | solution.py:29
  597.3 7.3 collective-permute-start.49
  604.7 14.7 %collective-permute-start.50 = (f32[2,2,2,2,128]{4,3,2,1,0:T(2,128)S(1)}, f32[2,2,2,2,128]{4,3,2,1,0:T(2,128)S(1)}, u32[]{:S(2)}, u32[]{:S(2)}) collective-permute-start(f32[2,2,2,2,128]{4,3,2,1,0:T(2,128)S(1)} %reverse_add_fusion.3), channel_id=1, source_target_pairs={{0,8},{8,0},{1,9},{9,1},{2,10},{10,2},{3,11},{11,3},{4,12},{12,4},... | collective-permute-start | bytes 24584 | tf_op jit(solution)/shard_map/cond/branch_1_fun/ppermute | solution.py:29
  637.8 102.2 %reduce-scatter.17.cloned.1.call-start = ((), (), s32[]{:S(2)}) async-start(), calls=%async_computation.15 | async-start | bytes 1572864 | tf_op jit(solution)/shard_map/reduce_scatter | solution.py:268
  637.9 27.0 %collective-permute-start.70 = (bf16[1024,512]{1,0:T(8,128)(2,1)}, bf16[1024,512]{1,0:T(8,128)(2,1)}, u32[]{:S(2)}, u32[]{:S(2)}) collective-permute-start(bf16[1024,512]{1,0:T(8,128)(2,1)} %get-tuple-element.730), channel_id=1, source_target_pairs={{0,4},{4,0},{1,5},{5,1},{2,6},{6,2},{3,7},{7,3},{8,12},{12,8},{9,1... | collective-permute-start | bytes 3145736 | tf_op jit(solution)/shard_map/ppermute | solution.py:29
  640.2 24.7 %collective-permute-start.71 = (bf16[256,1024]{1,0:T(8,128)(2,1)}, bf16[256,1024]{1,0:T(8,128)(2,1)}, u32[]{:S(2)}, u32[]{:S(2)}) collective-permute-start(bf16[256,1024]{1,0:T(8,128)(2,1)} %slice_select_fusion.8), channel_id=1, source_target_pairs={{0,8},{8,0},{1,9},{9,1},{2,10},{10,2},{3,11},{11,3},{4,12},{12,4},... | collective-permute-start | bytes 1572872 | tf_op jit(solution)/shard_map/ppermute | solution.py:29
  655.5 9.4 %collective-permute-start.52 = (bf16[512,2048]{0,1:T(8,128)(2,1)}, bf16[512,2048]{0,1:T(8,128)(2,1)}, u32[]{:S(2)}, u32[]{:S(2)}) collective-permute-start(bf16[512,2048]{0,1:T(8,128)(2,1)} %fusion.74), channel_id=1, source_target_pairs={{0,1},{1,0},{2,3},{3,2},{4,5},{5,4},{6,7},{7,6},{8,9},{9,8},{10,11... | collective-permute-start | bytes 6291464 | tf_op jit(solution)/shard_map/cond/branch_1_fun/ppermute | solution.py:29
  667.9 32.4 %collective-permute-start.22 = (f32[4,2048]{1,0:T(4,128)S(1)}, f32[4,2048]{1,0:T(4,128)S(1)}, u32[]{:S(2)}, u32[]{:S(2)}) collective-permute-start(f32[4,2048]{1,0:T(4,128)S(1)} %get-tuple-element.396), channel_id=1, source_target_pairs={{0,4},{4,0},{1,5},{5,1},{2,6},{6,2},{3,7},{7,3},{8,12},{12,8},{9,1... | collective-permute-start | bytes 98312 | tf_op jit(solution)/shard_map/cond/branch_1_fun/ppermute | solution.py:29
  669.4 47.7 %collective-permute-start.21 = (bf16[256,1024]{1,0:T(8,128)(2,1)}, bf16[256,1024]{1,0:T(8,128)(2,1)}, u32[]{:S(2)}, u32[]{:S(2)}) collective-permute-start(bf16[256,1024]{1,0:T(8,128)(2,1)} %broadcast_select_fusion.33), channel_id=1, source_target_pairs={{0,8},{8,0},{1,9},{9,1},{2,10},{10,2},{3,11},{11,3},{4,12},{12,4},... | collective-permute-start | bytes 1572872 | tf_op jit(solution)/shard_map/cond/branch_1_fun/ppermute | solution.py:29
  685.1 31.8 %collective-permute-start.19 = (bf16[128,2048]{1,0:T(8,128)(2,1)}, bf16[128,2048]{1,0:T(8,128)(2,1)S(1)}, u32[]{:S(2)}, u32[]{:S(2)}) collective-permute-start(bf16[128,2048]{1,0:T(8,128)(2,1)} %pad_maximum_fusion.36), channel_id=1, source_target_pairs={{0,2},{2,0},{1,3},{3,1},{4,6},{6,4},{5,7},{7,5},{8,10},{10,8},{9,1... | collective-permute-start | bytes 1572872 | tf_op jit(solution)/shard_map/cond/branch_1_fun/ppermute | solution.py:29
  687.7 27.6 %collective-permute-start.17 = (bf16[128,2048]{1,0:T(8,128)(2,1)}, bf16[128,2048]{1,0:T(8,128)(2,1)S(1)}, u32[]{:S(2)}, u32[]{:S(2)}) collective-permute-start(bf16[128,2048]{1,0:T(8,128)(2,1)} %pad_maximum_fusion.35), channel_id=1, source_target_pairs={{0,8},{8,0},{1,9},{9,1},{2,10},{10,2},{3,11},{11,3},{4,12},{12,4},... | collective-permute-start | bytes 1572872 | tf_op jit(solution)/shard_map/cond/branch_1_fun/ppermute | solution.py:29
  700.2 10.2 %collective-permute-start.23 = (f32[4,2048]{1,0:T(4,128)S(1)}, f32[4,2048]{1,0:T(4,128)S(1)}, u32[]{:S(2)}, u32[]{:S(2)}) collective-permute-start(f32[4,2048]{1,0:T(4,128)S(1)} %add.198), channel_id=1, source_target_pairs={{0,8},{8,0},{1,9},{9,1},{2,10},{10,2},{3,11},{11,3},{4,12},{12,4},... | collective-permute-start | bytes 98312 | tf_op jit(solution)/shard_map/cond/branch_1_fun/ppermute | solution.py:29
  731.4 7.5 collective-permute-start.73
  (91 other events, 797.6 us)
Sparse Core Ops, SparseCore 0:
  34.4 57.5 all-gather.4
  104.0 55.7 all-gather.6
  161.3 55.6 all-gather.8
  219.0 55.6 all-gather.10
  435.0 31.3 reduce-scatter.6
  468.5 31.5 reduce-scatter.8
  515.9 54.0 reduce-scatter.10
  589.1 53.7 reduce-scatter.14
  645.1 31.6 reduce-scatter.12
  679.0 31.6 reduce-scatter.16

commit v3 on v2

--- a/solution.py
+++ b/solution.py
@@ -3,6 +3,7 @@
 from jax import lax
 from jax.experimental import pallas as pl
 from jax.experimental.pallas import tpu as pltpu
+from jax.experimental.layout import Layout as Order, with_layout_constraint
 from jax.sharding import Mesh, PartitionSpec as P
 
 HEAD_DIM = 128
@@ -311,9 +312,10 @@
         other = net.send(mine, core)
         return jnp.concatenate([mine, other], 0), other
 
-    def scatter_begin(net, part):
-        n = part.shape[0] // 2
-        return part[:n], net.send(part[n:].astype(BF16), core)
+    def scatter_begin(net, product, n_rows):
+        half = n_rows // 2
+        received = net.send(product(slice(half, None)).astype(BF16), core)
+        return product(slice(half)), received
 
     def scatter_second(net, state):
         part = state[0] + state[1].astype(F32)
@@ -404,10 +406,12 @@
                 dot_rows_cols(left[:, j * piece : (j + 1) * piece], block[:, cols]) for j, block in enumerate(pieces)
             )
 
-        def weight_grad(seq, left, right, which):
+        def weight_grad(seq, left, right, which, cols=slice(None)):
             return [
                 seq.run(
-                    lambda a, b: contract_rows(a, b).astype(BF16), left[:, j * piece : (j + 1) * piece], right
+                    lambda a, b, j=j: contract_rows(a[:, j * piece : (j + 1) * piece], b[:, cols]).astype(BF16),
+                    left,
+                    right,
                 )
                 for j in which
             ]
@@ -416,24 +420,26 @@
 
         def part_first():
             block_attn = both_rows(attn_weights, net.send(leaving(attn_weights), col))
-            pos_rows, seg_rows = token_rows_of(positions, seg_ids, net)
-            return block_attn, leaving([w_gate]), leaving([w_up]), pos_rows, seg_rows, lay.to_relative(hidden_in)
-
-        block_attn, leave_gate, leave_up, pos_rows, seg_rows, x_low = region(flag, part_first)
+            return block_attn, leaving([w_gate]), leaving([w_up]), lay.to_relative(hidden_in)
+
+        block_attn, leave_gate, leave_up, x_low = region(flag, part_first)
         far_attn, own_attn = ahead(block_attn), spread(net, block_attn)[1:]
 
         def part_tokens():
-            state = gather_middle(net, gather_begin(net, x_low))
-            got_gate = net.send(after(leave_gate, *state[1]), col)
-            x_all, other = gather_end(net, state)
-            return x_all, leaving([w_down]), both_rows([w_gate], got_gate)
+            state = gather_begin(net, x_low)
+            got_gate = net.send(after(leave_gate, *state[2:]), col)
+            state = gather_middle(net, (*state[:3], after(state[3], got_gate)))
+            tables = token_rows_of(positions, seg_ids, net)
+            return state, leaving([w_down]), both_rows([w_gate], got_gate), tables
 
         out = region(flag, part_tokens)
-        far_attn, own_attn, (x_all, leave_down, block_gate) = meet(far_attn, own_attn, out)
+        far_attn, own_attn, (state, leave_down, block_gate, (pos_rows, seg_rows)) = meet(far_attn, own_attn, out)
+        got_up = net.send(leave_up, col)
         relay_attn = spread(net, beyond(far_attn))[1:]
-        far_gate, got_up = ahead(block_gate), net.send(leave_up, col)
+        far_gate = ahead(block_gate)
 
         def part_tables():
+            x_all, _ = gather_end(net, state)
             cos_tab, sin_tab = rope_tables(pos_rows.reshape(n_tokens, 1))
             ids_rows = token_rows(jnp.arange(seq_len, dtype=jnp.int32), lambda rows: rows)
             seg_seq, ids_seq = by_seq(seg_rows), by_seq(ids_rows)
@@ -443,10 +449,10 @@
             gain_key = lax.dynamic_slice_in_dim(gains[1], offset, head_cols)
             gain_post = lay.to_relative(gains[2:4])
             more = gain_query, gain_key, gain_post[0:1], gain_post[1:2], lay.to_relative(out_grad).astype(F32)
-            return cos_tab, sin_tab, mask, more
+            return x_all, cos_tab, sin_tab, mask, more
 
         out = region(flag, part_tables)
-        relay_attn, got_up, (cos_tab, sin_tab, mask, more) = meet(relay_attn, got_up, out)
+        relay_attn, got_up, (x_all, cos_tab, sin_tab, mask, more) = meet(relay_attn, got_up, out)
         gain_query, gain_key, gain_attn, gain_mlp, grad_out = more
         block_up = both_rows([w_up], got_up)
         far_up, own_up = ahead(block_up), spread(net, block_up)[1:]
@@ -455,28 +461,27 @@
 
         def part_qkv():
             near_attn = [far_attn, *(in_two(own, other) for own, other in zip(own_attn, relay_attn))]
-            qkv = by_rows(x_all, near_attn, qkv_cols)
+            qkv = with_layout_constraint(by_rows(x_all, near_attn, qkv_cols), Order((0, 1)))
             squares, _ = add_stats(
                 net,
                 jnp.stack(
                     [jnp.sum(part * part, -1) for part in (qkv[:, :head_cols], qkv[:, head_cols : 2 * head_cols])], 0
                 ),
             )
-            return near_attn, qkv, squares
+            return near_attn, qkv, squares, stack(*(block[:, out_cols] for block in near_attn))
 
         out = region(flag, part_qkv)
-        leave_down, (near_attn, qkv, squares) = meet(leave_down, out)
+        leave_down, (near_attn, qkv, squares, out_w) = meet(leave_down, out)
         got_down = net.send(leave_down, col)
 
         def part_attend():
             norms = lax.rsqrt(squares / model_width + EPS).T
             attn_low = attention(qkv, norms, gain_query, gain_key, cos_tab, sin_tab, mask)
-            out_w = stack(*(block[:, out_cols] for block in near_attn))
-            state = scatter_begin(net, contract_cols(attn_low, out_w))
-            return attn_low, norms, out_w, state
+            state = scatter_begin(net, lambda rows: contract_cols(attn_low[rows], out_w), n_tokens)
+            return attn_low, norms, state
 
         out = region(flag, part_attend)
-        own_up, far_gate, got_down, (attn_low, norms, out_w, state) = meet(own_up, far_gate, got_down, out)
+        own_up, far_gate, got_down, (attn_low, norms, state) = meet(own_up, far_gate, got_down, out)
         near_gate = spread(net, far_gate)
         block_down = both_rows([w_down], got_down)
         far_down = ahead(block_down)
@@ -505,16 +510,16 @@
             near_up = [far_up, *(in_two(own, other) for own, other in zip(own_up, relay_up))]
             up_proj = by_rows(mlp_in, near_up)
             hidden_act = (gate_proj * jax.nn.sigmoid(gate_proj) * up_proj).astype(BF16)
-            return up_proj, hidden_act, stack(*near_gate), stack(*near_up)
+            return up_proj, hidden_act, near_up
 
         out = region(flag, part_up)
-        relay_down, (up_proj, hidden_act, gate_w, up_w) = meet(relay_down, out)
+        relay_down, (up_proj, hidden_act, near_up) = meet(relay_down, out)
 
         act_halves = slice(hidden_act.shape[1] // 2), slice(hidden_act.shape[1] // 2, None)
 
         def part_down():
             down_w = stack(far_down, *(in_two(own, other) for own, other in zip(own_down, relay_down)))
-            state = scatter_begin(net, contract_cols(hidden_act, down_w))
+            state = scatter_begin(net, lambda rows: contract_cols(hidden_act[rows], down_w), n_tokens)
             mlp_sum = scatter_end(scatter_third(net, scatter_second(net, state)))
             norm_mlp = lax.rsqrt(jnp.mean(mlp_sum * mlp_sum, -1, keepdims=True) + EPS)
             mlp_hat = mlp_sum * norm_mlp
@@ -522,15 +527,15 @@
             grad_mlp = norm_mlp * (scaled - mlp_hat * jnp.mean(mlp_hat * scaled, -1, keepdims=True))
             grad_mlp_all, _ = gather_end(net, gather_middle(net, gather_begin(net, grad_mlp.astype(BF16))))
             seq = Sequence()
-            sends = [weight_grad(seq, grad_mlp_all, hidden_act[:, half], sent_pieces) for half in act_halves]
-            return down_w, mlp_hat, grad_mlp_all, sends
-
-        down_w, mlp_hat, grad_mlp_all, sends = region(flag, part_down)
-        got_first, got_second = [begin(net, grads) for grads in sends]
+            sends = weight_grad(seq, grad_mlp_all, hidden_act, sent_pieces, act_halves[0])
+            return down_w, mlp_hat, grad_mlp_all, sends, stack(*near_gate), stack(*near_up)
+
+        down_w, mlp_hat, grad_mlp_all, sends, gate_w, up_w = region(flag, part_down)
+        got_first = begin(net, sends)
 
         def part_back_act():
             seq = Sequence()
-            keeps_first = weight_grad(seq, grad_mlp_all, hidden_act[:, act_halves[0]], kept_pieces)
+            keeps_first = weight_grad(seq, grad_mlp_all, hidden_act, kept_pieces, act_halves[0])
 
             def back_act(grad_mlp_all, down_w):
                 sig_gate = jax.nn.sigmoid(gate_proj)
@@ -539,21 +544,32 @@
                 return grad_gate, (grad_act * (gate_proj * sig_gate)).astype(BF16)
 
             grad_gate, grad_up = seq.run(back_act, grad_mlp_all, down_w)
-            return keeps_first, grad_gate, grad_up, seq.run(contract_cols, grad_gate, gate_w)
+            down_sends = weight_grad(seq, grad_mlp_all, hidden_act, sent_pieces, act_halves[1])
+            gate_sends = weight_grad(seq, mlp_in, grad_gate, sent_pieces)
+            return keeps_first, grad_gate, grad_up, down_sends, gate_sends
 
         out = region(flag, part_back_act)
-        got_first, (keeps_first, grad_gate, grad_up, grad_part) = meet(got_first, out)
+        got_first, (keeps_first, grad_gate, grad_up, down_sends, gate_sends) = meet(got_first, out)
+        got_second, got_gate = begin(net, down_sends), begin(net, gate_sends)
         down_first = behind(finish(net, keeps_first, got_first))
 
         def part_back_resid():
             seq = Sequence()
-            state = scatter_begin(net, seq.run(lambda a, b, c: a + contract_cols(b, c), grad_part, grad_up, up_w))
-            keeps_second = weight_grad(seq, grad_mlp_all, hidden_act[:, act_halves[1]], kept_pieces)
-            return weight_grad(seq, mlp_in, grad_gate, sent_pieces), keeps_second, state
+            state = scatter_begin(
+                net,
+                lambda rows: seq.run(
+                    lambda a, b, c, d: contract_cols(a[rows], c) + contract_cols(b[rows], d),
+                    grad_gate,
+                    grad_up,
+                    gate_w,
+                    up_w,
+                ),
+                n_tokens,
+            )
+            return weight_grad(seq, grad_mlp_all, hidden_act, kept_pieces, act_halves[1]), state
 
         out = region(flag, part_back_resid)
-        got_second, (sends, keeps_second, state) = meet(got_second, out)
-        got_gate = begin(net, sends)
+        got_second, (keeps_second, state) = meet(got_second, out)
         down_second = behind(finish(net, keeps_second, got_second))
 
         def part_back_attn():
@@ -579,29 +595,34 @@
         total_gate = behind(finish(net, keeps_gate, got_gate))
 
         def part_back_heads():
-            seq = Sequence()
             grad_attn_all, _ = gather_end(net, gather_middle(net, state))
             grad_heads = dot_rows_cols(grad_attn_all, out_w).astype(BF16)
-            grads = attention(qkv, norms, gain_query, gain_key, cos_tab, sin_tab, mask, grad_heads)
+            return grad_attn_all, attention(qkv, norms, gain_query, gain_key, cos_tab, sin_tab, mask, grad_heads)
+
+        out = region(flag, part_back_heads)
+        got_up, down_second, (grad_attn_all, grads) = meet(got_up, down_second, out)
+        grad_query_n, grad_key_n, grad_value_low, inner_parts, head_gains = grads
+        total_up = behind(finish(net, keeps_up, got_up))
+
+        def part_back_value():
+            seq = Sequence()
+            inner, received = add_stats(net, jnp.sum(inner_parts, 0).reshape(n_tokens, 2).T)
             sends = [
                 jnp.concatenate(pair, 1)
                 for pair in zip(
-                    weight_grad(seq, x_all, grads[2], sent_pieces), weight_grad(seq, grad_attn_all, attn_low, sent_pieces)
+                    weight_grad(seq, x_all, grad_value_low, sent_pieces),
+                    weight_grad(seq, grad_attn_all, attn_low, sent_pieces),
                 )
             ]
-            return grad_attn_all, grads, sends
-
-        out = region(flag, part_back_heads)
-        got_up, down_second, (grad_attn_all, grads, sends) = meet(got_up, down_second, out)
-        grad_query_n, grad_key_n, grad_value_low, inner_parts, head_gains = grads
-        got_first = begin(net, sends)
-        total_up = behind(finish(net, keeps_up, got_up))
-        total_down = jnp.concatenate([down_first, down_second], 1)
-        got_down = net.send(to_leave(total_down), col)
+            total_down = jnp.concatenate([down_first, down_second], 1)
+            return inner, sends, total_down, to_leave(total_down)
+
+        inner, sends, total_down, leave = region(flag, part_back_value)
+        got_first, got_down = begin(net, sends), net.send(leave, col)
 
         def part_back_qkv():
             seq = Sequence()
-            inner, received = add_stats(net, jnp.sum(inner_parts, 0).reshape(n_tokens, 2).T)
+            qkv_w = stack(*(part[:, qkv_cols] for part in near_attn))
             keeps_first = [
                 jnp.concatenate(pair, 1)
                 for pair in zip(
@@ -609,12 +630,11 @@
                     weight_grad(seq, grad_attn_all, attn_low, kept_pieces),
                 )
             ]
-            seq.wait(received)
-            inner = inner.T / model_width
+            scale = inner.T / model_width
 
             def through_norm(grad, i, gain):
                 hat = qkv[:, i * head_cols : (i + 1) * head_cols] * norms[:, i : i + 1]
-                return (norms[:, i : i + 1] * (grad * gain - hat * inner[:, i : i + 1])).astype(BF16)
+                return (norms[:, i : i + 1] * (grad * gain - hat * scale[:, i : i + 1])).astype(BF16)
 
             qk_right = seq.run(
                 lambda a, b: jnp.concatenate(
@@ -623,10 +643,10 @@
                 grad_query_n,
                 grad_key_n,
             )
-            return qk_right, keeps_first, weight_grad(seq, x_all, qk_right, sent_pieces)
+            return qk_right, keeps_first, weight_grad(seq, x_all, qk_right, sent_pieces), qkv_w
 
         out = region(flag, part_back_qkv)
-        got_first, got_down, total_gate, (qk_right, keeps_first, sends) = meet(got_first, got_down, total_gate, out)
+        got_first, total_gate, (qk_right, keeps_first, sends, qkv_w) = meet(got_first, total_gate, out)
         got_second = begin(net, sends)
         vo_total = behind(finish(net, keeps_first, got_first))
         got_gate = net.send(to_leave(total_gate), col)
@@ -634,34 +654,42 @@
         def part_in_part():
             keeps_second = weight_grad(Sequence(), x_all, qk_right, kept_pieces)
             qkv_right = jnp.concatenate([qk_right, grad_value_low], 1)
-            in_part = jnp.concatenate([contract_cols(qkv_right, part[:, qkv_cols]) for part in near_attn], 1)
             head_rows = lax.dynamic_update_slice(
                 jnp.zeros((2, model_width), F32), head_gains, (jnp.int32(0), offset)
             )
             gain_row_mlp = jnp.sum(grad_out * mlp_hat, 0, keepdims=True)
             post_rows = lay.from_relative(jnp.concatenate([gain_row_attn, gain_row_mlp], 0))
             gain_rows = add_all(net, jnp.concatenate([head_rows, post_rows], 0), (side, core))
-            return keeps_second, scatter_begin(net, in_part), gain_rows
+            return keeps_second, scatter_begin(net, lambda rows: contract_cols(qkv_right[rows], qkv_w), n_tokens), gain_rows
 
         out = region(flag, part_in_part)
-        got_second, got_gate, total_up, (keeps_second, state, gain_rows) = meet(got_second, got_gate, total_up, out)
+        got_second, got_down, got_gate, total_up, out = meet(got_second, got_down, got_gate, total_up, out)
+        keeps_second, state, gain_rows = out
+        got_up = net.send(to_leave(total_up), col)
         qk_total = behind(finish(net, keeps_second, got_second))
 
         def part_outputs():
-            later = scatter_second(net, state)
-            gains_grad = add_all(net, gain_rows, lay.near + (lay.col_axis, lay.far))
-            got_up = net.send(to_leave(total_up), col)
+            ending = scatter_third(net, scatter_second(net, state))
+            gate_grad = jnp.concatenate(owned(total_gate, got_gate), 1)
             down_grad = jnp.concatenate(owned(total_down, got_down), 1)
-            in_grad = lay.from_relative(grad_resid + scatter_end(scatter_third(net, later)))
             hidden_out = lay.from_relative((resid + mlp_hat * gain_mlp).astype(BF16))
-            gate_grad = jnp.concatenate(owned(total_gate, got_gate), 1)
+            near_rows = add_all(net, gain_rows, lay.near)
+            return ending, gate_grad, down_grad, hidden_out, near_rows
+
+        out = region(flag, part_outputs)
+        vo_total, qk_total, got_up, out = meet(vo_total, qk_total, got_up, out)
+        state, gate_grad, down_grad, hidden_out, gain_rows = out
+        got_vo, got_qk = net.send(to_leave(vo_total), col), net.send(to_leave(qk_total), col)
+
+        def part_last():
+            gains_grad = add_all(net, gain_rows, (lay.far, lay.col_axis))
             up_grad = jnp.concatenate(owned(total_up, got_up), 1)
-            return in_grad, hidden_out, gate_grad, down_grad, up_grad, gains_grad
-
-        out = region(flag, part_outputs)
-        vo_total, (in_grad, hidden_out, gate_grad, down_grad, up_grad, gains_grad) = meet(vo_total, out)
-        vo_pair = owned(vo_total, net.send(to_leave(vo_total), col))
-        qk_pair = owned(qk_total, net.send(to_leave(qk_total), col))
+            return lay.from_relative(grad_resid + scatter_end(state)), up_grad, gains_grad
+
+        out = region(flag, part_last)
+        got_vo, got_qk, (in_grad, up_grad, gains_grad) = meet(got_vo, got_qk, out)
+        vo_pair = owned(vo_total, got_vo)
+        qk_pair = owned(qk_total, got_qk)
         query_grad, key_grad, value_grad, out_grad_own = (
             jnp.concatenate([part[:, i * head_cols : (i + 1) * head_cols] for part in pair], 1)
             for pair in (qk_pair, vo_pair)

time: 768 us -> 734 us (0.956)
  local copies, waits for them, and re-layouts: 131 us -> 89.4 us
  matrix products: 119 us -> 146 us
  other arithmetic: 143 us -> 126 us
    cond x43, other arithmetic: 25.9 us -> 9.99 us
    slice x18 -> x10, local copies, waits for them, and re-layouts: 24.7 us -> 9.01 us  [the longest x2 4.16 us: part_back_qkv(): qkv_w = stack(*(part[:, qkv_cols] for part in near_attn))]
    another operation x8 -> x3, local copies, waits for them, and re-layouts: 17 us -> 2.26 us
    dot_general x14, matrix products: 42.6 us -> 57.2 us  [contract_rows(): lax.dot_general(left, right, (((0,), (0,)), ((), ())), preferred_element_...]
    dot_general x6 -> x10, matrix products: 32.1 us -> 43.7 us  [contract_cols(): lax.dot_general(left, right, (((1,), (1,)), ((), ())), preferred_element_...]
    cond x127 -> x141, local copies, waits for them, and re-layouts: 49.7 us -> 45.2 us
    another operation x5 -> x3, other arithmetic: 15.7 us -> 13.3 us
    select_n x22 -> x21, other arithmetic: 23.7 us -> 25.5 us  [pick(): return jnp.where(flag, yes, no)]
  transfers between devices with their start and end apart: 84 -> 84, of which waited for: 40 -> 37; matrix products, arithmetic and copies ran while one was open for 46% -> 44% of each run, Pallas kernels for 3% -> 3%
where the time goes in v3:
time: 734 us; the launch traced here: 723 us
  waiting for transfers between devices  245 us (33%)
  matrix products  146 us (20%)
  other arithmetic  126 us (17%)
  local copies, waits for them, and re-layouts  89.4 us (12%)
  starting transfers between devices  76.3 us (10%)
  Pallas kernels  21.2 us (3%)
  between operations  15.6 us (2%)
    ppermute x74, waiting for transfers between devices, swap(): return lax.ppermute(values, axis, [(0, 1), (1, 0)])  243 us
    ppermute x74, starting transfers between devices, swap(): return lax.ppermute(values, axis, [(0, 1), (1, 0)])  75.9 us
    dot_general x14, matrix products, contract_rows(): lax.dot_general(left, right, (((0,), (0,)), ((), ())), preferred_element_...  57.2 us
    dot_general x8, matrix products, dot_rows_cols(): return jnp.dot(left, right, preferred_element_type=F32)  45 us
    dot_general x10, matrix products, contract_cols(): lax.dot_general(left, right, (((1,), (1,)), ((), ())), preferred_element_...  43.7 us
    cond x140, local copies, waits for them, and re-layouts  43 us
    select_n x21, other arithmetic, pick(): return jnp.where(flag, yes, no)  25.5 us
    pallas_call x2, Pallas kernels, attention(): pl.pallas_call(kernel, grid=(2, n_heads), in_specs=in_specs, out_specs=ou...  21.2 us
  transfers between devices with their start and end apart: 84, of which 37 were waited for; matrix products, arithmetic and copies ran while one was open for 44% of the time, Pallas kernels for 3%

profile of v3, /device:TPU:0, one launch (start us, length us, event | category | flops | bytes accessed | tf_op | source)
XLA Modules:
  0.0 723.3 jit_solution(15983893153913673791)
XLA Ops:
  9.1 21.4 %conditional.18 = (bf16[512,1024]{1,0:T(8,128)(2,1)}, bf16[256,1024]{1,0:T(8,128)(2,1)}, bf16[256,1024]{1,0:T(8,128)(2,1)}, bf16[128,2048]{1,0:T(8,128)(2,1)S(1)}) conditional(s32[]{:T(128)} %bitcast.58, () %tuple.183, (bf16[256,512]{1,0:T(8,128)(2,1)}, bf16[256,512]{1,0:T(8,128)(2,1)}, bf16[256,512]{1,0:T(8,128)(2,1)}, bf16[256,512]{1,0:T(8,128)(2,1)}, ...), branch_computations={%region_0.0_spmd, %region_1.2_spmd} | conditional | flops 12058631 | bytes 35127872 | solution.py:48
  17.1 10.9 %collective-permute-done.5 = bf16[256,1024]{1,0:T(8,128)(2,1)} collective-permute-done((bf16[256,1024]{1,0:T(8,128)(2,1)}, bf16[256,1024]{1,0:T(8,128)(2,1)}, u32[]{:S(2)}, u32[]{:S(2)}) %collective-permute-start.5) | collective-permute-done | bytes 524320 | tf_op jit(solution)/shard_map/cond/branch_1_fun/ppermute | solution.py:30
  32.3 54.7 %conditional.19 = (bf16[64,2048]{1,0:T(8,128)(2,1)S(1)}, bf16[64,2048]{1,0:T(8,128)(2,1)S(1)}, bf16[64,2048]{1,0:T(8,128)(2,1)S(1)}, bf16[64,2048]{1,0:T(8,128)(...) conditional(s32[]{:T(128)} %bitcast.58, () %tuple.185, ...), branch_computations={%region_2.3_spmd, %region_3.4_spmd} | conditional | flops 4982795 | bytes 32563916 | solution.py:48
  45.0 21.5 %collective-permute-done.8 = bf16[256,1024]{1,0:T(8,128)(2,1)S(1)} collective-permute-done((bf16[256,1024]{1,0:T(8,128)(2,1)}, bf16[256,1024]{1,0:T(8,128)(2,1)S(1)}, u32[]{:S(2)}, u32[]{:S(2)}) %collective-permute-start.8) | collective-permute-done | bytes 524320 | tf_op jit(solution)/shard_map/cond/branch_1_fun/ppermute | solution.py:30
  68.3 15.9 %collective-permute-done.10 = bf16[128,2048]{1,0:T(8,128)(2,1)} collective-permute-done((bf16[128,2048]{1,0:T(8,128)(2,1)S(1)}, bf16[128,2048]{1,0:T(8,128)(2,1)}, u32[]{:S(2)}, u32[]{:S(2)}) %collective-permute-start.10) | collective-permute-done | bytes 524320 | tf_op jit(solution)/shard_map/cond/branch_1_fun/ppermute | solution.py:30
  94.2 15.5 %conditional.20 = (bf16[1024,2048]{1,0:T(8,128)(2,1)}, f32[1024,128]{1,0:T(8,128)}, f32[1024,128]{1,0:T(8,128)}, f32[2,512,512]{2,1,0:T(8,128)S(1)}, f32[256]{0:...) conditional(s32[]{:T(128)} %bitcast.58, () %tuple.188, ...), branch_computations={%region_4.5_spmd, %region_5.6_spmd} | conditional | flops 2892172 | bytes 27435296 | solution.py:48
  112.3 4.0 collective-permute-done.55
  120.3 32.1 %conditional.21 = (bf16[1024,1024]{1,0:T(8,128)(2,1)}, bf16[1024,1024]{1,0:T(8,128)(2,1)}, f32[1024,768]{1,0:T(8,128)S(1)}, f32[2,1024]{1,0:T(2,128)S(1)}, bf16[2048,256]{1,0:T(8,128)(2,1)}) conditional(s32[]{:T(128)} %bitcast.58, () %tuple.191, (bf16[512,1024]{1,0:T(8,128)(2,1)}, bf16[512,1024]{1,0:T(8,128)(2,1)}, bf16[1024,2048]{1,0:T(8,128)(2,1)}, ...), branch_computations={%region_6.7_spmd, %region_7.10_spmd} | conditional | flops 3234607104 | bytes 71541024 | solution.py:48
  131.9 14.8 %collective-permute-done.1 = f32[2,2,2,2,128]{4,3,2,1,0:T(2,128)S(1)} collective-permute-done((f32[2,2,2,2,128]{4,3,2,1,0:T(2,128)S(1)}, f32[2,2,2,2,128]{4,3,2,1,0:T(2,128)S(1)}, u32[]{:S(2)}, u32[]{:S(2)}) %collective-permute-start.1) | collective-permute-done | bytes 8224 | tf_op jit(solution)/shard_map/cond/branch_1_fun/ppermute | solution.py:30
  154.0 18.2 %conditional.22 = (bf16[1024,256]{1,0:T(8,128)(2,1)}, f32[1024,2]{1,0:T(8,128)}, f32[512,2048]{1,0:T(8,128)}, bf16[512,2048]{1,0:T(8,128)(2,1)}) conditional(s32[]{:T(128)} %bitcast.58, () %tuple.194, (f32[1024,768]{1,0:T(8,128)S(1)}, f32[2,1024]{1,0:T(2,128)S(1)}, f32[256]{0:T(256)S(1)}, f32[256]{0:T(256)S(1)}, f32[1024,128]{1,0:T(8,128)}, ...), branch_computations={%region_10.11_spmd, %region_11.12_spmd} | conditional | flops 2148536320 | bytes 26779720 | solution.py:48
  157.2 7.6 %branch_1_fun.2 = bf16[2,2,256,256]{3,2,1,0:T(8,128)(2,1)} custom-call(f32[2,2,256,768]{3,2,1,0:T(8,128)S(1)} %bitcast.109, f32[2,2,256,768]{3,2,1,0:T(8,128)S(1)} %bitcast.110, f32[2,2,256,768]{3,2,1,0:T(8,128)S(1)} %bitcast.111, f32[2,2,256,2]{3,2,1,0:T(8,128)S(1)} %bitcast.107, f32[1,256]{1,0:T(1,128)S(1)} %bitcast.149, f32[1,256]{1,0:T(1,128)S(1)} %bitcast.146, ...), custom_call_target="tpu_custom_call" | custom-call | flops 1073741824 | bytes 8388608 | tf_op jit(solution)/shard_map/cond/branch_1_fun/pallas_call | solution.py:222
  167.9 3.9 fusion.169
  177.0 68.4 %conditional.23 = (f32[128,1]{0,1:T(1,128)S(1)}, f32[128,2048]{1,0:T(8,128)}, f32[128,2048]{1,0:T(8,128)}, bf16[64,2048]{1,0:T(8,128)(2,1)}, bf16[64,2048]{1,0:T...) conditional(s32[]{:T(128)} %bitcast.58, () %tuple.197, (bf16[512,2048]{1,0:T(8,128)(2,1)}, ...), branch_computations={%region_12.13_spmd, %region_13.15_spmd} | conditional | flops 9699456 | bytes 44575528 | solution.py:48
  182.2 32.1 %collective-permute-done.13 = bf16[128,2048]{1,0:T(8,128)(2,1)S(1)} collective-permute-done((bf16[128,2048]{1,0:T(8,128)(2,1)S(1)}, bf16[128,2048]{1,0:T(8,128)(2,1)S(1)}, u32[]{:S(2)}, u32[]{:S(2)}) %collective-permute-start.13) | collective-permute-done | bytes 524320 | tf_op jit(solution)/shard_map/cond/branch_1_fun/ppermute | solution.py:30
  216.5 5.8 collective-permute-done.14
  222.4 6.5 collective-permute-done.16
  233.8 11.6 %collective-permute-done.18 = bf16[64,2048]{1,0:T(8,128)(2,1)} collective-permute-done((bf16[64,2048]{1,0:T(8,128)(2,1)}, bf16[64,2048]{1,0:T(8,128)(2,1)}, u32[]{:S(2)}, u32[]{:S(2)}) %collective-permute-start.18) | collective-permute-done | bytes 262176 | tf_op jit(solution)/shard_map/cond/branch_1_fun/ppermute | solution.py:30
  249.3 40.5 %conditional.24 = (bf16[1024,2048]{1,0:T(8,128)(2,1)}, f32[1024,1024]{1,0:T(8,128)}) conditional(s32[]{:T(128)} %bitcast.58, () %tuple.200, (bf16[64,2048]{1,0:T(8,128)(2,1)}, bf16[64,2048]{1,0:T(8,128)(2,1)}, bf16[64,2048]{1,0:T(8,128)(2,1)}, bf16[64,2048]{1,0:T(8,128)(2,1)}, bf16[1024,1024]{1,0:T(8,128)(2,1)S(1)}, ...), branch_computations={%region_15.16_spmd, %region_16.17_spmd} | conditional | flops 4298113024 | bytes 47448200 | solution.py:48
  262.0 9.9 %collective-permute-done.36 = bf16[128,2048]{1,0:T(8,128)(2,1)S(1)} collective-permute-done((bf16[128,2048]{1,0:T(8,128)(2,1)S(1)}, bf16[128,2048]{1,0:T(8,128)(2,1)S(1)}, u32[]{:S(2)}, u32[]{:S(2)}) %collective-permute-start.36) | collective-permute-done | bytes 524320 | tf_op jit(solution)/shard_map/cond/branch_1_fun/ppermute | solution.py:30
  279.3 4.5 fusion.29
  283.8 5.9 fusion.33
  293.8 17.4 %conditional.25 = (f32[1024,1024]{1,0:T(8,128)}, bf16[1024,1024]{1,0:T(8,128)(2,1)}, bf16[1024,1024]{1,0:T(8,128)(2,1)S(1)}, bf16[1024,1024]{1,0:T(8,128)(2,1)}) conditional(s32[]{:T(128)} %bitcast.58, () %tuple.203, (bf16[1024,2048]{1,0:T(8,128)(2,1)}, bf16[1024,1024]{1,0:T(8,128)(2,1)}, bf16[512,1024]{1,0:T(8,128)(2,1)}, ...), branch_computations={%region_17.18_spmd, %region_18.19_spmd} | conditional | flops 4307550208 | bytes 48234596 | solution.py:48
  298.4 3.9 fusion.37
  302.4 8.9 %multiply_convert_fusion = (bf16[1024,1024]{1,0:T(8,128)(2,1)}, f32[1024,1024]{1,0:T(8,128)}) fusion(f32[1024,1024]{1,0:T(8,128)} %get-tuple-element.340, f32[1024,1024]{1,0:T(8,128)S(1)} %fusion.37, bf16[1024,1024]{1,0:T(8,128)(2,1)} %pad_maximum_fusion.14, bf16[1024,2048]{1,0:T(8,128)(2,1)} %get-tuple-element.336), kind=kOutput, calls=%fused_computation.168 | convolution fusion | flops 2154823680 | bytes 18874368 | tf_op jit(solution)/shard_map/cond/branch_1_fun/dot_general | solution.py:18
  311.3 6.7 collective-permute-done.62
  317.9 73.3 %conditional.26 = (bf16[2048,1024]{1,0:T(8,128)(2,1)S(1)}, f32[128,2048]{1,0:T(8,128)S(1)}, bf16[1024,2048]{1,0:T(8,128)(2,1)}, bf16[1024,512]{1,0:T(8,128)(2,1)...) conditional(s32[]{:T(128)} %bitcast.58, () %tuple.182, (bf16[512,1024]{1,0:T(8,128)(2,1)}, ...), branch_computations={%region_19.20_spmd, %region_20.23_spmd} | conditional | flops 5413535744 | bytes 181687440 | solution.py:48
  320.8 4.4 fusion.39
  325.3 4.1 collective-permute-done.24
  335.1 12.2 %collective-permute-done.25 = bf16[128,2048]{1,0:T(8,128)(2,1)S(1)} collective-permute-done((bf16[128,2048]{1,0:T(8,128)(2,1)S(1)}, bf16[128,2048]{1,0:T(8,128)(2,1)S(1)}, u32[]{:S(2)}, u32[]{:S(2)}) %collective-permute-start.25) | collective-permute-done | bytes 524320 | tf_op jit(solution)/shard_map/cond/branch_1_fun/ppermute | solution.py:30
  349.4 5.5 collective-permute-done.26
  359.5 4.8 collective-permute-done.30
  368.1 8.1 %collective-permute-done.31 = bf16[128,2048]{1,0:T(8,128)(2,1)S(1)} collective-permute-done((bf16[128,2048]{1,0:T(8,128)(2,1)S(1)}, bf16[128,2048]{1,0:T(8,128)(2,1)S(1)}, u32[]{:S(2)}, u32[]{:S(2)}) %collective-permute-start.31) | collective-permute-done | bytes 524320 | tf_op jit(solution)/shard_map/cond/branch_1_fun/ppermute | solution.py:30
  377.3 5.3 pad_maximum_fusion.16
  387.0 4.3 fusion.42
  392.8 26.5 %conditional.27 = (bf16[1024,512]{1,0:T(8,128)(2,1)S(1)}, bf16[1024,1024]{1,0:T(8,128)(2,1)}, bf16[1024,1024]{1,0:T(8,128)(2,1)}, bf16[1024,512]{1,0:T(8,128)(2,1)}, bf16[1024,1024]{1,0:T(8,128)(2,1)}) conditional(s32[]{:T(128)} %bitcast.58, () %tuple.207, (bf16[1024,2048]{1,0:T(8,128)(2,1)}, bf16[1024,1024]{1,0:T(8,128)(2,1)}, ...), branch_computations={%region_23.24_spmd, %region_24.25_spmd} | conditional | flops 8605663232 | bytes 69206112 | solution.py:48
  398.2 10.9 %multiply_convert_fusion.2 = (bf16[1024,1024]{1,0:T(8,128)(2,1)}, bf16[1024,1024]{1,0:T(8,128)(2,1)}) fusion(f32[1024,1024]{1,0:T(8,128)} %get-tuple-element.357, f32[1024,1024]{1,0:T(8,128)} %get-tuple-element.356, bf16[1024,2048]{1,0:T(8,128)(2,1)} %get-tuple-element.358, bf16[2048,1024]{1,0:T(8,128)(2,1)S(1)} %copy-done.26), kind=kOutput, calls=%fused_computation.221 | convolution fusion | flops 4308598784 | bytes 20971520 | tf_op jit(solution)/shard_map/cond/branch_1_fun/dot_general | solution.py:18
  409.1 4.1 fusion.61
  413.3 6.0 fusion.55
  423.9 22.0 %conditional.28 = (bf16[1024,512]{1,0:T(8,128)(2,1)S(1)}, f32[512,2048]{1,0:T(8,128)}, bf16[512,2048]{1,0:T(8,128)(2,1)}) conditional(s32[]{:T(128)} %bitcast.58, () %tuple.211, (bf16[1024,1024]{1,0:T(8,128)(2,1)}, bf16[2048,1024]{1,0:T(8,128)(2,1)}, bf16[1024,1024]{1,0:T(8,128)(2,1)}, bf16[2048,1024]{1,0:T(8,128)(2,1)}, ...), branch_computations={%region_26.27_spmd, %region_27.28_spmd} | conditional | flops 9667346432 | bytes 90177656 | solution.py:48
  424.3 5.4 fusion.76
  429.7 3.8 convolution_add_fusion.1
  437.2 5.6 convolution_add_fusion
  449.5 47.5 %conditional.29 = (bf16[1024,1024]{1,0:T(8,128)(2,1)}, bf16[1024,1024]{1,0:T(8,128)(2,1)}, bf16[1024,1024]{1,0:T(8,128)(2,1)}, f32[128,2048]{1,0:T(8,128)}, bf16...) conditional(s32[]{:T(128)} %bitcast.58, () %tuple.210, ...), branch_computations={%region_28.29_spmd, %region_29.32_spmd} | conditional | flops 6456080384 | bytes 65039160 | solution.py:48
  456.6 5.9 fusion.84
  462.7 10.5 %collective-permute-done.39 = bf16[128,2048]{1,0:T(8,128)(2,1)S(1)} collective-permute-done((bf16[128,2048]{1,0:T(8,128)(2,1)S(1)}, bf16[128,2048]{1,0:T(8,128)(2,1)S(1)}, u32[]{:S(2)}, u32[]{:S(2)}) %collective-permute-start.39) | collective-permute-done | bytes 524320 | tf_op jit(solution)/shard_map/cond/branch_1_fun/ppermute | solution.py:30
  477.9 6.0 fusion.87
  491.1 5.9 fusion.90
  497.0 4.7 add_convert_fusion.2
  503.4 48.5 %conditional.30 = (bf16[1024,2048]{1,0:T(8,128)(2,1)}, f32[1024,256]{1,0:T(8,128)}, f32[1024,256]{1,0:T(8,128)}, bf16[1024,256]{1,0:T(8,128)(2,1)}, f32[2,2,2,256,2]{4,3,2,1,0:T(8,128)}, /*index=5*/f32[2,256]{1,0:T(2,128)S(1)}) conditional(s32[]{:T(128)} %bitcast.58, () %tuple.216, (bf16[64,2048]{1,0:T(8,128)(2,1)}, bf16[64,2048]{1,0:T(8,128)(2,1)}, ...), branch_computations={%region_33.34_spmd, %region_34.36_spmd} | conditional | flops 2149843456 | bytes 49027272 | solution.py:48
  515.4 11.5 %collective-permute-done.46 = bf16[128,2048]{1,0:T(8,128)(2,1)S(1)} collective-permute-done((bf16[128,2048]{1,0:T(8,128)(2,1)S(1)}, bf16[128,2048]{1,0:T(8,128)(2,1)S(1)}, u32[]{:S(2)}, u32[]{:S(2)}) %collective-permute-start.46) | collective-permute-done | bytes 524320 | tf_op jit(solution)/shard_map/cond/branch_1_fun/ppermute | solution.py:30
  534.4 3.9 convolution_convert_fusion.2
  538.3 13.6 %branch_1_fun.3 = (f32[2,2,256,256]{3,2,1,0:T(8,128)}, f32[2,2,256,256]{3,2,1,0:T(8,128)}, bf16[2,2,256,256]{3,2,1,0:T(8,128)(2,1)}, f32[2,2,2,256,2]{4,3,2,1,0:T(8,128)}, f32[2,2,256]{2,1,0:T(2,128)S(1)}) custom-call(f32[2,2,256,768]{3,2,1,0:T(8,128)S(1)} %bitcast.112, f32[2,2,256,768]{3,2,1,0:T(8,128)S(1)} %bitcast.113, f32[2,2,256,768]{3,2,1,0:T(8,128)S(1)} %bitcast.114, ...), custom_call_target="tpu_custom_call" | custom-call | flops 1073741824 | bytes 8388608 | tf_op jit(solution)/shard_map/cond/branch_1_fun/pallas_call | solution.py:222
  552.0 4.5 add_convert_fusion.1
  556.5 20.3 %conditional.31 = (f32[2,1024]{1,0:T(2,128)S(1)}, bf16[1024,512]{0,1:T(8,128)(2,1)}, bf16[512,1024]{1,0:T(8,128)(2,1)}, bf16[256,1024]{1,0:T(8,128)(2,1)}) conditional(s32[]{:T(128)} %bitcast.58, () %tuple.181, (f32[2,2,2,256,2]{4,3,2,1,0:T(8,128)}, bf16[1024,2048]{1,0:T(8,128)(2,1)}, bf16[1024,256]{1,0:T(8,128)(2,1)}, ...), branch_computations={%region_36.37_spmd, %region_37.39_spmd} | conditional | flops 1076633600 | bytes 16515326 | solution.py:48
  579.7 20.8 %conditional.32 = (bf16[1024,512]{1,0:T(8,128)(2,1)}, bf16[1024,512]{0,1:T(8,128)(2,1)}, bf16[1024,512]{1,0:T(8,128)(2,1)}, bf16[2048,768]{1,0:T(8,128)(2,1)}) conditional(s32[]{:T(128)} %bitcast.58, () %tuple.220, (f32[1024,2]{1,0:T(8,128)}, bf16[1024,2048]{1,0:T(8,128)(2,1)}, bf16[1024,256]{1,0:T(8,128)(2,1)}, bf16[1024,2048]{1,0:T(8,128)(2,1)}, ...), branch_computations={%region_40.41_spmd, %region_41.42_spmd} | conditional | flops 2162165760 | bytes 38881340 | solution.py:48
  591.7 4.1 fusion.109
  611.6 19.0 %conditional.33 = (bf16[1024,512]{1,0:T(8,128)(2,1)S(1)}, f32[512,2048]{1,0:T(8,128)}, bf16[512,2048]{1,0:T(8,128)(2,1)}, f32[4,2048]{1,0:T(4,128)S(1)}) conditional(s32[]{:T(128)} %bitcast.58, () %tuple.223, (bf16[1024,2048]{1,0:T(8,128)(2,1)}, bf16[1024,512]{1,0:T(8,128)(2,1)}, bf16[1024,256]{1,0:T(8,128)(2,1)}, bf16[2048,768]{1,0:T(8,128)(2,1)}, ...), branch_computations={%region_44.45_spmd, %region_45.47_spmd} | conditional | flops 4297106944 | bytes 38977796 | solution.py:48
  614.0 5.6 convolution_convert_fusion.3
  621.2 6.0 fusion.124
  630.7 11.2 %collective-permute-done.70 = bf16[256,1024]{1,0:T(8,128)(2,1)} collective-permute-done((bf16[256,1024]{1,0:T(8,128)(2,1)}, bf16[256,1024]{1,0:T(8,128)(2,1)}, u32[]{:S(2)}, u32[]{:S(2)}) %collective-permute-start.70) | collective-permute-done | bytes 524320 | tf_op jit(solution)/shard_map/ppermute | solution.py:30
  647.8 43.1 %conditional.34 = (f32[64,2048]{1,0:T(8,128)}, f32[64,2048]{1,0:T(8,128)S(1)}, bf16[64,2048]{1,0:T(8,128)(2,1)}, bf16[64,2048]{1,0:T(8,128)(2,1)}, f32[256,2048]...) conditional(s32[]{:T(128)} %bitcast.58, () %tuple.226, ...), branch_computations={%region_48.49_spmd, %region_49.50_spmd} | conditional | flops 11542535 | bytes 66298312 | solution.py:48
  649.1 5.9 fusion.139
  674.5 8.7 %collective-permute-done.19 = bf16[128,2048]{1,0:T(8,128)(2,1)} collective-permute-done((bf16[128,2048]{1,0:T(8,128)(2,1)}, bf16[128,2048]{1,0:T(8,128)(2,1)}, u32[]{:S(2)}, u32[]{:S(2)}) %collective-permute-start.19) | collective-permute-done | bytes 524320 | tf_op jit(solution)/shard_map/cond/branch_1_fun/ppermute | solution.py:30
  695.8 15.0 %conditional.35 = (f32[128,2048]{1,0:T(8,128)}, f32[256,2048]{1,0:T(8,128)}, f32[4,2048]{1,0:T(4,128)S(1)}) conditional(s32[]{:T(128)} %bitcast.58, () %tuple.229, (bf16[64,2048]{1,0:T(8,128)(2,1)}, f32[64,2048]{1,0:T(8,128)}, bf16[64,2048]{1,0:T(8,128)(2,1)}, f32[64,2048]{1,0:T(8,128)S(1)}, f32[128,2048]{1,0:T(8,128)}, ...), branch_computations={%region_50.51_spmd, %region_51.52_spmd} | conditional | flops 3162119 | bytes 17236164 | solution.py:48
  (598 shorter events, 337.4 us)
Async XLA Ops:
  7.2 81.5 %all-gather.5.cloned.1.call-start = ((), (), s32[]{:S(2)}) async-start(), calls=%async_computation.6 | async-start | bytes 3145728 | tf_op jit(solution)/shard_map/all_gather | solution.py:258
  12.7 15.3 %collective-permute-start.5 = (bf16[256,1024]{1,0:T(8,128)(2,1)}, bf16[256,1024]{1,0:T(8,128)(2,1)}, u32[]{:S(2)}, u32[]{:S(2)}) collective-permute-start(bf16[256,1024]{1,0:T(8,128)(2,1)} %broadcast_select_fusion.2), channel_id=1, source_target_pairs={{0,8},{8,0},{1,9},{9,1},{2,10},{10,2},{3,11},{11,3},{4,12},{12,4},... | collective-permute-start | bytes 1572872 | tf_op jit(solution)/shard_map/cond/branch_1_fun/ppermute | solution.py:30
  30.5 141.6 %all-gather.7.cloned.1.call-start = ((), (), s32[]{:S(2)}) async-start(), calls=%async_computation.7 | async-start | bytes 3145728 | tf_op jit(solution)/shard_map/all_gather | solution.py:258
  30.6 56.5 %collective-permute-start.54 = (bf16[512,1024]{1,0:T(8,128)(2,1)}, bf16[512,1024]{1,0:T(8,128)(2,1)}, u32[]{:S(2)}, u32[]{:S(2)}) collective-permute-start(bf16[512,1024]{1,0:T(8,128)(2,1)} %get-tuple-element.686), channel_id=1, source_target_pairs={{0,4},{4,0},{1,5},{5,1},{2,6},{6,2},{3,7},{7,3},{8,12},{12,8},{9,1... | collective-permute-start | bytes 3145736 | tf_op jit(solution)/shard_map/ppermute | solution.py:30
  35.6 7.6 %collective-permute-start.11 = (s32[8,128]{1,0:T(8,128)S(1)}, s32[8,128]{1,0:T(8,128)S(1)}, u32[]{:S(2)}, u32[]{:S(2)}) collective-permute-start(s32[8,128]{1,0:T(8,128)S(1)} %concatenate.170), channel_id=1, source_target_pairs={{0,8},{8,0},{1,9},{9,1},{2,10},{10,2},{3,11},{11,3},{4,12},{12,4},... | collective-permute-start | bytes 12296 | tf_op jit(solution)/shard_map/cond/branch_1_fun/ppermute | solution.py:30
  40.7 25.8 %collective-permute-start.8 = (bf16[256,1024]{1,0:T(8,128)(2,1)}, bf16[256,1024]{1,0:T(8,128)(2,1)S(1)}, u32[]{:S(2)}, u32[]{:S(2)}) collective-permute-start(bf16[256,1024]{1,0:T(8,128)(2,1)} %get-tuple-element.295), channel_id=1, source_target_pairs={{0,8},{8,0},{1,9},{9,1},{2,10},{10,2},{3,11},{11,3},{4,12},{12,4},... | collective-permute-start | bytes 1572872 | tf_op jit(solution)/shard_map/cond/branch_1_fun/ppermute | solution.py:30
  43.4 40.8 %collective-permute-start.10 = (bf16[128,2048]{1,0:T(8,128)(2,1)S(1)}, bf16[128,2048]{1,0:T(8,128)(2,1)}, u32[]{:S(2)}, u32[]{:S(2)}) collective-permute-start(bf16[128,2048]{1,0:T(8,128)(2,1)S(1)} %pad_maximum_fusion.5), channel_id=1, source_target_pairs={{0,8},{8,0},{1,9},{9,1},{2,10},{10,2},{3,11},{11,3},{4,12},{12,4},... | collective-permute-start | bytes 1572872 | tf_op jit(solution)/shard_map/cond/branch_1_fun/ppermute | solution.py:30
  66.5 18.7 %collective-permute-start.9 = (bf16[128,2048]{1,0:T(8,128)(2,1)S(1)}, bf16[128,2048]{1,0:T(8,128)(2,1)}, u32[]{:S(2)}, u32[]{:S(2)}) collective-permute-start(bf16[128,2048]{1,0:T(8,128)(2,1)S(1)} %pad_maximum_fusion.4), channel_id=1, source_target_pairs={{0,2},{2,0},{1,3},{3,1},{4,6},{6,4},{5,7},{7,5},{8,10},{10,8},{9,1... | collective-permute-start | bytes 1572872 | tf_op jit(solution)/shard_map/cond/branch_1_fun/ppermute | solution.py:30
  88.7 156.7 %all-gather.9.cloned.1.call-start = ((), (), s32[]{:S(2)}) async-start(), calls=%async_computation.8 | async-start | bytes 3145728 | tf_op jit(solution)/shard_map/all_gather | solution.py:258
  91.0 25.2 %collective-permute-start.55 = (bf16[512,1024]{1,0:T(8,128)(2,1)}, bf16[512,1024]{1,0:T(8,128)(2,1)}, u32[]{:S(2)}, u32[]{:S(2)}) collective-permute-start(bf16[512,1024]{1,0:T(8,128)(2,1)} %constant_dynamic-slice_fusion.4), channel_id=1, source_target_pairs={{0,4},{4,0},{1,5},{5,1},{2,6},{6,2},{3,7},{7,3},{8,12},{12,8},{9,1... | collective-permute-start | bytes 3145736 | tf_op jit(solution)/shard_map/ppermute | solution.py:30
  92.5 19.8 %collective-permute-start.56 = (bf16[256,1024]{1,0:T(8,128)(2,1)}, bf16[256,1024]{1,0:T(8,128)(2,1)}, u32[]{:S(2)}, u32[]{:S(2)}) collective-permute-start(bf16[256,1024]{1,0:T(8,128)(2,1)} %get-tuple-element.702), channel_id=1, source_target_pairs={{0,8},{8,0},{1,9},{9,1},{2,10},{10,2},{3,11},{11,3},{4,12},{12,4},... | collective-permute-start | bytes 1572872 | tf_op jit(solution)/shard_map/ppermute | solution.py:30
  118.7 53.5 %collective-permute-start.57 = (bf16[512,1024]{1,0:T(8,128)(2,1)}, bf16[512,1024]{1,0:T(8,128)(2,1)}, u32[]{:S(2)}, u32[]{:S(2)}) collective-permute-start(bf16[512,1024]{1,0:T(8,128)(2,1)} %pad_maximum_fusion.38), channel_id=1, source_target_pairs={{0,4},{4,0},{1,5},{5,1},{2,6},{6,2},{3,7},{7,3},{8,12},{12,8},{9,1... | collective-permute-start | bytes 3145736 | tf_op jit(solution)/shard_map/ppermute | solution.py:30
  120.2 169.5 %all-gather.11.cloned.1.call-start = ((), (), s32[]{:S(2)}) async-start(), calls=%async_computation.9 | async-start | bytes 3145728 | tf_op jit(solution)/shard_map/all_gather | solution.py:258
  130.8 15.9 %collective-permute-start.1 = (f32[2,2,2,2,128]{4,3,2,1,0:T(2,128)S(1)}, f32[2,2,2,2,128]{4,3,2,1,0:T(2,128)S(1)}, u32[]{:S(2)}, u32[]{:S(2)}) collective-permute-start(f32[2,2,2,2,128]{4,3,2,1,0:T(2,128)S(1)} %reverse_add_fusion.1), channel_id=1, source_target_pairs={{0,8},{8,0},{1,9},{9,1},{2,10},{10,2},{3,11},{11,3},{4,12},{12,4},... | collective-permute-start | bytes 24584 | tf_op jit(solution)/shard_map/cond/branch_1_fun/ppermute | solution.py:30
  152.4 19.8 %collective-permute-start.58 = (bf16[256,1024]{1,0:T(8,128)(2,1)}, bf16[256,1024]{1,0:T(8,128)(2,1)}, u32[]{:S(2)}, u32[]{:S(2)}) collective-permute-start(bf16[256,1024]{1,0:T(8,128)(2,1)} %get-tuple-element.733), channel_id=1, source_target_pairs={{0,8},{8,0},{1,9},{9,1},{2,10},{10,2},{3,11},{11,3},{4,12},{12,4},... | collective-permute-start | bytes 1572872 | tf_op jit(solution)/shard_map/ppermute | solution.py:30
  172.2 73.2 %collective-permute-start.59 = (bf16[1024,1024]{1,0:T(8,128)(2,1)}, bf16[1024,1024]{1,0:T(8,128)(2,1)}, u32[]{:S(2)}, u32[]{:S(2)}) collective-permute-start(bf16[1024,1024]{1,0:T(8,128)(2,1)} %all-gather.7.cloned.1.call-done), channel_id=1, source_target_pairs={{0,4},{4,0},{1,5},{5,1},{2,6},{6,2},{3,7},{7,3},{8,12},{12,8},{9,1... | collective-permute-start | bytes 6291464 | tf_op jit(solution)/shard_map/ppermute | solution.py:30
  176.3 320.7 %reduce-scatter.7.cloned.1.call-start = ((), (), s32[]{:S(2)}) async-start(), calls=%async_computation.10 | async-start | bytes 1572864 | tf_op jit(solution)/shard_map/reduce_scatter | solution.py:269
  176.4 113.3 %collective-permute-start.61 = (bf16[512,1024]{1,0:T(8,128)(2,1)}, bf16[512,1024]{1,0:T(8,128)(2,1)S(1)}, u32[]{:S(2)}, u32[]{:S(2)}) collective-permute-start(bf16[512,1024]{1,0:T(8,128)(2,1)} %pad_maximum_fusion.39), channel_id=1, source_target_pairs={{0,4},{4,0},{1,5},{5,1},{2,6},{6,2},{3,7},{7,3},{8,12},{12,8},{9,1... | collective-permute-start | bytes 3145736 | tf_op jit(solution)/shard_map/ppermute | solution.py:30
  180.8 33.5 %collective-permute-start.13 = (bf16[128,2048]{1,0:T(8,128)(2,1)S(1)}, bf16[128,2048]{1,0:T(8,128)(2,1)S(1)}, u32[]{:S(2)}, u32[]{:S(2)}) collective-permute-start(bf16[128,2048]{1,0:T(8,128)(2,1)S(1)} %pad_maximum_fusion.10), channel_id=1, source_target_pairs={{0,8},{8,0},{1,9},{9,1},{2,10},{10,2},{3,11},{11,3},{4,12},{12,4},... | collective-permute-start | bytes 1572872 | tf_op jit(solution)/shard_map/cond/branch_1_fun/ppermute | solution.py:30
  181.5 34.7 %collective-permute-start.15 = (bf16[128,2048]{1,0:T(8,128)(2,1)S(1)}, bf16[128,2048]{1,0:T(8,128)(2,1)S(1)}, u32[]{:S(2)}, u32[]{:S(2)}) collective-permute-start(bf16[128,2048]{1,0:T(8,128)(2,1)S(1)} %pad_maximum_fusion.11), channel_id=1, source_target_pairs={{0,2},{2,0},{1,3},{3,1},{4,6},{6,4},{5,7},{7,5},{8,10},{10,8},{9,1... | collective-permute-start | bytes 1572872 | tf_op jit(solution)/shard_map/cond/branch_1_fun/ppermute | solution.py:30
  214.5 7.8 %collective-permute-start.14 = (bf16[64,2048]{1,0:T(8,128)(2,1)S(1)}, bf16[64,2048]{1,0:T(8,128)(2,1)S(1)}, u32[]{:S(2)}, u32[]{:S(2)}) collective-permute-start(bf16[64,2048]{1,0:T(8,128)(2,1)S(1)} %slice.1479), channel_id=1, source_target_pairs={{0,2},{2,0},{1,3},{3,1},{4,6},{6,4},{5,7},{7,5},{8,10},{10,8},{9,1... | collective-permute-start | bytes 786440 | tf_op jit(solution)/shard_map/cond/branch_1_fun/ppermute | solution.py:30
  216.4 12.4 %collective-permute-start.16 = (bf16[64,2048]{1,0:T(8,128)(2,1)S(1)}, bf16[64,2048]{1,0:T(8,128)(2,1)S(1)}, u32[]{:S(2)}, u32[]{:S(2)}) collective-permute-start(bf16[64,2048]{1,0:T(8,128)(2,1)S(1)} %slice.1478), channel_id=1, source_target_pairs={{0,8},{8,0},{1,9},{9,1},{2,10},{10,2},{3,11},{11,3},{4,12},{12,4},... | collective-permute-start | bytes 786440 | tf_op jit(solution)/shard_map/cond/branch_1_fun/ppermute | solution.py:30
  231.5 13.9 %collective-permute-start.18 = (bf16[64,2048]{1,0:T(8,128)(2,1)}, bf16[64,2048]{1,0:T(8,128)(2,1)}, u32[]{:S(2)}, u32[]{:S(2)}) collective-permute-start(bf16[64,2048]{1,0:T(8,128)(2,1)} %get-tuple-element.1331), channel_id=1, source_target_pairs={{0,8},{8,0},{1,9},{9,1},{2,10},{10,2},{3,11},{11,3},{4,12},{12,4},... | collective-permute-start | bytes 786440 | tf_op jit(solution)/shard_map/cond/branch_1_fun/ppermute | solution.py:30
  233.5 11.9 %collective-permute-start.17 = (bf16[64,2048]{1,0:T(8,128)(2,1)}, bf16[64,2048]{1,0:T(8,128)(2,1)}, u32[]{:S(2)}, u32[]{:S(2)}) collective-permute-start(bf16[64,2048]{1,0:T(8,128)(2,1)} %get-tuple-element.1330), channel_id=1, source_target_pairs={{0,2},{2,0},{1,3},{3,1},{4,6},{6,4},{5,7},{7,5},{8,10},{10,8},{9,1... | collective-permute-start | bytes 786440 | tf_op jit(solution)/shard_map/cond/branch_1_fun/ppermute | solution.py:30
  247.8 41.9 %collective-permute-start.60 = (bf16[512,1024]{1,0:T(8,128)(2,1)}, bf16[512,1024]{1,0:T(8,128)(2,1)}, u32[]{:S(2)}, u32[]{:S(2)}) collective-permute-start(bf16[512,1024]{1,0:T(8,128)(2,1)} %constant_dynamic-slice_fusion.3), channel_id=1, source_target_pairs={{0,4},{4,0},{1,5},{5,1},{2,6},{6,2},{3,7},{7,3},{8,12},{12,8},{9,1... | collective-permute-start | bytes 3145736 | tf_op jit(solution)/shard_map/ppermute | solution.py:30
  250.3 11.7 %collective-permute-start.35 = (bf16[128,2048]{1,0:T(8,128)(2,1)S(1)}, bf16[128,2048]{1,0:T(8,128)(2,1)S(1)}, u32[]{:S(2)}, u32[]{:S(2)}) collective-permute-start(bf16[128,2048]{1,0:T(8,128)(2,1)S(1)} %pad_maximum_fusion.12), channel_id=1, source_target_pairs={{0,2},{2,0},{1,3},{3,1},{4,6},{6,4},{5,7},{7,5},{8,10},{10,8},{9,1... | collective-permute-start | bytes 1572872 | tf_op jit(solution)/shard_map/cond/branch_1_fun/ppermute | solution.py:30
  251.8 20.1 %collective-permute-start.36 = (bf16[128,2048]{1,0:T(8,128)(2,1)S(1)}, bf16[128,2048]{1,0:T(8,128)(2,1)S(1)}, u32[]{:S(2)}, u32[]{:S(2)}) collective-permute-start(bf16[128,2048]{1,0:T(8,128)(2,1)S(1)} %pad_maximum_fusion.13), channel_id=1, source_target_pairs={{0,8},{8,0},{1,9},{9,1},{2,10},{10,2},{3,11},{11,3},{4,12},{12,4},... | collective-permute-start | bytes 1572872 | tf_op jit(solution)/shard_map/cond/branch_1_fun/ppermute | solution.py:30
  292.4 25.6 %collective-permute-start.62 = (bf16[512,1024]{1,0:T(8,128)(2,1)}, bf16[512,1024]{1,0:T(8,128)(2,1)}, u32[]{:S(2)}, u32[]{:S(2)}) collective-permute-start(bf16[512,1024]{1,0:T(8,128)(2,1)} %constant_dynamic-slice_fusion.2), channel_id=1, source_target_pairs={{0,4},{4,0},{1,5},{5,1},{2,6},{6,2},{3,7},{7,3},{8,12},{12,8},{9,1... | collective-permute-start | bytes 3145736 | tf_op jit(solution)/shard_map/ppermute | solution.py:30
  333.2 14.0 %collective-permute-start.25 = (bf16[128,2048]{1,0:T(8,128)(2,1)S(1)}, bf16[128,2048]{1,0:T(8,128)(2,1)S(1)}, u32[]{:S(2)}, u32[]{:S(2)}) collective-permute-start(bf16[128,2048]{1,0:T(8,128)(2,1)S(1)} %pad_maximum_fusion.19), channel_id=1, source_target_pairs={{0,8},{8,0},{1,9},{9,1},{2,10},{10,2},{3,11},{11,3},{4,12},{12,4},... | collective-permute-start | bytes 1572872 | tf_op jit(solution)/shard_map/cond/branch_1_fun/ppermute | solution.py:30
  333.3 15.6 %collective-permute-start.27 = (bf16[128,2048]{1,0:T(8,128)(2,1)S(1)}, bf16[128,2048]{1,0:T(8,128)(2,1)S(1)}, u32[]{:S(2)}, u32[]{:S(2)}) collective-permute-start(bf16[128,2048]{1,0:T(8,128)(2,1)S(1)} %pad_maximum_fusion.20), channel_id=1, source_target_pairs={{0,2},{2,0},{1,3},{3,1},{4,6},{6,4},{5,7},{7,5},{8,10},{10,8},{9,1... | collective-permute-start | bytes 1572872 | tf_op jit(solution)/shard_map/cond/branch_1_fun/ppermute | solution.py:30
  364.3 11.8 %collective-permute-start.31 = (bf16[128,2048]{1,0:T(8,128)(2,1)S(1)}, bf16[128,2048]{1,0:T(8,128)(2,1)S(1)}, u32[]{:S(2)}, u32[]{:S(2)}) collective-permute-start(bf16[128,2048]{1,0:T(8,128)(2,1)S(1)} %pad_maximum_fusion.21), channel_id=1, source_target_pairs={{0,2},{2,0},{1,3},{3,1},{4,6},{6,4},{5,7},{7,5},{8,10},{10,8},{9,1... | collective-permute-start | bytes 1572872 | tf_op jit(solution)/shard_map/cond/branch_1_fun/ppermute | solution.py:30
  365.9 10.6 %collective-permute-start.32 = (bf16[128,2048]{1,0:T(8,128)(2,1)S(1)}, bf16[128,2048]{1,0:T(8,128)(2,1)S(1)}, u32[]{:S(2)}, u32[]{:S(2)}) collective-permute-start(bf16[128,2048]{1,0:T(8,128)(2,1)S(1)} %pad_maximum_fusion.22), channel_id=1, source_target_pairs={{0,8},{8,0},{1,9},{9,1},{2,10},{10,2},{3,11},{11,3},{4,12},{12,4},... | collective-permute-start | bytes 1572872 | tf_op jit(solution)/shard_map/cond/branch_1_fun/ppermute | solution.py:30
  377.3 8.2 %collective-permute-start.33 = (bf16[512,2048]{1,0:T(8,128)(2,1)S(1)}, bf16[512,2048]{1,0:T(8,128)(2,1)S(1)}, u32[]{:S(2)}, u32[]{:S(2)}) collective-permute-start(bf16[512,2048]{1,0:T(8,128)(2,1)S(1)} %get-tuple-element.1196), channel_id=1, source_target_pairs={{0,1},{1,0},{2,3},{3,2},{4,5},{5,4},{6,7},{7,6},{8,9},{9,8},{10,11... | collective-permute-start | bytes 6291464 | tf_op jit(solution)/shard_map/cond/branch_1_fun/ppermute | solution.py:30
  391.2 28.0 %collective-permute-start.63 = (bf16[1024,512]{1,0:T(8,128)(2,1)}, bf16[1024,512]{1,0:T(8,128)(2,1)}, u32[]{:S(2)}, u32[]{:S(2)}) collective-permute-start(bf16[1024,512]{1,0:T(8,128)(2,1)} %get-tuple-element.783), channel_id=1, source_target_pairs={{0,4},{4,0},{1,5},{5,1},{2,6},{6,2},{3,7},{7,3},{8,12},{12,8},{9,1... | collective-permute-start | bytes 3145736 | tf_op jit(solution)/shard_map/ppermute | solution.py:30
  421.8 130.2 %reduce-scatter.9.cloned.1.call-start = ((), (), s32[]{:S(2)}) async-start(), calls=%async_computation.11 | async-start | bytes 1572864 | tf_op jit(solution)/shard_map/reduce_scatter | solution.py:269
  421.8 26.3 %collective-permute-start.65 = (bf16[1024,512]{1,0:T(8,128)(2,1)}, bf16[1024,512]{1,0:T(8,128)(2,1)S(1)}, u32[]{:S(2)}, u32[]{:S(2)}) collective-permute-start(bf16[1024,512]{1,0:T(8,128)(2,1)} %get-tuple-element.796), channel_id=1, source_target_pairs={{0,4},{4,0},{1,5},{5,1},{2,6},{6,2},{3,7},{7,3},{8,12},{12,8},{9,1... | collective-permute-start | bytes 3145736 | tf_op jit(solution)/shard_map/ppermute | solution.py:30
  422.8 74.2 %collective-permute-start.64 = (bf16[1024,1024]{1,0:T(8,128)(2,1)}, bf16[1024,1024]{1,0:T(8,128)(2,1)}, u32[]{:S(2)}, u32[]{:S(2)}) collective-permute-start(bf16[1024,1024]{1,0:T(8,128)(2,1)} %get-tuple-element.792), channel_id=1, source_target_pairs={{0,4},{4,0},{1,5},{5,1},{2,6},{6,2},{3,7},{7,3},{8,12},{12,8},{9,1... | collective-permute-start | bytes 6291464 | tf_op jit(solution)/shard_map/ppermute | solution.py:30
  433.5 12.4 %collective-permute-start.38 = (bf16[512,2048]{1,0:T(8,128)(2,1)S(1)}, bf16[512,2048]{1,0:T(8,128)(2,1)}, u32[]{:S(2)}, u32[]{:S(2)}) collective-permute-start(bf16[512,2048]{1,0:T(8,128)(2,1)S(1)} %convolution_add_fusion.1), channel_id=1, source_target_pairs={{0,1},{1,0},{2,3},{3,2},{4,5},{5,4},{6,7},{7,6},{8,9},{9,8},{10,11... | collective-permute-start | bytes 6291464 | tf_op jit(solution)/shard_map/cond/branch_1_fun/ppermute | solution.py:30
  449.4 154.5 %reduce-scatter.11.cloned.1.call-start = ((), (), s32[]{:S(2)}) async-start(), calls=%async_computation.12 | async-start | bytes 3145728 | tf_op jit(solution)/shard_map/reduce_scatter | solution.py:269
  453.5 19.6 %collective-permute-start.39 = (bf16[128,2048]{1,0:T(8,128)(2,1)S(1)}, bf16[128,2048]{1,0:T(8,128)(2,1)S(1)}, u32[]{:S(2)}, u32[]{:S(2)}) collective-permute-start(bf16[128,2048]{1,0:T(8,128)(2,1)S(1)} %pad_maximum_fusion.23), channel_id=1, source_target_pairs={{0,8},{8,0},{1,9},{9,1},{2,10},{10,2},{3,11},{11,3},{4,12},{12,4},... | collective-permute-start | bytes 1572872 | tf_op jit(solution)/shard_map/cond/branch_1_fun/ppermute | solution.py:30
  454.8 18.3 %collective-permute-start.40 = (bf16[128,2048]{1,0:T(8,128)(2,1)S(1)}, bf16[128,2048]{1,0:T(8,128)(2,1)S(1)}, u32[]{:S(2)}, u32[]{:S(2)}) collective-permute-start(bf16[128,2048]{1,0:T(8,128)(2,1)S(1)} %pad_maximum_fusion.24), channel_id=1, source_target_pairs={{0,2},{2,0},{1,3},{3,1},{4,6},{6,4},{5,7},{7,5},{8,10},{10,8},{9,1... | collective-permute-start | bytes 1572872 | tf_op jit(solution)/shard_map/cond/branch_1_fun/ppermute | solution.py:30
  473.3 10.5 %collective-permute-start.42 = (bf16[64,2048]{1,0:T(8,128)(2,1)S(1)}, bf16[64,2048]{1,0:T(8,128)(2,1)S(1)}, u32[]{:S(2)}, u32[]{:S(2)}) collective-permute-start(bf16[64,2048]{1,0:T(8,128)(2,1)S(1)} %slice.1482), channel_id=1, source_target_pairs={{0,8},{8,0},{1,9},{9,1},{2,10},{10,2},{3,11},{11,3},{4,12},{12,4},... | collective-permute-start | bytes 786440 | tf_op jit(solution)/shard_map/cond/branch_1_fun/ppermute | solution.py:30
  476.1 7.8 %collective-permute-start.41 = (bf16[64,2048]{1,0:T(8,128)(2,1)S(1)}, bf16[64,2048]{1,0:T(8,128)(2,1)S(1)}, u32[]{:S(2)}, u32[]{:S(2)}) collective-permute-start(bf16[64,2048]{1,0:T(8,128)(2,1)S(1)} %slice.1483), channel_id=1, source_target_pairs={{0,2},{2,0},{1,3},{3,1},{4,6},{6,4},{5,7},{7,5},{8,10},{10,8},{9,1... | collective-permute-start | bytes 786440 | tf_op jit(solution)/shard_map/cond/branch_1_fun/ppermute | solution.py:30
  489.0 7.9 %collective-permute-start.44 = (bf16[64,2048]{1,0:T(8,128)(2,1)}, bf16[64,2048]{1,0:T(8,128)(2,1)}, u32[]{:S(2)}, u32[]{:S(2)}) collective-permute-start(bf16[64,2048]{1,0:T(8,128)(2,1)} %get-tuple-element.1388), channel_id=1, source_target_pairs={{0,8},{8,0},{1,9},{9,1},{2,10},{10,2},{3,11},{11,3},{4,12},{12,4},... | collective-permute-start | bytes 786440 | tf_op jit(solution)/shard_map/cond/branch_1_fun/ppermute | solution.py:30
  501.8 140.1 %reduce-scatter.15.cloned.1.call-start = ((), (), s32[]{:S(2)}) async-start(), calls=%async_computation.14 | async-start | bytes 3145728 | tf_op jit(solution)/shard_map/reduce_scatter | solution.py:269
  501.8 50.1 %collective-permute-start.66 = (bf16[1024,1024]{1,0:T(8,128)(2,1)}, bf16[1024,1024]{1,0:T(8,128)(2,1)}, u32[]{:S(2)}, u32[]{:S(2)}) collective-permute-start(bf16[1024,1024]{1,0:T(8,128)(2,1)} %get-tuple-element.816), channel_id=1, source_target_pairs={{0,4},{4,0},{1,5},{5,1},{2,6},{6,2},{3,7},{7,3},{8,12},{12,8},{9,1... | collective-permute-start | bytes 6291464 | tf_op jit(solution)/shard_map/ppermute | solution.py:30
  504.7 10.7 %collective-permute-start.45 = (bf16[128,2048]{1,0:T(8,128)(2,1)S(1)}, bf16[128,2048]{1,0:T(8,128)(2,1)S(1)}, u32[]{:S(2)}, u32[]{:S(2)}) collective-permute-start(bf16[128,2048]{1,0:T(8,128)(2,1)S(1)} %pad_maximum_fusion.25), channel_id=1, source_target_pairs={{0,2},{2,0},{1,3},{3,1},{4,6},{6,4},{5,7},{7,5},{8,10},{10,8},{9,1... | collective-permute-start | bytes 1572872 | tf_op jit(solution)/shard_map/cond/branch_1_fun/ppermute | solution.py:30
  506.7 20.2 %collective-permute-start.46 = (bf16[128,2048]{1,0:T(8,128)(2,1)S(1)}, bf16[128,2048]{1,0:T(8,128)(2,1)S(1)}, u32[]{:S(2)}, u32[]{:S(2)}) collective-permute-start(bf16[128,2048]{1,0:T(8,128)(2,1)S(1)} %pad_maximum_fusion.26), channel_id=1, source_target_pairs={{0,8},{8,0},{1,9},{9,1},{2,10},{10,2},{3,11},{11,3},{4,12},{12,4},... | collective-permute-start | bytes 1572872 | tf_op jit(solution)/shard_map/cond/branch_1_fun/ppermute | solution.py:30
  556.5 134.4 %reduce-scatter.13.cloned.1.call-start = ((), (), s32[]{:S(2)}) async-start(), calls=%async_computation.13 | async-start | bytes 1572864 | tf_op jit(solution)/shard_map/reduce_scatter | solution.py:269
  560.0 8.5 %collective-permute-start.48 = (f32[2,2,2,2,128]{4,3,2,1,0:T(2,128)S(1)}, f32[2,2,2,2,128]{4,3,2,1,0:T(2,128)S(1)}, u32[]{:S(2)}, u32[]{:S(2)}) collective-permute-start(f32[2,2,2,2,128]{4,3,2,1,0:T(2,128)S(1)} %reshape.238), channel_id=1, source_target_pairs={{0,1},{1,0},{2,3},{3,2},{4,5},{5,4},{6,7},{7,6},{8,9},{9,8},{10,11... | collective-permute-start | bytes 24584 | tf_op jit(solution)/shard_map/cond/branch_1_fun/ppermute | solution.py:30
  579.1 24.8 %collective-permute-start.67 = (bf16[1024,512]{1,0:T(8,128)(2,1)}, bf16[1024,512]{1,0:T(8,128)(2,1)}, u32[]{:S(2)}, u32[]{:S(2)}) collective-permute-start(bf16[1024,512]{1,0:T(8,128)(2,1)} %copy.62), channel_id=1, source_target_pairs={{0,4},{4,0},{1,5},{5,1},{2,6},{6,2},{3,7},{7,3},{8,12},{12,8},{9,1... | collective-permute-start | bytes 3145736 | tf_op jit(solution)/shard_map/ppermute | solution.py:30
  608.0 82.9 %reduce-scatter.17.cloned.1.call-start = ((), (), s32[]{:S(2)}) async-start(), calls=%async_computation.15 | async-start | bytes 1572864 | tf_op jit(solution)/shard_map/reduce_scatter | solution.py:269
  608.0 33.9 %collective-permute-start.68 = (bf16[1024,512]{1,0:T(8,128)(2,1)}, bf16[1024,512]{1,0:T(8,128)(2,1)}, u32[]{:S(2)}, u32[]{:S(2)}) collective-permute-start(bf16[1024,512]{1,0:T(8,128)(2,1)} %get-tuple-element.850), channel_id=1, source_target_pairs={{0,4},{4,0},{1,5},{5,1},{2,6},{6,2},{3,7},{7,3},{8,12},{12,8},{9,1... | collective-permute-start | bytes 3145736 | tf_op jit(solution)/shard_map/ppermute | solution.py:30
  608.7 21.9 %collective-permute-start.69 = (bf16[256,1024]{1,0:T(8,128)(2,1)}, bf16[256,1024]{1,0:T(8,128)(2,1)}, u32[]{:S(2)}, u32[]{:S(2)}) collective-permute-start(bf16[256,1024]{1,0:T(8,128)(2,1)} %get-tuple-element.851), channel_id=1, source_target_pairs={{0,8},{8,0},{1,9},{9,1},{2,10},{10,2},{3,11},{11,3},{4,12},{12,4},... | collective-permute-start | bytes 1572872 | tf_op jit(solution)/shard_map/ppermute | solution.py:30
  610.8 31.1 %collective-permute-start.70 = (bf16[256,1024]{1,0:T(8,128)(2,1)}, bf16[256,1024]{1,0:T(8,128)(2,1)}, u32[]{:S(2)}, u32[]{:S(2)}) collective-permute-start(bf16[256,1024]{1,0:T(8,128)(2,1)} %slice_select_fusion.10), channel_id=1, source_target_pairs={{0,8},{8,0},{1,9},{9,1},{2,10},{10,2},{3,11},{11,3},{4,12},{12,4},... | collective-permute-start | bytes 1572872 | tf_op jit(solution)/shard_map/ppermute | solution.py:30
  619.6 11.0 %collective-permute-start.51 = (bf16[512,2048]{1,0:T(8,128)(2,1)}, bf16[512,2048]{1,0:T(8,128)(2,1)}, u32[]{:S(2)}, u32[]{:S(2)}) collective-permute-start(bf16[512,2048]{1,0:T(8,128)(2,1)} %convolution_convert_fusion.3), channel_id=1, source_target_pairs={{0,1},{1,0},{2,3},{3,2},{4,5},{5,4},{6,7},{7,6},{8,9},{9,8},{10,11... | collective-permute-start | bytes 6291464 | tf_op jit(solution)/shard_map/cond/branch_1_fun/ppermute | solution.py:30
  645.3 45.5 %collective-permute-start.71 = (bf16[256,1024]{1,0:T(8,128)(2,1)}, bf16[256,1024]{1,0:T(8,128)(2,1)}, u32[]{:S(2)}, u32[]{:S(2)}) collective-permute-start(bf16[256,1024]{1,0:T(8,128)(2,1)} %slice_select_fusion.9), channel_id=1, source_target_pairs={{0,8},{8,0},{1,9},{9,1},{2,10},{10,2},{3,11},{11,3},{4,12},{12,4},... | collective-permute-start | bytes 1572872 | tf_op jit(solution)/shard_map/ppermute | solution.py:30
  647.8 39.4 %collective-permute-start.23 = (f32[4,2048]{1,0:T(4,128)S(1)}, f32[4,2048]{1,0:T(4,128)S(1)}, u32[]{:S(2)}, u32[]{:S(2)}) collective-permute-start(f32[4,2048]{1,0:T(4,128)S(1)} %get-tuple-element.451), channel_id=1, source_target_pairs={{0,4},{4,0},{1,5},{5,1},{2,6},{6,2},{3,7},{7,3},{8,12},{12,8},{9,1... | collective-permute-start | bytes 98312 | tf_op jit(solution)/shard_map/cond/branch_1_fun/ppermute | solution.py:30
  655.9 27.2 %collective-permute-start.19 = (bf16[128,2048]{1,0:T(8,128)(2,1)}, bf16[128,2048]{1,0:T(8,128)(2,1)}, u32[]{:S(2)}, u32[]{:S(2)}) collective-permute-start(bf16[128,2048]{1,0:T(8,128)(2,1)} %pad_maximum_fusion.35), channel_id=1, source_target_pairs={{0,8},{8,0},{1,9},{9,1},{2,10},{10,2},{3,11},{11,3},{4,12},{12,4},... | collective-permute-start | bytes 1572872 | tf_op jit(solution)/shard_map/cond/branch_1_fun/ppermute | solution.py:30
  656.8 14.7 %collective-permute-start.20 = (bf16[128,2048]{1,0:T(8,128)(2,1)}, bf16[128,2048]{1,0:T(8,128)(2,1)}, u32[]{:S(2)}, u32[]{:S(2)}) collective-permute-start(bf16[128,2048]{1,0:T(8,128)(2,1)} %pad_maximum_fusion.36), channel_id=1, source_target_pairs={{0,2},{2,0},{1,3},{3,1},{4,6},{6,4},{5,7},{7,5},{8,10},{10,8},{9,1... | collective-permute-start | bytes 1572872 | tf_op jit(solution)/shard_map/cond/branch_1_fun/ppermute | solution.py:30
  672.7 15.4 %collective-permute-start.22 = (bf16[64,2048]{1,0:T(8,128)(2,1)S(1)}, bf16[64,2048]{1,0:T(8,128)(2,1)}, u32[]{:S(2)}, u32[]{:S(2)}) collective-permute-start(bf16[64,2048]{1,0:T(8,128)(2,1)S(1)} %slice.1484), channel_id=1, source_target_pairs={{0,8},{8,0},{1,9},{9,1},{2,10},{10,2},{3,11},{11,3},{4,12},{12,4},... | collective-permute-start | bytes 786440 | tf_op jit(solution)/shard_map/cond/branch_1_fun/ppermute | solution.py:30
  693.7 17.1 %collective-permute-start.73 = (bf16[256,512]{1,0:T(8,128)(2,1)}, bf16[256,512]{1,0:T(8,128)(2,1)}, u32[]{:S(2)}, u32[]{:S(2)}) collective-permute-start(bf16[256,512]{1,0:T(8,128)(2,1)} %broadcast_select_fusion.35), channel_id=1, source_target_pairs={{0,8},{8,0},{1,9},{9,1},{2,10},{10,2},{3,11},{11,3},{4,12},{12,4},... | collective-permute-start | bytes 786440 | tf_op jit(solution)/shard_map/ppermute | solution.py:30
  693.7 17.1 %collective-permute-start.72 = (bf16[256,512]{1,0:T(8,128)(2,1)S(1)}, bf16[256,512]{1,0:T(8,128)(2,1)}, u32[]{:S(2)}, u32[]{:S(2)}) collective-permute-start(bf16[256,512]{1,0:T(8,128)(2,1)S(1)} %broadcast_select_fusion.36), channel_id=1, source_target_pairs={{0,8},{8,0},{1,9},{9,1},{2,10},{10,2},{3,11},{11,3},{4,12},{12,4},... | collective-permute-start | bytes 786440 | tf_op jit(solution)/shard_map/ppermute | solution.py:30
  695.8 11.0 %collective-permute-start.3 = (f32[4,2048]{1,0:T(4,128)S(1)}, f32[4,2048]{1,0:T(4,128)S(1)}, u32[]{:S(2)}, u32[]{:S(2)}) collective-permute-start(f32[4,2048]{1,0:T(4,128)S(1)} %get-tuple-element.459), channel_id=1, source_target_pairs={{0,16},{16,0},{1,17},{17,1},{2,18},{18,2},{3,19},{19,3},{4,20},{20... | collective-permute-start | bytes 98312 | tf_op jit(solution)/shard_map/cond/branch_1_fun/ppermute | solution.py:30
  (94 other events, 820.4 us)
Sparse Core Ops, SparseCore 0:
  30.7 57.9 all-gather.4
  90.2 56.5 all-gather.6
  148.3 55.6 all-gather.8
  205.4 55.5 all-gather.10
  421.9 31.0 reduce-scatter.6
  455.2 31.5 reduce-scatter.8
  501.9 53.4 reduce-scatter.10
  558.3 54.3 reduce-scatter.14
  615.0 31.5 reduce-scatter.12
  649.3 30.4 reduce-scatter.16

commit v4 on v3

--- a/solution.py
+++ b/solution.py
@@ -308,17 +308,19 @@
         return [a0, b0, a_side, b_far[:half], a_far[:half], b_col, a_far[half:], b_far[half:]], (a_far, b_far)
 
     def gather_end(net, state):
-        mine = jnp.concatenate(state[0], 0)
+        return gather_cores(net, jnp.concatenate(state[0], 0))
+
+    def gather_cores(net, mine):
         other = net.send(mine, core)
         return jnp.concatenate([mine, other], 0), other
 
     def scatter_begin(net, product, n_rows):
         half = n_rows // 2
         received = net.send(product(slice(half, None)).astype(BF16), core)
-        return product(slice(half)), received
+        return product(slice(half)).astype(BF16), received
 
     def scatter_second(net, state):
-        part = state[0] + state[1].astype(F32)
+        part = state[0].astype(F32) + state[1].astype(F32)
         half = part.shape[0] // 8
         a0, b0, a_side, b_side, a_col, b_col, a_both, b_both = (part[i * half : (i + 1) * half] for i in range(8))
         received = (
@@ -498,13 +500,19 @@
         relay_up = spread(net, beyond(far_up))[1:]
         own_down = spread(net, block_down)[1:]
 
+        def part_middle():
+            return jnp.concatenate(gather_middle(net, state)[0], 0)
+
+        mlp_mine = region(flag, part_middle)
+        far_down, relay_up, mlp_mine = meet(far_down, relay_up, mlp_mine)
+        relay_down = spread(net, beyond(far_down))[1:]
+
         def part_gate():
-            mlp_in, _ = gather_end(net, gather_middle(net, state))
+            mlp_in, _ = gather_cores(net, mlp_mine)
             return mlp_in, by_rows(mlp_in, near_gate)
 
         out = region(flag, part_gate)
-        relay_up, own_down, far_down, (mlp_in, gate_proj) = meet(relay_up, own_down, far_down, out)
-        relay_down = spread(net, beyond(far_down))[1:]
+        own_down, (mlp_in, gate_proj) = meet(own_down, out)
 
         def part_up():
             near_up = [far_up, *(in_two(own, other) for own, other in zip(own_up, relay_up))]

time: 734 us -> 734 us (level)
    cond x140 -> x141, local copies, waits for them, and re-layouts: 43 us -> 45.4 us
  transfers between devices with their start and end apart: 84 -> 84, of which waited for: 37 -> 40; matrix products, arithmetic and copies ran while one was open for 44% -> 44% of each run, Pallas kernels for 3% -> 3%
where the time goes in v4:
time: 734 us; the launch traced here: 723 us
  waiting for transfers between devices  246 us (34%)
  matrix products  142 us (19%)
  other arithmetic  125 us (17%)
  local copies, waits for them, and re-layouts  93.4 us (13%)
  starting transfers between devices  76.1 us (10%)
  Pallas kernels  21.3 us (3%)
  between operations  15.6 us (2%)
    ppermute x74, waiting for transfers between devices, swap(): return lax.ppermute(values, axis, [(0, 1), (1, 0)])  244 us
    ppermute x74, starting transfers between devices, swap(): return lax.ppermute(values, axis, [(0, 1), (1, 0)])  75.7 us
    dot_general x14, matrix products, contract_rows(): lax.dot_general(left, right, (((0,), (0,)), ((), ())), preferred_element_...  57.3 us
    cond x141, local copies, waits for them, and re-layouts  45.4 us
    dot_general x8, matrix products, dot_rows_cols(): return jnp.dot(left, right, preferred_element_type=F32)  44.3 us
    dot_general x10, matrix products, contract_cols(): lax.dot_general(left, right, (((1,), (1,)), ((), ())), preferred_element_...  40.5 us
    select_n x21, other arithmetic, pick(): return jnp.where(flag, yes, no)  25.5 us
    pallas_call x2, Pallas kernels, attention(): pl.pallas_call(kernel, grid=(2, n_heads), in_specs=in_specs, out_specs=ou...  21.3 us
  transfers between devices with their start and end apart: 84, of which 40 were waited for; matrix products, arithmetic and copies ran while one was open for 44% of the time, Pallas kernels for 3%

profile of v4, /device:TPU:0, one launch (start us, length us, event | category | flops | bytes accessed | tf_op | source)
XLA Modules:
  0.0 723.2 jit_solution(9532532674426322810)
XLA Ops:
  9.1 21.4 %conditional.19 = (bf16[512,1024]{1,0:T(8,128)(2,1)}, bf16[256,1024]{1,0:T(8,128)(2,1)}, bf16[256,1024]{1,0:T(8,128)(2,1)}, bf16[128,2048]{1,0:T(8,128)(2,1)S(1)}) conditional(s32[]{:T(128)} %bitcast.58, () %tuple.190, (bf16[256,512]{1,0:T(8,128)(2,1)}, bf16[256,512]{1,0:T(8,128)(2,1)}, bf16[256,512]{1,0:T(8,128)(2,1)}, bf16[256,512]{1,0:T(8,128)(2,1)}, ...), branch_computations={%region_0.0_spmd, %region_1.2_spmd} | conditional | flops 12058631 | bytes 35127872 | solution.py:48
  17.1 10.9 %collective-permute-done.7 = bf16[256,1024]{1,0:T(8,128)(2,1)} collective-permute-done((bf16[256,1024]{1,0:T(8,128)(2,1)}, bf16[256,1024]{1,0:T(8,128)(2,1)}, u32[]{:S(2)}, u32[]{:S(2)}) %collective-permute-start.7) | collective-permute-done | bytes 524320 | tf_op jit(solution)/shard_map/cond/branch_1_fun/ppermute | solution.py:30
  32.3 54.7 %conditional.20 = (bf16[64,2048]{1,0:T(8,128)(2,1)S(1)}, bf16[64,2048]{1,0:T(8,128)(2,1)S(1)}, bf16[64,2048]{1,0:T(8,128)(2,1)S(1)}, bf16[64,2048]{1,0:T(8,128)(...) conditional(s32[]{:T(128)} %bitcast.58, () %tuple.192, ...), branch_computations={%region_2.3_spmd, %region_3.4_spmd} | conditional | flops 4982795 | bytes 32563916 | solution.py:48
  45.0 21.5 %collective-permute-done.10 = bf16[256,1024]{1,0:T(8,128)(2,1)S(1)} collective-permute-done((bf16[256,1024]{1,0:T(8,128)(2,1)}, bf16[256,1024]{1,0:T(8,128)(2,1)S(1)}, u32[]{:S(2)}, u32[]{:S(2)}) %collective-permute-start.10) | collective-permute-done | bytes 524320 | tf_op jit(solution)/shard_map/cond/branch_1_fun/ppermute | solution.py:30
  68.3 15.9 %collective-permute-done.12 = bf16[128,2048]{1,0:T(8,128)(2,1)} collective-permute-done((bf16[128,2048]{1,0:T(8,128)(2,1)S(1)}, bf16[128,2048]{1,0:T(8,128)(2,1)}, u32[]{:S(2)}, u32[]{:S(2)}) %collective-permute-start.12) | collective-permute-done | bytes 524320 | tf_op jit(solution)/shard_map/cond/branch_1_fun/ppermute | solution.py:30
  94.2 15.5 %conditional.21 = (bf16[1024,2048]{1,0:T(8,128)(2,1)}, f32[1024,128]{1,0:T(8,128)}, f32[1024,128]{1,0:T(8,128)}, f32[2,512,512]{2,1,0:T(8,128)S(1)}, f32[256]{0:...) conditional(s32[]{:T(128)} %bitcast.58, () %tuple.195, ...), branch_computations={%region_4.5_spmd, %region_5.6_spmd} | conditional | flops 2892172 | bytes 27435296 | solution.py:48
  112.3 4.0 collective-permute-done.55
  120.3 32.1 %conditional.22 = (bf16[1024,1024]{1,0:T(8,128)(2,1)}, bf16[1024,1024]{1,0:T(8,128)(2,1)}, f32[1024,768]{1,0:T(8,128)S(1)}, f32[2,1024]{1,0:T(2,128)S(1)}, bf16[2048,256]{1,0:T(8,128)(2,1)}) conditional(s32[]{:T(128)} %bitcast.58, () %tuple.198, (bf16[512,1024]{1,0:T(8,128)(2,1)}, bf16[512,1024]{1,0:T(8,128)(2,1)}, bf16[1024,2048]{1,0:T(8,128)(2,1)}, ...), branch_computations={%region_6.7_spmd, %region_7.10_spmd} | conditional | flops 3234607104 | bytes 71541024 | solution.py:48
  131.9 14.8 %collective-permute-done.1 = f32[2,2,2,2,128]{4,3,2,1,0:T(2,128)S(1)} collective-permute-done((f32[2,2,2,2,128]{4,3,2,1,0:T(2,128)S(1)}, f32[2,2,2,2,128]{4,3,2,1,0:T(2,128)S(1)}, u32[]{:S(2)}, u32[]{:S(2)}) %collective-permute-start.1) | collective-permute-done | bytes 8224 | tf_op jit(solution)/shard_map/cond/branch_1_fun/ppermute | solution.py:30
  154.0 18.2 %conditional.23 = (bf16[1024,256]{1,0:T(8,128)(2,1)}, f32[1024,2]{1,0:T(8,128)}, bf16[512,2048]{1,0:T(8,128)(2,1)}, bf16[512,2048]{1,0:T(8,128)(2,1)}) conditional(s32[]{:T(128)} %bitcast.58, () %tuple.201, (f32[1024,768]{1,0:T(8,128)S(1)}, f32[2,1024]{1,0:T(2,128)S(1)}, f32[256]{0:T(256)S(1)}, f32[256]{0:T(256)S(1)}, f32[1024,128]{1,0:T(8,128)}, ...), branch_computations={%region_10.11_spmd, %region_11.12_spmd} | conditional | flops 2149584896 | bytes 24682568 | solution.py:48
  157.2 7.6 %branch_1_fun.2 = bf16[2,2,256,256]{3,2,1,0:T(8,128)(2,1)} custom-call(f32[2,2,256,768]{3,2,1,0:T(8,128)S(1)} %bitcast.109, f32[2,2,256,768]{3,2,1,0:T(8,128)S(1)} %bitcast.110, f32[2,2,256,768]{3,2,1,0:T(8,128)S(1)} %bitcast.111, f32[2,2,256,2]{3,2,1,0:T(8,128)S(1)} %bitcast.107, f32[1,256]{1,0:T(1,128)S(1)} %bitcast.149, f32[1,256]{1,0:T(1,128)S(1)} %bitcast.146, ...), custom_call_target="tpu_custom_call" | custom-call | flops 1073741824 | bytes 8388608 | tf_op jit(solution)/shard_map/cond/branch_1_fun/pallas_call | solution.py:222
  176.4 67.9 %conditional.24 = (f32[128,1]{0,1:T(1,128)S(1)}, f32[128,2048]{1,0:T(8,128)}, f32[128,2048]{1,0:T(8,128)}, bf16[64,2048]{1,0:T(8,128)(2,1)}, bf16[64,2048]{1,0:T...) conditional(s32[]{:T(128)} %bitcast.58, () %tuple.205, (bf16[512,2048]{1,0:T(8,128)(2,1)}, ...), branch_computations={%region_12.13_spmd, %region_13.15_spmd} | conditional | flops 10748032 | bytes 42478376 | solution.py:48
  181.0 32.4 %collective-permute-done.20 = bf16[128,2048]{1,0:T(8,128)(2,1)S(1)} collective-permute-done((bf16[128,2048]{1,0:T(8,128)(2,1)S(1)}, bf16[128,2048]{1,0:T(8,128)(2,1)S(1)}, u32[]{:S(2)}, u32[]{:S(2)}) %collective-permute-start.20) | collective-permute-done | bytes 524320 | tf_op jit(solution)/shard_map/cond/branch_1_fun/ppermute | solution.py:30
  215.6 5.6 collective-permute-done.21
  221.3 6.1 collective-permute-done.23
  232.8 11.5 %collective-permute-done.25 = bf16[64,2048]{1,0:T(8,128)(2,1)} collective-permute-done((bf16[64,2048]{1,0:T(8,128)(2,1)}, bf16[64,2048]{1,0:T(8,128)(2,1)}, u32[]{:S(2)}, u32[]{:S(2)}) %collective-permute-start.25) | collective-permute-done | bytes 262176 | tf_op jit(solution)/shard_map/cond/branch_1_fun/ppermute | solution.py:30
  249.5 26.3 %conditional.25 = (bf16[512,2048]{1,0:T(8,128)(2,1)}) conditional(s32[]{:T(128)} %bitcast.58, () %tuple.208, (bf16[64,2048]{1,0:T(8,128)(2,1)}, bf16[64,2048]{1,0:T(8,128)(2,1)}, bf16[64,2048]{1,0:T(8,128)(2,1)}, bf16[64,2048]{1,0:T(8,128)(2,1)}) %tuple.209), branch_computations={%region_15.16_spmd, %region_16.17_spmd} | conditional | flops 2097152 | bytes 10485848 | solution.py:48
  262.5 9.4 %collective-permute-done.4 = bf16[128,2048]{1,0:T(8,128)(2,1)S(1)} collective-permute-done((bf16[128,2048]{1,0:T(8,128)(2,1)S(1)}, bf16[128,2048]{1,0:T(8,128)(2,1)S(1)}, u32[]{:S(2)}, u32[]{:S(2)}) %collective-permute-start.4) | collective-permute-done | bytes 524320 | tf_op jit(solution)/shard_map/cond/branch_1_fun/ppermute | solution.py:30
  279.7 15.6 %conditional.26 = (bf16[1024,2048]{1,0:T(8,128)(2,1)}, f32[1024,1024]{1,0:T(8,128)}) conditional(s32[]{:T(128)} %bitcast.58, () %tuple.204, (bf16[512,2048]{1,0:T(8,128)(2,1)}, bf16[1024,1024]{1,0:T(8,128)(2,1)S(1)}, bf16[1024,1024]{1,0:T(8,128)(2,1)}) %tuple.445), branch_computations={%region_17.18_spmd, %region_18.19_spmd} | conditional | flops 4296015872 | bytes 46137428 | solution.py:48
  285.5 3.9 fusion.30
  289.4 5.9 fusion.34
  296.3 17.4 %conditional.27 = (f32[1024,1024]{1,0:T(8,128)}, bf16[1024,1024]{1,0:T(8,128)(2,1)}, bf16[1024,1024]{1,0:T(8,128)(2,1)S(1)}, bf16[1024,1024]{1,0:T(8,128)(2,1)}) conditional(s32[]{:T(128)} %bitcast.58, () %tuple.213, (bf16[1024,2048]{1,0:T(8,128)(2,1)}, bf16[1024,1024]{1,0:T(8,128)(2,1)}, bf16[512,1024]{1,0:T(8,128)(2,1)}, ...), branch_computations={%region_19.20_spmd, %region_20.21_spmd} | conditional | flops 4307550208 | bytes 48234596 | solution.py:48
  300.9 3.9 fusion.38
  304.9 8.9 %multiply_convert_fusion = (bf16[1024,1024]{1,0:T(8,128)(2,1)}, f32[1024,1024]{1,0:T(8,128)}) fusion(f32[1024,1024]{1,0:T(8,128)} %get-tuple-element.346, f32[1024,1024]{1,0:T(8,128)S(1)} %fusion.38, bf16[1024,1024]{1,0:T(8,128)(2,1)} %pad_maximum_fusion.14, bf16[1024,2048]{1,0:T(8,128)(2,1)} %get-tuple-element.342), kind=kOutput, calls=%fused_computation.163 | convolution fusion | flops 2154823680 | bytes 18874368 | tf_op jit(solution)/shard_map/cond/branch_1_fun/dot_general | solution.py:18
  315.6 74.9 %conditional.28 = (bf16[2048,1024]{1,0:T(8,128)(2,1)S(1)}, f32[128,2048]{1,0:T(8,128)S(1)}, bf16[1024,2048]{1,0:T(8,128)(2,1)}, bf16[1024,512]{1,0:T(8,128)(2,1)...) conditional(s32[]{:T(128)} %bitcast.58, () %tuple.189, (bf16[512,1024]{1,0:T(8,128)(2,1)}, ...), branch_computations={%region_21.22_spmd, %region_22.25_spmd} | conditional | flops 5415632896 | bytes 190076080 | solution.py:48
  318.5 4.4 fusion.40
  323.0 4.1 collective-permute-done.26
  333.7 11.9 %collective-permute-done.27 = bf16[128,2048]{1,0:T(8,128)(2,1)S(1)} collective-permute-done((bf16[128,2048]{1,0:T(8,128)(2,1)S(1)}, bf16[128,2048]{1,0:T(8,128)(2,1)S(1)}, u32[]{:S(2)}, u32[]{:S(2)}) %collective-permute-start.27) | collective-permute-done | bytes 524320 | tf_op jit(solution)/shard_map/cond/branch_1_fun/ppermute | solution.py:30
  347.9 5.8 collective-permute-done.28
  358.6 3.9 collective-permute-done.32
  366.9 7.6 %collective-permute-done.33 = bf16[128,2048]{1,0:T(8,128)(2,1)S(1)} collective-permute-done((bf16[128,2048]{1,0:T(8,128)(2,1)S(1)}, bf16[128,2048]{1,0:T(8,128)(2,1)S(1)}, u32[]{:S(2)}, u32[]{:S(2)}) %collective-permute-start.33) | collective-permute-done | bytes 524320 | tf_op jit(solution)/shard_map/cond/branch_1_fun/ppermute | solution.py:30
  376.9 5.0 pad_maximum_fusion.16
  386.2 4.3 fusion.43
  391.5 26.4 %conditional.29 = (bf16[1024,512]{1,0:T(8,128)(2,1)S(1)}, bf16[1024,1024]{1,0:T(8,128)(2,1)}, bf16[1024,1024]{1,0:T(8,128)(2,1)}, bf16[1024,512]{1,0:T(8,128)(2,1)}, bf16[1024,1024]{1,0:T(8,128)(2,1)}) conditional(s32[]{:T(128)} %bitcast.58, () %tuple.217, (bf16[1024,2048]{1,0:T(8,128)(2,1)}, bf16[1024,1024]{1,0:T(8,128)(2,1)}, ...), branch_computations={%region_25.26_spmd, %region_26.27_spmd} | conditional | flops 8605663232 | bytes 69206112 | solution.py:48
  396.9 10.9 %multiply_convert_fusion.2 = (bf16[1024,1024]{1,0:T(8,128)(2,1)}, bf16[1024,1024]{1,0:T(8,128)(2,1)}) fusion(f32[1024,1024]{1,0:T(8,128)} %get-tuple-element.363, f32[1024,1024]{1,0:T(8,128)} %get-tuple-element.362, bf16[1024,2048]{1,0:T(8,128)(2,1)} %get-tuple-element.364, bf16[2048,1024]{1,0:T(8,128)(2,1)S(1)} %copy-done.26), kind=kOutput, calls=%fused_computation.217 | convolution fusion | flops 4308598784 | bytes 20971520 | tf_op jit(solution)/shard_map/cond/branch_1_fun/dot_general | solution.py:18
  407.8 4.1 fusion.62
  411.9 6.0 fusion.56
  422.5 20.0 %conditional.30 = (bf16[1024,512]{1,0:T(8,128)(2,1)S(1)}, bf16[512,2048]{1,0:T(8,128)(2,1)S(1)}, bf16[512,2048]{1,0:T(8,128)(2,1)}) conditional(s32[]{:T(128)} %bitcast.58, () %tuple.221, (bf16[1024,1024]{1,0:T(8,128)(2,1)}, bf16[2048,1024]{1,0:T(8,128)(2,1)}, bf16[1024,1024]{1,0:T(8,128)(2,1)}, bf16[2048,1024]{1,0:T(8,128)(2,1)}, ...), branch_computations={%region_28.29_spmd, %region_29.30_spmd} | conditional | flops 9668395008 | bytes 88080504 | solution.py:48
  422.9 5.3 fusion.77
  428.3 3.8 convolution_add_fusion.1
  435.7 3.6 convolution_add_fusion
  442.5 4.3 collective-permute-done.65
  449.3 47.5 %conditional.31 = (bf16[1024,1024]{1,0:T(8,128)(2,1)}, bf16[1024,1024]{1,0:T(8,128)(2,1)}, bf16[1024,1024]{1,0:T(8,128)(2,1)}, f32[128,2048]{1,0:T(8,128)}, bf16...) conditional(s32[]{:T(128)} %bitcast.58, () %tuple.220, ...), branch_computations={%region_30.31_spmd, %region_31.34_spmd} | conditional | flops 6457128960 | bytes 62942008 | solution.py:48
  454.0 6.0 fusion.85
  460.1 11.6 %collective-permute-done.39 = bf16[128,2048]{1,0:T(8,128)(2,1)S(1)} collective-permute-done((bf16[128,2048]{1,0:T(8,128)(2,1)S(1)}, bf16[128,2048]{1,0:T(8,128)(2,1)S(1)}, u32[]{:S(2)}, u32[]{:S(2)}) %collective-permute-start.39) | collective-permute-done | bytes 524320 | tf_op jit(solution)/shard_map/cond/branch_1_fun/ppermute | solution.py:30
  474.7 5.9 fusion.88
  490.9 5.9 fusion.91
  496.9 4.8 add_convert_fusion.2
  502.3 49.0 %conditional.32 = (bf16[1024,2048]{1,0:T(8,128)(2,1)}, f32[1024,256]{1,0:T(8,128)}, f32[1024,256]{1,0:T(8,128)}, bf16[1024,256]{1,0:T(8,128)(2,1)}, f32[2,2,2,256,2]{4,3,2,1,0:T(8,128)}, /*index=5*/f32[2,256]{1,0:T(2,128)S(1)}) conditional(s32[]{:T(128)} %bitcast.58, () %tuple.226, (bf16[64,2048]{1,0:T(8,128)(2,1)}, bf16[64,2048]{1,0:T(8,128)(2,1)}, ...), branch_computations={%region_35.36_spmd, %region_36.38_spmd} | conditional | flops 2149843456 | bytes 49027272 | solution.py:48
  513.2 13.1 %collective-permute-done.46 = bf16[128,2048]{1,0:T(8,128)(2,1)S(1)} collective-permute-done((bf16[128,2048]{1,0:T(8,128)(2,1)S(1)}, bf16[128,2048]{1,0:T(8,128)(2,1)S(1)}, u32[]{:S(2)}, u32[]{:S(2)}) %collective-permute-start.46) | collective-permute-done | bytes 524320 | tf_op jit(solution)/shard_map/cond/branch_1_fun/ppermute | solution.py:30
  533.7 3.9 convolution_convert_fusion.4
  537.6 13.7 %branch_1_fun.3 = (f32[2,2,256,256]{3,2,1,0:T(8,128)}, f32[2,2,256,256]{3,2,1,0:T(8,128)}, bf16[2,2,256,256]{3,2,1,0:T(8,128)(2,1)}, f32[2,2,2,256,2]{4,3,2,1,0:T(8,128)}, f32[2,2,256]{2,1,0:T(2,128)S(1)}) custom-call(f32[2,2,256,768]{3,2,1,0:T(8,128)S(1)} %bitcast.112, f32[2,2,256,768]{3,2,1,0:T(8,128)S(1)} %bitcast.113, f32[2,2,256,768]{3,2,1,0:T(8,128)S(1)} %bitcast.114, ...), custom_call_target="tpu_custom_call" | custom-call | flops 1073741824 | bytes 8388608 | tf_op jit(solution)/shard_map/cond/branch_1_fun/pallas_call | solution.py:222
  551.4 4.5 add_convert_fusion.1
  555.9 20.4 %conditional.33 = (f32[2,1024]{1,0:T(2,128)S(1)}, bf16[1024,512]{0,1:T(8,128)(2,1)}, bf16[512,1024]{1,0:T(8,128)(2,1)}, bf16[256,1024]{1,0:T(8,128)(2,1)}) conditional(s32[]{:T(128)} %bitcast.58, () %tuple.188, (f32[2,2,2,256,2]{4,3,2,1,0:T(8,128)}, bf16[1024,2048]{1,0:T(8,128)(2,1)}, bf16[1024,256]{1,0:T(8,128)(2,1)}, ...), branch_computations={%region_38.39_spmd, %region_39.41_spmd} | conditional | flops 1076633600 | bytes 16515326 | solution.py:48
  579.7 21.3 %conditional.34 = (bf16[1024,512]{1,0:T(8,128)(2,1)}, bf16[1024,512]{0,1:T(8,128)(2,1)}, bf16[1024,512]{1,0:T(8,128)(2,1)}, bf16[2048,768]{1,0:T(8,128)(2,1)}) conditional(s32[]{:T(128)} %bitcast.58, () %tuple.230, (f32[1024,2]{1,0:T(8,128)}, bf16[1024,2048]{1,0:T(8,128)(2,1)}, bf16[1024,256]{1,0:T(8,128)(2,1)}, bf16[1024,2048]{1,0:T(8,128)(2,1)}, ...), branch_computations={%region_42.43_spmd, %region_43.44_spmd} | conditional | flops 2162165760 | bytes 38881340 | solution.py:48
  591.7 4.1 fusion.111
  611.5 18.4 %conditional.35 = (bf16[1024,512]{1,0:T(8,128)(2,1)S(1)}, bf16[512,2048]{1,0:T(8,128)(2,1)}, bf16[512,2048]{1,0:T(8,128)(2,1)}, f32[4,2048]{1,0:T(4,128)S(1)}) conditional(s32[]{:T(128)} %bitcast.58, () %tuple.233, (bf16[1024,2048]{1,0:T(8,128)(2,1)}, bf16[1024,512]{1,0:T(8,128)(2,1)}, bf16[1024,256]{1,0:T(8,128)(2,1)}, ...), branch_computations={%region_46.47_spmd, %region_47.49_spmd} | conditional | flops 4298155520 | bytes 36880644 | solution.py:48
  613.9 5.6 convolution_convert_fusion.5
  621.1 5.3 convolution_convert_fusion.6
  629.9 12.5 %collective-permute-done.70 = bf16[256,1024]{1,0:T(8,128)(2,1)} collective-permute-done((bf16[256,1024]{1,0:T(8,128)(2,1)}, bf16[256,1024]{1,0:T(8,128)(2,1)}, u32[]{:S(2)}, u32[]{:S(2)}) %collective-permute-start.70) | collective-permute-done | bytes 524320 | tf_op jit(solution)/shard_map/ppermute | solution.py:30
  648.3 40.9 %conditional.36 = (f32[64,2048]{1,0:T(8,128)}, f32[64,2048]{1,0:T(8,128)S(1)}, bf16[64,2048]{1,0:T(8,128)(2,1)}, bf16[64,2048]{1,0:T(8,128)(2,1)}, f32[256,2048]...) conditional(s32[]{:T(128)} %bitcast.58, () %tuple.236, ...), branch_computations={%region_50.51_spmd, %region_51.52_spmd} | conditional | flops 12591111 | bytes 64201160 | solution.py:48
  649.7 5.1 fusion.135
  674.2 7.4 %collective-permute-done.15 = bf16[128,2048]{1,0:T(8,128)(2,1)} collective-permute-done((bf16[128,2048]{1,0:T(8,128)(2,1)}, bf16[128,2048]{1,0:T(8,128)(2,1)}, u32[]{:S(2)}, u32[]{:S(2)}) %collective-permute-start.15) | collective-permute-done | bytes 524320 | tf_op jit(solution)/shard_map/cond/branch_1_fun/ppermute | solution.py:30
  694.1 16.4 %conditional.37 = (f32[128,2048]{1,0:T(8,128)}, f32[256,2048]{1,0:T(8,128)}, f32[4,2048]{1,0:T(4,128)S(1)}) conditional(s32[]{:T(128)} %bitcast.58, () %tuple.239, (bf16[64,2048]{1,0:T(8,128)(2,1)}, f32[64,2048]{1,0:T(8,128)}, bf16[64,2048]{1,0:T(8,128)(2,1)}, f32[64,2048]{1,0:T(8,128)S(1)}, f32[128,2048]{1,0:T(8,128)}, ...), branch_computations={%region_52.53_spmd, %region_53.54_spmd} | conditional | flops 3162119 | bytes 17236164 | solution.py:48
  (602 shorter events, 347.4 us)
Async XLA Ops:
  7.2 81.5 %all-gather.5.cloned.1.call-start = ((), (), s32[]{:S(2)}) async-start(), calls=%async_computation.6 | async-start | bytes 3145728 | tf_op jit(solution)/shard_map/all_gather | solution.py:258
  12.7 15.3 %collective-permute-start.7 = (bf16[256,1024]{1,0:T(8,128)(2,1)}, bf16[256,1024]{1,0:T(8,128)(2,1)}, u32[]{:S(2)}, u32[]{:S(2)}) collective-permute-start(bf16[256,1024]{1,0:T(8,128)(2,1)} %broadcast_select_fusion.2), channel_id=1, source_target_pairs={{0,8},{8,0},{1,9},{9,1},{2,10},{10,2},{3,11},{11,3},{4,12},{12,4},... | collective-permute-start | bytes 1572872 | tf_op jit(solution)/shard_map/cond/branch_1_fun/ppermute | solution.py:30
  30.5 141.6 %all-gather.7.cloned.1.call-start = ((), (), s32[]{:S(2)}) async-start(), calls=%async_computation.7 | async-start | bytes 3145728 | tf_op jit(solution)/shard_map/all_gather | solution.py:258
  30.6 56.5 %collective-permute-start.54 = (bf16[512,1024]{1,0:T(8,128)(2,1)}, bf16[512,1024]{1,0:T(8,128)(2,1)}, u32[]{:S(2)}, u32[]{:S(2)}) collective-permute-start(bf16[512,1024]{1,0:T(8,128)(2,1)} %get-tuple-element.693), channel_id=1, source_target_pairs={{0,4},{4,0},{1,5},{5,1},{2,6},{6,2},{3,7},{7,3},{8,12},{12,8},{9,1... | collective-permute-start | bytes 3145736 | tf_op jit(solution)/shard_map/ppermute | solution.py:30
  40.7 25.8 %collective-permute-start.10 = (bf16[256,1024]{1,0:T(8,128)(2,1)}, bf16[256,1024]{1,0:T(8,128)(2,1)S(1)}, u32[]{:S(2)}, u32[]{:S(2)}) collective-permute-start(bf16[256,1024]{1,0:T(8,128)(2,1)} %get-tuple-element.300), channel_id=1, source_target_pairs={{0,8},{8,0},{1,9},{9,1},{2,10},{10,2},{3,11},{11,3},{4,12},{12,4},... | collective-permute-start | bytes 1572872 | tf_op jit(solution)/shard_map/cond/branch_1_fun/ppermute | solution.py:30
  43.4 40.8 %collective-permute-start.12 = (bf16[128,2048]{1,0:T(8,128)(2,1)S(1)}, bf16[128,2048]{1,0:T(8,128)(2,1)}, u32[]{:S(2)}, u32[]{:S(2)}) collective-permute-start(bf16[128,2048]{1,0:T(8,128)(2,1)S(1)} %pad_maximum_fusion.5), channel_id=1, source_target_pairs={{0,8},{8,0},{1,9},{9,1},{2,10},{10,2},{3,11},{11,3},{4,12},{12,4},... | collective-permute-start | bytes 1572872 | tf_op jit(solution)/shard_map/cond/branch_1_fun/ppermute | solution.py:30
  66.5 18.7 %collective-permute-start.11 = (bf16[128,2048]{1,0:T(8,128)(2,1)S(1)}, bf16[128,2048]{1,0:T(8,128)(2,1)}, u32[]{:S(2)}, u32[]{:S(2)}) collective-permute-start(bf16[128,2048]{1,0:T(8,128)(2,1)S(1)} %pad_maximum_fusion.4), channel_id=1, source_target_pairs={{0,2},{2,0},{1,3},{3,1},{4,6},{6,4},{5,7},{7,5},{8,10},{10,8},{9,1... | collective-permute-start | bytes 1572872 | tf_op jit(solution)/shard_map/cond/branch_1_fun/ppermute | solution.py:30
  88.7 155.7 %all-gather.11.cloned.1.call-start = ((), (), s32[]{:S(2)}) async-start(), calls=%async_computation.9 | async-start | bytes 3145728 | tf_op jit(solution)/shard_map/all_gather | solution.py:258
  91.0 25.2 %collective-permute-start.55 = (bf16[512,1024]{1,0:T(8,128)(2,1)}, bf16[512,1024]{1,0:T(8,128)(2,1)}, u32[]{:S(2)}, u32[]{:S(2)}) collective-permute-start(bf16[512,1024]{1,0:T(8,128)(2,1)} %constant_dynamic-slice_fusion.4), channel_id=1, source_target_pairs={{0,4},{4,0},{1,5},{5,1},{2,6},{6,2},{3,7},{7,3},{8,12},{12,8},{9,1... | collective-permute-start | bytes 3145736 | tf_op jit(solution)/shard_map/ppermute | solution.py:30
  92.5 19.8 %collective-permute-start.56 = (bf16[256,1024]{1,0:T(8,128)(2,1)}, bf16[256,1024]{1,0:T(8,128)(2,1)}, u32[]{:S(2)}, u32[]{:S(2)}) collective-permute-start(bf16[256,1024]{1,0:T(8,128)(2,1)} %get-tuple-element.709), channel_id=1, source_target_pairs={{0,8},{8,0},{1,9},{9,1},{2,10},{10,2},{3,11},{11,3},{4,12},{12,4},... | collective-permute-start | bytes 1572872 | tf_op jit(solution)/shard_map/ppermute | solution.py:30
  118.7 53.5 %collective-permute-start.57 = (bf16[512,1024]{1,0:T(8,128)(2,1)}, bf16[512,1024]{1,0:T(8,128)(2,1)}, u32[]{:S(2)}, u32[]{:S(2)}) collective-permute-start(bf16[512,1024]{1,0:T(8,128)(2,1)} %pad_maximum_fusion.38), channel_id=1, source_target_pairs={{0,4},{4,0},{1,5},{5,1},{2,6},{6,2},{3,7},{7,3},{8,12},{12,8},{9,1... | collective-permute-start | bytes 3145736 | tf_op jit(solution)/shard_map/ppermute | solution.py:30
  120.3 155.5 %all-gather.9.cloned.1.call-start = ((), (), s32[]{:S(2)}) async-start(), calls=%async_computation.8 | async-start | bytes 3145728 | tf_op jit(solution)/shard_map/all_gather | solution.py:258
  130.8 15.9 %collective-permute-start.1 = (f32[2,2,2,2,128]{4,3,2,1,0:T(2,128)S(1)}, f32[2,2,2,2,128]{4,3,2,1,0:T(2,128)S(1)}, u32[]{:S(2)}, u32[]{:S(2)}) collective-permute-start(f32[2,2,2,2,128]{4,3,2,1,0:T(2,128)S(1)} %reverse_add_fusion.1), channel_id=1, source_target_pairs={{0,8},{8,0},{1,9},{9,1},{2,10},{10,2},{3,11},{11,3},{4,12},{12,4},... | collective-permute-start | bytes 24584 | tf_op jit(solution)/shard_map/cond/branch_1_fun/ppermute | solution.py:30
  152.4 19.8 %collective-permute-start.58 = (bf16[256,1024]{1,0:T(8,128)(2,1)}, bf16[256,1024]{1,0:T(8,128)(2,1)}, u32[]{:S(2)}, u32[]{:S(2)}) collective-permute-start(bf16[256,1024]{1,0:T(8,128)(2,1)} %get-tuple-element.740), channel_id=1, source_target_pairs={{0,8},{8,0},{1,9},{9,1},{2,10},{10,2},{3,11},{11,3},{4,12},{12,4},... | collective-permute-start | bytes 1572872 | tf_op jit(solution)/shard_map/ppermute | solution.py:30
  172.2 72.2 %collective-permute-start.60 = (bf16[1024,1024]{1,0:T(8,128)(2,1)}, bf16[1024,1024]{1,0:T(8,128)(2,1)S(1)}, u32[]{:S(2)}, u32[]{:S(2)}) collective-permute-start(bf16[1024,1024]{1,0:T(8,128)(2,1)} %all-gather.7.cloned.1.call-done), channel_id=1, source_target_pairs={{0,4},{4,0},{1,5},{5,1},{2,6},{6,2},{3,7},{7,3},{8,12},{12,8},{9,1... | collective-permute-start | bytes 6291464 | tf_op jit(solution)/shard_map/ppermute | solution.py:30
  176.3 320.5 %reduce-scatter.7.cloned.1.call-start = ((), (), s32[]{:S(2)}) async-start(), calls=%async_computation.10 | async-start | bytes 1572864 | tf_op jit(solution)/shard_map/reduce_scatter | solution.py:269
  179.7 33.7 %collective-permute-start.20 = (bf16[128,2048]{1,0:T(8,128)(2,1)S(1)}, bf16[128,2048]{1,0:T(8,128)(2,1)S(1)}, u32[]{:S(2)}, u32[]{:S(2)}) collective-permute-start(bf16[128,2048]{1,0:T(8,128)(2,1)S(1)} %pad_maximum_fusion.10), channel_id=1, source_target_pairs={{0,8},{8,0},{1,9},{9,1},{2,10},{10,2},{3,11},{11,3},{4,12},{12,4},... | collective-permute-start | bytes 1572872 | tf_op jit(solution)/shard_map/cond/branch_1_fun/ppermute | solution.py:30
  180.4 35.0 %collective-permute-start.22 = (bf16[128,2048]{1,0:T(8,128)(2,1)S(1)}, bf16[128,2048]{1,0:T(8,128)(2,1)S(1)}, u32[]{:S(2)}, u32[]{:S(2)}) collective-permute-start(bf16[128,2048]{1,0:T(8,128)(2,1)S(1)} %pad_maximum_fusion.11), channel_id=1, source_target_pairs={{0,2},{2,0},{1,3},{3,1},{4,6},{6,4},{5,7},{7,5},{8,10},{10,8},{9,1... | collective-permute-start | bytes 1572872 | tf_op jit(solution)/shard_map/cond/branch_1_fun/ppermute | solution.py:30
  215.5 11.9 %collective-permute-start.23 = (bf16[64,2048]{1,0:T(8,128)(2,1)S(1)}, bf16[64,2048]{1,0:T(8,128)(2,1)S(1)}, u32[]{:S(2)}, u32[]{:S(2)}) collective-permute-start(bf16[64,2048]{1,0:T(8,128)(2,1)S(1)} %slice.1474), channel_id=1, source_target_pairs={{0,8},{8,0},{1,9},{9,1},{2,10},{10,2},{3,11},{11,3},{4,12},{12,4},... | collective-permute-start | bytes 786440 | tf_op jit(solution)/shard_map/cond/branch_1_fun/ppermute | solution.py:30
  230.1 14.3 %collective-permute-start.25 = (bf16[64,2048]{1,0:T(8,128)(2,1)}, bf16[64,2048]{1,0:T(8,128)(2,1)}, u32[]{:S(2)}, u32[]{:S(2)}) collective-permute-start(bf16[64,2048]{1,0:T(8,128)(2,1)} %get-tuple-element.1331), channel_id=1, source_target_pairs={{0,8},{8,0},{1,9},{9,1},{2,10},{10,2},{3,11},{11,3},{4,12},{12,4},... | collective-permute-start | bytes 786440 | tf_op jit(solution)/shard_map/cond/branch_1_fun/ppermute | solution.py:30
  232.5 11.8 %collective-permute-start.24 = (bf16[64,2048]{1,0:T(8,128)(2,1)}, bf16[64,2048]{1,0:T(8,128)(2,1)}, u32[]{:S(2)}, u32[]{:S(2)}) collective-permute-start(bf16[64,2048]{1,0:T(8,128)(2,1)} %get-tuple-element.1330), channel_id=1, source_target_pairs={{0,2},{2,0},{1,3},{3,1},{4,6},{6,4},{5,7},{7,5},{8,10},{10,8},{9,1... | collective-permute-start | bytes 786440 | tf_op jit(solution)/shard_map/cond/branch_1_fun/ppermute | solution.py:30
  247.4 28.3 %collective-permute-start.61 = (bf16[512,1024]{1,0:T(8,128)(2,1)}, bf16[512,1024]{1,0:T(8,128)(2,1)}, u32[]{:S(2)}, u32[]{:S(2)}) collective-permute-start(bf16[512,1024]{1,0:T(8,128)(2,1)} %constant_dynamic-slice_fusion.3), channel_id=1, source_target_pairs={{0,4},{4,0},{1,5},{5,1},{2,6},{6,2},{3,7},{7,3},{8,12},{12,8},{9,1... | collective-permute-start | bytes 3145736 | tf_op jit(solution)/shard_map/ppermute | solution.py:30
  247.8 48.5 %collective-permute-start.59 = (bf16[512,1024]{1,0:T(8,128)(2,1)S(1)}, bf16[512,1024]{1,0:T(8,128)(2,1)}, u32[]{:S(2)}, u32[]{:S(2)}) collective-permute-start(bf16[512,1024]{1,0:T(8,128)(2,1)S(1)} %copy-done.30), channel_id=1, source_target_pairs={{0,4},{4,0},{1,5},{5,1},{2,6},{6,2},{3,7},{7,3},{8,12},{12,8},{9,1... | collective-permute-start | bytes 3145736 | tf_op jit(solution)/shard_map/ppermute | solution.py:30
  250.6 11.2 %collective-permute-start.3 = (bf16[128,2048]{1,0:T(8,128)(2,1)S(1)}, bf16[128,2048]{1,0:T(8,128)(2,1)S(1)}, u32[]{:S(2)}, u32[]{:S(2)}) collective-permute-start(bf16[128,2048]{1,0:T(8,128)(2,1)S(1)} %pad_maximum_fusion.12), channel_id=1, source_target_pairs={{0,2},{2,0},{1,3},{3,1},{4,6},{6,4},{5,7},{7,5},{8,10},{10,8},{9,1... | collective-permute-start | bytes 1572872 | tf_op jit(solution)/shard_map/cond/branch_1_fun/ppermute | solution.py:30
  251.9 20.0 %collective-permute-start.4 = (bf16[128,2048]{1,0:T(8,128)(2,1)S(1)}, bf16[128,2048]{1,0:T(8,128)(2,1)S(1)}, u32[]{:S(2)}, u32[]{:S(2)}) collective-permute-start(bf16[128,2048]{1,0:T(8,128)(2,1)S(1)} %pad_maximum_fusion.13), channel_id=1, source_target_pairs={{0,8},{8,0},{1,9},{9,1},{2,10},{10,2},{3,11},{11,3},{4,12},{12,4},... | collective-permute-start | bytes 1572872 | tf_op jit(solution)/shard_map/cond/branch_1_fun/ppermute | solution.py:30
  278.2 37.4 %collective-permute-start.62 = (bf16[512,1024]{1,0:T(8,128)(2,1)}, bf16[512,1024]{1,0:T(8,128)(2,1)}, u32[]{:S(2)}, u32[]{:S(2)}) collective-permute-start(bf16[512,1024]{1,0:T(8,128)(2,1)} %constant_dynamic-slice_fusion.2), channel_id=1, source_target_pairs={{0,4},{4,0},{1,5},{5,1},{2,6},{6,2},{3,7},{7,3},{8,12},{12,8},{9,1... | collective-permute-start | bytes 3145736 | tf_op jit(solution)/shard_map/ppermute | solution.py:30
  330.8 14.8 %collective-permute-start.27 = (bf16[128,2048]{1,0:T(8,128)(2,1)S(1)}, bf16[128,2048]{1,0:T(8,128)(2,1)S(1)}, u32[]{:S(2)}, u32[]{:S(2)}) collective-permute-start(bf16[128,2048]{1,0:T(8,128)(2,1)S(1)} %pad_maximum_fusion.19), channel_id=1, source_target_pairs={{0,8},{8,0},{1,9},{9,1},{2,10},{10,2},{3,11},{11,3},{4,12},{12,4},... | collective-permute-start | bytes 1572872 | tf_op jit(solution)/shard_map/cond/branch_1_fun/ppermute | solution.py:30
  333.4 13.8 %collective-permute-start.29 = (bf16[128,2048]{1,0:T(8,128)(2,1)S(1)}, bf16[128,2048]{1,0:T(8,128)(2,1)S(1)}, u32[]{:S(2)}, u32[]{:S(2)}) collective-permute-start(bf16[128,2048]{1,0:T(8,128)(2,1)S(1)} %pad_maximum_fusion.20), channel_id=1, source_target_pairs={{0,2},{2,0},{1,3},{3,1},{4,6},{6,4},{5,7},{7,5},{8,10},{10,8},{9,1... | collective-permute-start | bytes 1572872 | tf_op jit(solution)/shard_map/cond/branch_1_fun/ppermute | solution.py:30
  345.8 7.9 %collective-permute-start.28 = (bf16[64,2048]{1,0:T(8,128)(2,1)S(1)}, bf16[64,2048]{1,0:T(8,128)(2,1)S(1)}, u32[]{:S(2)}, u32[]{:S(2)}) collective-permute-start(bf16[64,2048]{1,0:T(8,128)(2,1)S(1)} %slice.1477), channel_id=1, source_target_pairs={{0,2},{2,0},{1,3},{3,1},{4,6},{6,4},{5,7},{7,5},{8,10},{10,8},{9,1... | collective-permute-start | bytes 786440 | tf_op jit(solution)/shard_map/cond/branch_1_fun/ppermute | solution.py:30
  356.9 7.9 %collective-permute-start.31 = (bf16[64,2048]{1,0:T(8,128)(2,1)S(1)}, bf16[64,2048]{1,0:T(8,128)(2,1)S(1)}, u32[]{:S(2)}, u32[]{:S(2)}) collective-permute-start(bf16[64,2048]{1,0:T(8,128)(2,1)S(1)} %get-tuple-element.1211), channel_id=1, source_target_pairs={{0,2},{2,0},{1,3},{3,1},{4,6},{6,4},{5,7},{7,5},{8,10},{10,8},{9,1... | collective-permute-start | bytes 786440 | tf_op jit(solution)/shard_map/cond/branch_1_fun/ppermute | solution.py:30
  362.6 11.9 %collective-permute-start.33 = (bf16[128,2048]{1,0:T(8,128)(2,1)S(1)}, bf16[128,2048]{1,0:T(8,128)(2,1)S(1)}, u32[]{:S(2)}, u32[]{:S(2)}) collective-permute-start(bf16[128,2048]{1,0:T(8,128)(2,1)S(1)} %pad_maximum_fusion.21), channel_id=1, source_target_pairs={{0,2},{2,0},{1,3},{3,1},{4,6},{6,4},{5,7},{7,5},{8,10},{10,8},{9,1... | collective-permute-start | bytes 1572872 | tf_op jit(solution)/shard_map/cond/branch_1_fun/ppermute | solution.py:30
  364.9 11.1 %collective-permute-start.34 = (bf16[128,2048]{1,0:T(8,128)(2,1)S(1)}, bf16[128,2048]{1,0:T(8,128)(2,1)S(1)}, u32[]{:S(2)}, u32[]{:S(2)}) collective-permute-start(bf16[128,2048]{1,0:T(8,128)(2,1)S(1)} %pad_maximum_fusion.22), channel_id=1, source_target_pairs={{0,8},{8,0},{1,9},{9,1},{2,10},{10,2},{3,11},{11,3},{4,12},{12,4},... | collective-permute-start | bytes 1572872 | tf_op jit(solution)/shard_map/cond/branch_1_fun/ppermute | solution.py:30
  376.9 7.9 %collective-permute-start.35 = (bf16[512,2048]{1,0:T(8,128)(2,1)S(1)}, bf16[512,2048]{1,0:T(8,128)(2,1)S(1)}, u32[]{:S(2)}, u32[]{:S(2)}) collective-permute-start(bf16[512,2048]{1,0:T(8,128)(2,1)S(1)} %get-tuple-element.1208), channel_id=1, source_target_pairs={{0,1},{1,0},{2,3},{3,2},{4,5},{5,4},{6,7},{7,6},{8,9},{9,8},{10,11... | collective-permute-start | bytes 6291464 | tf_op jit(solution)/shard_map/cond/branch_1_fun/ppermute | solution.py:30
  390.5 27.4 %collective-permute-start.63 = (bf16[1024,512]{1,0:T(8,128)(2,1)}, bf16[1024,512]{1,0:T(8,128)(2,1)}, u32[]{:S(2)}, u32[]{:S(2)}) collective-permute-start(bf16[1024,512]{1,0:T(8,128)(2,1)} %get-tuple-element.791), channel_id=1, source_target_pairs={{0,4},{4,0},{1,5},{5,1},{2,6},{6,2},{3,7},{7,3},{8,12},{12,8},{9,1... | collective-permute-start | bytes 3145736 | tf_op jit(solution)/shard_map/ppermute | solution.py:30
  420.4 131.0 %reduce-scatter.9.cloned.1.call-start = ((), (), s32[]{:S(2)}) async-start(), calls=%async_computation.11 | async-start | bytes 1572864 | tf_op jit(solution)/shard_map/reduce_scatter | solution.py:269
  420.4 26.3 %collective-permute-start.65 = (bf16[1024,512]{1,0:T(8,128)(2,1)}, bf16[1024,512]{1,0:T(8,128)(2,1)}, u32[]{:S(2)}, u32[]{:S(2)}) collective-permute-start(bf16[1024,512]{1,0:T(8,128)(2,1)} %get-tuple-element.804), channel_id=1, source_target_pairs={{0,4},{4,0},{1,5},{5,1},{2,6},{6,2},{3,7},{7,3},{8,12},{12,8},{9,1... | collective-permute-start | bytes 3145736 | tf_op jit(solution)/shard_map/ppermute | solution.py:30
  421.6 75.3 %collective-permute-start.64 = (bf16[1024,1024]{1,0:T(8,128)(2,1)}, bf16[1024,1024]{1,0:T(8,128)(2,1)}, u32[]{:S(2)}, u32[]{:S(2)}) collective-permute-start(bf16[1024,1024]{1,0:T(8,128)(2,1)} %get-tuple-element.800), channel_id=1, source_target_pairs={{0,4},{4,0},{1,5},{5,1},{2,6},{6,2},{3,7},{7,3},{8,12},{12,8},{9,1... | collective-permute-start | bytes 6291464 | tf_op jit(solution)/shard_map/ppermute | solution.py:30
  432.0 10.5 %collective-permute-start.38 = (bf16[512,2048]{1,0:T(8,128)(2,1)S(1)}, bf16[512,2048]{1,0:T(8,128)(2,1)}, u32[]{:S(2)}, u32[]{:S(2)}) collective-permute-start(bf16[512,2048]{1,0:T(8,128)(2,1)S(1)} %convolution_add_fusion.1), channel_id=1, source_target_pairs={{0,1},{1,0},{2,3},{3,2},{4,5},{5,4},{6,7},{7,6},{8,9},{9,8},{10,11... | collective-permute-start | bytes 6291464 | tf_op jit(solution)/shard_map/cond/branch_1_fun/ppermute | solution.py:30
  449.3 154.0 %reduce-scatter.11.cloned.1.call-start = ((), (), s32[]{:S(2)}) async-start(), calls=%async_computation.12 | async-start | bytes 3145728 | tf_op jit(solution)/shard_map/reduce_scatter | solution.py:269
  452.2 19.5 %collective-permute-start.39 = (bf16[128,2048]{1,0:T(8,128)(2,1)S(1)}, bf16[128,2048]{1,0:T(8,128)(2,1)S(1)}, u32[]{:S(2)}, u32[]{:S(2)}) collective-permute-start(bf16[128,2048]{1,0:T(8,128)(2,1)S(1)} %pad_maximum_fusion.23), channel_id=1, source_target_pairs={{0,8},{8,0},{1,9},{9,1},{2,10},{10,2},{3,11},{11,3},{4,12},{12,4},... | collective-permute-start | bytes 1572872 | tf_op jit(solution)/shard_map/cond/branch_1_fun/ppermute | solution.py:30
  452.9 19.1 %collective-permute-start.40 = (bf16[128,2048]{1,0:T(8,128)(2,1)S(1)}, bf16[128,2048]{1,0:T(8,128)(2,1)S(1)}, u32[]{:S(2)}, u32[]{:S(2)}) collective-permute-start(bf16[128,2048]{1,0:T(8,128)(2,1)S(1)} %pad_maximum_fusion.24), channel_id=1, source_target_pairs={{0,2},{2,0},{1,3},{3,1},{4,6},{6,4},{5,7},{7,5},{8,10},{10,8},{9,1... | collective-permute-start | bytes 1572872 | tf_op jit(solution)/shard_map/cond/branch_1_fun/ppermute | solution.py:30
  471.9 8.8 %collective-permute-start.41 = (bf16[64,2048]{1,0:T(8,128)(2,1)S(1)}, bf16[64,2048]{1,0:T(8,128)(2,1)S(1)}, u32[]{:S(2)}, u32[]{:S(2)}) collective-permute-start(bf16[64,2048]{1,0:T(8,128)(2,1)S(1)} %slice.1479), channel_id=1, source_target_pairs={{0,2},{2,0},{1,3},{3,1},{4,6},{6,4},{5,7},{7,5},{8,10},{10,8},{9,1... | collective-permute-start | bytes 786440 | tf_op jit(solution)/shard_map/cond/branch_1_fun/ppermute | solution.py:30
  472.1 11.7 %collective-permute-start.42 = (bf16[64,2048]{1,0:T(8,128)(2,1)S(1)}, bf16[64,2048]{1,0:T(8,128)(2,1)S(1)}, u32[]{:S(2)}, u32[]{:S(2)}) collective-permute-start(bf16[64,2048]{1,0:T(8,128)(2,1)S(1)} %slice.1478), channel_id=1, source_target_pairs={{0,8},{8,0},{1,9},{9,1},{2,10},{10,2},{3,11},{11,3},{4,12},{12,4},... | collective-permute-start | bytes 786440 | tf_op jit(solution)/shard_map/cond/branch_1_fun/ppermute | solution.py:30
  489.0 7.8 %collective-permute-start.44 = (bf16[64,2048]{1,0:T(8,128)(2,1)}, bf16[64,2048]{1,0:T(8,128)(2,1)}, u32[]{:S(2)}, u32[]{:S(2)}) collective-permute-start(bf16[64,2048]{1,0:T(8,128)(2,1)} %get-tuple-element.1388), channel_id=1, source_target_pairs={{0,8},{8,0},{1,9},{9,1},{2,10},{10,2},{3,11},{11,3},{4,12},{12,4},... | collective-permute-start | bytes 786440 | tf_op jit(solution)/shard_map/cond/branch_1_fun/ppermute | solution.py:30
  501.7 140.7 %reduce-scatter.15.cloned.1.call-start = ((), (), s32[]{:S(2)}) async-start(), calls=%async_computation.14 | async-start | bytes 3145728 | tf_op jit(solution)/shard_map/reduce_scatter | solution.py:269
  501.7 49.6 %collective-permute-start.66 = (bf16[1024,1024]{1,0:T(8,128)(2,1)}, bf16[1024,1024]{1,0:T(8,128)(2,1)}, u32[]{:S(2)}, u32[]{:S(2)}) collective-permute-start(bf16[1024,1024]{1,0:T(8,128)(2,1)} %get-tuple-element.824), channel_id=1, source_target_pairs={{0,4},{4,0},{1,5},{5,1},{2,6},{6,2},{3,7},{7,3},{8,12},{12,8},{9,1... | collective-permute-start | bytes 6291464 | tf_op jit(solution)/shard_map/ppermute | solution.py:30
  503.6 9.5 %collective-permute-start.45 = (bf16[128,2048]{1,0:T(8,128)(2,1)S(1)}, bf16[128,2048]{1,0:T(8,128)(2,1)S(1)}, u32[]{:S(2)}, u32[]{:S(2)}) collective-permute-start(bf16[128,2048]{1,0:T(8,128)(2,1)S(1)} %pad_maximum_fusion.25), channel_id=1, source_target_pairs={{0,2},{2,0},{1,3},{3,1},{4,6},{6,4},{5,7},{7,5},{8,10},{10,8},{9,1... | collective-permute-start | bytes 1572872 | tf_op jit(solution)/shard_map/cond/branch_1_fun/ppermute | solution.py:30
  505.5 20.8 %collective-permute-start.46 = (bf16[128,2048]{1,0:T(8,128)(2,1)S(1)}, bf16[128,2048]{1,0:T(8,128)(2,1)S(1)}, u32[]{:S(2)}, u32[]{:S(2)}) collective-permute-start(bf16[128,2048]{1,0:T(8,128)(2,1)S(1)} %pad_maximum_fusion.26), channel_id=1, source_target_pairs={{0,8},{8,0},{1,9},{9,1},{2,10},{10,2},{3,11},{11,3},{4,12},{12,4},... | collective-permute-start | bytes 1572872 | tf_op jit(solution)/shard_map/cond/branch_1_fun/ppermute | solution.py:30
  555.9 133.4 %reduce-scatter.13.cloned.1.call-start = ((), (), s32[]{:S(2)}) async-start(), calls=%async_computation.13 | async-start | bytes 1572864 | tf_op jit(solution)/shard_map/reduce_scatter | solution.py:269
  559.4 8.5 %collective-permute-start.48 = (f32[2,2,2,2,128]{4,3,2,1,0:T(2,128)S(1)}, f32[2,2,2,2,128]{4,3,2,1,0:T(2,128)S(1)}, u32[]{:S(2)}, u32[]{:S(2)}) collective-permute-start(f32[2,2,2,2,128]{4,3,2,1,0:T(2,128)S(1)} %reshape.238), channel_id=1, source_target_pairs={{0,1},{1,0},{2,3},{3,2},{4,5},{5,4},{6,7},{7,6},{8,9},{9,8},{10,11... | collective-permute-start | bytes 24584 | tf_op jit(solution)/shard_map/cond/branch_1_fun/ppermute | solution.py:30
  578.6 24.7 %collective-permute-start.67 = (bf16[1024,512]{1,0:T(8,128)(2,1)}, bf16[1024,512]{1,0:T(8,128)(2,1)}, u32[]{:S(2)}, u32[]{:S(2)}) collective-permute-start(bf16[1024,512]{1,0:T(8,128)(2,1)} %copy.62), channel_id=1, source_target_pairs={{0,4},{4,0},{1,5},{5,1},{2,6},{6,2},{3,7},{7,3},{8,12},{12,8},{9,1... | collective-permute-start | bytes 3145736 | tf_op jit(solution)/shard_map/ppermute | solution.py:30
  607.3 81.9 %reduce-scatter.17.cloned.1.call-start = ((), (), s32[]{:S(2)}) async-start(), calls=%async_computation.15 | async-start | bytes 1572864 | tf_op jit(solution)/shard_map/reduce_scatter | solution.py:269
  607.4 35.0 %collective-permute-start.68 = (bf16[1024,512]{1,0:T(8,128)(2,1)}, bf16[1024,512]{1,0:T(8,128)(2,1)}, u32[]{:S(2)}, u32[]{:S(2)}) collective-permute-start(bf16[1024,512]{1,0:T(8,128)(2,1)} %get-tuple-element.858), channel_id=1, source_target_pairs={{0,4},{4,0},{1,5},{5,1},{2,6},{6,2},{3,7},{7,3},{8,12},{12,8},{9,1... | collective-permute-start | bytes 3145736 | tf_op jit(solution)/shard_map/ppermute | solution.py:30
  608.6 21.3 %collective-permute-start.69 = (bf16[256,1024]{1,0:T(8,128)(2,1)}, bf16[256,1024]{1,0:T(8,128)(2,1)}, u32[]{:S(2)}, u32[]{:S(2)}) collective-permute-start(bf16[256,1024]{1,0:T(8,128)(2,1)} %get-tuple-element.859), channel_id=1, source_target_pairs={{0,8},{8,0},{1,9},{9,1},{2,10},{10,2},{3,11},{11,3},{4,12},{12,4},... | collective-permute-start | bytes 1572872 | tf_op jit(solution)/shard_map/ppermute | solution.py:30
  610.6 31.8 %collective-permute-start.70 = (bf16[256,1024]{1,0:T(8,128)(2,1)}, bf16[256,1024]{1,0:T(8,128)(2,1)}, u32[]{:S(2)}, u32[]{:S(2)}) collective-permute-start(bf16[256,1024]{1,0:T(8,128)(2,1)} %slice_select_fusion.10), channel_id=1, source_target_pairs={{0,8},{8,0},{1,9},{9,1},{2,10},{10,2},{3,11},{11,3},{4,12},{12,4},... | collective-permute-start | bytes 1572872 | tf_op jit(solution)/shard_map/ppermute | solution.py:30
  619.5 10.4 %collective-permute-start.51 = (bf16[512,2048]{1,0:T(8,128)(2,1)}, bf16[512,2048]{1,0:T(8,128)(2,1)}, u32[]{:S(2)}, u32[]{:S(2)}) collective-permute-start(bf16[512,2048]{1,0:T(8,128)(2,1)} %convolution_convert_fusion.5), channel_id=1, source_target_pairs={{0,1},{1,0},{2,3},{3,2},{4,5},{5,4},{6,7},{7,6},{8,9},{9,8},{10,11... | collective-permute-start | bytes 6291464 | tf_op jit(solution)/shard_map/cond/branch_1_fun/ppermute | solution.py:30
  645.9 43.4 %collective-permute-start.71 = (bf16[256,1024]{1,0:T(8,128)(2,1)}, bf16[256,1024]{1,0:T(8,128)(2,1)}, u32[]{:S(2)}, u32[]{:S(2)}) collective-permute-start(bf16[256,1024]{1,0:T(8,128)(2,1)} %slice_select_fusion.9), channel_id=1, source_target_pairs={{0,8},{8,0},{1,9},{9,1},{2,10},{10,2},{3,11},{11,3},{4,12},{12,4},... | collective-permute-start | bytes 1572872 | tf_op jit(solution)/shard_map/ppermute | solution.py:30
  648.3 37.2 %collective-permute-start.19 = (f32[4,2048]{1,0:T(4,128)S(1)}, f32[4,2048]{1,0:T(4,128)S(1)}, u32[]{:S(2)}, u32[]{:S(2)}) collective-permute-start(f32[4,2048]{1,0:T(4,128)S(1)} %get-tuple-element.457), channel_id=1, source_target_pairs={{0,4},{4,0},{1,5},{5,1},{2,6},{6,2},{3,7},{7,3},{8,12},{12,8},{9,1... | collective-permute-start | bytes 98312 | tf_op jit(solution)/shard_map/cond/branch_1_fun/ppermute | solution.py:30
  655.7 25.8 %collective-permute-start.15 = (bf16[128,2048]{1,0:T(8,128)(2,1)}, bf16[128,2048]{1,0:T(8,128)(2,1)}, u32[]{:S(2)}, u32[]{:S(2)}) collective-permute-start(bf16[128,2048]{1,0:T(8,128)(2,1)} %pad_maximum_fusion.35), channel_id=1, source_target_pairs={{0,8},{8,0},{1,9},{9,1},{2,10},{10,2},{3,11},{11,3},{4,12},{12,4},... | collective-permute-start | bytes 1572872 | tf_op jit(solution)/shard_map/cond/branch_1_fun/ppermute | solution.py:30
  656.6 14.3 %collective-permute-start.16 = (bf16[128,2048]{1,0:T(8,128)(2,1)}, bf16[128,2048]{1,0:T(8,128)(2,1)}, u32[]{:S(2)}, u32[]{:S(2)}) collective-permute-start(bf16[128,2048]{1,0:T(8,128)(2,1)} %pad_maximum_fusion.36), channel_id=1, source_target_pairs={{0,2},{2,0},{1,3},{3,1},{4,6},{6,4},{5,7},{7,5},{8,10},{10,8},{9,1... | collective-permute-start | bytes 1572872 | tf_op jit(solution)/shard_map/cond/branch_1_fun/ppermute | solution.py:30
  672.1 14.4 %collective-permute-start.18 = (bf16[64,2048]{1,0:T(8,128)(2,1)S(1)}, bf16[64,2048]{1,0:T(8,128)(2,1)}, u32[]{:S(2)}, u32[]{:S(2)}) collective-permute-start(bf16[64,2048]{1,0:T(8,128)(2,1)S(1)} %slice.1480), channel_id=1, source_target_pairs={{0,8},{8,0},{1,9},{9,1},{2,10},{10,2},{3,11},{11,3},{4,12},{12,4},... | collective-permute-start | bytes 786440 | tf_op jit(solution)/shard_map/cond/branch_1_fun/ppermute | solution.py:30
  692.1 18.5 %collective-permute-start.73 = (bf16[256,512]{1,0:T(8,128)(2,1)}, bf16[256,512]{1,0:T(8,128)(2,1)}, u32[]{:S(2)}, u32[]{:S(2)}) collective-permute-start(bf16[256,512]{1,0:T(8,128)(2,1)} %broadcast_select_fusion.35), channel_id=1, source_target_pairs={{0,8},{8,0},{1,9},{9,1},{2,10},{10,2},{3,11},{11,3},{4,12},{12,4},... | collective-permute-start | bytes 786440 | tf_op jit(solution)/shard_map/ppermute | solution.py:30
  692.1 18.5 %collective-permute-start.72 = (bf16[256,512]{1,0:T(8,128)(2,1)S(1)}, bf16[256,512]{1,0:T(8,128)(2,1)}, u32[]{:S(2)}, u32[]{:S(2)}) collective-permute-start(bf16[256,512]{1,0:T(8,128)(2,1)S(1)} %broadcast_select_fusion.36), channel_id=1, source_target_pairs={{0,8},{8,0},{1,9},{9,1},{2,10},{10,2},{3,11},{11,3},{4,12},{12,4},... | collective-permute-start | bytes 786440 | tf_op jit(solution)/shard_map/ppermute | solution.py:30
  694.1 12.4 %collective-permute-start.5 = (f32[4,2048]{1,0:T(4,128)S(1)}, f32[4,2048]{1,0:T(4,128)S(1)}, u32[]{:S(2)}, u32[]{:S(2)}) collective-permute-start(f32[4,2048]{1,0:T(4,128)S(1)} %get-tuple-element.465), channel_id=1, source_target_pairs={{0,16},{16,0},{1,17},{17,1},{2,18},{18,2},{3,19},{19,3},{4,20},{20... | collective-permute-start | bytes 98312 | tf_op jit(solution)/shard_map/cond/branch_1_fun/ppermute | solution.py:30
  (97 other events, 831.3 us)
Sparse Core Ops, SparseCore 0:
  30.7 57.9 all-gather.4
  90.2 56.5 all-gather.6
  148.3 55.5 all-gather.10
  205.4 55.6 all-gather.8
  420.5 29.8 reduce-scatter.6
  452.6 31.6 reduce-scatter.8
  501.8 53.2 reduce-scatter.10
  558.0 54.2 reduce-scatter.14
  614.5 31.5 reduce-scatter.12
  648.9 30.4 reduce-scatter.16

commit v5 on v3

--- a/solution.py
+++ b/solution.py
@@ -315,10 +315,10 @@
     def scatter_begin(net, product, n_rows):
         half = n_rows // 2
         received = net.send(product(slice(half, None)).astype(BF16), core)
-        return product(slice(half)), received
+        return product(slice(half)).astype(BF16), received
 
     def scatter_second(net, state):
-        part = state[0] + state[1].astype(F32)
+        part = state[0].astype(F32) + state[1].astype(F32)
         half = part.shape[0] // 8
         a0, b0, a_side, b_side, a_col, b_col, a_both, b_both = (part[i * half : (i + 1) * half] for i in range(8))
         received = (

time: 734 us -> 736 us (level)
  transfers between devices with their start and end apart: 84 -> 84, of which waited for: 37 -> 39; matrix products, arithmetic and copies ran while one was open for 44% -> 43% of each run, Pallas kernels for 3% -> 3%
where the time goes in v5:
time: 736 us; the launch traced here: 725 us
  waiting for transfers between devices  249 us (34%)
  matrix products  143 us (19%)
  other arithmetic  125 us (17%)
  local copies, waits for them, and re-layouts  90 us (12%)
  starting transfers between devices  78.3 us (11%)
  Pallas kernels  21.2 us (3%)
  between operations  15.6 us (2%)
    ppermute x74, waiting for transfers between devices, swap(): return lax.ppermute(values, axis, [(0, 1), (1, 0)])  247 us
    ppermute x74, starting transfers between devices, swap(): return lax.ppermute(values, axis, [(0, 1), (1, 0)])  77.9 us
    dot_general x14, matrix products, contract_rows(): lax.dot_general(left, right, (((0,), (0,)), ((), ())), preferred_element_...  57.4 us
    dot_general x8, matrix products, dot_rows_cols(): return jnp.dot(left, right, preferred_element_type=F32)  45 us
    cond x140, local copies, waits for them, and re-layouts  43.2 us
    dot_general x10, matrix products, contract_cols(): lax.dot_general(left, right, (((1,), (1,)), ((), ())), preferred_element_...  40.5 us
    select_n x21, other arithmetic, pick(): return jnp.where(flag, yes, no)  25.5 us
    pallas_call x2, Pallas kernels, attention(): pl.pallas_call(kernel, grid=(2, n_heads), in_specs=in_specs, out_specs=ou...  21.2 us
  transfers between devices with their start and end apart: 84, of which 39 were waited for; matrix products, arithmetic and copies ran while one was open for 43% of the time, Pallas kernels for 3%

profile of v5, /device:TPU:0, one launch (start us, length us, event | category | flops | bytes accessed | tf_op | source)
XLA Modules:
  0.0 725.5 jit_solution(17320483778638088704)
XLA Ops:
  9.1 21.4 %conditional.18 = (bf16[512,1024]{1,0:T(8,128)(2,1)}, bf16[256,1024]{1,0:T(8,128)(2,1)}, bf16[256,1024]{1,0:T(8,128)(2,1)}, bf16[128,2048]{1,0:T(8,128)(2,1)S(1)}) conditional(s32[]{:T(128)} %bitcast.58, () %tuple.183, (bf16[256,512]{1,0:T(8,128)(2,1)}, bf16[256,512]{1,0:T(8,128)(2,1)}, bf16[256,512]{1,0:T(8,128)(2,1)}, bf16[256,512]{1,0:T(8,128)(2,1)}, ...), branch_computations={%region_0.0_spmd, %region_1.2_spmd} | conditional | flops 12058631 | bytes 35127872 | solution.py:48
  17.1 10.9 %collective-permute-done.5 = bf16[256,1024]{1,0:T(8,128)(2,1)} collective-permute-done((bf16[256,1024]{1,0:T(8,128)(2,1)}, bf16[256,1024]{1,0:T(8,128)(2,1)}, u32[]{:S(2)}, u32[]{:S(2)}) %collective-permute-start.5) | collective-permute-done | bytes 524320 | tf_op jit(solution)/shard_map/cond/branch_1_fun/ppermute | solution.py:30
  32.3 54.7 %conditional.19 = (bf16[64,2048]{1,0:T(8,128)(2,1)S(1)}, bf16[64,2048]{1,0:T(8,128)(2,1)S(1)}, bf16[64,2048]{1,0:T(8,128)(2,1)S(1)}, bf16[64,2048]{1,0:T(8,128)(...) conditional(s32[]{:T(128)} %bitcast.58, () %tuple.185, ...), branch_computations={%region_2.3_spmd, %region_3.4_spmd} | conditional | flops 4982795 | bytes 32563916 | solution.py:48
  45.0 21.5 %collective-permute-done.8 = bf16[256,1024]{1,0:T(8,128)(2,1)S(1)} collective-permute-done((bf16[256,1024]{1,0:T(8,128)(2,1)}, bf16[256,1024]{1,0:T(8,128)(2,1)S(1)}, u32[]{:S(2)}, u32[]{:S(2)}) %collective-permute-start.8) | collective-permute-done | bytes 524320 | tf_op jit(solution)/shard_map/cond/branch_1_fun/ppermute | solution.py:30
  68.3 15.8 %collective-permute-done.10 = bf16[128,2048]{1,0:T(8,128)(2,1)} collective-permute-done((bf16[128,2048]{1,0:T(8,128)(2,1)S(1)}, bf16[128,2048]{1,0:T(8,128)(2,1)}, u32[]{:S(2)}, u32[]{:S(2)}) %collective-permute-start.10) | collective-permute-done | bytes 524320 | tf_op jit(solution)/shard_map/cond/branch_1_fun/ppermute | solution.py:30
  94.1 15.5 %conditional.20 = (bf16[1024,2048]{1,0:T(8,128)(2,1)}, f32[1024,128]{1,0:T(8,128)}, f32[1024,128]{1,0:T(8,128)}, f32[2,512,512]{2,1,0:T(8,128)S(1)}, f32[256]{0:...) conditional(s32[]{:T(128)} %bitcast.58, () %tuple.188, ...), branch_computations={%region_4.5_spmd, %region_5.6_spmd} | conditional | flops 2892172 | bytes 27435296 | solution.py:48
  112.3 4.0 collective-permute-done.55
  120.3 32.0 %conditional.21 = (bf16[1024,1024]{1,0:T(8,128)(2,1)}, bf16[1024,1024]{1,0:T(8,128)(2,1)}, f32[1024,768]{1,0:T(8,128)S(1)}, f32[2,1024]{1,0:T(2,128)S(1)}, bf16[2048,256]{1,0:T(8,128)(2,1)}) conditional(s32[]{:T(128)} %bitcast.58, () %tuple.191, (bf16[512,1024]{1,0:T(8,128)(2,1)}, bf16[512,1024]{1,0:T(8,128)(2,1)}, bf16[1024,2048]{1,0:T(8,128)(2,1)}, ...), branch_computations={%region_6.7_spmd, %region_7.10_spmd} | conditional | flops 3234607104 | bytes 71541024 | solution.py:48
  131.9 14.7 %collective-permute-done.1 = f32[2,2,2,2,128]{4,3,2,1,0:T(2,128)S(1)} collective-permute-done((f32[2,2,2,2,128]{4,3,2,1,0:T(2,128)S(1)}, f32[2,2,2,2,128]{4,3,2,1,0:T(2,128)S(1)}, u32[]{:S(2)}, u32[]{:S(2)}) %collective-permute-start.1) | collective-permute-done | bytes 8224 | tf_op jit(solution)/shard_map/cond/branch_1_fun/ppermute | solution.py:30
  154.0 18.2 %conditional.22 = (bf16[1024,256]{1,0:T(8,128)(2,1)}, f32[1024,2]{1,0:T(8,128)}, bf16[512,2048]{1,0:T(8,128)(2,1)}, bf16[512,2048]{1,0:T(8,128)(2,1)}) conditional(s32[]{:T(128)} %bitcast.58, () %tuple.194, (f32[1024,768]{1,0:T(8,128)S(1)}, f32[2,1024]{1,0:T(2,128)S(1)}, f32[256]{0:T(256)S(1)}, f32[256]{0:T(256)S(1)}, f32[1024,128]{1,0:T(8,128)}, ...), branch_computations={%region_10.11_spmd, %region_11.12_spmd} | conditional | flops 2149584896 | bytes 24682568 | solution.py:48
  157.1 7.6 %branch_1_fun.2 = bf16[2,2,256,256]{3,2,1,0:T(8,128)(2,1)} custom-call(f32[2,2,256,768]{3,2,1,0:T(8,128)S(1)} %bitcast.109, f32[2,2,256,768]{3,2,1,0:T(8,128)S(1)} %bitcast.110, f32[2,2,256,768]{3,2,1,0:T(8,128)S(1)} %bitcast.111, f32[2,2,256,2]{3,2,1,0:T(8,128)S(1)} %bitcast.107, f32[1,256]{1,0:T(1,128)S(1)} %bitcast.149, f32[1,256]{1,0:T(1,128)S(1)} %bitcast.146, ...), custom_call_target="tpu_custom_call" | custom-call | flops 1073741824 | bytes 8388608 | tf_op jit(solution)/shard_map/cond/branch_1_fun/pallas_call | solution.py:222
  176.9 67.6 %conditional.23 = (f32[128,1]{0,1:T(1,128)S(1)}, f32[128,2048]{1,0:T(8,128)}, f32[128,2048]{1,0:T(8,128)}, bf16[64,2048]{1,0:T(8,128)(2,1)}, bf16[64,2048]{1,0:T...) conditional(s32[]{:T(128)} %bitcast.58, () %tuple.197, (bf16[512,2048]{1,0:T(8,128)(2,1)}, ...), branch_computations={%region_12.13_spmd, %region_13.15_spmd} | conditional | flops 10748032 | bytes 42478376 | solution.py:48
  181.6 32.1 %collective-permute-done.18 = bf16[128,2048]{1,0:T(8,128)(2,1)S(1)} collective-permute-done((bf16[128,2048]{1,0:T(8,128)(2,1)S(1)}, bf16[128,2048]{1,0:T(8,128)(2,1)S(1)}, u32[]{:S(2)}, u32[]{:S(2)}) %collective-permute-start.18) | collective-permute-done | bytes 524320 | tf_op jit(solution)/shard_map/cond/branch_1_fun/ppermute | solution.py:30
  215.8 5.5 collective-permute-done.19
  221.4 6.2 collective-permute-done.21
  233.0 11.5 %collective-permute-done.23 = bf16[64,2048]{1,0:T(8,128)(2,1)} collective-permute-done((bf16[64,2048]{1,0:T(8,128)(2,1)}, bf16[64,2048]{1,0:T(8,128)(2,1)}, u32[]{:S(2)}, u32[]{:S(2)}) %collective-permute-start.23) | collective-permute-done | bytes 262176 | tf_op jit(solution)/shard_map/cond/branch_1_fun/ppermute | solution.py:30
  248.4 41.3 %conditional.24 = (bf16[1024,2048]{1,0:T(8,128)(2,1)}, f32[1024,1024]{1,0:T(8,128)}) conditional(s32[]{:T(128)} %bitcast.58, () %tuple.200, (bf16[64,2048]{1,0:T(8,128)(2,1)}, bf16[64,2048]{1,0:T(8,128)(2,1)}, bf16[64,2048]{1,0:T(8,128)(2,1)}, bf16[64,2048]{1,0:T(8,128)(2,1)}, bf16[1024,1024]{1,0:T(8,128)(2,1)S(1)}, ...), branch_computations={%region_15.16_spmd, %region_16.17_spmd} | conditional | flops 4298113024 | bytes 47448200 | solution.py:48
  260.8 11.0 %collective-permute-done.36 = bf16[128,2048]{1,0:T(8,128)(2,1)S(1)} collective-permute-done((bf16[128,2048]{1,0:T(8,128)(2,1)S(1)}, bf16[128,2048]{1,0:T(8,128)(2,1)S(1)}, u32[]{:S(2)}, u32[]{:S(2)}) %collective-permute-start.36) | collective-permute-done | bytes 524320 | tf_op jit(solution)/shard_map/cond/branch_1_fun/ppermute | solution.py:30
  279.2 4.5 fusion.30
  283.8 5.9 fusion.34
  293.8 17.4 %conditional.25 = (f32[1024,1024]{1,0:T(8,128)}, bf16[1024,1024]{1,0:T(8,128)(2,1)}, bf16[1024,1024]{1,0:T(8,128)(2,1)S(1)}, bf16[1024,1024]{1,0:T(8,128)(2,1)}) conditional(s32[]{:T(128)} %bitcast.58, () %tuple.203, (bf16[1024,2048]{1,0:T(8,128)(2,1)}, bf16[1024,1024]{1,0:T(8,128)(2,1)}, bf16[512,1024]{1,0:T(8,128)(2,1)}, ...), branch_computations={%region_17.18_spmd, %region_18.19_spmd} | conditional | flops 4307550208 | bytes 48234596 | solution.py:48
  298.5 3.9 fusion.38
  302.4 8.9 %multiply_convert_fusion = (bf16[1024,1024]{1,0:T(8,128)(2,1)}, f32[1024,1024]{1,0:T(8,128)}) fusion(f32[1024,1024]{1,0:T(8,128)} %get-tuple-element.340, f32[1024,1024]{1,0:T(8,128)S(1)} %fusion.38, bf16[1024,1024]{1,0:T(8,128)(2,1)} %pad_maximum_fusion.14, bf16[1024,2048]{1,0:T(8,128)(2,1)} %get-tuple-element.336), kind=kOutput, calls=%fused_computation.170 | convolution fusion | flops 2154823680 | bytes 18874368 | tf_op jit(solution)/shard_map/cond/branch_1_fun/dot_general | solution.py:18
  311.3 6.7 collective-permute-done.62
  317.9 73.3 %conditional.26 = (bf16[2048,1024]{1,0:T(8,128)(2,1)S(1)}, f32[128,2048]{1,0:T(8,128)S(1)}, bf16[1024,2048]{1,0:T(8,128)(2,1)}, bf16[1024,512]{1,0:T(8,128)(2,1)...) conditional(s32[]{:T(128)} %bitcast.58, () %tuple.182, (bf16[512,1024]{1,0:T(8,128)(2,1)}, ...), branch_computations={%region_19.20_spmd, %region_20.23_spmd} | conditional | flops 5415632896 | bytes 181687440 | solution.py:48
  320.8 4.4 fusion.40
  325.3 4.1 collective-permute-done.24
  335.1 12.2 %collective-permute-done.25 = bf16[128,2048]{1,0:T(8,128)(2,1)S(1)} collective-permute-done((bf16[128,2048]{1,0:T(8,128)(2,1)S(1)}, bf16[128,2048]{1,0:T(8,128)(2,1)S(1)}, u32[]{:S(2)}, u32[]{:S(2)}) %collective-permute-start.25) | collective-permute-done | bytes 524320 | tf_op jit(solution)/shard_map/cond/branch_1_fun/ppermute | solution.py:30
  349.5 5.5 collective-permute-done.26
  359.5 4.8 collective-permute-done.30
  368.1 8.1 %collective-permute-done.31 = bf16[128,2048]{1,0:T(8,128)(2,1)S(1)} collective-permute-done((bf16[128,2048]{1,0:T(8,128)(2,1)S(1)}, bf16[128,2048]{1,0:T(8,128)(2,1)S(1)}, u32[]{:S(2)}, u32[]{:S(2)}) %collective-permute-start.31) | collective-permute-done | bytes 524320 | tf_op jit(solution)/shard_map/cond/branch_1_fun/ppermute | solution.py:30
  377.3 5.3 pad_maximum_fusion.16
  386.9 4.2 fusion.43
  392.8 26.4 %conditional.27 = (bf16[1024,512]{1,0:T(8,128)(2,1)S(1)}, bf16[1024,1024]{1,0:T(8,128)(2,1)}, bf16[1024,1024]{1,0:T(8,128)(2,1)}, bf16[1024,512]{1,0:T(8,128)(2,1)}, bf16[1024,1024]{1,0:T(8,128)(2,1)}) conditional(s32[]{:T(128)} %bitcast.58, () %tuple.207, (bf16[1024,2048]{1,0:T(8,128)(2,1)}, bf16[1024,1024]{1,0:T(8,128)(2,1)}, ...), branch_computations={%region_23.24_spmd, %region_24.25_spmd} | conditional | flops 8605663232 | bytes 69206112 | solution.py:48
  398.2 10.9 %multiply_convert_fusion.2 = (bf16[1024,1024]{1,0:T(8,128)(2,1)}, bf16[1024,1024]{1,0:T(8,128)(2,1)}) fusion(f32[1024,1024]{1,0:T(8,128)} %get-tuple-element.357, f32[1024,1024]{1,0:T(8,128)} %get-tuple-element.356, bf16[1024,2048]{1,0:T(8,128)(2,1)} %get-tuple-element.358, bf16[2048,1024]{1,0:T(8,128)(2,1)S(1)} %copy-done.26), kind=kOutput, calls=%fused_computation.224 | convolution fusion | flops 4308598784 | bytes 20971520 | tf_op jit(solution)/shard_map/cond/branch_1_fun/dot_general | solution.py:18
  409.1 4.1 fusion.62
  413.2 5.9 fusion.56
  423.8 20.0 %conditional.28 = (bf16[1024,512]{1,0:T(8,128)(2,1)S(1)}, bf16[512,2048]{1,0:T(8,128)(2,1)S(1)}, bf16[512,2048]{1,0:T(8,128)(2,1)}) conditional(s32[]{:T(128)} %bitcast.58, () %tuple.211, (bf16[1024,1024]{1,0:T(8,128)(2,1)}, bf16[2048,1024]{1,0:T(8,128)(2,1)}, bf16[1024,1024]{1,0:T(8,128)(2,1)}, bf16[2048,1024]{1,0:T(8,128)(2,1)}, ...), branch_computations={%region_26.27_spmd, %region_27.28_spmd} | conditional | flops 9668395008 | bytes 88080504 | solution.py:48
  424.2 5.4 fusion.77
  429.6 3.8 convolution_add_fusion.1
  437.1 3.6 convolution_add_fusion
  443.8 4.3 collective-permute-done.65
  450.6 48.1 %conditional.29 = (bf16[1024,1024]{1,0:T(8,128)(2,1)}, bf16[1024,1024]{1,0:T(8,128)(2,1)}, bf16[1024,1024]{1,0:T(8,128)(2,1)}, f32[128,2048]{1,0:T(8,128)}, bf16...) conditional(s32[]{:T(128)} %bitcast.58, () %tuple.210, ...), branch_computations={%region_28.29_spmd, %region_29.32_spmd} | conditional | flops 6457128960 | bytes 62942008 | solution.py:48
  456.5 6.0 fusion.85
  462.6 9.9 %collective-permute-done.39 = bf16[128,2048]{1,0:T(8,128)(2,1)S(1)} collective-permute-done((bf16[128,2048]{1,0:T(8,128)(2,1)S(1)}, bf16[128,2048]{1,0:T(8,128)(2,1)S(1)}, u32[]{:S(2)}, u32[]{:S(2)}) %collective-permute-start.39) | collective-permute-done | bytes 524320 | tf_op jit(solution)/shard_map/cond/branch_1_fun/ppermute | solution.py:30
  477.7 6.0 fusion.88
  492.1 5.9 fusion.91
  498.8 4.8 add_convert_fusion.2
  504.6 48.7 %conditional.30 = (bf16[1024,2048]{1,0:T(8,128)(2,1)}, f32[1024,256]{1,0:T(8,128)}, f32[1024,256]{1,0:T(8,128)}, bf16[1024,256]{1,0:T(8,128)(2,1)}, f32[2,2,2,256,2]{4,3,2,1,0:T(8,128)}, /*index=5*/f32[2,256]{1,0:T(2,128)S(1)}) conditional(s32[]{:T(128)} %bitcast.58, () %tuple.216, (bf16[64,2048]{1,0:T(8,128)(2,1)}, bf16[64,2048]{1,0:T(8,128)(2,1)}, ...), branch_computations={%region_33.34_spmd, %region_34.36_spmd} | conditional | flops 2149843456 | bytes 49027272 | solution.py:48
  515.7 12.6 %collective-permute-done.46 = bf16[128,2048]{1,0:T(8,128)(2,1)S(1)} collective-permute-done((bf16[128,2048]{1,0:T(8,128)(2,1)S(1)}, bf16[128,2048]{1,0:T(8,128)(2,1)S(1)}, u32[]{:S(2)}, u32[]{:S(2)}) %collective-permute-start.46) | collective-permute-done | bytes 524320 | tf_op jit(solution)/shard_map/cond/branch_1_fun/ppermute | solution.py:30
  535.7 3.9 convolution_convert_fusion.4
  539.6 13.6 %branch_1_fun.3 = (f32[2,2,256,256]{3,2,1,0:T(8,128)}, f32[2,2,256,256]{3,2,1,0:T(8,128)}, bf16[2,2,256,256]{3,2,1,0:T(8,128)(2,1)}, f32[2,2,2,256,2]{4,3,2,1,0:T(8,128)}, f32[2,2,256]{2,1,0:T(2,128)S(1)}) custom-call(f32[2,2,256,768]{3,2,1,0:T(8,128)S(1)} %bitcast.112, f32[2,2,256,768]{3,2,1,0:T(8,128)S(1)} %bitcast.113, f32[2,2,256,768]{3,2,1,0:T(8,128)S(1)} %bitcast.114, ...), custom_call_target="tpu_custom_call" | custom-call | flops 1073741824 | bytes 8388608 | tf_op jit(solution)/shard_map/cond/branch_1_fun/pallas_call | solution.py:222
  553.3 4.5 add_convert_fusion.1
  557.9 20.4 %conditional.31 = (f32[2,1024]{1,0:T(2,128)S(1)}, bf16[1024,512]{0,1:T(8,128)(2,1)}, bf16[512,1024]{1,0:T(8,128)(2,1)}, bf16[256,1024]{1,0:T(8,128)(2,1)}) conditional(s32[]{:T(128)} %bitcast.58, () %tuple.181, (f32[2,2,2,256,2]{4,3,2,1,0:T(8,128)}, bf16[1024,2048]{1,0:T(8,128)(2,1)}, bf16[1024,256]{1,0:T(8,128)(2,1)}, ...), branch_computations={%region_36.37_spmd, %region_37.39_spmd} | conditional | flops 1076633600 | bytes 16515326 | solution.py:48
  581.8 21.3 %conditional.32 = (bf16[1024,512]{1,0:T(8,128)(2,1)}, bf16[1024,512]{0,1:T(8,128)(2,1)}, bf16[1024,512]{1,0:T(8,128)(2,1)}, bf16[2048,768]{1,0:T(8,128)(2,1)}) conditional(s32[]{:T(128)} %bitcast.58, () %tuple.220, (f32[1024,2]{1,0:T(8,128)}, bf16[1024,2048]{1,0:T(8,128)(2,1)}, bf16[1024,256]{1,0:T(8,128)(2,1)}, bf16[1024,2048]{1,0:T(8,128)(2,1)}, ...), branch_computations={%region_40.41_spmd, %region_41.42_spmd} | conditional | flops 2162165760 | bytes 38881340 | solution.py:48
  593.8 4.1 fusion.111
  613.5 18.4 %conditional.33 = (bf16[1024,512]{1,0:T(8,128)(2,1)S(1)}, bf16[512,2048]{1,0:T(8,128)(2,1)}, bf16[512,2048]{1,0:T(8,128)(2,1)}, f32[4,2048]{1,0:T(4,128)S(1)}) conditional(s32[]{:T(128)} %bitcast.58, () %tuple.223, (bf16[1024,2048]{1,0:T(8,128)(2,1)}, bf16[1024,512]{1,0:T(8,128)(2,1)}, bf16[1024,256]{1,0:T(8,128)(2,1)}, ...), branch_computations={%region_44.45_spmd, %region_45.47_spmd} | conditional | flops 4298155520 | bytes 36880644 | solution.py:48
  615.9 5.6 convolution_convert_fusion.5
  623.2 5.3 convolution_convert_fusion.6
  632.0 13.0 %collective-permute-done.70 = bf16[256,1024]{1,0:T(8,128)(2,1)} collective-permute-done((bf16[256,1024]{1,0:T(8,128)(2,1)}, bf16[256,1024]{1,0:T(8,128)(2,1)}, u32[]{:S(2)}, u32[]{:S(2)}) %collective-permute-start.70) | collective-permute-done | bytes 524320 | tf_op jit(solution)/shard_map/ppermute | solution.py:30
  650.9 41.2 %conditional.34 = (f32[64,2048]{1,0:T(8,128)}, f32[64,2048]{1,0:T(8,128)S(1)}, bf16[64,2048]{1,0:T(8,128)(2,1)}, bf16[64,2048]{1,0:T(8,128)(2,1)}, f32[256,2048]...) conditional(s32[]{:T(128)} %bitcast.58, () %tuple.226, ...), branch_computations={%region_48.49_spmd, %region_49.50_spmd} | conditional | flops 12591111 | bytes 64201160 | solution.py:48
  651.5 5.1 fusion.135
  676.2 8.1 %collective-permute-done.13 = bf16[128,2048]{1,0:T(8,128)(2,1)} collective-permute-done((bf16[128,2048]{1,0:T(8,128)(2,1)}, bf16[128,2048]{1,0:T(8,128)(2,1)}, u32[]{:S(2)}, u32[]{:S(2)}) %collective-permute-start.13) | collective-permute-done | bytes 524320 | tf_op jit(solution)/shard_map/cond/branch_1_fun/ppermute | solution.py:30
  696.9 16.0 %conditional.35 = (f32[128,2048]{1,0:T(8,128)}, f32[256,2048]{1,0:T(8,128)}, f32[4,2048]{1,0:T(4,128)S(1)}) conditional(s32[]{:T(128)} %bitcast.58, () %tuple.229, (bf16[64,2048]{1,0:T(8,128)(2,1)}, f32[64,2048]{1,0:T(8,128)}, bf16[64,2048]{1,0:T(8,128)(2,1)}, f32[64,2048]{1,0:T(8,128)S(1)}, f32[128,2048]{1,0:T(8,128)}, ...), branch_computations={%region_50.51_spmd, %region_51.52_spmd} | conditional | flops 3162119 | bytes 17236164 | solution.py:48
  (598 shorter events, 340.6 us)
Async XLA Ops:
  7.2 81.5 %all-gather.5.cloned.1.call-start = ((), (), s32[]{:S(2)}) async-start(), calls=%async_computation.6 | async-start | bytes 3145728 | tf_op jit(solution)/shard_map/all_gather | solution.py:258
  12.7 15.3 %collective-permute-start.5 = (bf16[256,1024]{1,0:T(8,128)(2,1)}, bf16[256,1024]{1,0:T(8,128)(2,1)}, u32[]{:S(2)}, u32[]{:S(2)}) collective-permute-start(bf16[256,1024]{1,0:T(8,128)(2,1)} %broadcast_select_fusion.2), channel_id=1, source_target_pairs={{0,8},{8,0},{1,9},{9,1},{2,10},{10,2},{3,11},{11,3},{4,12},{12,4},... | collective-permute-start | bytes 1572872 | tf_op jit(solution)/shard_map/cond/branch_1_fun/ppermute | solution.py:30
  30.5 141.6 %all-gather.7.cloned.1.call-start = ((), (), s32[]{:S(2)}) async-start(), calls=%async_computation.7 | async-start | bytes 3145728 | tf_op jit(solution)/shard_map/all_gather | solution.py:258
  30.6 56.5 %collective-permute-start.54 = (bf16[512,1024]{1,0:T(8,128)(2,1)}, bf16[512,1024]{1,0:T(8,128)(2,1)}, u32[]{:S(2)}, u32[]{:S(2)}) collective-permute-start(bf16[512,1024]{1,0:T(8,128)(2,1)} %get-tuple-element.686), channel_id=1, source_target_pairs={{0,4},{4,0},{1,5},{5,1},{2,6},{6,2},{3,7},{7,3},{8,12},{12,8},{9,1... | collective-permute-start | bytes 3145736 | tf_op jit(solution)/shard_map/ppermute | solution.py:30
  35.6 7.6 %collective-permute-start.11 = (s32[8,128]{1,0:T(8,128)S(1)}, s32[8,128]{1,0:T(8,128)S(1)}, u32[]{:S(2)}, u32[]{:S(2)}) collective-permute-start(s32[8,128]{1,0:T(8,128)S(1)} %concatenate.170), channel_id=1, source_target_pairs={{0,8},{8,0},{1,9},{9,1},{2,10},{10,2},{3,11},{11,3},{4,12},{12,4},... | collective-permute-start | bytes 12296 | tf_op jit(solution)/shard_map/cond/branch_1_fun/ppermute | solution.py:30
  40.7 25.8 %collective-permute-start.8 = (bf16[256,1024]{1,0:T(8,128)(2,1)}, bf16[256,1024]{1,0:T(8,128)(2,1)S(1)}, u32[]{:S(2)}, u32[]{:S(2)}) collective-permute-start(bf16[256,1024]{1,0:T(8,128)(2,1)} %get-tuple-element.295), channel_id=1, source_target_pairs={{0,8},{8,0},{1,9},{9,1},{2,10},{10,2},{3,11},{11,3},{4,12},{12,4},... | collective-permute-start | bytes 1572872 | tf_op jit(solution)/shard_map/cond/branch_1_fun/ppermute | solution.py:30
  43.4 40.8 %collective-permute-start.10 = (bf16[128,2048]{1,0:T(8,128)(2,1)S(1)}, bf16[128,2048]{1,0:T(8,128)(2,1)}, u32[]{:S(2)}, u32[]{:S(2)}) collective-permute-start(bf16[128,2048]{1,0:T(8,128)(2,1)S(1)} %pad_maximum_fusion.5), channel_id=1, source_target_pairs={{0,8},{8,0},{1,9},{9,1},{2,10},{10,2},{3,11},{11,3},{4,12},{12,4},... | collective-permute-start | bytes 1572872 | tf_op jit(solution)/shard_map/cond/branch_1_fun/ppermute | solution.py:30
  66.5 18.7 %collective-permute-start.9 = (bf16[128,2048]{1,0:T(8,128)(2,1)S(1)}, bf16[128,2048]{1,0:T(8,128)(2,1)}, u32[]{:S(2)}, u32[]{:S(2)}) collective-permute-start(bf16[128,2048]{1,0:T(8,128)(2,1)S(1)} %pad_maximum_fusion.4), channel_id=1, source_target_pairs={{0,2},{2,0},{1,3},{3,1},{4,6},{6,4},{5,7},{7,5},{8,10},{10,8},{9,1... | collective-permute-start | bytes 1572872 | tf_op jit(solution)/shard_map/cond/branch_1_fun/ppermute | solution.py:30
  88.7 155.8 %all-gather.9.cloned.1.call-start = ((), (), s32[]{:S(2)}) async-start(), calls=%async_computation.8 | async-start | bytes 3145728 | tf_op jit(solution)/shard_map/all_gather | solution.py:258
  91.0 25.2 %collective-permute-start.55 = (bf16[512,1024]{1,0:T(8,128)(2,1)}, bf16[512,1024]{1,0:T(8,128)(2,1)}, u32[]{:S(2)}, u32[]{:S(2)}) collective-permute-start(bf16[512,1024]{1,0:T(8,128)(2,1)} %constant_dynamic-slice_fusion.4), channel_id=1, source_target_pairs={{0,4},{4,0},{1,5},{5,1},{2,6},{6,2},{3,7},{7,3},{8,12},{12,8},{9,1... | collective-permute-start | bytes 3145736 | tf_op jit(solution)/shard_map/ppermute | solution.py:30
  92.5 19.8 %collective-permute-start.56 = (bf16[256,1024]{1,0:T(8,128)(2,1)}, bf16[256,1024]{1,0:T(8,128)(2,1)}, u32[]{:S(2)}, u32[]{:S(2)}) collective-permute-start(bf16[256,1024]{1,0:T(8,128)(2,1)} %get-tuple-element.702), channel_id=1, source_target_pairs={{0,8},{8,0},{1,9},{9,1},{2,10},{10,2},{3,11},{11,3},{4,12},{12,4},... | collective-permute-start | bytes 1572872 | tf_op jit(solution)/shard_map/ppermute | solution.py:30
  118.7 53.4 %collective-permute-start.57 = (bf16[512,1024]{1,0:T(8,128)(2,1)}, bf16[512,1024]{1,0:T(8,128)(2,1)}, u32[]{:S(2)}, u32[]{:S(2)}) collective-permute-start(bf16[512,1024]{1,0:T(8,128)(2,1)} %pad_maximum_fusion.38), channel_id=1, source_target_pairs={{0,4},{4,0},{1,5},{5,1},{2,6},{6,2},{3,7},{7,3},{8,12},{12,8},{9,1... | collective-permute-start | bytes 3145736 | tf_op jit(solution)/shard_map/ppermute | solution.py:30
  120.3 169.4 %all-gather.11.cloned.1.call-start = ((), (), s32[]{:S(2)}) async-start(), calls=%async_computation.9 | async-start | bytes 3145728 | tf_op jit(solution)/shard_map/all_gather | solution.py:258
  130.8 15.8 %collective-permute-start.1 = (f32[2,2,2,2,128]{4,3,2,1,0:T(2,128)S(1)}, f32[2,2,2,2,128]{4,3,2,1,0:T(2,128)S(1)}, u32[]{:S(2)}, u32[]{:S(2)}) collective-permute-start(f32[2,2,2,2,128]{4,3,2,1,0:T(2,128)S(1)} %reverse_add_fusion.1), channel_id=1, source_target_pairs={{0,8},{8,0},{1,9},{9,1},{2,10},{10,2},{3,11},{11,3},{4,12},{12,4},... | collective-permute-start | bytes 24584 | tf_op jit(solution)/shard_map/cond/branch_1_fun/ppermute | solution.py:30
  152.3 19.8 %collective-permute-start.58 = (bf16[256,1024]{1,0:T(8,128)(2,1)}, bf16[256,1024]{1,0:T(8,128)(2,1)}, u32[]{:S(2)}, u32[]{:S(2)}) collective-permute-start(bf16[256,1024]{1,0:T(8,128)(2,1)} %get-tuple-element.733), channel_id=1, source_target_pairs={{0,8},{8,0},{1,9},{9,1},{2,10},{10,2},{3,11},{11,3},{4,12},{12,4},... | collective-permute-start | bytes 1572872 | tf_op jit(solution)/shard_map/ppermute | solution.py:30
  172.2 72.4 %collective-permute-start.59 = (bf16[1024,1024]{1,0:T(8,128)(2,1)}, bf16[1024,1024]{1,0:T(8,128)(2,1)}, u32[]{:S(2)}, u32[]{:S(2)}) collective-permute-start(bf16[1024,1024]{1,0:T(8,128)(2,1)} %all-gather.7.cloned.1.call-done), channel_id=1, source_target_pairs={{0,4},{4,0},{1,5},{5,1},{2,6},{6,2},{3,7},{7,3},{8,12},{12,8},{9,1... | collective-permute-start | bytes 6291464 | tf_op jit(solution)/shard_map/ppermute | solution.py:30
  176.3 322.5 %reduce-scatter.7.cloned.1.call-start = ((), (), s32[]{:S(2)}) async-start(), calls=%async_computation.10 | async-start | bytes 1572864 | tf_op jit(solution)/shard_map/reduce_scatter | solution.py:269
  176.3 113.4 %collective-permute-start.61 = (bf16[512,1024]{1,0:T(8,128)(2,1)}, bf16[512,1024]{1,0:T(8,128)(2,1)S(1)}, u32[]{:S(2)}, u32[]{:S(2)}) collective-permute-start(bf16[512,1024]{1,0:T(8,128)(2,1)} %pad_maximum_fusion.39), channel_id=1, source_target_pairs={{0,4},{4,0},{1,5},{5,1},{2,6},{6,2},{3,7},{7,3},{8,12},{12,8},{9,1... | collective-permute-start | bytes 3145736 | tf_op jit(solution)/shard_map/ppermute | solution.py:30
  180.2 33.5 %collective-permute-start.18 = (bf16[128,2048]{1,0:T(8,128)(2,1)S(1)}, bf16[128,2048]{1,0:T(8,128)(2,1)S(1)}, u32[]{:S(2)}, u32[]{:S(2)}) collective-permute-start(bf16[128,2048]{1,0:T(8,128)(2,1)S(1)} %pad_maximum_fusion.10), channel_id=1, source_target_pairs={{0,8},{8,0},{1,9},{9,1},{2,10},{10,2},{3,11},{11,3},{4,12},{12,4},... | collective-permute-start | bytes 1572872 | tf_op jit(solution)/shard_map/cond/branch_1_fun/ppermute | solution.py:30
  180.9 34.7 %collective-permute-start.20 = (bf16[128,2048]{1,0:T(8,128)(2,1)S(1)}, bf16[128,2048]{1,0:T(8,128)(2,1)S(1)}, u32[]{:S(2)}, u32[]{:S(2)}) collective-permute-start(bf16[128,2048]{1,0:T(8,128)(2,1)S(1)} %pad_maximum_fusion.11), channel_id=1, source_target_pairs={{0,2},{2,0},{1,3},{3,1},{4,6},{6,4},{5,7},{7,5},{8,10},{10,8},{9,1... | collective-permute-start | bytes 1572872 | tf_op jit(solution)/shard_map/cond/branch_1_fun/ppermute | solution.py:30
  213.8 7.5 %collective-permute-start.19 = (bf16[64,2048]{1,0:T(8,128)(2,1)S(1)}, bf16[64,2048]{1,0:T(8,128)(2,1)S(1)}, u32[]{:S(2)}, u32[]{:S(2)}) collective-permute-start(bf16[64,2048]{1,0:T(8,128)(2,1)S(1)} %slice.1479), channel_id=1, source_target_pairs={{0,2},{2,0},{1,3},{3,1},{4,6},{6,4},{5,7},{7,5},{8,10},{10,8},{9,1... | collective-permute-start | bytes 786440 | tf_op jit(solution)/shard_map/cond/branch_1_fun/ppermute | solution.py:30
  215.8 11.8 %collective-permute-start.21 = (bf16[64,2048]{1,0:T(8,128)(2,1)S(1)}, bf16[64,2048]{1,0:T(8,128)(2,1)S(1)}, u32[]{:S(2)}, u32[]{:S(2)}) collective-permute-start(bf16[64,2048]{1,0:T(8,128)(2,1)S(1)} %slice.1478), channel_id=1, source_target_pairs={{0,8},{8,0},{1,9},{9,1},{2,10},{10,2},{3,11},{11,3},{4,12},{12,4},... | collective-permute-start | bytes 786440 | tf_op jit(solution)/shard_map/cond/branch_1_fun/ppermute | solution.py:30
  230.3 14.2 %collective-permute-start.23 = (bf16[64,2048]{1,0:T(8,128)(2,1)}, bf16[64,2048]{1,0:T(8,128)(2,1)}, u32[]{:S(2)}, u32[]{:S(2)}) collective-permute-start(bf16[64,2048]{1,0:T(8,128)(2,1)} %get-tuple-element.1331), channel_id=1, source_target_pairs={{0,8},{8,0},{1,9},{9,1},{2,10},{10,2},{3,11},{11,3},{4,12},{12,4},... | collective-permute-start | bytes 786440 | tf_op jit(solution)/shard_map/cond/branch_1_fun/ppermute | solution.py:30
  232.7 11.8 %collective-permute-start.22 = (bf16[64,2048]{1,0:T(8,128)(2,1)}, bf16[64,2048]{1,0:T(8,128)(2,1)}, u32[]{:S(2)}, u32[]{:S(2)}) collective-permute-start(bf16[64,2048]{1,0:T(8,128)(2,1)} %get-tuple-element.1330), channel_id=1, source_target_pairs={{0,2},{2,0},{1,3},{3,1},{4,6},{6,4},{5,7},{7,5},{8,10},{10,8},{9,1... | collective-permute-start | bytes 786440 | tf_op jit(solution)/shard_map/cond/branch_1_fun/ppermute | solution.py:30
  247.0 42.7 %collective-permute-start.60 = (bf16[512,1024]{1,0:T(8,128)(2,1)}, bf16[512,1024]{1,0:T(8,128)(2,1)}, u32[]{:S(2)}, u32[]{:S(2)}) collective-permute-start(bf16[512,1024]{1,0:T(8,128)(2,1)} %constant_dynamic-slice_fusion.3), channel_id=1, source_target_pairs={{0,4},{4,0},{1,5},{5,1},{2,6},{6,2},{3,7},{7,3},{8,12},{12,8},{9,1... | collective-permute-start | bytes 3145736 | tf_op jit(solution)/shard_map/ppermute | solution.py:30
  249.5 11.3 %collective-permute-start.35 = (bf16[128,2048]{1,0:T(8,128)(2,1)S(1)}, bf16[128,2048]{1,0:T(8,128)(2,1)S(1)}, u32[]{:S(2)}, u32[]{:S(2)}) collective-permute-start(bf16[128,2048]{1,0:T(8,128)(2,1)S(1)} %pad_maximum_fusion.12), channel_id=1, source_target_pairs={{0,2},{2,0},{1,3},{3,1},{4,6},{6,4},{5,7},{7,5},{8,10},{10,8},{9,1... | collective-permute-start | bytes 1572872 | tf_op jit(solution)/shard_map/cond/branch_1_fun/ppermute | solution.py:30
  250.9 21.0 %collective-permute-start.36 = (bf16[128,2048]{1,0:T(8,128)(2,1)S(1)}, bf16[128,2048]{1,0:T(8,128)(2,1)S(1)}, u32[]{:S(2)}, u32[]{:S(2)}) collective-permute-start(bf16[128,2048]{1,0:T(8,128)(2,1)S(1)} %pad_maximum_fusion.13), channel_id=1, source_target_pairs={{0,8},{8,0},{1,9},{9,1},{2,10},{10,2},{3,11},{11,3},{4,12},{12,4},... | collective-permute-start | bytes 1572872 | tf_op jit(solution)/shard_map/cond/branch_1_fun/ppermute | solution.py:30
  292.4 25.6 %collective-permute-start.62 = (bf16[512,1024]{1,0:T(8,128)(2,1)}, bf16[512,1024]{1,0:T(8,128)(2,1)}, u32[]{:S(2)}, u32[]{:S(2)}) collective-permute-start(bf16[512,1024]{1,0:T(8,128)(2,1)} %constant_dynamic-slice_fusion.2), channel_id=1, source_target_pairs={{0,4},{4,0},{1,5},{5,1},{2,6},{6,2},{3,7},{7,3},{8,12},{12,8},{9,1... | collective-permute-start | bytes 3145736 | tf_op jit(solution)/shard_map/ppermute | solution.py:30
  333.2 14.0 %collective-permute-start.25 = (bf16[128,2048]{1,0:T(8,128)(2,1)S(1)}, bf16[128,2048]{1,0:T(8,128)(2,1)S(1)}, u32[]{:S(2)}, u32[]{:S(2)}) collective-permute-start(bf16[128,2048]{1,0:T(8,128)(2,1)S(1)} %pad_maximum_fusion.19), channel_id=1, source_target_pairs={{0,8},{8,0},{1,9},{9,1},{2,10},{10,2},{3,11},{11,3},{4,12},{12,4},... | collective-permute-start | bytes 1572872 | tf_op jit(solution)/shard_map/cond/branch_1_fun/ppermute | solution.py:30
  333.3 15.6 %collective-permute-start.27 = (bf16[128,2048]{1,0:T(8,128)(2,1)S(1)}, bf16[128,2048]{1,0:T(8,128)(2,1)S(1)}, u32[]{:S(2)}, u32[]{:S(2)}) collective-permute-start(bf16[128,2048]{1,0:T(8,128)(2,1)S(1)} %pad_maximum_fusion.20), channel_id=1, source_target_pairs={{0,2},{2,0},{1,3},{3,1},{4,6},{6,4},{5,7},{7,5},{8,10},{10,8},{9,1... | collective-permute-start | bytes 1572872 | tf_op jit(solution)/shard_map/cond/branch_1_fun/ppermute | solution.py:30
  347.4 7.6 %collective-permute-start.26 = (bf16[64,2048]{1,0:T(8,128)(2,1)S(1)}, bf16[64,2048]{1,0:T(8,128)(2,1)S(1)}, u32[]{:S(2)}, u32[]{:S(2)}) collective-permute-start(bf16[64,2048]{1,0:T(8,128)(2,1)S(1)} %slice.1481), channel_id=1, source_target_pairs={{0,2},{2,0},{1,3},{3,1},{4,6},{6,4},{5,7},{7,5},{8,10},{10,8},{9,1... | collective-permute-start | bytes 786440 | tf_op jit(solution)/shard_map/cond/branch_1_fun/ppermute | solution.py:30
  364.3 11.8 %collective-permute-start.31 = (bf16[128,2048]{1,0:T(8,128)(2,1)S(1)}, bf16[128,2048]{1,0:T(8,128)(2,1)S(1)}, u32[]{:S(2)}, u32[]{:S(2)}) collective-permute-start(bf16[128,2048]{1,0:T(8,128)(2,1)S(1)} %pad_maximum_fusion.21), channel_id=1, source_target_pairs={{0,2},{2,0},{1,3},{3,1},{4,6},{6,4},{5,7},{7,5},{8,10},{10,8},{9,1... | collective-permute-start | bytes 1572872 | tf_op jit(solution)/shard_map/cond/branch_1_fun/ppermute | solution.py:30
  365.9 10.6 %collective-permute-start.32 = (bf16[128,2048]{1,0:T(8,128)(2,1)S(1)}, bf16[128,2048]{1,0:T(8,128)(2,1)S(1)}, u32[]{:S(2)}, u32[]{:S(2)}) collective-permute-start(bf16[128,2048]{1,0:T(8,128)(2,1)S(1)} %pad_maximum_fusion.22), channel_id=1, source_target_pairs={{0,8},{8,0},{1,9},{9,1},{2,10},{10,2},{3,11},{11,3},{4,12},{12,4},... | collective-permute-start | bytes 1572872 | tf_op jit(solution)/shard_map/cond/branch_1_fun/ppermute | solution.py:30
  377.3 8.2 %collective-permute-start.33 = (bf16[512,2048]{1,0:T(8,128)(2,1)S(1)}, bf16[512,2048]{1,0:T(8,128)(2,1)S(1)}, u32[]{:S(2)}, u32[]{:S(2)}) collective-permute-start(bf16[512,2048]{1,0:T(8,128)(2,1)S(1)} %get-tuple-element.1208), channel_id=1, source_target_pairs={{0,1},{1,0},{2,3},{3,2},{4,5},{5,4},{6,7},{7,6},{8,9},{9,8},{10,11... | collective-permute-start | bytes 6291464 | tf_op jit(solution)/shard_map/cond/branch_1_fun/ppermute | solution.py:30
  391.2 27.9 %collective-permute-start.63 = (bf16[1024,512]{1,0:T(8,128)(2,1)}, bf16[1024,512]{1,0:T(8,128)(2,1)}, u32[]{:S(2)}, u32[]{:S(2)}) collective-permute-start(bf16[1024,512]{1,0:T(8,128)(2,1)} %get-tuple-element.783), channel_id=1, source_target_pairs={{0,4},{4,0},{1,5},{5,1},{2,6},{6,2},{3,7},{7,3},{8,12},{12,8},{9,1... | collective-permute-start | bytes 3145736 | tf_op jit(solution)/shard_map/ppermute | solution.py:30
  421.7 131.6 %reduce-scatter.9.cloned.1.call-start = ((), (), s32[]{:S(2)}) async-start(), calls=%async_computation.11 | async-start | bytes 1572864 | tf_op jit(solution)/shard_map/reduce_scatter | solution.py:269
  421.7 26.4 %collective-permute-start.65 = (bf16[1024,512]{1,0:T(8,128)(2,1)}, bf16[1024,512]{1,0:T(8,128)(2,1)}, u32[]{:S(2)}, u32[]{:S(2)}) collective-permute-start(bf16[1024,512]{1,0:T(8,128)(2,1)} %get-tuple-element.796), channel_id=1, source_target_pairs={{0,4},{4,0},{1,5},{5,1},{2,6},{6,2},{3,7},{7,3},{8,12},{12,8},{9,1... | collective-permute-start | bytes 3145736 | tf_op jit(solution)/shard_map/ppermute | solution.py:30
  422.7 76.1 %collective-permute-start.64 = (bf16[1024,1024]{1,0:T(8,128)(2,1)}, bf16[1024,1024]{1,0:T(8,128)(2,1)}, u32[]{:S(2)}, u32[]{:S(2)}) collective-permute-start(bf16[1024,1024]{1,0:T(8,128)(2,1)} %get-tuple-element.792), channel_id=1, source_target_pairs={{0,4},{4,0},{1,5},{5,1},{2,6},{6,2},{3,7},{7,3},{8,12},{12,8},{9,1... | collective-permute-start | bytes 6291464 | tf_op jit(solution)/shard_map/ppermute | solution.py:30
  433.4 10.5 %collective-permute-start.38 = (bf16[512,2048]{1,0:T(8,128)(2,1)S(1)}, bf16[512,2048]{1,0:T(8,128)(2,1)}, u32[]{:S(2)}, u32[]{:S(2)}) collective-permute-start(bf16[512,2048]{1,0:T(8,128)(2,1)S(1)} %convolution_add_fusion.1), channel_id=1, source_target_pairs={{0,1},{1,0},{2,3},{3,2},{4,5},{5,4},{6,7},{7,6},{8,9},{9,8},{10,11... | collective-permute-start | bytes 6291464 | tf_op jit(solution)/shard_map/cond/branch_1_fun/ppermute | solution.py:30
  450.6 154.7 %reduce-scatter.11.cloned.1.call-start = ((), (), s32[]{:S(2)}) async-start(), calls=%async_computation.12 | async-start | bytes 3145728 | tf_op jit(solution)/shard_map/reduce_scatter | solution.py:269
  453.5 19.0 %collective-permute-start.39 = (bf16[128,2048]{1,0:T(8,128)(2,1)S(1)}, bf16[128,2048]{1,0:T(8,128)(2,1)S(1)}, u32[]{:S(2)}, u32[]{:S(2)}) collective-permute-start(bf16[128,2048]{1,0:T(8,128)(2,1)S(1)} %pad_maximum_fusion.23), channel_id=1, source_target_pairs={{0,8},{8,0},{1,9},{9,1},{2,10},{10,2},{3,11},{11,3},{4,12},{12,4},... | collective-permute-start | bytes 1572872 | tf_op jit(solution)/shard_map/cond/branch_1_fun/ppermute | solution.py:30
  454.7 20.3 %collective-permute-start.40 = (bf16[128,2048]{1,0:T(8,128)(2,1)S(1)}, bf16[128,2048]{1,0:T(8,128)(2,1)S(1)}, u32[]{:S(2)}, u32[]{:S(2)}) collective-permute-start(bf16[128,2048]{1,0:T(8,128)(2,1)S(1)} %pad_maximum_fusion.24), channel_id=1, source_target_pairs={{0,2},{2,0},{1,3},{3,1},{4,6},{6,4},{5,7},{7,5},{8,10},{10,8},{9,1... | collective-permute-start | bytes 1572872 | tf_op jit(solution)/shard_map/cond/branch_1_fun/ppermute | solution.py:30
  472.7 11.0 %collective-permute-start.41 = (bf16[64,2048]{1,0:T(8,128)(2,1)S(1)}, bf16[64,2048]{1,0:T(8,128)(2,1)S(1)}, u32[]{:S(2)}, u32[]{:S(2)}) collective-permute-start(bf16[64,2048]{1,0:T(8,128)(2,1)S(1)} %slice.1483), channel_id=1, source_target_pairs={{0,2},{2,0},{1,3},{3,1},{4,6},{6,4},{5,7},{7,5},{8,10},{10,8},{9,1... | collective-permute-start | bytes 786440 | tf_op jit(solution)/shard_map/cond/branch_1_fun/ppermute | solution.py:30
  475.1 11.7 %collective-permute-start.42 = (bf16[64,2048]{1,0:T(8,128)(2,1)S(1)}, bf16[64,2048]{1,0:T(8,128)(2,1)S(1)}, u32[]{:S(2)}, u32[]{:S(2)}) collective-permute-start(bf16[64,2048]{1,0:T(8,128)(2,1)S(1)} %slice.1482), channel_id=1, source_target_pairs={{0,8},{8,0},{1,9},{9,1},{2,10},{10,2},{3,11},{11,3},{4,12},{12,4},... | collective-permute-start | bytes 786440 | tf_op jit(solution)/shard_map/cond/branch_1_fun/ppermute | solution.py:30
  503.6 141.3 %reduce-scatter.15.cloned.1.call-start = ((), (), s32[]{:S(2)}) async-start(), calls=%async_computation.14 | async-start | bytes 3145728 | tf_op jit(solution)/shard_map/reduce_scatter | solution.py:269
  503.7 49.7 %collective-permute-start.66 = (bf16[1024,1024]{1,0:T(8,128)(2,1)}, bf16[1024,1024]{1,0:T(8,128)(2,1)}, u32[]{:S(2)}, u32[]{:S(2)}) collective-permute-start(bf16[1024,1024]{1,0:T(8,128)(2,1)} %get-tuple-element.816), channel_id=1, source_target_pairs={{0,4},{4,0},{1,5},{5,1},{2,6},{6,2},{3,7},{7,3},{8,12},{12,8},{9,1... | collective-permute-start | bytes 6291464 | tf_op jit(solution)/shard_map/ppermute | solution.py:30
  505.9 9.8 %collective-permute-start.45 = (bf16[128,2048]{1,0:T(8,128)(2,1)S(1)}, bf16[128,2048]{1,0:T(8,128)(2,1)S(1)}, u32[]{:S(2)}, u32[]{:S(2)}) collective-permute-start(bf16[128,2048]{1,0:T(8,128)(2,1)S(1)} %pad_maximum_fusion.25), channel_id=1, source_target_pairs={{0,2},{2,0},{1,3},{3,1},{4,6},{6,4},{5,7},{7,5},{8,10},{10,8},{9,1... | collective-permute-start | bytes 1572872 | tf_op jit(solution)/shard_map/cond/branch_1_fun/ppermute | solution.py:30
  508.3 20.0 %collective-permute-start.46 = (bf16[128,2048]{1,0:T(8,128)(2,1)S(1)}, bf16[128,2048]{1,0:T(8,128)(2,1)S(1)}, u32[]{:S(2)}, u32[]{:S(2)}) collective-permute-start(bf16[128,2048]{1,0:T(8,128)(2,1)S(1)} %pad_maximum_fusion.26), channel_id=1, source_target_pairs={{0,8},{8,0},{1,9},{9,1},{2,10},{10,2},{3,11},{11,3},{4,12},{12,4},... | collective-permute-start | bytes 1572872 | tf_op jit(solution)/shard_map/cond/branch_1_fun/ppermute | solution.py:30
  557.8 134.2 %reduce-scatter.13.cloned.1.call-start = ((), (), s32[]{:S(2)}) async-start(), calls=%async_computation.13 | async-start | bytes 1572864 | tf_op jit(solution)/shard_map/reduce_scatter | solution.py:269
  561.3 8.7 %collective-permute-start.48 = (f32[2,2,2,2,128]{4,3,2,1,0:T(2,128)S(1)}, f32[2,2,2,2,128]{4,3,2,1,0:T(2,128)S(1)}, u32[]{:S(2)}, u32[]{:S(2)}) collective-permute-start(f32[2,2,2,2,128]{4,3,2,1,0:T(2,128)S(1)} %reshape.238), channel_id=1, source_target_pairs={{0,1},{1,0},{2,3},{3,2},{4,5},{5,4},{6,7},{7,6},{8,9},{9,8},{10,11... | collective-permute-start | bytes 24584 | tf_op jit(solution)/shard_map/cond/branch_1_fun/ppermute | solution.py:30
  580.6 24.7 %collective-permute-start.67 = (bf16[1024,512]{1,0:T(8,128)(2,1)}, bf16[1024,512]{1,0:T(8,128)(2,1)}, u32[]{:S(2)}, u32[]{:S(2)}) collective-permute-start(bf16[1024,512]{1,0:T(8,128)(2,1)} %copy.62), channel_id=1, source_target_pairs={{0,4},{4,0},{1,5},{5,1},{2,6},{6,2},{3,7},{7,3},{8,12},{12,8},{9,1... | collective-permute-start | bytes 3145736 | tf_op jit(solution)/shard_map/ppermute | solution.py:30
  609.3 82.7 %reduce-scatter.17.cloned.1.call-start = ((), (), s32[]{:S(2)}) async-start(), calls=%async_computation.15 | async-start | bytes 1572864 | tf_op jit(solution)/shard_map/reduce_scatter | solution.py:269
  609.4 35.5 %collective-permute-start.68 = (bf16[1024,512]{1,0:T(8,128)(2,1)}, bf16[1024,512]{1,0:T(8,128)(2,1)}, u32[]{:S(2)}, u32[]{:S(2)}) collective-permute-start(bf16[1024,512]{1,0:T(8,128)(2,1)} %get-tuple-element.850), channel_id=1, source_target_pairs={{0,4},{4,0},{1,5},{5,1},{2,6},{6,2},{3,7},{7,3},{8,12},{12,8},{9,1... | collective-permute-start | bytes 3145736 | tf_op jit(solution)/shard_map/ppermute | solution.py:30
  610.7 21.3 %collective-permute-start.69 = (bf16[256,1024]{1,0:T(8,128)(2,1)}, bf16[256,1024]{1,0:T(8,128)(2,1)}, u32[]{:S(2)}, u32[]{:S(2)}) collective-permute-start(bf16[256,1024]{1,0:T(8,128)(2,1)} %get-tuple-element.851), channel_id=1, source_target_pairs={{0,8},{8,0},{1,9},{9,1},{2,10},{10,2},{3,11},{11,3},{4,12},{12,4},... | collective-permute-start | bytes 1572872 | tf_op jit(solution)/shard_map/ppermute | solution.py:30
  612.8 32.2 %collective-permute-start.70 = (bf16[256,1024]{1,0:T(8,128)(2,1)}, bf16[256,1024]{1,0:T(8,128)(2,1)}, u32[]{:S(2)}, u32[]{:S(2)}) collective-permute-start(bf16[256,1024]{1,0:T(8,128)(2,1)} %slice_select_fusion.10), channel_id=1, source_target_pairs={{0,8},{8,0},{1,9},{9,1},{2,10},{10,2},{3,11},{11,3},{4,12},{12,4},... | collective-permute-start | bytes 1572872 | tf_op jit(solution)/shard_map/ppermute | solution.py:30
  621.5 10.4 %collective-permute-start.51 = (bf16[512,2048]{1,0:T(8,128)(2,1)}, bf16[512,2048]{1,0:T(8,128)(2,1)}, u32[]{:S(2)}, u32[]{:S(2)}) collective-permute-start(bf16[512,2048]{1,0:T(8,128)(2,1)} %convolution_convert_fusion.5), channel_id=1, source_target_pairs={{0,1},{1,0},{2,3},{3,2},{4,5},{5,4},{6,7},{7,6},{8,9},{9,8},{10,11... | collective-permute-start | bytes 6291464 | tf_op jit(solution)/shard_map/cond/branch_1_fun/ppermute | solution.py:30
  648.4 43.7 %collective-permute-start.71 = (bf16[256,1024]{1,0:T(8,128)(2,1)}, bf16[256,1024]{1,0:T(8,128)(2,1)}, u32[]{:S(2)}, u32[]{:S(2)}) collective-permute-start(bf16[256,1024]{1,0:T(8,128)(2,1)} %slice_select_fusion.9), channel_id=1, source_target_pairs={{0,8},{8,0},{1,9},{9,1},{2,10},{10,2},{3,11},{11,3},{4,12},{12,4},... | collective-permute-start | bytes 1572872 | tf_op jit(solution)/shard_map/ppermute | solution.py:30
  650.9 37.5 %collective-permute-start.17 = (f32[4,2048]{1,0:T(4,128)S(1)}, f32[4,2048]{1,0:T(4,128)S(1)}, u32[]{:S(2)}, u32[]{:S(2)}) collective-permute-start(f32[4,2048]{1,0:T(4,128)S(1)} %get-tuple-element.451), channel_id=1, source_target_pairs={{0,4},{4,0},{1,5},{5,1},{2,6},{6,2},{3,7},{7,3},{8,12},{12,8},{9,1... | collective-permute-start | bytes 98312 | tf_op jit(solution)/shard_map/cond/branch_1_fun/ppermute | solution.py:30
  657.5 26.8 %collective-permute-start.13 = (bf16[128,2048]{1,0:T(8,128)(2,1)}, bf16[128,2048]{1,0:T(8,128)(2,1)}, u32[]{:S(2)}, u32[]{:S(2)}) collective-permute-start(bf16[128,2048]{1,0:T(8,128)(2,1)} %pad_maximum_fusion.35), channel_id=1, source_target_pairs={{0,8},{8,0},{1,9},{9,1},{2,10},{10,2},{3,11},{11,3},{4,12},{12,4},... | collective-permute-start | bytes 1572872 | tf_op jit(solution)/shard_map/cond/branch_1_fun/ppermute | solution.py:30
  658.4 14.5 %collective-permute-start.14 = (bf16[128,2048]{1,0:T(8,128)(2,1)}, bf16[128,2048]{1,0:T(8,128)(2,1)}, u32[]{:S(2)}, u32[]{:S(2)}) collective-permute-start(bf16[128,2048]{1,0:T(8,128)(2,1)} %pad_maximum_fusion.36), channel_id=1, source_target_pairs={{0,2},{2,0},{1,3},{3,1},{4,6},{6,4},{5,7},{7,5},{8,10},{10,8},{9,1... | collective-permute-start | bytes 1572872 | tf_op jit(solution)/shard_map/cond/branch_1_fun/ppermute | solution.py:30
  674.1 15.1 %collective-permute-start.16 = (bf16[64,2048]{1,0:T(8,128)(2,1)S(1)}, bf16[64,2048]{1,0:T(8,128)(2,1)}, u32[]{:S(2)}, u32[]{:S(2)}) collective-permute-start(bf16[64,2048]{1,0:T(8,128)(2,1)S(1)} %slice.1484), channel_id=1, source_target_pairs={{0,8},{8,0},{1,9},{9,1},{2,10},{10,2},{3,11},{11,3},{4,12},{12,4},... | collective-permute-start | bytes 786440 | tf_op jit(solution)/shard_map/cond/branch_1_fun/ppermute | solution.py:30
  694.9 18.0 %collective-permute-start.73 = (bf16[256,512]{1,0:T(8,128)(2,1)}, bf16[256,512]{1,0:T(8,128)(2,1)}, u32[]{:S(2)}, u32[]{:S(2)}) collective-permute-start(bf16[256,512]{1,0:T(8,128)(2,1)} %broadcast_select_fusion.35), channel_id=1, source_target_pairs={{0,8},{8,0},{1,9},{9,1},{2,10},{10,2},{3,11},{11,3},{4,12},{12,4},... | collective-permute-start | bytes 786440 | tf_op jit(solution)/shard_map/ppermute | solution.py:30
  694.9 18.0 %collective-permute-start.72 = (bf16[256,512]{1,0:T(8,128)(2,1)S(1)}, bf16[256,512]{1,0:T(8,128)(2,1)}, u32[]{:S(2)}, u32[]{:S(2)}) collective-permute-start(bf16[256,512]{1,0:T(8,128)(2,1)S(1)} %broadcast_select_fusion.36), channel_id=1, source_target_pairs={{0,8},{8,0},{1,9},{9,1},{2,10},{10,2},{3,11},{11,3},{4,12},{12,4},... | collective-permute-start | bytes 786440 | tf_op jit(solution)/shard_map/ppermute | solution.py:30
  696.9 12.0 %collective-permute-start.3 = (f32[4,2048]{1,0:T(4,128)S(1)}, f32[4,2048]{1,0:T(4,128)S(1)}, u32[]{:S(2)}, u32[]{:S(2)}) collective-permute-start(f32[4,2048]{1,0:T(4,128)S(1)} %get-tuple-element.459), channel_id=1, source_target_pairs={{0,16},{16,0},{1,17},{17,1},{2,18},{18,2},{3,19},{19,3},{4,20},{20... | collective-permute-start | bytes 98312 | tf_op jit(solution)/shard_map/cond/branch_1_fun/ppermute | solution.py:30
  (94 other events, 816.2 us)
Sparse Core Ops, SparseCore 0:
  30.7 57.9 all-gather.4
  90.2 56.4 all-gather.6
  148.3 55.5 all-gather.8
  205.3 55.5 all-gather.10
  421.8 31.0 reduce-scatter.6
  455.1 31.5 reduce-scatter.8
  503.7 54.0 reduce-scatter.10
  560.7 54.3 reduce-scatter.14
  617.3 31.5 reduce-scatter.12
  651.7 30.4 reduce-scatter.16
